TPU v7x, 32 devices: a whole 2x2x4 slice. The times are simulated.
32 devices in a mesh: dp: 8 (over y, x, core), tensor: 4 (over z).
Axes of the slice: x: 2, y: 2, z: 4, core: 2. Of those that a mesh axis runs over, the one named last changes fastest.
Arguments:
- tokens: bfloat16 [16384, 768], P('dp'), may hold values from -6 to 6
- w_query: bfloat16 [768, 768], P(None, 'tensor'), may hold values from -0.21875 to 0.21875
- b_query: bfloat16 [768], P('tensor'), may hold values from -3 to 3
- w_key: bfloat16 [768, 768], P(None, 'tensor'), may hold values from -0.21875 to 0.21875
- w_value: bfloat16 [768, 768], P(None, 'tensor'), may hold values from -0.21875 to 0.21875
- b_value: bfloat16 [768], P('tensor'), may hold values from -3 to 3
- w_attn_out: bfloat16 [768, 768], P('tensor'), may hold values from -0.875 to 0.875
- b_attn_out: bfloat16 [768], replicated, may hold values from -3 to 3
- gain_one: bfloat16 [768], replicated, may hold values from 0.5 to 1.5
- shift_one: bfloat16 [768], replicated, may hold values from -2 to 2
- w_inner: bfloat16 [768, 3072], P(None, 'tensor'), may hold values from -0.21875 to 0.21875
- b_inner: bfloat16 [3072], P('tensor'), may hold values from -3 to 3
- w_outer: bfloat16 [3072, 768], P('tensor'), may hold values from -0.109375 to 0.109375
- b_outer: bfloat16 [768], replicated, may hold values from -3 to 3
- gain_two: bfloat16 [768], replicated, may hold values from 0.5 to 1.5
- shift_two: bfloat16 [768], replicated, may hold values from -2 to 2
- cotangent: bfloat16 [16384, 768], P('dp'), may hold values from -6 to 6
- lengths: int32 [32], P('dp'), may hold values from 1 to 512, 12288 in all
- row_ids: int32 [32, 512], P('dp'), may hold values from 0 to 63
- col_ids: int32 [32, 512], P('dp'), may hold values from 0 to 7
Outputs:
- layer_out: bfloat16 [16384, 768], P('dp')
- grad_tokens: bfloat16 [16384, 768], P('dp')
- grad_w_query: float32 [768, 768], P(None, 'tensor')
- grad_b_query: float32 [768], P('tensor')
- grad_w_key: float32 [768, 768], P(None, 'tensor')
- grad_w_value: float32 [768, 768], P(None, 'tensor')
- grad_b_value: float32 [768], P('tensor')
- grad_w_attn_out: float32 [768, 768], P('tensor')
- grad_b_attn_out: float32 [768], replicated
- grad_gain_one: float32 [768], replicated
- grad_shift_one: float32 [768], replicated
- grad_w_inner: float32 [768, 3072], P(None, 'tensor')
- grad_b_inner: float32 [3072], P('tensor')
- grad_w_outer: float32 [3072, 768], P('tensor')
- grad_b_outer: float32 [768], replicated
- grad_gain_two: float32 [768], replicated
- grad_shift_two: float32 [768], replicated
Inputs may be any that keep to these rules, and one draw needn't show every extreme that they name: `lengths`: the longest table in every draw has exactly 512 real tokens; positions from a table's length on are padding.
All inputs are finite; a program needn't handle non-finite values. No bound on the sum of `lengths` on one device may be relied on, other than what follows from the above.
Results may differ from a plain program's by a relative error of at most 0.022.
Values may be sent and summed in bfloat16 or wider, within the bound.
No kernel may reach another device: no remote copies, remote signals or barrier semaphores. Data moves between devices by JAX's collectives and lax.ppermute only.
A program may use at most 128 MiB of HBM per device.

v0:
```python
import functools

import jax
import jax.numpy as jnp
from jax import lax
from jax.experimental import pallas as pl
from jax.experimental.pallas import tpu as pltpu
from jax.sharding import PartitionSpec as P

F32 = jnp.float32
BF = jnp.bfloat16
HD = 64
D = 768
HALF = D // 2
BLOCKS = 4
QKV = 48
epsilon = 1e-12
masked_value = -1e30
CHUNK = 128
SCALE = 0.05
VECTORS = 16

NN = (((1,), (0,)), ((), ()))
NT = (((1,), (1,)), ((), ()))
TN = (((0,), (0,)), ((), ()))


def product(left, right, dims):
    return lax.dot_general(left, right, dims, preferred_element_type=F32)


def shape_of(shape, dtype):
    return jax.ShapeDtypeStruct(shape, dtype)


def whole(shape):
    return pl.BlockSpec(shape, lambda r, *_: (0,) * len(shape))


def each(shape, shift=0):
    return pl.BlockSpec((1,) + shape, lambda r, *_: (r + shift,) + (0,) * len(shape))


def params():
    return pltpu.CompilerParams(vmem_limit_bytes=24 * 1024 * 1024)


def cost(flops, moved, exps=0):
    return pl.CostEstimate(flops=int(flops * SCALE), bytes_accessed=int(moved * SCALE), transcendentals=int(exps))


def rows_of(ref, kind):
    width = 3 * QKV
    return jnp.concatenate(
        [ref[0, width * j + QKV * kind : width * j + QKV * (kind + 1)] for j in range(BLOCKS)], axis=0
    )


class Masks:
    def __init__(self, scalars, row_ref, col_ref):
        length, table = scalars[0], scalars[3]
        row_q = row_ref[pl.ds(table, 1), :].astype(F32)
        col_q = col_ref[pl.ds(table, 1), :].astype(F32)
        row_k, col_k = as_column(row_q), as_column(col_q)
        position = lax.broadcasted_iota(jnp.int32, row_k.shape, 0)
        self.here = position < length
        self.leading = position == 0
        self.row_k = jnp.where(self.here, row_k, -1.0)
        self.col_k = jnp.where(self.here, col_k, -1.0)
        self.row_q, self.col_q = row_q, col_q

    def scores(self, logits, kind):
        if kind == 0:
            visible = self.here
        elif kind == 1:
            visible = (self.row_k == self.row_q) | self.leading
        else:
            visible = (self.col_k == self.col_q) | self.leading
        return jnp.where(visible, logits, masked_value)


def as_column(row):
    return jnp.broadcast_to(row, (8, row.shape[1])).T[:, 0:1]


def projection_rows(w_ref):
    return jnp.concatenate([w_ref[0, 4 * QKV * j : 4 * QKV * j + 3 * QKV] for j in range(BLOCKS)], axis=0)


def output_rows(w_ref, shard=0):
    return jnp.concatenate(
        [w_ref[shard, 4 * QKV * j + 3 * QKV : 4 * QKV * (j + 1)] for j in range(BLOCKS)], axis=0
    )


def attention_forward_kernel(scalars, x_ref, w_ref, b_ref, row_ref, col_ref, *rest):
    qkv_ref, o_ref, lse_ref = rest[-3:]
    seq = x_ref.shape[0]
    bias = b_ref[0].astype(F32)
    bias = jnp.concatenate([bias[0:1], bias[1:2, : 3 * BLOCKS * QKV - HALF]], axis=1)
    qkv = product(projection_rows(w_ref), x_ref[...], NT) + as_column(bias)
    low = qkv.astype(BF)
    is_query = lax.broadcasted_iota(jnp.int32, (qkv.shape[0], 1), 0) % (3 * QKV) < QKV
    low = jnp.where(is_query, low * jnp.asarray(HD**-0.5, BF), low)
    qkv_ref[0] = low
    masks = Masks(scalars, row_ref, col_ref)
    q_t, k_t, v_t = rows_of(qkv_ref, 0), rows_of(qkv_ref, 1), rows_of(qkv_ref, 2)
    outs, logs = [], []
    for head in range(q_t.shape[0] // HD):
        rows = slice(HD * head, HD * (head + 1))
        scores = masks.scores(product(k_t[rows].T, q_t[rows], NN), head % 3)
        highest = jnp.max(scores, axis=0, keepdims=True)
        weights = jnp.exp(scores - highest).astype(BF)
        with_ones = jnp.concatenate([v_t[rows], jnp.ones((16, seq), BF)], axis=0)
        blended = product(with_ones, weights, NN)
        total = blended[HD : HD + 1]
        outs.append(blended[:HD] * (1.0 / total))
        logs.append(highest + jnp.log(total))
    o_ref[0] = jnp.concatenate(outs, axis=0).astype(BF)
    logs.append(jnp.zeros((8 - len(logs), seq), F32))
    lse_ref[0] = jnp.concatenate(logs, axis=0)


def in_hbm():
    return pl.BlockSpec(memory_space=pltpu.HBM)


def table_rows(seq):
    return pl.BlockSpec((seq, D), lambda r, scalars: (scalars[3], 0))


def bias_rows(shift=0):
    return pl.BlockSpec((1, VECTORS, HALF), lambda r, *_: (r + shift, 4 * QKV // VECTORS, 0))


def attention_forward(scalars, tokens, weights, pieces, tags, shards, first, carried=None):
    wide, seq = 3 * BLOCKS * QKV, tags[0].shape[1]
    count, at = pieces.shape[0], first if carried else 0
    out_shape = [
        shape_of((shards, wide, seq), BF),
        shape_of((shards, wide // 3, seq), BF),
        shape_of((shards, 8, seq), F32),
    ]
    kept = list(carried) if carried else []
    return pl.pallas_call(
        attention_forward_kernel,
        grid_spec=pltpu.PrefetchScalarGridSpec(
            num_scalar_prefetch=1,
            grid=(count,),
            in_specs=[
                table_rows(seq),
                each((weights.shape[1], D), at),
                bias_rows(),
                whole(tags[0].shape),
                whole(tags[1].shape),
            ]
            + [pl.BlockSpec(memory_space=pl.ANY)] * len(kept),
            out_specs=[each(s.shape[1:], first) for s in out_shape],
        ),
        out_shape=out_shape,
        input_output_aliases={6 + i: i for i in range(len(kept))},
        compiler_params=params(),
        cost_estimate=cost(count * 3e9, count * 3e6),
    )(scalars, tokens, weights, pieces, *tags, *kept)


def attention_backward_kernel(
    scalars, x_hbm, w_hbm, qkv_hbm, o_hbm, lse_hbm, up_hbm, start_hbm, row_ref, col_ref, dbi_ref, one_ref, two_ref,
    *refs, shard, carried,
):
    dx_ref, mine_ref, other_ref, d_ref, x_ref, w_ref, qkv_ref, o_ref, lse_ref, low_ref, start_ref, sems = refs[carried:]
    seq = x_ref.shape[0]
    at = pl.ds(shard, 1)
    copies = [
        (w_hbm.at[at], w_ref),
        (up_hbm, low_ref),
        (qkv_hbm.at[at], qkv_ref),
        (o_hbm.at[at], o_ref),
        (lse_hbm.at[at], lse_ref),
        (x_hbm.at[pl.ds(pl.multiple_of(scalars[3] * seq, 128), seq)], x_ref),
        (start_hbm, start_ref),
    ]
    started = [pltpu.make_async_copy(source, target, sems.at[i]) for i, (source, target) in enumerate(copies)]
    for copy in started:
        copy.start()
    for copy in started[:5]:
        copy.wait()
    masks = Masks(scalars, row_ref, col_ref)
    q_t, k_t, v_t = rows_of(qkv_ref, 0), rows_of(qkv_ref, 1), rows_of(qkv_ref, 2)
    grad_heads = product(output_rows(w_ref), low_ref[...], NT).astype(BF)
    heads_out = o_ref[0]
    parts = [[], [], []]
    for head in range(q_t.shape[0] // HD):
        rows = slice(HD * head, HD * (head + 1))
        queries_t, keys_t, grad_t = q_t[rows], k_t[rows], grad_heads[rows]
        scores = masks.scores(product(keys_t.T, queries_t, NN), head % 3)
        chances = jnp.exp(scores - lse_ref[0, head : head + 1])
        grad_chances = product(v_t[rows].T, grad_t, NN)
        inner = jnp.sum(grad_t.astype(F32) * heads_out[rows].astype(F32), axis=0, keepdims=True)
        grad_logits = (chances * (grad_chances - inner)).astype(BF)
        parts[2].append(product(chances.astype(BF), grad_t.T, NN).T)
        parts[1].append(product(grad_logits, queries_t.T, NN).T)
        parts[0].append(product(keys_t, grad_logits, NN) * HD**-0.5)
    for kind in range(3):
        joined = jnp.concatenate(parts[kind], axis=0).astype(BF)
        for j in range(BLOCKS):
            base = 3 * QKV * j + QKV * kind
            d_ref[base : base + QKV, :] = joined[QKV * j : QKV * (j + 1)]
    grads_low = d_ref[...]
    for copy in started[5:]:
        copy.wait()
    dx_ref[...] = (start_ref[...] + product(grads_low, projection_rows(w_ref), TN)).astype(dx_ref.dtype)
    db = product(jnp.ones((8, seq), BF), grads_low, NT)[:1]
    vectors = [dbi_ref[0, :, :HALF], dbi_ref[0, :, HALF:], db[:, :HALF]]
    vectors.append(jnp.concatenate([db[:, HALF:], jnp.zeros((1, 2 * HALF - db.shape[1]), F32)], axis=1))
    for sums_ref in (one_ref, two_ref):
        for i in range(3):
            vectors += [sums_ref[i : i + 1, :HALF], sums_ref[i : i + 1, HALF:]]
    vectors = jnp.concatenate(vectors, axis=0).astype(BF)
    c, my = scalars[1], scalars[2]
    for half, out_ref in enumerate((mine_ref, other_ref)):
        start = pl.multiple_of(jnp.where(c == half, 0, HALF), 128)
        grad_w = product(grads_low, x_ref[:, pl.ds(start, HALF)], NN).astype(BF)
        grad_wo = product(heads_out, low_ref[:, pl.ds(start, HALF)], NN).astype(BF)
        for j in range(BLOCKS):
            out_ref[j ^ my, 0, : 3 * QKV] = grad_w[3 * QKV * j : 3 * QKV * (j + 1)]
            out_ref[j ^ my, 0, 3 * QKV : 4 * QKV] = grad_wo[QKV * j : QKV * (j + 1)]
            here = jnp.where(c == half, 1.0, 0.0).astype(BF) if j == 0 else jnp.zeros((), BF)
            out_ref[j ^ my, 0, 4 * QKV :] = vectors * here


def attention_backward(
    scalars, tokens, weights, qkv, heads_out, lse, upstream, start, tags, vectors, shard, dtype, carried
):
    shards, wide, seq = qkv.shape
    rows = 4 * QKV + VECTORS
    pieces = shape_of((BLOCKS, shards, rows, HALF), BF)
    piece = pl.BlockSpec((BLOCKS, 1, rows, HALF), lambda r, *_: (0, shard, 0, 0))
    return pl.pallas_call(
        functools.partial(attention_backward_kernel, shard=shard, carried=len(carried)),
        grid_spec=pltpu.PrefetchScalarGridSpec(
            num_scalar_prefetch=1,
            grid=(1,),
            in_specs=[in_hbm()] * 7
            + [whole(tags[0].shape), whole(tags[1].shape), each(vectors[0].shape[1:], shard)]
            + [whole((8, D)), whole((8, D))]
            + [in_hbm()] * len(carried),
            out_specs=[whole((seq, D)), piece, piece],
            scratch_shapes=[
                pltpu.VMEM((wide, seq), BF),
                pltpu.VMEM((seq, D), BF),
                pltpu.VMEM((1,) + weights.shape[1:], BF),
                pltpu.VMEM((1, wide, seq), BF),
                pltpu.VMEM((1, wide // 3, seq), BF),
                pltpu.VMEM((1, 8, seq), F32),
                pltpu.VMEM((seq, D), BF),
                pltpu.VMEM((seq, D), F32),
                pltpu.SemaphoreType.DMA((7,)),
            ],
        ),
        out_shape=[shape_of((seq, D), dtype), pieces, pieces],
        input_output_aliases={13 + i: 1 + i for i in range(len(carried))},
        compiler_params=params(),
        cost_estimate=cost(5e9, 5e6),
    )(scalars, tokens, weights, qkv, heads_out, lse, upstream, start, *tags, *vectors, *carried)


def gelu_pair(x):
    bell = jnp.exp(x * x * -0.5)
    t = 1.0 / (1.0 + (0.3275911 * 0.70710678118654752) * jnp.abs(x))
    series = 0.5 * 1.061405429
    for factor in (-1.453152027, 1.421413741, -0.284496736, 0.254829592):
        series = series * t + 0.5 * factor
    tail = series * t * bell
    below = jnp.where(x < 0, tail, 1.0 - tail)
    return x * below, below + x * (bell * 0.3989422804014327)


def normalize(residual):
    centre = residual - jnp.mean(residual, axis=-1, keepdims=True)
    inv_spread = lax.rsqrt(jnp.mean(centre * centre, axis=-1, keepdims=True) + epsilon)
    return centre * inv_spread, inv_spread


def norm_back(upstream, normed, inv_spread, gain):
    scaled = upstream * gain
    return inv_spread * (
        scaled
        - jnp.mean(scaled, axis=-1, keepdims=True)
        - normed * jnp.mean(scaled * normed, axis=-1, keepdims=True)
    )


def add_sums(sums, *terms):
    return [total + jnp.sum(term, axis=0, keepdims=True) for total, term in zip(sums, terms)]


def store_sums(ref, sums):
    ref[...] = jnp.concatenate(sums + [jnp.zeros((8 - len(sums), D), F32)], axis=0)


def inner_kernel(
    scalars, o_ref, wo_ref, x_ref, vec_ref, wi_ref, own_ref, others_ref,
    normed_ref, inv_ref, hidden_ref, low_ref, act_ref, slope_ref,
):
    seq, r = x_ref.shape[0], pl.program_id(0)
    bias = jnp.where(r == 0, own_ref[0].astype(F32), others_ref[jnp.maximum(r - 1, 0)].astype(F32))
    bias = jnp.concatenate([bias[2:3], bias[3:4]], axis=1)

    @pl.when(r == 0)
    def _():
        for start in range(0, seq, CHUNK):
            rows = slice(start, start + CHUNK)
            residual = vec_ref[0:1] + x_ref[rows].astype(F32)
            for shard in range(o_ref.shape[0]):
                residual = residual + product(o_ref[shard, :, rows], output_rows(wo_ref, shard), TN)
            normed, inv_spread = normalize(residual)
            hidden = normed * vec_ref[1:2] + vec_ref[2:3]
            normed_ref[rows], inv_ref[rows], hidden_ref[rows] = normed, inv_spread, hidden
            low_ref[rows] = hidden.astype(BF)

    for start in range(0, seq, CHUNK):
        rows = slice(start, start + CHUNK)
        act, slope = gelu_pair(product(low_ref[rows], wi_ref[0], NT) + bias)
        act_ref[0, rows] = act.astype(BF)
        slope_ref[0, rows] = slope.astype(BF)


def inner_half(scalars, heads_out, w_out, tokens, vectors, w_inner, own_piece, pieces):
    shards, wide, seq = w_inner.shape[0], w_inner.shape[1], heads_out.shape[2]
    return pl.pallas_call(
        inner_kernel,
        grid_spec=pltpu.PrefetchScalarGridSpec(
            num_scalar_prefetch=1,
            grid=(shards,),
            in_specs=[
                whole(heads_out.shape),
                whole(w_out.shape),
                table_rows(seq),
                whole(vectors.shape),
                each((wide, D)),
                pl.BlockSpec((1, VECTORS, HALF), lambda r, *_: (0, 4 * QKV // VECTORS, 0)),
                pl.BlockSpec((shards - 1, VECTORS, HALF), lambda r, *_: (0, 4 * QKV // VECTORS, 0)),
            ],
            out_specs=[
                whole((seq, D)),
                whole((seq, 1)),
                whole((seq, D)),
                whole((seq, D)),
                each((seq, wide)),
                each((seq, wide)),
            ],
        ),
        out_shape=[
            shape_of((seq, D), F32),
            shape_of((seq, 1), F32),
            shape_of((seq, D), F32),
            shape_of((seq, D), BF),
            shape_of((shards, seq, wide), BF),
            shape_of((shards, seq, wide), BF),
        ],
        compiler_params=params(),
        cost_estimate=cost(12e9, 20e6),
    )(scalars, heads_out, w_out, tokens, vectors, w_inner, own_piece, pieces)


def outer_kernel(scalars, act_ref, wu_ref, hidden_ref, cot_ref, vec_ref, out_ref, grad_ref, sums_ref, acc_ref):
    r, last, seq = pl.program_id(0), pl.num_programs(0) - 1, hidden_ref.shape[0]

    @pl.when(r == 0)
    def _():
        acc_ref[...] = hidden_ref[...] + vec_ref[0:1]

    acc_ref[...] = acc_ref[...] + product(act_ref[0], wu_ref[0], NN)

    @pl.when(r == last)
    def _():
        sums = [jnp.zeros((1, D), F32)] * 3
        gain = vec_ref[1:2]
        for start in range(0, seq, CHUNK):
            rows = slice(start, start + CHUNK)
            normed, inv_spread = normalize(acc_ref[rows])
            out_ref[rows] = (normed * gain + vec_ref[2:3]).astype(BF)
            upstream = cot_ref[rows].astype(F32)
            grad = norm_back(upstream, normed, inv_spread, gain)
            grad_ref[rows] = grad
            sums = add_sums(sums, upstream * normed, upstream, grad)
        store_sums(sums_ref, sums)


def outer_half(scalars, act, w_outer, hidden, cotangent, vectors):
    shards, seq, wide = act.shape
    return pl.pallas_call(
        outer_kernel,
        grid_spec=pltpu.PrefetchScalarGridSpec(
            num_scalar_prefetch=1,
            grid=(shards,),
            in_specs=[
                each((seq, wide)),
                each((wide, D)),
                whole((seq, D)),
                table_rows(seq),
                whole(vectors.shape),
            ],
            out_specs=[whole((seq, D)), whole((seq, D)), whole((8, D))],
            scratch_shapes=[pltpu.VMEM((seq, D), F32)],
        ),
        out_shape=[shape_of((seq, D), BF), shape_of((seq, D), F32), shape_of((8, D), F32)],
        compiler_params=params(),
        cost_estimate=cost(5e9, 14e6),
    )(scalars, act, w_outer, hidden, cotangent, vectors)


def ffn_back_kernel(
    up_ref, slope_ref, wu_ref, wi_ref, normed_ref, inv_ref, vec_ref, grad_ref, grad_low_ref, inner_ref, db_ref, sums_ref,
    acc_ref, low_ref,
):
    r, last = pl.program_id(0), pl.num_programs(0) - 1
    seq, wide = up_ref.shape[0], wi_ref.shape[1]

    @pl.when(r == 0)
    def _():
        acc_ref[...] = up_ref[...]
        low_ref[...] = up_ref[...].astype(BF)

    db = jnp.zeros((1, wide), F32)
    for start in range(0, seq, CHUNK):
        rows = slice(start, start + CHUNK)
        grad_inner = product(low_ref[rows], wu_ref[0], NT) * slope_ref[0, rows].astype(F32)
        db = db + jnp.sum(grad_inner, axis=0, keepdims=True)
        inner_ref[0, rows] = grad_inner.astype(BF)
    db_ref[0] = db
    acc_ref[...] = acc_ref[...] + product(inner_ref[0], wi_ref[0], NN)

    @pl.when(r == last)
    def _():
        sums = [jnp.zeros((1, D), F32)] * 3
        for start in range(0, seq, CHUNK):
            rows = slice(start, start + CHUNK)
            upstream, normed = acc_ref[rows], normed_ref[rows]
            grad = norm_back(upstream, normed, inv_ref[rows], vec_ref[1:2])
            grad_ref[rows] = grad
            grad_low_ref[rows] = grad.astype(BF)
            sums = add_sums(sums, upstream * normed, upstream, grad)
        store_sums(sums_ref, sums)


def ffn_back(upstream, slope, w_outer, w_inner, normed, inv_spread, vectors):
    shards, seq, wide = slope.shape
    return pl.pallas_call(
        ffn_back_kernel,
        grid=(shards,),
        in_specs=[
            whole((seq, D)),
            each((seq, wide)),
            each((wide, D)),
            each((wide, D)),
            whole((seq, D)),
            whole((seq, 1)),
            whole(vectors.shape),
        ],
        out_specs=[whole((seq, D)), whole((seq, D)), each((seq, wide)), each((1, wide)), whole((8, D))],
        out_shape=[
            shape_of((seq, D), F32),
            shape_of((seq, D), BF),
            shape_of((shards, seq, wide), BF),
            shape_of((shards, 1, wide), F32),
            shape_of((8, D), F32),
        ],
        scratch_shapes=[pltpu.VMEM((seq, D), F32), pltpu.VMEM((seq, D), BF)],
        compiler_params=params(),
        cost_estimate=cost(shards * 3e9, shards * 4e6),
    )(upstream, slope, w_outer, w_inner, normed, inv_spread, vectors)


def weight_grad_kernel(scalars, left_ref, right_ref, mine_ref, other_ref, low_ref):
    @pl.when(pl.program_id(0) == 0)
    def _():
        low_ref[...] = right_ref[...].astype(BF)

    c, my = scalars[1], scalars[2]
    rows = mine_ref.shape[2]
    for half, out_ref in enumerate((mine_ref, other_ref)):
        start = pl.multiple_of(jnp.where(c == half, 0, HALF), 128)
        grad = product(left_ref[0], low_ref[:, pl.ds(start, HALF)], TN).astype(BF)
        for j in range(BLOCKS):
            out_ref[j ^ my, 0] = grad[rows * j : rows * (j + 1)]


def weight_grad(scalars, left, right):
    shards, seq, wide = left.shape
    piece = pl.BlockSpec((BLOCKS, 1, wide // BLOCKS, HALF), lambda r, *_: (0, r, 0, 0))
    pieces = shape_of((BLOCKS, shards, wide // BLOCKS, HALF), BF)
    return pl.pallas_call(
        weight_grad_kernel,
        grid_spec=pltpu.PrefetchScalarGridSpec(
            num_scalar_prefetch=1,
            grid=(shards,),
            in_specs=[each((seq, wide)), whole((seq, D))],
            out_specs=[piece, piece],
            scratch_shapes=[pltpu.VMEM((seq, D), BF)],
        ),
        out_shape=[pieces, pieces],
        compiler_params=params(),
        cost_estimate=cost(shards * 1.5e9, shards * 2e6),
    )(scalars, left, right)


def run_copies(copies, sems):
    started = [pltpu.make_async_copy(source, target, sems.at[i]) for i, (source, target) in enumerate(copies)]
    for copy in started:
        copy.start()
    for copy in started:
        copy.wait()


def any_place():
    return pl.BlockSpec(memory_space=pl.ANY)


def slab_places(first, columns):
    col = lax.broadcasted_iota(jnp.int32, (columns, BLOCKS * QKV), 0) + first
    feature = lax.broadcasted_iota(jnp.int32, (columns, BLOCKS * QKV), 1)
    block = sum((feature >= QKV * j).astype(jnp.int32) for j in range(1, BLOCKS))
    return lambda kind: (col == feature + block * 2 * QKV + QKV * kind).astype(BF)


def attention_piece(scalars, w_query, w_key, w_value, w_out, bias):
    heads = BLOCKS * QKV

    def kernel(scalars, *refs):
        *w_refs, bias_ref, slab_ref, piece_ref = refs
        for j in range(BLOCKS):
            for kind, w_ref in enumerate(w_refs):
                base = QKV * (4 * j + kind)
                slab_ref[0, base : base + QKV] = w_ref[QKV * j : QKV * (j + 1)]
        c, my = scalars[1], scalars[2]
        rows = pl.ds(pl.multiple_of(my * 4 * QKV, 16), 4 * QKV)
        piece_ref[0, : 4 * QKV] = slab_ref[0, rows, pl.ds(pl.multiple_of(c * HALF, 128), HALF)]
        every = jnp.broadcast_to(bias_ref[...], (16, bias_ref.shape[1]))
        of_query, of_value = every[:, :heads], every[:, heads : 2 * heads]
        low = []
        for first in (0, HALF):
            places = slab_places(first, HALF)
            low.append(product(of_query, places(0), NT) + product(of_value, places(2), NT))
        inner = every[:, 2 * heads :].astype(F32)
        rows = [low[0], low[1], inner[:, :HALF], inner[:, HALF:]]
        at = lax.broadcasted_iota(jnp.int32, (16, HALF), 0)
        piece_ref[0, 4 * QKV :] = sum(jnp.where(at == i, row, 0.0) for i, row in enumerate(rows)).astype(BF)

    weights = (w_query.T, w_key.T, w_value.T, w_out)
    return pl.pallas_call(
        kernel,
        grid_spec=pltpu.PrefetchScalarGridSpec(
            num_scalar_prefetch=1,
            grid=(1,),
            in_specs=[whole(w.shape) for w in weights] + [whole(bias.shape)],
            out_specs=[whole((1, 4 * heads, D)), whole((1, 4 * QKV + VECTORS, HALF))],
        ),
        out_shape=[shape_of((1, 4 * heads, D), BF), shape_of((1, 4 * QKV + VECTORS, HALF), BF)],
        compiler_params=params(),
        cost_estimate=cost(2e9, 0),
    )(scalars, *weights, bias)


def ffn_pieces(scalars, w_inner, w_outer):
    wide = w_inner.shape[1]
    rows = wide // BLOCKS

    def kernel(scalars, wi_ref, wu_ref, wt_ref, i_ref, u_ref):
        wt_ref[...] = wi_ref[...].T
        c, my = scalars[1], scalars[2]
        block = pl.ds(pl.multiple_of(my * rows, 16), rows)
        columns = pl.ds(pl.multiple_of(c * HALF, 128), HALF)
        i_ref[...] = wt_ref[block, columns]
        u_ref[...] = wu_ref[block, columns]

    return pl.pallas_call(
        kernel,
        grid_spec=pltpu.PrefetchScalarGridSpec(
            num_scalar_prefetch=1,
            grid=(1,),
            in_specs=[whole(w_inner.shape), whole(w_outer.shape)],
            out_specs=[whole((wide, D)), whole((rows, HALF)), whole((rows, HALF))],
        ),
        out_shape=[shape_of((wide, D), BF), shape_of((rows, HALF), BF), shape_of((rows, HALF), BF)],
        compiler_params=params(),
        cost_estimate=cost(2e9, 0),
    )(scalars, w_inner, w_outer)


def assemble(scalars, near, far, own, rows):
    count = near.shape[1]

    def kernel(scalars, near_ref, far_ref, own_ref, out_ref, sems):
        c, my = scalars[1], scalars[2]
        copies = [(own_ref, out_ref.at[0])]
        for m in range(BLOCKS):
            for source, side in ((near_ref, c), (far_ref, 1 - c)):
                target = out_ref.at[
                    pl.ds(1, count),
                    pl.ds(pl.multiple_of((m ^ my) * rows, 16), rows),
                    pl.ds(pl.multiple_of(side * HALF, 128), HALF),
                ]
                copies.append((source.at[m, :, pl.ds(0, rows)], target))
        run_copies(copies, sems)

    shape = (1 + count, BLOCKS * rows, D)
    return pl.pallas_call(
        kernel,
        grid_spec=pltpu.PrefetchScalarGridSpec(
            num_scalar_prefetch=1,
            grid=(1,),
            in_specs=[any_place()] * 3,
            out_specs=whole(shape),
            scratch_shapes=[pltpu.SemaphoreType.DMA((2 * BLOCKS + 1,))],
        ),
        out_shape=shape_of(shape, own.dtype),
        compiler_params=params(),
        cost_estimate=cost(2e9, 0),
    )(scalars, near, far, own)


def finish(scalars, near, far, wide, narrow):
    total, base = near.shape[1], 4 * narrow

    def kernel(scalars, near_ref, far_ref, *refs):
        *outs, held, sems = refs
        c, my = scalars[1], scalars[2]
        copies = []
        for m in range(BLOCKS):
            for source, side in ((near_ref, c), (far_ref, 1 - c)):
                copies.append((source.at[m], held.at[m ^ my, :, pl.ds(pl.multiple_of(side * HALF, 128), HALF)]))
        run_copies(copies, sems)
        for kind in range(4):
            for j in range(BLOCKS):
                outs[kind][narrow * j : narrow * (j + 1)] = held[j, narrow * kind : narrow * (kind + 1)].astype(F32)
        for j in range(BLOCKS):
            at = base + VECTORS
            outs[4][wide * j : wide * (j + 1)] = held[j, at : at + wide].astype(F32)
        last = jnp.concatenate([held[j, base + VECTORS + wide :] for j in range(BLOCKS)], axis=0)
        outs[5][...] = last.astype(F32).T
        low = held[0, base : base + VECTORS, :HALF]
        vectors = low.astype(F32)
        for out, kind in zip(outs[6:8], (0, 2)):
            halves = [product(low, slab_places(first, HALF)(kind), NN) for first in (0, HALF)]
            out[...] = halves[0][2:3] + halves[1][3:4]
        for out, i in zip(outs[8:], (0, 4, 6, 8, 10, 12, 14)):
            out[...] = jnp.concatenate([vectors[i : i + 1], vectors[i + 1 : i + 2]], axis=1)

    heads = BLOCKS * narrow
    shapes = [(heads, D)] * 4 + [(BLOCKS * wide, D), (D, BLOCKS * wide)] + [(1, heads)] * 2 + [(1, D)] * 7
    return pl.pallas_call(
        kernel,
        grid_spec=pltpu.PrefetchScalarGridSpec(
            num_scalar_prefetch=1,
            grid=(1,),
            in_specs=[any_place()] * 2,
            out_specs=[whole(shape) for shape in shapes],
            scratch_shapes=[pltpu.VMEM((BLOCKS, total, D), BF), pltpu.SemaphoreType.DMA((2 * BLOCKS,))],
        ),
        out_shape=[shape_of(shape, F32) for shape in shapes],
        compiler_params=params(),
        cost_estimate=cost(2e9, 0),
    )(scalars, near, far)


def core_add(mine, theirs):
    _, shards, rows, columns = mine.shape
    half = shards // 2

    def kernel(mine_ref, theirs_ref, own_ref, x_ref, y_ref, first_ref, second_ref):
        r = pl.program_id(0)
        total = lambda m: (mine_ref[m, 0].astype(F32) + theirs_ref[m, 0].astype(F32)).astype(BF)
        own_ref[0], x_ref[0], y_ref[0] = total(0), total(1), total(2)

        @pl.when(r < half)
        def _():
            first_ref[0] = total(3)

        @pl.when(r >= half)
        def _():
            second_ref[0] = total(3)

    blocks = pl.BlockSpec((BLOCKS, 1, rows, columns), lambda r: (0, r, 0, 0))
    block = lambda index: pl.BlockSpec((1, rows, columns), lambda r: (index(r), 0, 0))
    return pl.pallas_call(
        kernel,
        grid=(shards,),
        in_specs=[blocks, blocks],
        out_specs=[block(lambda r: r)] * 3
        + [block(lambda r: jnp.minimum(r, half - 1)), block(lambda r: jnp.maximum(r - half, 0))],
        out_shape=[shape_of((shards, rows, columns), BF)] * 3 + [shape_of((half, rows, columns), BF)] * 2,
        compiler_params=params(),
        cost_estimate=cost(1e9, 0),
    )(mine, theirs)


def plane_add(for_x, for_y, via_y, via_x):
    half, rows, columns = via_y.shape

    def kernel(x_ref, y_ref, via_y_ref, via_x_ref, x_out, y_out):
        x_out[...] = (x_ref[...].astype(F32) + via_y_ref[...].astype(F32)).astype(BF)
        y_out[...] = (y_ref[...].astype(F32) + via_x_ref[...].astype(F32)).astype(BF)

    block = lambda shift: pl.BlockSpec((1, rows, columns), lambda r: (r + shift, 0, 0))
    return pl.pallas_call(
        kernel,
        grid=(half,),
        in_specs=[block(0), block(half), block(0), block(0)],
        out_specs=[block(0), block(half)],
        out_shape=[shape_of(for_x.shape, BF)] * 2,
        input_output_aliases={0: 0, 1: 1},
        compiler_params=params(),
        cost_estimate=cost(1e9, 0),
    )(for_x, for_y, via_y, via_x)


def tie(array, *before):
    return lax.optimization_barrier((array,) + before)[0]


def build(n_dp, n_tensor):
    flip = {bit: [(i, i ^ bit) for i in range(n_dp)] for bit in (1, 2, 4, 6)}
    f32 = lambda array: array.astype(F32)
    half = n_tensor // 2

    def across(array, bit):
        return lax.ppermute(array, "dp", flip[bit])

    def along(array, r):
        return lax.ppermute(array, "tensor", [(i, i ^ r) for i in range(n_tensor)])

    def from_all(array):
        return [along(array, r) for r in range(1, n_tensor)]

    def from_all_by_steps(array):
        two = along(array, 2)
        one, three = along(jnp.stack([array, two]), 1)
        return [one, two, three]

    def plane(array):
        return [across(array, bit) for bit in (2, 4, 6)]

    def rows_round(k, up, down):
        up = lax.ppermute(up, "tensor", [(i, i + 1) for i in range(k - 1, n_tensor - 1)])
        return up, lax.ppermute(down, "tensor", [(i + 1, i) for i in range(n_tensor - k)])

    def place_rows(z, own, ups, downs):
        seq = own.shape[0]
        rows = jnp.zeros((n_tensor * seq, D), own.dtype)
        rows = lax.dynamic_update_slice(rows, own, (z * seq, 0))
        for k in (2, 1, 3):
            got = jnp.where(z >= k, ups[k - 1], downs[n_tensor - 1 - k])
            rows = lax.dynamic_update_slice(rows, got, (((z - k) & (n_tensor - 1)) * seq, 0))
        return rows

    def add(*terms):
        return sum(f32(term) for term in terms).astype(BF)

    def plane_one(diagonal_y, diagonal_x):
        return across(diagonal_y, 4), across(diagonal_x, 2)

    def plane_two(for_x, for_y):
        return across(for_x, 2), across(for_y, 4)

    def line_ends(far):
        return lax.ppermute(far, "tensor", [(0, 1), (3, 2)])

    def line_middle(far):
        return lax.ppermute(far, "tensor", [(1, 2), (2, 1)])

    def line_end(own, last):
        total = own + f32(last)
        step = 8
        while step < n_dp:
            total = total + lax.ppermute(total, "dp", [(i, i ^ step) for i in range(n_dp)])
            step *= 2
        return total.astype(BF)

    def body(
        tokens, w_query, b_query, w_key, w_value, b_value, w_attn_out, b_attn_out, gain_one, shift_one,
        w_inner, b_inner, w_outer, b_outer, gain_two, shift_two, cotangent, lengths, row_ids, col_ids,
    ):
        block = w_inner.shape[1] // BLOCKS
        index = lax.axis_index("dp")
        z = lax.axis_index("tensor")
        c, my = index & 1, (index >> 1) & 3
        scalars = jnp.stack([lax.dynamic_index_in_dim(lengths, z, keepdims=False), c, my, z]).astype(jnp.int32)
        tags = (row_ids, col_ids)
        vectors_one = f32(jnp.stack([b_attn_out, gain_one, shift_one]))
        vectors_two = f32(jnp.stack([b_outer, gain_two, shift_two]))

        bias = jnp.concatenate([b_query, b_value, b_inner])[None]
        slab, piece_a = attention_piece(scalars, w_query, w_key, w_value, w_attn_out, bias)
        with jax.named_scope("line attention weights"):
            line_a = from_all(piece_a)
        first = attention_forward(scalars, tokens, slab, piece_a, tags, n_tensor, 0)
        w_inner_t, piece_i, piece_u = ffn_pieces(tie(scalars, slab), w_inner, w_outer)

        with jax.named_scope("line inner weights"):
            line_i = from_all(tie(piece_i, *line_a, first[2]))
        own_a = jnp.concatenate([tie(line_a[0], piece_i, first[2])] + line_a[1:])
        with jax.named_scope("plane attention weights"):
            plane_a = plane(own_a)

        own_i = jnp.stack([tie(line_i[0], *plane_a)] + line_i[1:])
        near_a = jnp.stack([tie(own_a, *line_i), *plane_a])
        with jax.named_scope("core attention weights"):
            far_a = across(near_a, 1)
        with jax.named_scope("plane inner weights"):
            plane_i = plane(own_i)
        with jax.named_scope("line outer weights"):
            line_u = from_all(tie(piece_u, *line_i, far_a))

        w_attn = assemble(scalars, near_a, far_a, slab[0], 4 * QKV)
        qkv, heads_out, lse = attention_forward(scalars, tokens, w_attn, own_a, tags, n_tensor, 1, first)
        own_u = jnp.stack([tie(line_u[0], lse, *plane_i)] + line_u[1:])
        near_i = jnp.stack([tie(own_i, *line_u, lse), *plane_i])
        with jax.named_scope("core inner weights"):
            far_i = across(near_i, 1)
        with jax.named_scope("plane outer weights"):
            plane_u = plane(own_u)

        w_in = assemble(scalars, near_i, far_i, w_inner_t, block)
        normed, inv_spread, hidden, low, act, slope = inner_half(
            scalars, heads_out, w_attn, tokens, vectors_one, w_in, piece_a, own_a
        )
        near_u = jnp.stack([tie(own_u, inv_spread), *plane_u])
        with jax.named_scope("core outer weights"):
            far_u = across(near_u, 1)
        w_up = assemble(scalars, near_u, far_u, w_outer, block)
        out_rows, grad_two, sums_two = outer_half(scalars, act, w_up, hidden, cotangent, vectors_two)

        barrier = lambda *arrays: lax.optimization_barrier(arrays)
        with jax.named_scope("rows 1"):
            up_1, down_1 = rows_round(1, out_rows, out_rows)
        mine_u, other_u = weight_grad(scalars, act, grad_two)
        with jax.named_scope("core outer grad"):
            theirs_u = across(other_u, 1)
        grad_one, grad_one_low, grad_inner, db_inner, sums_one = ffn_back(
            tie(grad_two, mine_u), slope, w_up, w_in, normed, inv_spread, vectors_one
        )
        grad_one, grad_inner, theirs_u, up_1, down_1 = barrier(grad_one, grad_inner, theirs_u, up_1, down_1)
        with jax.named_scope("rows 2"):
            up_2, down_2 = rows_round(2, up_1, down_1)
        own_u, x_u, y_u, *via_u = core_add(mine_u, theirs_u)
        with jax.named_scope("plane one outer grad"):
            via_u = plane_one(*via_u)
        mine_i, other_i = weight_grad(scalars, tie(grad_inner, own_u), low)
        vectors = (db_inner, sums_one, sums_two)
        pieces = ()

        def shard_back(start, r):
            dtype = F32 if r else BF
            return attention_backward(
                scalars, tokens, w_attn, qkv, heads_out, lse, grad_one_low, start, tags, vectors, r, dtype, pieces
            )

        start, *pieces = shard_back(tie(grad_one, mine_i), 3)
        start, *via_u = barrier(start, *via_u)
        x_u, y_u = plane_add(x_u, y_u, *via_u)
        with jax.named_scope("plane two outer grad"):
            plane_u = plane_two(x_u, y_u)
        start, *pieces = shard_back(tie(start, x_u), 2)
        with jax.named_scope("core inner grad"):
            theirs_i = across(tie(other_i, start), 1)
        start, up_2, down_2 = barrier(start, up_2, down_2)
        with jax.named_scope("rows 3"):
            up_3, down_3 = rows_round(3, up_2, down_2)
        start, *pieces = shard_back(start, 1)
        start, theirs_i, *plane_u = barrier(start, theirs_i, *plane_u)
        own_i, x_i, y_i, *via_i = core_add(mine_i, theirs_i)
        with jax.named_scope("plane one inner grad"):
            via_i = plane_one(*via_i)
        grad_rows, mine_a, other_a = shard_back(tie(start, own_i), 0)
        grad_rows, mine_a, other_a, up_3, down_3, *via_i = barrier(grad_rows, mine_a, other_a, up_3, down_3, *via_i)

        with jax.named_scope("grad rows 1"):
            go_1, back_1 = rows_round(1, grad_rows, grad_rows)
        with jax.named_scope("core attention grad"):
            theirs_a = across(other_a, 1)
        x_i, y_i = plane_add(x_i, y_i, *via_i)
        with jax.named_scope("plane two inner grad"):
            plane_i = plane_two(x_i, y_i)
        own_a, x_a, y_a, *via_a = core_add(mine_a, theirs_a)
        *via_a, plane_i_x, plane_i_y = barrier(*via_a, *plane_i)
        with jax.named_scope("plane one attention grad"):
            via_a = plane_one(*via_a)
        groups = ((own_u, *plane_u), (own_i, plane_i_x, plane_i_y))
        near_f = jnp.concatenate([sum(f32(a[:half]) for a in group) for group in groups], axis=1)
        far_f = jnp.concatenate([add(*[a[half:] for a in group]) for group in groups], axis=1)
        with jax.named_scope("line ends ffn grad"):
            ends_f = line_ends(far_f)
        go_1, back_1, *via_a = barrier(go_1, back_1, *via_a)
        with jax.named_scope("grad rows 2"):
            go_2, back_2 = rows_round(2, go_1, back_1)
        x_a, y_a = plane_add(x_a, y_a, *via_a)
        with jax.named_scope("plane two attention grad"):
            plane_a = plane_two(x_a, y_a)
        layer_out = place_rows(z, tie(out_rows, *via_a), (up_1, up_2, up_3), (down_1, down_2, down_3))
        go_2, back_2, ends_f, layer_out, *plane_a = barrier(go_2, back_2, ends_f, layer_out, *plane_a)
        with jax.named_scope("grad rows 3"):
            go_3, back_3 = rows_round(3, go_2, back_2)
        with jax.named_scope("line middle ffn grad"):
            middle_f = line_middle(add(far_f, ends_f[::-1]))
        group = (own_a, *plane_a)
        odd_a = add(*[a[1::2] for a in group])
        with jax.named_scope("line one attention grad"):
            odd_a = along(odd_a, 1)
        even_a = sum(f32(a[0::2]) for a in group)
        odd_a, middle_f = barrier(odd_a, middle_f)
        near_f = near_f + f32(middle_f[::-1])
        with jax.named_scope("line pair ffn grad"):
            pair_f = along(near_f[1].astype(BF), 1)
        even_a = even_a + f32(odd_a)
        with jax.named_scope("line two attention grad"):
            last_a = along(even_a[1].astype(BF), 2)
        last_a, pair_f = barrier(last_a, pair_f)
        done = jnp.concatenate([line_end(even_a[0], last_a), line_end(near_f[0], pair_f)])
        done, go_3, back_3 = barrier(done, go_3, back_3)
        with jax.named_scope("plane result"):
            found = plane(done)
        grad_tokens = place_rows(z, grad_rows, (go_1, go_2, go_3), (back_1, back_2, back_3))
        near = jnp.stack([done, *found])
        with jax.named_scope("core result"):
            far = across(near, 1)
        grads = finish(scalars, near, far, block, QKV)
        grad_wq, grad_wk, grad_wv, grad_wo, grad_wu, grad_wi, *vectors = grads
        grad_bq, grad_bv, grad_bi, gain_1, shift_1, b_1, gain_2, shift_2, b_2 = [v.reshape(-1) for v in vectors]

        return (
            layer_out,
            grad_tokens,
            grad_wq.T,
            grad_bq,
            grad_wk.T,
            grad_wv.T,
            grad_bv,
            grad_wo,
            b_1,
            gain_1,
            shift_1,
            grad_wi,
            grad_bi,
            grad_wu,
            b_2,
            gain_2,
            shift_2,
        )

    return body


def solution(mesh):
    rows, columns, out = P("dp", None), P(None, "tensor"), P("tensor", None)
    one = P("tensor")
    in_specs = (
        rows, columns, one, columns, columns, one, out, P(), P(), P(), columns, one, out, P(), P(), P(),
        rows, P("dp"), rows, rows,
    )
    out_specs = (
        rows, rows, columns, one, columns, columns, one, out, P(), P(), P(), columns, one, out, P(), P(), P(),
    )
    body = build(mesh.shape["dp"], mesh.shape["tensor"])
    return jax.shard_map(body, mesh=mesh, in_specs=in_specs, out_specs=out_specs, check_vma=False)
```

profile of v0, /device:TPU:0, one launch (start us, length us, event | category | flops | bytes accessed | tf_op | source)
XLA Modules:
  0.0 329.7 jit_solution(2880222028895293838)
XLA Ops:
  0.7 2.4 concatenate.15
  9.8 3.1 collective-permute-start
  12.9 2.6 collective-permute-start.1
  19.0 2.8 shard_map.325
  21.8 5.9 %collective-permute-done.1 = bf16[1,208,384]{2,1,0:T(8,128)(2,1)S(1)} collective-permute-done((bf16[1,208,384]{2,1,0:T(8,128)(2,1)S(1)}, bf16[1,208,384]{2,1,0:T(8,128)(2,1)S(1)}, u32[]{:S(2)}, u32[]{:S(2)}) %collective-permute-start.1) | collective-permute-done | bytes 159776 | tf_op jit(solution)/shard_map/line attention weights/ppermute | solution.py:732
  27.7 2.5 collective-permute-start.8
  31.3 2.5 collective-permute-start.3
  34.8 3.2 collective-permute-done.3
  38.0 2.2 collective-permute-start.5
  40.3 5.8 %collective-permute-done.4 = bf16[192,384]{1,0:T(8,128)(2,1)S(1)} collective-permute-done((bf16[192,384]{1,0:T(8,128)(2,1)S(1)}, bf16[192,384]{1,0:T(8,128)(2,1)S(1)}, u32[]{:S(2)}, u32[]{:S(2)}) %collective-permute-start.4) | collective-permute-done | bytes 147488 | tf_op jit(solution)/shard_map/line inner weights/ppermute | solution.py:732
  46.0 3.1 collective-permute-done.7
  49.7 1.7 collective-permute-start.15
  51.4 1.3 collective-permute-start.14
  53.5 3.9 %collective-permute-start.10 = (bf16[192,384]{1,0:T(8,128)(2,1)S(1)}, bf16[192,384]{1,0:T(8,128)(2,1)S(1)}, u32[]{:S(2)}, u32[]{:S(2)}) collective-permute-start(bf16[192,384]{1,0:T(8,128)(2,1)S(1)} %get-tuple-element.168), channel_id=1, source_target_pairs={{0,1},{1,0},{2,3},{3,2},{4,5},{5,4},{6,7},{7,6},{8,9},{9,8},{10,11... | collective-permute-start | bytes 442376 | tf_op jit(solution)/shard_map/line outer weights/ppermute | solution.py:732
  58.6 6.0 %collective-permute-done.10 = bf16[192,384]{1,0:T(8,128)(2,1)S(1)} collective-permute-done((bf16[192,384]{1,0:T(8,128)(2,1)S(1)}, bf16[192,384]{1,0:T(8,128)(2,1)S(1)}, u32[]{:S(2)}, u32[]{:S(2)}) %collective-permute-start.10) | collective-permute-done | bytes 147488 | tf_op jit(solution)/shard_map/line outer weights/ppermute | solution.py:732
  65.9 1.4 shard_map.326.w_ref.wo_ref.w_hbm
  67.3 7.2 %shard_map.327 = (bf16[4,576,512]{2,1,0:T(8,128)(2,1)S(1)}, bf16[4,192,512]{2,1,0:T(8,128)(2,1)S(1)}, f32[4,8,512]{2,1,0:T(8,128)S(1)}) custom-call(s32[4]{0:T(128)S(1)} %pad_add_fusion.scalars, bf16[2048,768]{1,0:T(8,128)(2,1)S(1)} %copy-done, ...), custom_call_target="tpu_custom_call", output_to_operand_aliasing={{0}: (6, {}), {1}: (7, {}), {2}: (8, {})} | custom-call | flops 450000000 | bytes 450000 | tf_op jit(solution)/shard_map/pallas_call | solution.py:145
  75.1 1.7 collective-permute-start.19
  76.8 1.3 collective-permute-start.18
  80.0 11.7 %shard_map.329 = (f32[512,768]{1,0:T(8,128)S(1)}, f32[512,1]{1,0:T(8,128)S(1)}, f32[512,768]{1,0:T(8,128)S(1)}, bf16[512,768]{1,0:T(8,128)(2,1)S(1)}, bf16[4,512...) custom-call(s32[4]{0:T(128)S(1)} %pad_add_fusion.scalars, ...), custom_call_target="tpu_custom_call" | custom-call | flops 600000000 | bytes 1000000 | tf_op jit(solution)/shard_map/pallas_call | solution.py:331
  91.7 1.7 copy-done.8
  93.4 4.7 %collective-permute-done.18 = bf16[3,192,384]{2,1,0:T(8,128)(2,1)S(1)} collective-permute-done((bf16[3,192,384]{2,1,0:T(8,128)(2,1)S(1)}, bf16[3,192,384]{2,1,0:T(8,128)(2,1)S(1)}, u32[]{:S(2)}, u32[]{:S(2)}) %collective-permute-start.18) | collective-permute-done | bytes 442400 | tf_op jit(solution)/shard_map/plane outer weights/ppermute | solution.py:729
  98.6 3.6 %collective-permute-done.20.far_ref = bf16[4,3,192,384]{3,2,1,0:T(8,128)(2,1)S(1)} collective-permute-done((bf16[4,3,192,384]{3,2,1,0:T(8,128)(2,1)S(1)}, bf16[4,3,192,384]{3,2,1,0:T(8,128)(2,1)S(1)}, u32[]{:S(2)}, u32[]{:S(2)}) %collective-permute-start.20) | collective-permute-done | bytes 1769504 | tf_op jit(solution)/shard_map/core outer weights/ppermute | solution.py:729
  104.1 5.1 %shard_map.331 = (bf16[512,768]{1,0:T(8,128)(2,1)S(1)}, f32[512,768]{1,0:T(8,128)S(1)}, f32[8,768]{1,0:T(8,128)S(1)}) custom-call(s32[4]{0:T(128)S(1)} %pad_add_fusion.scalars, bf16[4,512,768]{2,1,0:T(8,128)(2,1)S(1)} %get-tuple-element.171.act_ref.left_ref, bf16[4,768,768]{2,1,0:T(8,128)(2,1)S(1)} %shard_map.330.wu_ref, ...), custom_call_target="tpu_custom_call" | custom-call | flops 250000000 | bytes 700000 | tf_op jit(solution)/shard_map/pallas_call | solution.py:393
  109.2 5.7 %shard_map.332 = (bf16[4,4,192,384]{3,2,1,0:T(8,128)(2,1)S(1)}, bf16[4,4,192,384]{3,2,1,0:T(8,128)(2,1)}) custom-call(s32[4]{0:T(128)S(1)} %pad_add_fusion.scalars, bf16[4,512,768]{2,1,0:T(8,128)(2,1)S(1)} %get-tuple-element.171.act_ref.left_ref, f32[512,768]{1,0:T(8,128)S(1)} %get-tuple-element.178.right_ref.up_ref), custom_call_target="tpu_custom_call" | custom-call | flops 300000000 | bytes 400000 | tf_op jit(solution)/shard_map/pallas_call | solution.py:494
  115.0 1.4 copy-done.10
  116.5 3.9 %collective-permute-start.22 = (bf16[512,768]{1,0:T(8,128)(2,1)S(1)}, bf16[512,768]{1,0:T(8,128)(2,1)S(1)}, u32[]{:S(2)}, u32[]{:S(2)}) collective-permute-start(bf16[512,768]{1,0:T(8,128)(2,1)S(1)} %get-tuple-element.253), channel_id=1, source_target_pairs={{0,1},{1,2},{2,3},{4,5},{5,6},{6,7},{8,9},{9,10},{10,11},{12,13},{... | collective-permute-start | bytes 2359304 | tf_op jit(solution)/shard_map/rows 1/ppermute | solution.py:746
  121.8 1.9 copy-done.9
  123.6 1.4 copy-done.13
  125.0 10.8 %shard_map.333 = (f32[512,768]{1,0:T(8,128)S(1)}, bf16[512,768]{1,0:T(8,128)(2,1)S(1)}, bf16[4,512,768]{2,1,0:T(8,128)(2,1)S(1)}, f32[4,1,768]{2,1,0:T(1,128)S(1)}, f32[8,768]{1,0:T(8,128)S(1)}) custom-call(f32[512,768]{1,0:T(8,128)S(1)} %get-tuple-element.178.right_ref.up_ref, bf16[4,512,768]{2,1,0:T(8,128)(2,1)S(1)} %copy-done.9, ...), custom_call_target="tpu_custom_call" | custom-call | flops 600000000 | bytes 800000 | tf_op jit(solution)/shard_map/pallas_call | solution.py:450
  135.8 1.8 collective-permute-done.22
  137.7 4.2 %collective-permute-done.23 = bf16[512,768]{1,0:T(8,128)(2,1)S(1)} collective-permute-done((bf16[512,768]{1,0:T(8,128)(2,1)S(1)}, bf16[512,768]{1,0:T(8,128)(2,1)S(1)}, u32[]{:S(2)}, u32[]{:S(2)}) %collective-permute-start.23) | collective-permute-done | bytes 786464 | tf_op jit(solution)/shard_map/rows 1/ppermute | solution.py:747
  143.9 1.5 collective-permute-start.24
  146.2 5.1 %shard_map.335 = (bf16[4,4,192,384]{3,2,1,0:T(8,128)(2,1)S(1)}, bf16[4,4,192,384]{3,2,1,0:T(8,128)(2,1)S(1)}) custom-call(s32[4]{0:T(128)S(1)} %pad_add_fusion.scalars, bf16[4,512,768]{2,1,0:T(8,128)(2,1)S(1)} %get-tuple-element.190.left_ref, bf16[512,768]{1,0:T(8,128)(2,1)S(1)} %copy-done.18), custom_call_target="tpu_custom_call" | custom-call | flops 300000000 | bytes 400000 | tf_op jit(solution)/shard_map/pallas_call | solution.py:494
  151.3 6.6 %shard_map.336 = (f32[512,768]{1,0:T(8,128)S(1)}, bf16[4,4,208,384]{3,2,1,0:T(8,128)(2,1)S(1)}, bf16[4,4,208,384]{3,2,1,0:T(8,128)(2,1)}) custom-call(s32[4]{0:T(128)S(1)} %pad_add_fusion.scalars, bf16[2048,768]{1,0:T(8,128)(2,1)S(1)} %copy-done, bf16[4,768,768]{2,1,0:T(8,128)(2,1)S(1)} %shard_map.326.w_ref.wo_ref.w_hbm, ...), custom_call_target="tpu_custom_call" | custom-call | flops 250000000 | bytes 250000 | tf_op jit(solution)/shard_map/pallas_call | solution.py:239
  158.2 6.6 %shard_map.338 = (f32[512,768]{1,0:T(8,128)S(1)}, bf16[4,4,208,384]{3,2,1,0:T(8,128)(2,1)S(1)}, bf16[4,4,208,384]{3,2,1,0:T(8,128)(2,1)}) custom-call(s32[4]{0:T(128)S(1)} %pad_add_fusion.scalars, bf16[2048,768]{1,0:T(8,128)(2,1)S(1)} %copy-done, ...), custom_call_target="tpu_custom_call", output_to_operand_aliasing={{1}: (13, {}), {2}: (14, {})} | custom-call | flops 250000000 | bytes 250000 | tf_op jit(solution)/shard_map/pallas_call | solution.py:239
  167.0 1.3 collective-permute-start.29
  168.9 19.9 %collective-permute-done.27 = bf16[512,768]{1,0:T(8,128)(2,1)S(1)} collective-permute-done((bf16[512,768]{1,0:T(8,128)(2,1)S(1)}, bf16[512,768]{1,0:T(8,128)(2,1)S(1)}, u32[]{:S(2)}, u32[]{:S(2)}) %collective-permute-start.27) | collective-permute-done | bytes 786464 | tf_op jit(solution)/shard_map/rows 2/ppermute | solution.py:747
  190.7 6.8 %shard_map.339 = (f32[512,768]{1,0:T(8,128)S(1)}, bf16[4,4,208,384]{3,2,1,0:T(8,128)(2,1)S(1)}, bf16[4,4,208,384]{3,2,1,0:T(8,128)(2,1)}) custom-call(s32[4]{0:T(128)S(1)} %pad_add_fusion.scalars, bf16[2048,768]{1,0:T(8,128)(2,1)S(1)} %copy-done, ...), custom_call_target="tpu_custom_call", output_to_operand_aliasing={{1}: (13, {}), {2}: (14, {})} | custom-call | flops 250000000 | bytes 250000 | tf_op jit(solution)/shard_map/pallas_call | solution.py:239
  197.6 2.3 shard_map.340
  202.6 6.7 %shard_map.341 = (bf16[512,768]{1,0:T(8,128)(2,1)}, bf16[4,4,208,384]{3,2,1,0:T(8,128)(2,1)S(1)}, bf16[4,4,208,384]{3,2,1,0:T(8,128)(2,1)}) custom-call(s32[4]{0:T(128)S(1)} %pad_add_fusion.scalars, bf16[2048,768]{1,0:T(8,128)(2,1)S(1)} %copy-done, ...), custom_call_target="tpu_custom_call", output_to_operand_aliasing={{1}: (13, {}), {2}: (14, {})} | custom-call | flops 250000000 | bytes 250000 | tf_op jit(solution)/shard_map/pallas_call | solution.py:239
  209.3 1.5 copy-done.3
  210.9 2.5 shard_map.343
  213.4 1.6 collective-permute-start.38
  215.7 5.5 %collective-permute-start.35 = (bf16[512,768]{1,0:T(8,128)(2,1)}, bf16[512,768]{1,0:T(8,128)(2,1)}, u32[]{:S(2)}, u32[]{:S(2)}) collective-permute-start(bf16[512,768]{1,0:T(8,128)(2,1)} %get-tuple-element.232), channel_id=1, source_target_pairs={{0,1},{1,2},{2,3},{4,5},{5,6},{6,7},{8,9},{9,10},{10,11},{12,13},{... | collective-permute-start | bytes 2359304 | tf_op jit(solution)/shard_map/grad rows 1/ppermute | solution.py:746
  222.5 1.4 convert_add_fusion.2
  224.0 3.0 shard_map.342
  227.0 2.0 collective-permute-done.38
  232.2 1.4 convert_add_fusion.1
  233.7 4.6 %collective-permute-start.44 = (bf16[2,384,384]{2,1,0:T(8,128)(2,1)S(1)}, bf16[2,384,384]{2,1,0:T(8,128)(2,1)S(1)}, u32[]{:S(2)}, u32[]{:S(2)}) collective-permute-start(bf16[2,384,384]{2,1,0:T(8,128)(2,1)S(1)} %pad_maximum_fusion.4), channel_id=1, source_target_pairs={{0,1},{3,2},{4,5},{7,6},{8,9},{11,10},{12,13},{15,14},{16,17},{19,... | collective-permute-start | bytes 1769480 | tf_op jit(solution)/shard_map/line ends ffn grad/ppermute | solution.py:768
  238.3 3.6 %collective-permute-done.36 = bf16[512,768]{1,0:T(8,128)(2,1)} collective-permute-done((bf16[512,768]{1,0:T(8,128)(2,1)}, bf16[512,768]{1,0:T(8,128)(2,1)}, u32[]{:S(2)}, u32[]{:S(2)}) %collective-permute-start.36) | collective-permute-done | bytes 786464 | tf_op jit(solution)/shard_map/grad rows 1/ppermute | solution.py:747
  249.5 9.3 %collective-permute-done.45 = bf16[4,208,384]{2,1,0:T(8,128)(2,1)S(1)} collective-permute-done((bf16[4,208,384]{2,1,0:T(8,128)(2,1)S(1)}, bf16[4,208,384]{2,1,0:T(8,128)(2,1)S(1)}, u32[]{:S(2)}, u32[]{:S(2)}) %collective-permute-start.45) | collective-permute-done | bytes 639008 | tf_op jit(solution)/shard_map/plane two attention grad/ppermute | solution.py:729
  259.8 2.7 collective-permute-done.43
  263.7 1.6 collective-permute-start.47
  267.3 6.9 %collective-permute-done.47 = bf16[2,208,384]{2,1,0:T(8,128)(2,1)S(1)} collective-permute-done((bf16[2,208,384]{2,1,0:T(8,128)(2,1)S(1)}, bf16[2,208,384]{2,1,0:T(8,128)(2,1)S(1)}, u32[]{:S(2)}, u32[]{:S(2)}) %collective-permute-start.47) | collective-permute-done | bytes 319520 | tf_op jit(solution)/shard_map/line one attention grad/ppermute | solution.py:732
  274.5 2.8 collective-permute-start.50
  277.7 7.8 %collective-permute-done.49 = bf16[208,384]{1,0:T(8,128)(2,1)S(1)} collective-permute-done((bf16[208,384]{1,0:T(8,128)(2,1)S(1)}, bf16[208,384]{1,0:T(8,128)(2,1)S(1)}, u32[]{:S(2)}, u32[]{:S(2)}) %collective-permute-start.49) | collective-permute-done | bytes 159776 | tf_op jit(solution)/shard_map/line two attention grad/ppermute | solution.py:732
  285.5 11.6 %collective-permute-done.50 = bf16[384,384]{1,0:T(8,128)(2,1)S(1)} collective-permute-done((bf16[384,384]{1,0:T(8,128)(2,1)S(1)}, bf16[384,384]{1,0:T(8,128)(2,1)S(1)}, u32[]{:S(2)}, u32[]{:S(2)}) %collective-permute-start.50) | collective-permute-done | bytes 294944 | tf_op jit(solution)/shard_map/line pair ffn grad/ppermute | solution.py:732
  297.3 1.3 collective-permute-start.55
  298.6 1.4 collective-permute-start.54
  300.8 10.8 %collective-permute-done.55 = bf16[592,384]{1,0:T(8,128)(2,1)S(1)} collective-permute-done((bf16[592,384]{1,0:T(8,128)(2,1)S(1)}, bf16[592,384]{1,0:T(8,128)(2,1)S(1)}, u32[]{:S(2)}, u32[]{:S(2)}) %collective-permute-start.55) | collective-permute-done | bytes 454688 | tf_op jit(solution)/shard_map/plane result/ppermute | solution.py:729
  311.6 5.1 %collective-permute-done.54 = bf16[592,384]{1,0:T(8,128)(2,1)S(1)} collective-permute-done((bf16[592,384]{1,0:T(8,128)(2,1)S(1)}, bf16[592,384]{1,0:T(8,128)(2,1)S(1)}, u32[]{:S(2)}, u32[]{:S(2)}) %collective-permute-start.54) | collective-permute-done | bytes 454688 | tf_op jit(solution)/shard_map/plane result/ppermute | solution.py:729
  318.9 1.4 select_dynamic-update-slice_fusion
  320.8 4.4 %shard_map.345 = (f32[192,768]{1,0:T(8,128)}, f32[192,768]{1,0:T(8,128)}, f32[192,768]{1,0:T(8,128)}, f32[192,768]{1,0:T(8,128)}, f32[768,768]{1,0:T(8,128)}, /*...) custom-call(s32[4]{0:T(128)S(1)} %pad_add_fusion.scalars, ...), custom_call_target="tpu_custom_call" | custom-call | flops 100000000 | tf_op jit(solution)/shard_map/pallas_call | solution.py:653
  (227 shorter events, 58.0 us)
Async XLA Ops:
  0.7 18.3 %copy-start = (bf16[2048,768]{1,0:T(8,128)(2,1)S(1)}, bf16[2048,768]{1,0:T(8,128)(2,1)}, u32[]{:S(2)}) copy-start(bf16[2048,768]{1,0:T(8,128)(2,1)} %x_hbm.7) | copy-start | bytes 9437188
  9.8 12.0 %collective-permute-start = (bf16[1,208,384]{2,1,0:T(8,128)(2,1)S(1)}, bf16[1,208,384]{2,1,0:T(8,128)(2,1)S(1)}, u32[]{:S(2)}, u32[]{:S(2)}) collective-permute-start(bf16[1,208,384]{2,1,0:T(8,128)(2,1)S(1)} %get-tuple-element.153.b_ref.own_ref), channel_id=1, source_target_pairs={{0,1},{1,0},{2,3},{3,2},{4,5},{5,4},{6,7},{7,6},{8,9},{9,8},{10,11... | collective-permute-start | bytes 479240 | tf_op jit(solution)/shard_map/line attention weights/ppermute | solution.py:732
  12.9 14.8 %collective-permute-start.1 = (bf16[1,208,384]{2,1,0:T(8,128)(2,1)S(1)}, bf16[1,208,384]{2,1,0:T(8,128)(2,1)S(1)}, u32[]{:S(2)}, u32[]{:S(2)}) collective-permute-start(bf16[1,208,384]{2,1,0:T(8,128)(2,1)S(1)} %get-tuple-element.153.b_ref.own_ref), channel_id=1, source_target_pairs={{0,2},{1,3},{2,0},{3,1},{4,6},{5,7},{6,4},{7,5},{8,10},{9,11},{10,... | collective-permute-start | bytes 479240 | tf_op jit(solution)/shard_map/line attention weights/ppermute | solution.py:732
  15.5 12.2 %collective-permute-start.2 = (bf16[1,208,384]{2,1,0:T(8,128)(2,1)S(1)}, bf16[1,208,384]{2,1,0:T(8,128)(2,1)S(1)}, u32[]{:S(2)}, u32[]{:S(2)}) collective-permute-start(bf16[1,208,384]{2,1,0:T(8,128)(2,1)S(1)} %get-tuple-element.153.b_ref.own_ref), channel_id=1, source_target_pairs={{0,3},{1,2},{2,1},{3,0},{4,7},{5,6},{6,5},{7,4},{8,11},{9,10},{10,... | collective-permute-start | bytes 479240 | tf_op jit(solution)/shard_map/line attention weights/ppermute | solution.py:732
  27.7 18.3 %collective-permute-start.8 = (bf16[3,208,384]{2,1,0:T(8,128)(2,1)S(1)}, bf16[3,208,384]{2,1,0:T(8,128)(2,1)S(1)}, u32[]{:S(2)}, u32[]{:S(2)}) collective-permute-start(bf16[3,208,384]{2,1,0:T(8,128)(2,1)S(1)} %constant_dynamic-update-slice_fusion.b_ref.others_ref), channel_id=1, source_target_pairs={{0,24},{4,28},{8,16},{12,20},{16,8},{20,12},{24,0},{28,4},{1,25},{... | collective-permute-start | bytes 1437704 | tf_op jit(solution)/shard_map/plane attention weights/ppermute | solution.py:729
  30.3 18.9 %collective-permute-start.7 = (bf16[3,208,384]{2,1,0:T(8,128)(2,1)S(1)}, bf16[3,208,384]{2,1,0:T(8,128)(2,1)S(1)}, u32[]{:S(2)}, u32[]{:S(2)}) collective-permute-start(bf16[3,208,384]{2,1,0:T(8,128)(2,1)S(1)} %constant_dynamic-update-slice_fusion.b_ref.others_ref), channel_id=1, source_target_pairs={{0,16},{4,20},{8,24},{12,28},{16,0},{20,4},{24,8},{28,12},{1,17},{... | collective-permute-start | bytes 1437704 | tf_op jit(solution)/shard_map/plane attention weights/ppermute | solution.py:729
  30.8 18.5 %collective-permute-start.6 = (bf16[3,208,384]{2,1,0:T(8,128)(2,1)S(1)}, bf16[3,208,384]{2,1,0:T(8,128)(2,1)S(1)}, u32[]{:S(2)}, u32[]{:S(2)}) collective-permute-start(bf16[3,208,384]{2,1,0:T(8,128)(2,1)S(1)} %constant_dynamic-update-slice_fusion.b_ref.others_ref), channel_id=1, source_target_pairs={{0,8},{4,12},{8,0},{12,4},{16,24},{20,28},{24,16},{28,20},{1,9},{5... | collective-permute-start | bytes 1437704 | tf_op jit(solution)/shard_map/plane attention weights/ppermute | solution.py:729
  31.3 6.7 %collective-permute-start.3 = (bf16[192,384]{1,0:T(8,128)(2,1)S(1)}, bf16[192,384]{1,0:T(8,128)(2,1)S(1)}, u32[]{:S(2)}, u32[]{:S(2)}) collective-permute-start(bf16[192,384]{1,0:T(8,128)(2,1)S(1)} %get-tuple-element.159), channel_id=1, source_target_pairs={{0,1},{1,0},{2,3},{3,2},{4,5},{5,4},{6,7},{7,6},{8,9},{9,8},{10,11... | collective-permute-start | bytes 442376 | tf_op jit(solution)/shard_map/line inner weights/ppermute | solution.py:732
  33.8 12.2 %collective-permute-start.4 = (bf16[192,384]{1,0:T(8,128)(2,1)S(1)}, bf16[192,384]{1,0:T(8,128)(2,1)S(1)}, u32[]{:S(2)}, u32[]{:S(2)}) collective-permute-start(bf16[192,384]{1,0:T(8,128)(2,1)S(1)} %get-tuple-element.159), channel_id=1, source_target_pairs={{0,2},{1,3},{2,0},{3,1},{4,6},{5,7},{6,4},{7,5},{8,10},{9,11},{10,... | collective-permute-start | bytes 442376 | tf_op jit(solution)/shard_map/line inner weights/ppermute | solution.py:732
  38.0 8.0 %collective-permute-start.5 = (bf16[192,384]{1,0:T(8,128)(2,1)S(1)}, bf16[192,384]{1,0:T(8,128)(2,1)S(1)}, u32[]{:S(2)}, u32[]{:S(2)}) collective-permute-start(bf16[192,384]{1,0:T(8,128)(2,1)S(1)} %get-tuple-element.159), channel_id=1, source_target_pairs={{0,3},{1,2},{2,1},{3,0},{4,7},{5,6},{6,5},{7,4},{8,11},{9,10},{10,... | collective-permute-start | bytes 442376 | tf_op jit(solution)/shard_map/line inner weights/ppermute | solution.py:732
  49.6 4.0 %collective-permute-start.9 = (bf16[4,3,208,384]{3,2,1,0:T(8,128)(2,1)S(1)}, bf16[4,3,208,384]{3,2,1,0:T(8,128)(2,1)S(1)}, u32[]{:S(2)}, u32[]{:S(2)}) collective-permute-start(bf16[4,3,208,384]{3,2,1,0:T(8,128)(2,1)S(1)} %pad_maximum_fusion.near_ref), channel_id=1, source_target_pairs={{0,4},{4,0},{8,12},{12,8},{16,20},{20,16},{24,28},{28,24},{1,5},{5... | collective-permute-start | bytes 5750792 | tf_op jit(solution)/shard_map/core attention weights/ppermute | solution.py:729
  49.7 24.9 %collective-permute-start.15 = (bf16[3,192,384]{2,1,0:T(8,128)(2,1)S(1)}, bf16[3,192,384]{2,1,0:T(8,128)(2,1)S(1)}, u32[]{:S(2)}, u32[]{:S(2)}) collective-permute-start(bf16[3,192,384]{2,1,0:T(8,128)(2,1)S(1)} %pad_maximum_fusion.6), channel_id=1, source_target_pairs={{0,24},{4,28},{8,16},{12,20},{16,8},{20,12},{24,0},{28,4},{1,25},{... | collective-permute-start | bytes 1327112 | tf_op jit(solution)/shard_map/plane inner weights/ppermute | solution.py:729
  51.4 23.2 %collective-permute-start.14 = (bf16[3,192,384]{2,1,0:T(8,128)(2,1)S(1)}, bf16[3,192,384]{2,1,0:T(8,128)(2,1)S(1)}, u32[]{:S(2)}, u32[]{:S(2)}) collective-permute-start(bf16[3,192,384]{2,1,0:T(8,128)(2,1)S(1)} %pad_maximum_fusion.6), channel_id=1, source_target_pairs={{0,16},{4,20},{8,24},{12,28},{16,0},{20,4},{24,8},{28,12},{1,17},{... | collective-permute-start | bytes 1327112 | tf_op jit(solution)/shard_map/plane inner weights/ppermute | solution.py:729
  52.7 21.9 %collective-permute-start.13 = (bf16[3,192,384]{2,1,0:T(8,128)(2,1)S(1)}, bf16[3,192,384]{2,1,0:T(8,128)(2,1)S(1)}, u32[]{:S(2)}, u32[]{:S(2)}) collective-permute-start(bf16[3,192,384]{2,1,0:T(8,128)(2,1)S(1)} %pad_maximum_fusion.6), channel_id=1, source_target_pairs={{0,8},{4,12},{8,0},{12,4},{16,24},{20,28},{24,16},{28,20},{1,9},{5... | collective-permute-start | bytes 1327112 | tf_op jit(solution)/shard_map/plane inner weights/ppermute | solution.py:729
  53.5 11.1 %collective-permute-start.10 = (bf16[192,384]{1,0:T(8,128)(2,1)S(1)}, bf16[192,384]{1,0:T(8,128)(2,1)S(1)}, u32[]{:S(2)}, u32[]{:S(2)}) collective-permute-start(bf16[192,384]{1,0:T(8,128)(2,1)S(1)} %get-tuple-element.168), channel_id=1, source_target_pairs={{0,1},{1,0},{2,3},{3,2},{4,5},{5,4},{6,7},{7,6},{8,9},{9,8},{10,11... | collective-permute-start | bytes 442376 | tf_op jit(solution)/shard_map/line outer weights/ppermute | solution.py:732
  57.4 17.2 %collective-permute-start.11 = (bf16[192,384]{1,0:T(8,128)(2,1)S(1)}, bf16[192,384]{1,0:T(8,128)(2,1)S(1)}, u32[]{:S(2)}, u32[]{:S(2)}) collective-permute-start(bf16[192,384]{1,0:T(8,128)(2,1)S(1)} %get-tuple-element.168), channel_id=1, source_target_pairs={{0,2},{1,3},{2,0},{3,1},{4,6},{5,7},{6,4},{7,5},{8,10},{9,11},{10,... | collective-permute-start | bytes 442376 | tf_op jit(solution)/shard_map/line outer weights/ppermute | solution.py:732
  64.7 10.0 %collective-permute-start.12 = (bf16[192,384]{1,0:T(8,128)(2,1)S(1)}, bf16[192,384]{1,0:T(8,128)(2,1)S(1)}, u32[]{:S(2)}, u32[]{:S(2)}) collective-permute-start(bf16[192,384]{1,0:T(8,128)(2,1)S(1)} %get-tuple-element.168), channel_id=1, source_target_pairs={{0,3},{1,2},{2,1},{3,0},{4,7},{5,6},{6,5},{7,4},{8,11},{9,10},{10,... | collective-permute-start | bytes 442376 | tf_op jit(solution)/shard_map/line outer weights/ppermute | solution.py:732
  75.0 3.8 %collective-permute-start.16 = (bf16[4,3,192,384]{3,2,1,0:T(8,128)(2,1)S(1)}, bf16[4,3,192,384]{3,2,1,0:T(8,128)(2,1)S(1)}, u32[]{:S(2)}, u32[]{:S(2)}) collective-permute-start(bf16[4,3,192,384]{3,2,1,0:T(8,128)(2,1)S(1)} %pad_maximum_fusion.2.near_ref), channel_id=1, source_target_pairs={{0,4},{4,0},{8,12},{12,8},{16,20},{20,16},{24,28},{28,24},{1,5},{5... | collective-permute-start | bytes 5308424 | tf_op jit(solution)/shard_map/core inner weights/ppermute | solution.py:729
  75.1 18.3 %collective-permute-start.19 = (bf16[3,192,384]{2,1,0:T(8,128)(2,1)S(1)}, bf16[3,192,384]{2,1,0:T(8,128)(2,1)S(1)}, u32[]{:S(2)}, u32[]{:S(2)}) collective-permute-start(bf16[3,192,384]{2,1,0:T(8,128)(2,1)S(1)} %pad_maximum_fusion.7), channel_id=1, source_target_pairs={{0,24},{4,28},{8,16},{12,20},{16,8},{20,12},{24,0},{28,4},{1,25},{... | collective-permute-start | bytes 1327112 | tf_op jit(solution)/shard_map/plane outer weights/ppermute | solution.py:729
  76.8 21.3 %collective-permute-start.18 = (bf16[3,192,384]{2,1,0:T(8,128)(2,1)S(1)}, bf16[3,192,384]{2,1,0:T(8,128)(2,1)S(1)}, u32[]{:S(2)}, u32[]{:S(2)}) collective-permute-start(bf16[3,192,384]{2,1,0:T(8,128)(2,1)S(1)} %pad_maximum_fusion.7), channel_id=1, source_target_pairs={{0,16},{4,20},{8,24},{12,28},{16,0},{20,4},{24,8},{28,12},{1,17},{... | collective-permute-start | bytes 1327112 | tf_op jit(solution)/shard_map/plane outer weights/ppermute | solution.py:729
  78.1 20.0 %collective-permute-start.17 = (bf16[3,192,384]{2,1,0:T(8,128)(2,1)S(1)}, bf16[3,192,384]{2,1,0:T(8,128)(2,1)S(1)}, u32[]{:S(2)}, u32[]{:S(2)}) collective-permute-start(bf16[3,192,384]{2,1,0:T(8,128)(2,1)S(1)} %pad_maximum_fusion.7), channel_id=1, source_target_pairs={{0,8},{4,12},{8,0},{12,4},{16,24},{20,28},{24,16},{28,20},{1,9},{5... | collective-permute-start | bytes 1327112 | tf_op jit(solution)/shard_map/plane outer weights/ppermute | solution.py:729
  98.4 3.8 %collective-permute-start.20 = (bf16[4,3,192,384]{3,2,1,0:T(8,128)(2,1)S(1)}, bf16[4,3,192,384]{3,2,1,0:T(8,128)(2,1)S(1)}, u32[]{:S(2)}, u32[]{:S(2)}) collective-permute-start(bf16[4,3,192,384]{3,2,1,0:T(8,128)(2,1)S(1)} %pad_maximum_fusion.3.near_ref), channel_id=1, source_target_pairs={{0,4},{4,0},{8,12},{12,8},{16,20},{20,16},{24,28},{28,24},{1,5},{5... | collective-permute-start | bytes 5308424 | tf_op jit(solution)/shard_map/core outer weights/ppermute | solution.py:729
  109.2 12.5 %copy-start.2 = (bf16[4,768,768]{2,1,0:T(8,128)(2,1)S(1)}, bf16[4,768,768]{2,1,0:T(8,128)(2,1)}, u32[]{:S(2)}) copy-start(bf16[4,768,768]{2,1,0:T(8,128)(2,1)} %copy-done.1) | copy-start | bytes 14155780
  116.4 25.5 %collective-permute-start.21 = (bf16[4,4,192,384]{3,2,1,0:T(8,128)(2,1)}, bf16[4,4,192,384]{3,2,1,0:T(8,128)(2,1)S(1)}, u32[]{:S(2)}, u32[]{:S(2)}) collective-permute-start(bf16[4,4,192,384]{3,2,1,0:T(8,128)(2,1)} %get-tuple-element.184), channel_id=1, source_target_pairs={{0,4},{4,0},{8,12},{12,8},{16,20},{20,16},{24,28},{28,24},{1,5},{5... | collective-permute-start | bytes 7077896 | tf_op jit(solution)/shard_map/core outer grad/ppermute | solution.py:729
  116.5 21.1 %collective-permute-start.22 = (bf16[512,768]{1,0:T(8,128)(2,1)S(1)}, bf16[512,768]{1,0:T(8,128)(2,1)S(1)}, u32[]{:S(2)}, u32[]{:S(2)}) collective-permute-start(bf16[512,768]{1,0:T(8,128)(2,1)S(1)} %get-tuple-element.253), channel_id=1, source_target_pairs={{0,1},{1,2},{2,3},{4,5},{5,6},{6,7},{8,9},{9,10},{10,11},{12,13},{... | collective-permute-start | bytes 2359304 | tf_op jit(solution)/shard_map/rows 1/ppermute | solution.py:746
  120.4 21.4 %collective-permute-start.23 = (bf16[512,768]{1,0:T(8,128)(2,1)S(1)}, bf16[512,768]{1,0:T(8,128)(2,1)S(1)}, u32[]{:S(2)}, u32[]{:S(2)}) collective-permute-start(bf16[512,768]{1,0:T(8,128)(2,1)S(1)} %get-tuple-element.253), channel_id=1, source_target_pairs={{1,0},{2,1},{3,2},{5,4},{6,5},{7,6},{9,8},{10,9},{11,10},{13,12},{... | collective-permute-start | bytes 2359304 | tf_op jit(solution)/shard_map/rows 1/ppermute | solution.py:747
  125.0 17.7 %copy-start.11 = (bf16[4,4,192,384]{3,2,1,0:T(8,128)(2,1)S(1)}, bf16[4,4,192,384]{3,2,1,0:T(8,128)(2,1)}, u32[]{:S(2)}) copy-start(bf16[4,4,192,384]{3,2,1,0:T(8,128)(2,1)} %copy-done.10) | copy-start | bytes 7077892
  143.9 14.0 %collective-permute-start.24 = (bf16[2,192,384]{2,1,0:T(8,128)(2,1)S(1)}, bf16[2,192,384]{2,1,0:T(8,128)(2,1)S(1)}, u32[]{:S(2)}, u32[]{:S(2)}) collective-permute-start(bf16[2,192,384]{2,1,0:T(8,128)(2,1)S(1)} %get-tuple-element.198), channel_id=1, source_target_pairs={{0,16},{4,20},{8,24},{12,28},{16,0},{20,4},{24,8},{28,12},{1,17},{... | collective-permute-start | bytes 884744 | tf_op jit(solution)/shard_map/plane one outer grad/ppermute | solution.py:729
  145.4 12.6 %collective-permute-start.25 = (bf16[2,192,384]{2,1,0:T(8,128)(2,1)S(1)}, bf16[2,192,384]{2,1,0:T(8,128)(2,1)S(1)}, u32[]{:S(2)}, u32[]{:S(2)}) collective-permute-start(bf16[2,192,384]{2,1,0:T(8,128)(2,1)S(1)} %get-tuple-element.199), channel_id=1, source_target_pairs={{0,8},{4,12},{8,0},{12,4},{16,24},{20,28},{24,16},{28,20},{1,9},{5... | collective-permute-start | bytes 884744 | tf_op jit(solution)/shard_map/plane one outer grad/ppermute | solution.py:729
  164.8 32.8 %collective-permute-start.28 = (bf16[4,4,192,384]{3,2,1,0:T(8,128)(2,1)S(1)}, bf16[4,4,192,384]{3,2,1,0:T(8,128)(2,1)S(1)}, u32[]{:S(2)}, u32[]{:S(2)}) collective-permute-start(bf16[4,4,192,384]{3,2,1,0:T(8,128)(2,1)S(1)} %get-tuple-element.217), channel_id=1, source_target_pairs={{0,4},{4,0},{8,12},{12,8},{16,20},{20,16},{24,28},{28,24},{1,5},{5... | collective-permute-start | bytes 7077896 | tf_op jit(solution)/shard_map/core inner grad/ppermute | solution.py:729
  164.9 3.9 %collective-permute-start.26 = (bf16[512,768]{1,0:T(8,128)(2,1)S(1)}, bf16[512,768]{1,0:T(8,128)(2,1)S(1)}, u32[]{:S(2)}, u32[]{:S(2)}) collective-permute-start(bf16[512,768]{1,0:T(8,128)(2,1)S(1)} %copy-done.32), channel_id=1, source_target_pairs={{1,2},{2,3},{5,6},{6,7},{9,10},{10,11},{13,14},{14,15},{17,18},{18... | collective-permute-start | bytes 2359304 | tf_op jit(solution)/shard_map/rows 2/ppermute | solution.py:746
  165.7 23.1 %collective-permute-start.27 = (bf16[512,768]{1,0:T(8,128)(2,1)S(1)}, bf16[512,768]{1,0:T(8,128)(2,1)S(1)}, u32[]{:S(2)}, u32[]{:S(2)}) collective-permute-start(bf16[512,768]{1,0:T(8,128)(2,1)S(1)} %copy-done.35), channel_id=1, source_target_pairs={{1,0},{2,1},{5,4},{6,5},{9,8},{10,9},{13,12},{14,13},{17,16},{18,1... | collective-permute-start | bytes 2359304 | tf_op jit(solution)/shard_map/rows 2/ppermute | solution.py:747
  167.0 30.6 %collective-permute-start.29 = (bf16[4,192,384]{2,1,0:T(8,128)(2,1)S(1)}, bf16[4,192,384]{2,1,0:T(8,128)(2,1)S(1)}, u32[]{:S(2)}, u32[]{:S(2)}) collective-permute-start(bf16[4,192,384]{2,1,0:T(8,128)(2,1)S(1)} %get-tuple-element.205), channel_id=1, source_target_pairs={{0,8},{4,12},{8,0},{12,4},{16,24},{20,28},{24,16},{28,20},{1,9},{5... | collective-permute-start | bytes 1769480 | tf_op jit(solution)/shard_map/plane two outer grad/ppermute | solution.py:729
  168.3 29.3 %collective-permute-start.30 = (bf16[4,192,384]{2,1,0:T(8,128)(2,1)S(1)}, bf16[4,192,384]{2,1,0:T(8,128)(2,1)}, u32[]{:S(2)}, u32[]{:S(2)}) collective-permute-start(bf16[4,192,384]{2,1,0:T(8,128)(2,1)S(1)} %get-tuple-element.218), channel_id=1, source_target_pairs={{0,16},{4,20},{8,24},{12,28},{16,0},{20,4},{24,8},{28,12},{1,17},{... | collective-permute-start | bytes 1769480 | tf_op jit(solution)/shard_map/plane two outer grad/ppermute | solution.py:729
  168.9 28.7 %copy-start.37 = (bf16[512,768]{1,0:T(8,128)(2,1)}, bf16[512,768]{1,0:T(8,128)(2,1)S(1)}, u32[]{:S(2)}) copy-start(bf16[512,768]{1,0:T(8,128)(2,1)S(1)} %collective-permute-done.26) | copy-start | bytes 2359300
  188.7 22.0 %collective-permute-start.31 = (bf16[512,768]{1,0:T(8,128)(2,1)S(1)}, bf16[512,768]{1,0:T(8,128)(2,1)S(1)}, u32[]{:S(2)}, u32[]{:S(2)}) collective-permute-start(bf16[512,768]{1,0:T(8,128)(2,1)S(1)} %collective-permute-done.26), channel_id=1, source_target_pairs={{2,3},{6,7},{10,11},{14,15},{18,19},{22,23},{26,27},{30,31}} | collective-permute-start | bytes 2359304 | tf_op jit(solution)/shard_map/rows 3/ppermute | solution.py:746
  189.4 21.3 %collective-permute-start.32 = (bf16[512,768]{1,0:T(8,128)(2,1)S(1)}, bf16[512,768]{1,0:T(8,128)(2,1)S(1)}, u32[]{:S(2)}, u32[]{:S(2)}) collective-permute-start(bf16[512,768]{1,0:T(8,128)(2,1)S(1)} %collective-permute-done.27), channel_id=1, source_target_pairs={{1,0},{5,4},{9,8},{13,12},{17,16},{21,20},{25,24},{29,28}} | collective-permute-start | bytes 2359304 | tf_op jit(solution)/shard_map/rows 3/ppermute | solution.py:747
  200.7 10.0 %collective-permute-start.33 = (bf16[2,192,384]{2,1,0:T(8,128)(2,1)S(1)}, bf16[2,192,384]{2,1,0:T(8,128)(2,1)S(1)}, u32[]{:S(2)}, u32[]{:S(2)}) collective-permute-start(bf16[2,192,384]{2,1,0:T(8,128)(2,1)S(1)} %get-tuple-element.230), channel_id=1, source_target_pairs={{0,16},{4,20},{8,24},{12,28},{16,0},{20,4},{24,8},{28,12},{1,17},{... | collective-permute-start | bytes 884744 | tf_op jit(solution)/shard_map/plane one inner grad/ppermute | solution.py:729
  202.0 8.7 %collective-permute-start.34 = (bf16[2,192,384]{2,1,0:T(8,128)(2,1)S(1)}, bf16[2,192,384]{2,1,0:T(8,128)(2,1)S(1)}, u32[]{:S(2)}, u32[]{:S(2)}) collective-permute-start(bf16[2,192,384]{2,1,0:T(8,128)(2,1)S(1)} %get-tuple-element.231), channel_id=1, source_target_pairs={{0,8},{4,12},{8,0},{12,4},{16,24},{20,28},{24,16},{28,20},{1,9},{5... | collective-permute-start | bytes 884744 | tf_op jit(solution)/shard_map/plane one inner grad/ppermute | solution.py:729
  210.7 11.8 %copy-start.20 = (bf16[4,192,384]{2,1,0:T(8,128)(2,1)S(1)}, bf16[4,192,384]{2,1,0:T(8,128)(2,1)}, u32[]{:S(2)}) copy-start(bf16[4,192,384]{2,1,0:T(8,128)(2,1)} %copy-done.19) | copy-start | bytes 1769476
  210.8 13.2 %collective-permute-start.37 = (bf16[4,4,208,384]{3,2,1,0:T(8,128)(2,1)}, bf16[4,4,208,384]{3,2,1,0:T(8,128)(2,1)}, u32[]{:S(2)}, u32[]{:S(2)}) collective-permute-start(bf16[4,4,208,384]{3,2,1,0:T(8,128)(2,1)} %get-tuple-element.234), channel_id=1, source_target_pairs={{0,4},{4,0},{8,12},{12,8},{16,20},{20,16},{24,28},{28,24},{1,5},{5... | collective-permute-start | bytes 7667720 | tf_op jit(solution)/shard_map/core attention grad/ppermute | solution.py:729
  210.9 13.1 %copy-start.4 = (bf16[4,4,208,384]{3,2,1,0:T(8,128)(2,1)S(1)}, bf16[4,4,208,384]{3,2,1,0:T(8,128)(2,1)}, u32[]{:S(2)}) copy-start(bf16[4,4,208,384]{3,2,1,0:T(8,128)(2,1)} %copy-done.3) | copy-start | bytes 7667716
  213.4 15.6 %collective-permute-start.38 = (bf16[4,192,384]{2,1,0:T(8,128)(2,1)}, bf16[4,192,384]{2,1,0:T(8,128)(2,1)}, u32[]{:S(2)}, u32[]{:S(2)}) collective-permute-start(bf16[4,192,384]{2,1,0:T(8,128)(2,1)} %get-tuple-element.241), channel_id=1, source_target_pairs={{0,8},{4,12},{8,0},{12,4},{16,24},{20,28},{24,16},{28,20},{1,9},{5... | collective-permute-start | bytes 1769480 | tf_op jit(solution)/shard_map/plane two inner grad/ppermute | solution.py:729
  215.0 15.3 %collective-permute-start.39 = (bf16[4,192,384]{2,1,0:T(8,128)(2,1)}, bf16[4,192,384]{2,1,0:T(8,128)(2,1)}, u32[]{:S(2)}, u32[]{:S(2)}) collective-permute-start(bf16[4,192,384]{2,1,0:T(8,128)(2,1)} %get-tuple-element.242), channel_id=1, source_target_pairs={{0,16},{4,20},{8,24},{12,28},{16,0},{20,4},{24,8},{28,12},{1,17},{... | collective-permute-start | bytes 1769480 | tf_op jit(solution)/shard_map/plane two inner grad/ppermute | solution.py:729
  215.7 22.6 %collective-permute-start.35 = (bf16[512,768]{1,0:T(8,128)(2,1)}, bf16[512,768]{1,0:T(8,128)(2,1)}, u32[]{:S(2)}, u32[]{:S(2)}) collective-permute-start(bf16[512,768]{1,0:T(8,128)(2,1)} %get-tuple-element.232), channel_id=1, source_target_pairs={{0,1},{1,2},{2,3},{4,5},{5,6},{6,7},{8,9},{9,10},{10,11},{12,13},{... | collective-permute-start | bytes 2359304 | tf_op jit(solution)/shard_map/grad rows 1/ppermute | solution.py:746
  221.2 20.8 %collective-permute-start.36 = (bf16[512,768]{1,0:T(8,128)(2,1)}, bf16[512,768]{1,0:T(8,128)(2,1)}, u32[]{:S(2)}, u32[]{:S(2)}) collective-permute-start(bf16[512,768]{1,0:T(8,128)(2,1)} %get-tuple-element.232), channel_id=1, source_target_pairs={{1,0},{2,1},{3,2},{5,4},{6,5},{7,6},{9,8},{10,9},{11,10},{13,12},{... | collective-permute-start | bytes 2359304 | tf_op jit(solution)/shard_map/grad rows 1/ppermute | solution.py:747
  230.2 11.8 %collective-permute-start.40 = (bf16[2,208,384]{2,1,0:T(8,128)(2,1)S(1)}, bf16[2,208,384]{2,1,0:T(8,128)(2,1)S(1)}, u32[]{:S(2)}, u32[]{:S(2)}) collective-permute-start(bf16[2,208,384]{2,1,0:T(8,128)(2,1)S(1)} %get-tuple-element.243), channel_id=1, source_target_pairs={{0,16},{4,20},{8,24},{12,28},{16,0},{20,4},{24,8},{28,12},{1,17},{... | collective-permute-start | bytes 958472 | tf_op jit(solution)/shard_map/plane one attention grad/ppermute | solution.py:729
  230.9 11.0 %collective-permute-start.41 = (bf16[2,208,384]{2,1,0:T(8,128)(2,1)S(1)}, bf16[2,208,384]{2,1,0:T(8,128)(2,1)S(1)}, u32[]{:S(2)}, u32[]{:S(2)}) collective-permute-start(bf16[2,208,384]{2,1,0:T(8,128)(2,1)S(1)} %get-tuple-element.244), channel_id=1, source_target_pairs={{0,8},{4,12},{8,0},{12,4},{16,24},{20,28},{24,16},{28,20},{1,9},{5... | collective-permute-start | bytes 958472 | tf_op jit(solution)/shard_map/plane one attention grad/ppermute | solution.py:729
  233.7 15.8 %collective-permute-start.44 = (bf16[2,384,384]{2,1,0:T(8,128)(2,1)S(1)}, bf16[2,384,384]{2,1,0:T(8,128)(2,1)S(1)}, u32[]{:S(2)}, u32[]{:S(2)}) collective-permute-start(bf16[2,384,384]{2,1,0:T(8,128)(2,1)S(1)} %pad_maximum_fusion.4), channel_id=1, source_target_pairs={{0,1},{3,2},{4,5},{7,6},{8,9},{11,10},{12,13},{15,14},{16,17},{19,... | collective-permute-start | bytes 1769480 | tf_op jit(solution)/shard_map/line ends ffn grad/ppermute | solution.py:768
  242.0 17.8 %collective-permute-start.42 = (bf16[512,768]{1,0:T(8,128)(2,1)}, bf16[512,768]{1,0:T(8,128)(2,1)S(1)}, u32[]{:S(2)}, u32[]{:S(2)}) collective-permute-start(bf16[512,768]{1,0:T(8,128)(2,1)} %collective-permute-done.35), channel_id=1, source_target_pairs={{1,2},{2,3},{5,6},{6,7},{9,10},{10,11},{13,14},{14,15},{17,18},{18... | collective-permute-start | bytes 2359304 | tf_op jit(solution)/shard_map/grad rows 2/ppermute | solution.py:746
  242.7 19.8 %collective-permute-start.43 = (bf16[512,768]{1,0:T(8,128)(2,1)}, bf16[512,768]{1,0:T(8,128)(2,1)S(1)}, u32[]{:S(2)}, u32[]{:S(2)}) collective-permute-start(bf16[512,768]{1,0:T(8,128)(2,1)} %collective-permute-done.36), channel_id=1, source_target_pairs={{1,0},{2,1},{5,4},{6,5},{9,8},{10,9},{13,12},{14,13},{17,16},{18,1... | collective-permute-start | bytes 2359304 | tf_op jit(solution)/shard_map/grad rows 2/ppermute | solution.py:747
  244.2 14.6 %collective-permute-start.45 = (bf16[4,208,384]{2,1,0:T(8,128)(2,1)S(1)}, bf16[4,208,384]{2,1,0:T(8,128)(2,1)S(1)}, u32[]{:S(2)}, u32[]{:S(2)}) collective-permute-start(bf16[4,208,384]{2,1,0:T(8,128)(2,1)S(1)} %get-tuple-element.258), channel_id=1, source_target_pairs={{0,8},{4,12},{8,0},{12,4},{16,24},{20,28},{24,16},{28,20},{1,9},{5... | collective-permute-start | bytes 1916936 | tf_op jit(solution)/shard_map/plane two attention grad/ppermute | solution.py:729
  245.5 14.2 %collective-permute-start.46 = (bf16[4,208,384]{2,1,0:T(8,128)(2,1)S(1)}, bf16[4,208,384]{2,1,0:T(8,128)(2,1)S(1)}, u32[]{:S(2)}, u32[]{:S(2)}) collective-permute-start(bf16[4,208,384]{2,1,0:T(8,128)(2,1)S(1)} %get-tuple-element.259), channel_id=1, source_target_pairs={{0,16},{4,20},{8,24},{12,28},{16,0},{20,4},{24,8},{28,12},{1,17},{... | collective-permute-start | bytes 1916936 | tf_op jit(solution)/shard_map/plane two attention grad/ppermute | solution.py:729
  248.6 25.7 %copy-start.30 = (bf16[2048,768]{1,0:T(8,128)(2,1)}, bf16[2048,768]{1,0:T(8,128)(2,1)S(1)}, u32[]{:S(2)}) copy-start(bf16[2048,768]{1,0:T(8,128)(2,1)S(1)} %select_dynamic-update-slice_fusion.3) | copy-start | bytes 9437188
  262.6 11.6 %collective-permute-start.48 = (bf16[2,384,384]{2,1,0:T(8,128)(2,1)S(1)}, bf16[2,384,384]{2,1,0:T(8,128)(2,1)S(1)}, u32[]{:S(2)}, u32[]{:S(2)}) collective-permute-start(bf16[2,384,384]{2,1,0:T(8,128)(2,1)S(1)} %add_convert_fusion), channel_id=1, source_target_pairs={{1,2},{2,1},{5,6},{6,5},{9,10},{10,9},{13,14},{14,13},{17,18},{18,... | collective-permute-start | bytes 1769480 | tf_op jit(solution)/shard_map/line middle ffn grad/ppermute | solution.py:771
  263.7 10.5 %collective-permute-start.47 = (bf16[2,208,384]{2,1,0:T(8,128)(2,1)S(1)}, bf16[2,208,384]{2,1,0:T(8,128)(2,1)S(1)}, u32[]{:S(2)}, u32[]{:S(2)}) collective-permute-start(bf16[2,208,384]{2,1,0:T(8,128)(2,1)S(1)} %add_convert_fusion.1), channel_id=1, source_target_pairs={{0,1},{1,0},{2,3},{3,2},{4,5},{5,4},{6,7},{7,6},{8,9},{9,8},{10,11... | collective-permute-start | bytes 958472 | tf_op jit(solution)/shard_map/line one attention grad/ppermute | solution.py:732
  265.3 32.0 %collective-permute-start.51 = (bf16[512,768]{1,0:T(8,128)(2,1)S(1)}, bf16[512,768]{1,0:T(8,128)(2,1)S(1)}, u32[]{:S(2)}, u32[]{:S(2)}) collective-permute-start(bf16[512,768]{1,0:T(8,128)(2,1)S(1)} %collective-permute-done.42), channel_id=1, source_target_pairs={{2,3},{6,7},{10,11},{14,15},{18,19},{22,23},{26,27},{30,31}} | collective-permute-start | bytes 2359304 | tf_op jit(solution)/shard_map/grad rows 3/ppermute | solution.py:746
  266.0 31.3 %collective-permute-start.52 = (bf16[512,768]{1,0:T(8,128)(2,1)S(1)}, bf16[512,768]{1,0:T(8,128)(2,1)S(1)}, u32[]{:S(2)}, u32[]{:S(2)}) collective-permute-start(bf16[512,768]{1,0:T(8,128)(2,1)S(1)} %collective-permute-done.43), channel_id=1, source_target_pairs={{1,0},{5,4},{9,8},{13,12},{17,16},{21,20},{25,24},{29,28}} | collective-permute-start | bytes 2359304 | tf_op jit(solution)/shard_map/grad rows 3/ppermute | solution.py:747
  274.5 22.5 %collective-permute-start.50 = (bf16[384,384]{1,0:T(8,128)(2,1)S(1)}, bf16[384,384]{1,0:T(8,128)(2,1)S(1)}, u32[]{:S(2)}, u32[]{:S(2)}) collective-permute-start(bf16[384,384]{1,0:T(8,128)(2,1)S(1)} %fusion.4), channel_id=1, source_target_pairs={{0,1},{1,0},{2,3},{3,2},{4,5},{5,4},{6,7},{7,6},{8,9},{9,8},{10,11... | collective-permute-start | bytes 884744 | tf_op jit(solution)/shard_map/line pair ffn grad/ppermute | solution.py:732
  277.4 8.1 %collective-permute-start.49 = (bf16[208,384]{1,0:T(8,128)(2,1)S(1)}, bf16[208,384]{1,0:T(8,128)(2,1)S(1)}, u32[]{:S(2)}, u32[]{:S(2)}) collective-permute-start(bf16[208,384]{1,0:T(8,128)(2,1)S(1)} %fusion.5), channel_id=1, source_target_pairs={{0,2},{1,3},{2,0},{3,1},{4,6},{5,7},{6,4},{7,5},{8,10},{9,11},{10,... | collective-permute-start | bytes 479240 | tf_op jit(solution)/shard_map/line two attention grad/ppermute | solution.py:732
  297.3 14.3 %collective-permute-start.55 = (bf16[592,384]{1,0:T(8,128)(2,1)S(1)}, bf16[592,384]{1,0:T(8,128)(2,1)S(1)}, u32[]{:S(2)}, u32[]{:S(2)}) collective-permute-start(bf16[592,384]{1,0:T(8,128)(2,1)S(1)} %pad_maximum_fusion.5), channel_id=1, source_target_pairs={{0,24},{4,28},{8,16},{12,20},{16,8},{20,12},{24,0},{28,4},{1,25},{... | collective-permute-start | bytes 1363976 | tf_op jit(solution)/shard_map/plane result/ppermute | solution.py:729
  298.6 18.1 %collective-permute-start.54 = (bf16[592,384]{1,0:T(8,128)(2,1)S(1)}, bf16[592,384]{1,0:T(8,128)(2,1)S(1)}, u32[]{:S(2)}, u32[]{:S(2)}) collective-permute-start(bf16[592,384]{1,0:T(8,128)(2,1)S(1)} %pad_maximum_fusion.5), channel_id=1, source_target_pairs={{0,16},{4,20},{8,24},{12,28},{16,0},{20,4},{24,8},{28,12},{1,17},{... | collective-permute-start | bytes 1363976 | tf_op jit(solution)/shard_map/plane result/ppermute | solution.py:729
  300.0 16.7 %collective-permute-start.53 = (bf16[592,384]{1,0:T(8,128)(2,1)S(1)}, bf16[592,384]{1,0:T(8,128)(2,1)S(1)}, u32[]{:S(2)}, u32[]{:S(2)}) collective-permute-start(bf16[592,384]{1,0:T(8,128)(2,1)S(1)} %pad_maximum_fusion.5), channel_id=1, source_target_pairs={{0,8},{4,12},{8,0},{12,4},{16,24},{20,28},{24,16},{28,20},{1,9},{5... | collective-permute-start | bytes 1363976 | tf_op jit(solution)/shard_map/plane result/ppermute | solution.py:729
  317.0 3.8 %collective-permute-start.56 = (bf16[4,592,384]{2,1,0:T(8,128)(2,1)S(1)}, bf16[4,592,384]{2,1,0:T(8,128)(2,1)S(1)}, u32[]{:S(2)}, u32[]{:S(2)}) collective-permute-start(bf16[4,592,384]{2,1,0:T(8,128)(2,1)S(1)} %pad_maximum_fusion.1.near_ref), channel_id=1, source_target_pairs={{0,4},{4,0},{8,12},{12,8},{16,20},{20,16},{24,28},{28,24},{1,5},{5... | collective-permute-start | bytes 5455880 | tf_op jit(solution)/shard_map/core result/ppermute | solution.py:729
  (45 other events, 170.3 us)
where the time goes:
time: 334 us; the launch traced here: 330 us
  waiting for transfers between devices  122 us (37%)
  Pallas kernels  94.8 us (28%)
  starting transfers between devices  75 us (22%)
  local copies, waits for them, and re-layouts  23.6 us (7%)
  other arithmetic  12.4 us (4%)
    ppermute x12, waiting for transfers between devices, along(): return lax.ppermute(array, 'tensor', [(i, i ^ r) for i in range(n_tensor)])  47.2 us
    ppermute x31, waiting for transfers between devices, across(): return lax.ppermute(array, 'dp', flip[bit])  41.6 us
    ppermute x6, waiting for transfers between devices, rows_round(): lax.ppermute(down, 'tensor', [(i + 1, i) for i in range(n_tensor - k)])  30.4 us
    ppermute x31, starting transfers between devices, across(): return lax.ppermute(array, 'dp', flip[bit])  27 us
    pallas_call x4, Pallas kernels, attention_backward(): pl.pallas_call(functools.partial(attention_backward_kernel, shard=shard,...  26.8 us
    ppermute x12, starting transfers between devices, along(): return lax.ppermute(array, 'tensor', [(i, i ^ r) for i in range(n_tensor)])  22.5 us
    unnamed x106, local copies, waits for them, and re-layouts  18.2 us
    ppermute x6, starting transfers between devices, rows_round(): lax.ppermute(up, 'tensor', [(i, i + 1) for i in range(k - 1, n_tensor - 1)])  12.2 us
  transfers between devices with their start and end apart: 57, of which 25 were waited for; matrix products, arithmetic and copies ran while one was open for 2% of the time, Pallas kernels for 21%

commit v1 on v0

--- a/solution.py
+++ b/solution.py
@@ -41,8 +41,8 @@
     return pl.BlockSpec((1,) + shape, lambda r, *_: (r + shift,) + (0,) * len(shape))
 
 
-def params():
-    return pltpu.CompilerParams(vmem_limit_bytes=24 * 1024 * 1024)
+def params(mebibytes=16):
+    return pltpu.CompilerParams(vmem_limit_bytes=mebibytes * 1024 * 1024)
 
 
 def cost(flops, moved, exps=0):
@@ -57,8 +57,9 @@
 
 
 class Masks:
-    def __init__(self, scalars, row_ref, col_ref):
-        length, table = scalars[0], scalars[3]
+    def __init__(self, scalars, lengths, row_ref, col_ref):
+        table = scalars[2]
+        length = lengths[table]
         row_q = row_ref[pl.ds(table, 1), :].astype(F32)
         col_q = col_ref[pl.ds(table, 1), :].astype(F32)
         row_k, col_k = as_column(row_q), as_column(col_q)
@@ -93,7 +94,7 @@
     )
 
 
-def attention_forward_kernel(scalars, x_ref, w_ref, b_ref, row_ref, col_ref, *rest):
+def attention_forward_kernel(scalars, lengths, x_ref, w_ref, b_ref, row_ref, col_ref, *rest):
     qkv_ref, o_ref, lse_ref = rest[-3:]
     seq = x_ref.shape[0]
     bias = b_ref[0].astype(F32)
@@ -103,7 +104,7 @@
     is_query = lax.broadcasted_iota(jnp.int32, (qkv.shape[0], 1), 0) % (3 * QKV) < QKV
     low = jnp.where(is_query, low * jnp.asarray(HD**-0.5, BF), low)
     qkv_ref[0] = low
-    masks = Masks(scalars, row_ref, col_ref)
+    masks = Masks(scalars, lengths, row_ref, col_ref)
     q_t, k_t, v_t = rows_of(qkv_ref, 0), rows_of(qkv_ref, 1), rows_of(qkv_ref, 2)
     outs, logs = [], []
     for head in range(q_t.shape[0] // HD):
@@ -126,14 +127,14 @@
 
 
 def table_rows(seq):
-    return pl.BlockSpec((seq, D), lambda r, scalars: (scalars[3], 0))
+    return pl.BlockSpec((seq, D), lambda r, scalars, *_: (scalars[2], 0))
 
 
 def bias_rows(shift=0):
     return pl.BlockSpec((1, VECTORS, HALF), lambda r, *_: (r + shift, 4 * QKV // VECTORS, 0))
 
 
-def attention_forward(scalars, tokens, weights, pieces, tags, shards, first, carried=None):
+def attention_forward(scalars, lengths, tokens, weights, pieces, tags, shards, first, carried=None):
     wide, seq = 3 * BLOCKS * QKV, tags[0].shape[1]
     count, at = pieces.shape[0], first if carried else 0
     out_shape = [
@@ -145,7 +146,7 @@
     return pl.pallas_call(
         attention_forward_kernel,
         grid_spec=pltpu.PrefetchScalarGridSpec(
-            num_scalar_prefetch=1,
+            num_scalar_prefetch=2,
             grid=(count,),
             in_specs=[
                 table_rows(seq),
@@ -158,14 +159,14 @@
             out_specs=[each(s.shape[1:], first) for s in out_shape],
         ),
         out_shape=out_shape,
-        input_output_aliases={6 + i: i for i in range(len(kept))},
+        input_output_aliases={7 + i: i for i in range(len(kept))},
         compiler_params=params(),
         cost_estimate=cost(count * 3e9, count * 3e6),
-    )(scalars, tokens, weights, pieces, *tags, *kept)
+    )(scalars, lengths, tokens, weights, pieces, *tags, *kept)
 
 
 def attention_backward_kernel(
-    scalars, x_hbm, w_hbm, qkv_hbm, o_hbm, lse_hbm, up_hbm, start_hbm, row_ref, col_ref, dbi_ref, one_ref, two_ref,
+    scalars, lengths, x_hbm, w_hbm, qkv_hbm, o_hbm, lse_hbm, up_hbm, start_hbm, row_ref, col_ref, dbi_ref, one_ref, two_ref,
     *refs, shard, carried,
 ):
     dx_ref, mine_ref, other_ref, d_ref, x_ref, w_ref, qkv_ref, o_ref, lse_ref, low_ref, start_ref, sems = refs[carried:]
@@ -177,7 +178,7 @@
         (qkv_hbm.at[at], qkv_ref),
         (o_hbm.at[at], o_ref),
         (lse_hbm.at[at], lse_ref),
-        (x_hbm.at[pl.ds(pl.multiple_of(scalars[3] * seq, 128), seq)], x_ref),
+        (x_hbm.at[pl.ds(pl.multiple_of(scalars[2] * seq, 128), seq)], x_ref),
         (start_hbm, start_ref),
     ]
     started = [pltpu.make_async_copy(source, target, sems.at[i]) for i, (source, target) in enumerate(copies)]
@@ -185,7 +186,7 @@
         copy.start()
     for copy in started[:5]:
         copy.wait()
-    masks = Masks(scalars, row_ref, col_ref)
+    masks = Masks(scalars, lengths, row_ref, col_ref)
     q_t, k_t, v_t = rows_of(qkv_ref, 0), rows_of(qkv_ref, 1), rows_of(qkv_ref, 2)
     grad_heads = product(output_rows(w_ref), low_ref[...], NT).astype(BF)
     heads_out = o_ref[0]
@@ -217,7 +218,7 @@
         for i in range(3):
             vectors += [sums_ref[i : i + 1, :HALF], sums_ref[i : i + 1, HALF:]]
     vectors = jnp.concatenate(vectors, axis=0).astype(BF)
-    c, my = scalars[1], scalars[2]
+    c, my = scalars[0], scalars[1]
     for half, out_ref in enumerate((mine_ref, other_ref)):
         start = pl.multiple_of(jnp.where(c == half, 0, HALF), 128)
         grad_w = product(grads_low, x_ref[:, pl.ds(start, HALF)], NN).astype(BF)
@@ -230,7 +231,7 @@
 
 
 def attention_backward(
-    scalars, tokens, weights, qkv, heads_out, lse, upstream, start, tags, vectors, shard, dtype, carried
+    scalars, lengths, tokens, weights, qkv, heads_out, lse, upstream, start, tags, vectors, shard, dtype, carried
 ):
     shards, wide, seq = qkv.shape
     rows = 4 * QKV + VECTORS
@@ -239,7 +240,7 @@
     return pl.pallas_call(
         functools.partial(attention_backward_kernel, shard=shard, carried=len(carried)),
         grid_spec=pltpu.PrefetchScalarGridSpec(
-            num_scalar_prefetch=1,
+            num_scalar_prefetch=2,
             grid=(1,),
             in_specs=[in_hbm()] * 7
             + [whole(tags[0].shape), whole(tags[1].shape), each(vectors[0].shape[1:], shard)]
@@ -259,10 +260,10 @@
             ],
         ),
         out_shape=[shape_of((seq, D), dtype), pieces, pieces],
-        input_output_aliases={13 + i: 1 + i for i in range(len(carried))},
+        input_output_aliases={14 + i: 1 + i for i in range(len(carried))},
         compiler_params=params(),
         cost_estimate=cost(5e9, 5e6),
-    )(scalars, tokens, weights, qkv, heads_out, lse, upstream, start, *tags, *vectors, *carried)
+    )(scalars, lengths, tokens, weights, qkv, heads_out, lse, upstream, start, *tags, *vectors, *carried)
 
 
 def gelu_pair(x):
@@ -411,16 +412,18 @@
     )(scalars, act, w_outer, hidden, cotangent, vectors)
 
 
-def ffn_back_kernel(
-    up_ref, slope_ref, wu_ref, wi_ref, normed_ref, inv_ref, vec_ref, grad_ref, grad_low_ref, inner_ref, db_ref, sums_ref,
-    acc_ref, low_ref,
-):
+def ffn_back_kernel(up_ref, start_ref, slope_ref, wu_ref, wi_ref, *refs, final):
+    if final:
+        normed_ref, inv_ref, vec_ref, *refs = refs[:3] + refs[5:]
+        grad_ref, inner_ref, db_ref, grad_low_ref, sums_ref, acc_ref, low_ref = refs
+    else:
+        grad_ref, inner_ref, db_ref, acc_ref, low_ref = refs
     r, last = pl.program_id(0), pl.num_programs(0) - 1
     seq, wide = up_ref.shape[0], wi_ref.shape[1]
 
     @pl.when(r == 0)
     def _():
-        acc_ref[...] = up_ref[...]
+        acc_ref[...] = start_ref[...]
         low_ref[...] = up_ref[...].astype(BF)
 
     db = jnp.zeros((1, wide), F32)
@@ -434,6 +437,9 @@
 
     @pl.when(r == last)
     def _():
+        if not final:
+            grad_ref[...] = acc_ref[...]
+            return
         sums = [jnp.zeros((1, D), F32)] * 3
         for start in range(0, seq, CHUNK):
             rows = slice(start, start + CHUNK)
@@ -445,32 +451,33 @@
         store_sums(sums_ref, sums)
 
 
-def ffn_back(upstream, slope, w_outer, w_inner, normed, inv_spread, vectors):
+def ffn_back(upstream, start, slope, w_outer, w_inner, first, count, norm=(), carried=()):
     shards, seq, wide = slope.shape
-    return pl.pallas_call(
-        ffn_back_kernel,
-        grid=(shards,),
+    final = bool(norm)
+    out_specs = [whole((seq, D)), each((seq, wide), first), each((1, wide), first)]
+    out_shape = [shape_of((seq, D), F32), shape_of((shards, seq, wide), BF), shape_of((shards, 1, wide), F32)]
+    if final:
+        out_specs += [whole((seq, D)), whole((8, D))]
+        out_shape += [shape_of((seq, D), BF), shape_of((8, D), F32)]
+    return pl.pallas_call(
+        functools.partial(ffn_back_kernel, final=final),
+        grid=(count,),
         in_specs=[
             whole((seq, D)),
-            each((seq, wide)),
-            each((wide, D)),
-            each((wide, D)),
             whole((seq, D)),
-            whole((seq, 1)),
-            whole(vectors.shape),
-        ],
-        out_specs=[whole((seq, D)), whole((seq, D)), each((seq, wide)), each((1, wide)), whole((8, D))],
-        out_shape=[
-            shape_of((seq, D), F32),
-            shape_of((seq, D), BF),
-            shape_of((shards, seq, wide), BF),
-            shape_of((shards, 1, wide), F32),
-            shape_of((8, D), F32),
-        ],
+            each((seq, wide), first),
+            each((wide, D), first),
+            each((wide, D), first),
+        ]
+        + [whole(array.shape) for array in norm]
+        + [any_place()] * len(carried),
+        out_specs=out_specs,
+        out_shape=out_shape,
+        input_output_aliases={8 + i: 1 + i for i in range(len(carried))},
         scratch_shapes=[pltpu.VMEM((seq, D), F32), pltpu.VMEM((seq, D), BF)],
         compiler_params=params(),
-        cost_estimate=cost(shards * 3e9, shards * 4e6),
-    )(upstream, slope, w_outer, w_inner, normed, inv_spread, vectors)
+        cost_estimate=cost(count * 3e9, count * 4e6),
+    )(upstream, start, slope, w_outer, w_inner, *norm, *carried)
 
 
 def weight_grad_kernel(scalars, left_ref, right_ref, mine_ref, other_ref, low_ref):
@@ -478,7 +485,7 @@
     def _():
         low_ref[...] = right_ref[...].astype(BF)
 
-    c, my = scalars[1], scalars[2]
+    c, my = scalars[0], scalars[1]
     rows = mine_ref.shape[2]
     for half, out_ref in enumerate((mine_ref, other_ref)):
         start = pl.multiple_of(jnp.where(c == half, 0, HALF), 128)
@@ -525,28 +532,33 @@
     return lambda kind: (col == feature + block * 2 * QKV + QKV * kind).astype(BF)
 
 
-def attention_piece(scalars, w_query, w_key, w_value, w_out, bias):
+def attention_piece(scalars, w_query, w_key, w_value, w_out, biases):
     heads = BLOCKS * QKV
 
     def kernel(scalars, *refs):
-        *w_refs, bias_ref, slab_ref, piece_ref = refs
+        w_refs, (query_ref, value_ref, inner_ref, slab_ref, piece_ref, sems) = refs[:4], refs[4:]
+        copies = []
         for j in range(BLOCKS):
             for kind, w_ref in enumerate(w_refs):
                 base = QKV * (4 * j + kind)
-                slab_ref[0, base : base + QKV] = w_ref[QKV * j : QKV * (j + 1)]
-        c, my = scalars[1], scalars[2]
-        rows = pl.ds(pl.multiple_of(my * 4 * QKV, 16), 4 * QKV)
-        piece_ref[0, : 4 * QKV] = slab_ref[0, rows, pl.ds(pl.multiple_of(c * HALF, 128), HALF)]
-        every = jnp.broadcast_to(bias_ref[...], (16, bias_ref.shape[1]))
-        of_query, of_value = every[:, :heads], every[:, heads : 2 * heads]
+                copies.append((w_ref.at[pl.ds(QKV * j, QKV)], slab_ref.at[0, pl.ds(base, QKV)]))
+        started = [pltpu.make_async_copy(source, target, sems.at[i]) for i, (source, target) in enumerate(copies)]
+        for copy in started:
+            copy.start()
+        every = lambda ref: jnp.broadcast_to(ref[...].astype(F32).reshape(1, -1), (16, ref.shape[0]))
+        of_query, of_value, inner = every(query_ref), every(value_ref), every(inner_ref)
         low = []
         for first in (0, HALF):
             places = slab_places(first, HALF)
-            low.append(product(of_query, places(0), NT) + product(of_value, places(2), NT))
-        inner = every[:, 2 * heads :].astype(F32)
+            low.append(product(of_query.astype(BF), places(0), NT) + product(of_value.astype(BF), places(2), NT))
         rows = [low[0], low[1], inner[:, :HALF], inner[:, HALF:]]
         at = lax.broadcasted_iota(jnp.int32, (16, HALF), 0)
         piece_ref[0, 4 * QKV :] = sum(jnp.where(at == i, row, 0.0) for i, row in enumerate(rows)).astype(BF)
+        for copy in started:
+            copy.wait()
+        c, my = scalars[0], scalars[1]
+        rows = pl.ds(pl.multiple_of(my * 4 * QKV, 16), 4 * QKV)
+        piece_ref[0, : 4 * QKV] = slab_ref[0, rows, pl.ds(pl.multiple_of(c * HALF, 128), HALF)]
 
     weights = (w_query.T, w_key.T, w_value.T, w_out)
     return pl.pallas_call(
@@ -554,37 +566,39 @@
         grid_spec=pltpu.PrefetchScalarGridSpec(
             num_scalar_prefetch=1,
             grid=(1,),
-            in_specs=[whole(w.shape) for w in weights] + [whole(bias.shape)],
+            in_specs=[in_hbm()] * 4 + [whole(bias.shape) for bias in biases],
             out_specs=[whole((1, 4 * heads, D)), whole((1, 4 * QKV + VECTORS, HALF))],
+            scratch_shapes=[pltpu.SemaphoreType.DMA((4 * BLOCKS,))],
         ),
         out_shape=[shape_of((1, 4 * heads, D), BF), shape_of((1, 4 * QKV + VECTORS, HALF), BF)],
-        compiler_params=params(),
+        compiler_params=params(58),
         cost_estimate=cost(2e9, 0),
-    )(scalars, *weights, bias)
+    )(scalars, *weights, *biases)
 
 
 def ffn_pieces(scalars, w_inner, w_outer):
     wide = w_inner.shape[1]
     rows = wide // BLOCKS
 
-    def kernel(scalars, wi_ref, wu_ref, wt_ref, i_ref, u_ref):
-        wt_ref[...] = wi_ref[...].T
-        c, my = scalars[1], scalars[2]
+    def kernel(scalars, wi_hbm, wu_hbm, wt_ref, i_ref, u_ref, wi_ref, sems):
+        c, my = scalars[0], scalars[1]
         block = pl.ds(pl.multiple_of(my * rows, 16), rows)
         columns = pl.ds(pl.multiple_of(c * HALF, 128), HALF)
+        run_copies([(wi_hbm, wi_ref), (wu_hbm.at[block, columns], u_ref)], sems)
+        wt_ref[...] = wi_ref[...].T
         i_ref[...] = wt_ref[block, columns]
-        u_ref[...] = wu_ref[block, columns]
 
     return pl.pallas_call(
         kernel,
         grid_spec=pltpu.PrefetchScalarGridSpec(
             num_scalar_prefetch=1,
             grid=(1,),
-            in_specs=[whole(w_inner.shape), whole(w_outer.shape)],
+            in_specs=[in_hbm()] * 2,
             out_specs=[whole((wide, D)), whole((rows, HALF)), whole((rows, HALF))],
+            scratch_shapes=[pltpu.VMEM(w_inner.shape, BF), pltpu.SemaphoreType.DMA((2,))],
         ),
         out_shape=[shape_of((wide, D), BF), shape_of((rows, HALF), BF), shape_of((rows, HALF), BF)],
-        compiler_params=params(),
+        compiler_params=params(58),
         cost_estimate=cost(2e9, 0),
     )(scalars, w_inner, w_outer)
 
@@ -593,7 +607,7 @@
     count = near.shape[1]
 
     def kernel(scalars, near_ref, far_ref, own_ref, out_ref, sems):
-        c, my = scalars[1], scalars[2]
+        c, my = scalars[0], scalars[1]
         copies = [(own_ref, out_ref.at[0])]
         for m in range(BLOCKS):
             for source, side in ((near_ref, c), (far_ref, 1 - c)):
@@ -626,7 +640,7 @@
 
     def kernel(scalars, near_ref, far_ref, *refs):
         *outs, held, sems = refs
-        c, my = scalars[1], scalars[2]
+        c, my = scalars[0], scalars[1]
         copies = []
         for m in range(BLOCKS):
             for source, side in ((near_ref, c), (far_ref, 1 - c)):
@@ -644,12 +658,12 @@
         vectors = low.astype(F32)
         for out, kind in zip(outs[6:8], (0, 2)):
             halves = [product(low, slab_places(first, HALF)(kind), NN) for first in (0, HALF)]
-            out[...] = halves[0][2:3] + halves[1][3:4]
+            out[...] = (halves[0][2:3] + halves[1][3:4])[0]
         for out, i in zip(outs[8:], (0, 4, 6, 8, 10, 12, 14)):
-            out[...] = jnp.concatenate([vectors[i : i + 1], vectors[i + 1 : i + 2]], axis=1)
+            out[...] = jnp.concatenate([vectors[i : i + 1], vectors[i + 1 : i + 2]], axis=1)[0]
 
     heads = BLOCKS * narrow
-    shapes = [(heads, D)] * 4 + [(BLOCKS * wide, D), (D, BLOCKS * wide)] + [(1, heads)] * 2 + [(1, D)] * 7
+    shapes = [(heads, D)] * 4 + [(BLOCKS * wide, D), (D, BLOCKS * wide)] + [(heads,)] * 2 + [(D,)] * 7
     return pl.pallas_call(
         kernel,
         grid_spec=pltpu.PrefetchScalarGridSpec(
@@ -764,6 +778,9 @@
     def plane_two(for_x, for_y):
         return across(for_x, 2), across(for_y, 4)
 
+    def line_sums(group):
+        return sum(f32(a[:half]) for a in group), add(*[a[half:] for a in group])
+
     def line_ends(far):
         return lax.ppermute(far, "tensor", [(0, 1), (3, 2)])
 
@@ -786,16 +803,17 @@
         index = lax.axis_index("dp")
         z = lax.axis_index("tensor")
         c, my = index & 1, (index >> 1) & 3
-        scalars = jnp.stack([lax.dynamic_index_in_dim(lengths, z, keepdims=False), c, my, z]).astype(jnp.int32)
+        scalars = jnp.stack([c, my, z]).astype(jnp.int32)
         tags = (row_ids, col_ids)
         vectors_one = f32(jnp.stack([b_attn_out, gain_one, shift_one]))
         vectors_two = f32(jnp.stack([b_outer, gain_two, shift_two]))
 
-        bias = jnp.concatenate([b_query, b_value, b_inner])[None]
-        slab, piece_a = attention_piece(scalars, w_query, w_key, w_value, w_attn_out, bias)
+        slab, piece_a = attention_piece(
+            scalars, w_query, w_key, w_value, w_attn_out, (b_query, b_value, b_inner)
+        )
         with jax.named_scope("line attention weights"):
             line_a = from_all(piece_a)
-        first = attention_forward(scalars, tokens, slab, piece_a, tags, n_tensor, 0)
+        first = attention_forward(scalars, lengths, tokens, slab, piece_a, tags, n_tensor, 0)
         w_inner_t, piece_i, piece_u = ffn_pieces(tie(scalars, slab), w_inner, w_outer)
 
         with jax.named_scope("line inner weights"):
@@ -814,7 +832,7 @@
             line_u = from_all(tie(piece_u, *line_i, far_a))
 
         w_attn = assemble(scalars, near_a, far_a, slab[0], 4 * QKV)
-        qkv, heads_out, lse = attention_forward(scalars, tokens, w_attn, own_a, tags, n_tensor, 1, first)
+        qkv, heads_out, lse = attention_forward(scalars, lengths, tokens, w_attn, own_a, tags, n_tensor, 1, first)
         own_u = jnp.stack([tie(line_u[0], lse, *plane_i)] + line_u[1:])
         near_i = jnp.stack([tie(own_i, *line_u, lse), *plane_i])
         with jax.named_scope("core inner weights"):
@@ -838,96 +856,101 @@
         mine_u, other_u = weight_grad(scalars, act, grad_two)
         with jax.named_scope("core outer grad"):
             theirs_u = across(other_u, 1)
-        grad_one, grad_one_low, grad_inner, db_inner, sums_one = ffn_back(
-            tie(grad_two, mine_u), slope, w_up, w_in, normed, inv_spread, vectors_one
-        )
-        grad_one, grad_inner, theirs_u, up_1, down_1 = barrier(grad_one, grad_inner, theirs_u, up_1, down_1)
-        with jax.named_scope("rows 2"):
-            up_2, down_2 = rows_round(2, up_1, down_1)
+        partial, *carried = ffn_back(tie(grad_two, mine_u), grad_two, slope, w_up, w_in, 0, half)
+        partial, theirs_u = barrier(partial, theirs_u)
         own_u, x_u, y_u, *via_u = core_add(mine_u, theirs_u)
         with jax.named_scope("plane one outer grad"):
             via_u = plane_one(*via_u)
-        mine_i, other_i = weight_grad(scalars, tie(grad_inner, own_u), low)
+        grad_one, grad_inner, db_inner, grad_one_low, sums_one = ffn_back(
+            grad_two, tie(partial, own_u), slope, w_up, w_in, half, half, (normed, inv_spread, vectors_one), carried
+        )
+        grad_one, grad_inner, up_1, down_1, *via_u = barrier(grad_one, grad_inner, up_1, down_1, *via_u)
+        with jax.named_scope("rows 2"):
+            up_2, down_2 = rows_round(2, up_1, down_1)
+        x_u, y_u = plane_add(x_u, y_u, *via_u)
+        with jax.named_scope("plane two outer grad"):
+            plane_u = plane_two(x_u, y_u)
+        mine_i, other_i = weight_grad(scalars, tie(grad_inner, x_u), low)
+        with jax.named_scope("core inner grad"):
+            theirs_i = across(other_i, 1)
         vectors = (db_inner, sums_one, sums_two)
         pieces = ()
 
         def shard_back(start, r):
             dtype = F32 if r else BF
             return attention_backward(
-                scalars, tokens, w_attn, qkv, heads_out, lse, grad_one_low, start, tags, vectors, r, dtype, pieces
+                scalars, lengths, tokens, w_attn, qkv, heads_out, lse, grad_one_low, start, tags, vectors, r, dtype, pieces
             )
 
         start, *pieces = shard_back(tie(grad_one, mine_i), 3)
-        start, *via_u = barrier(start, *via_u)
-        x_u, y_u = plane_add(x_u, y_u, *via_u)
-        with jax.named_scope("plane two outer grad"):
-            plane_u = plane_two(x_u, y_u)
-        start, *pieces = shard_back(tie(start, x_u), 2)
-        with jax.named_scope("core inner grad"):
-            theirs_i = across(tie(other_i, start), 1)
-        start, up_2, down_2 = barrier(start, up_2, down_2)
+        start, theirs_i = barrier(start, theirs_i)
+        own_i, x_i, y_i, *via_i = core_add(mine_i, theirs_i)
+        start, *pieces = shard_back(tie(start, own_i), 2)
+        start, up_2, down_2, *plane_u = barrier(start, up_2, down_2, *plane_u)
         with jax.named_scope("rows 3"):
             up_3, down_3 = rows_round(3, up_2, down_2)
-        start, *pieces = shard_back(start, 1)
-        start, theirs_i, *plane_u = barrier(start, theirs_i, *plane_u)
-        own_i, x_i, y_i, *via_i = core_add(mine_i, theirs_i)
         with jax.named_scope("plane one inner grad"):
-            via_i = plane_one(*via_i)
-        grad_rows, mine_a, other_a = shard_back(tie(start, own_i), 0)
-        grad_rows, mine_a, other_a, up_3, down_3, *via_i = barrier(grad_rows, mine_a, other_a, up_3, down_3, *via_i)
-
-        with jax.named_scope("grad rows 1"):
-            go_1, back_1 = rows_round(1, grad_rows, grad_rows)
-        with jax.named_scope("core attention grad"):
-            theirs_a = across(other_a, 1)
+            via_i = plane_one(*[tie(v, *plane_u) for v in via_i])
+        near_u, far_u = line_sums((own_u, *plane_u))
+        with jax.named_scope("line ends outer grad"):
+            ends_u = line_ends(far_u)
+        start, *pieces = shard_back(tie(start, far_u), 1)
+        start, *via_i = barrier(start, *via_i)
         x_i, y_i = plane_add(x_i, y_i, *via_i)
         with jax.named_scope("plane two inner grad"):
             plane_i = plane_two(x_i, y_i)
+        grad_rows, mine_a, other_a = shard_back(tie(start, x_i), 0)
+        grad_rows, mine_a, other_a, ends_u, up_3, down_3 = barrier(grad_rows, mine_a, other_a, ends_u, up_3, down_3)
+        far_u = add(far_u, ends_u[::-1])
+        with jax.named_scope("line middle outer grad"):
+            middle_u = line_middle(far_u)
+
+        with jax.named_scope("core attention grad"):
+            theirs_a = across(other_a, 1)
+        with jax.named_scope("grad rows 1"):
+            go_1, back_1 = rows_round(1, grad_rows, grad_rows)
         own_a, x_a, y_a, *via_a = core_add(mine_a, theirs_a)
-        *via_a, plane_i_x, plane_i_y = barrier(*via_a, *plane_i)
+        *via_a, middle_u, plane_i_x, plane_i_y = barrier(*via_a, middle_u, *plane_i)
         with jax.named_scope("plane one attention grad"):
             via_a = plane_one(*via_a)
-        groups = ((own_u, *plane_u), (own_i, plane_i_x, plane_i_y))
-        near_f = jnp.concatenate([sum(f32(a[:half]) for a in group) for group in groups], axis=1)
-        far_f = jnp.concatenate([add(*[a[half:] for a in group]) for group in groups], axis=1)
-        with jax.named_scope("line ends ffn grad"):
-            ends_f = line_ends(far_f)
-        go_1, back_1, *via_a = barrier(go_1, back_1, *via_a)
+        near_i, far_i = line_sums((own_i, plane_i_x, plane_i_y))
+        with jax.named_scope("line ends inner grad"):
+            ends_i = line_ends(far_i)
+        go_1, back_1, ends_i, *via_a = barrier(go_1, back_1, ends_i, *via_a)
         with jax.named_scope("grad rows 2"):
             go_2, back_2 = rows_round(2, go_1, back_1)
         x_a, y_a = plane_add(x_a, y_a, *via_a)
         with jax.named_scope("plane two attention grad"):
             plane_a = plane_two(x_a, y_a)
         layer_out = place_rows(z, tie(out_rows, *via_a), (up_1, up_2, up_3), (down_1, down_2, down_3))
-        go_2, back_2, ends_f, layer_out, *plane_a = barrier(go_2, back_2, ends_f, layer_out, *plane_a)
+        far_i = add(far_i, ends_i[::-1])
+        with jax.named_scope("line middle inner grad"):
+            middle_i = line_middle(far_i)
+        layer_out, _, *plane_a = barrier(layer_out, far_i, *plane_a)
+        group = (own_a, *plane_a)
+        low_a = [add(*[a[r] for a in group]) for r in range(1, n_tensor)]
+        with jax.named_scope("line attention grad"):
+            got_a = [along(a, r) for r, a in enumerate(low_a, 1)]
+        near_u, near_i, go_2, back_2, *_ = barrier(near_u, near_i, go_2, back_2, *plane_a)
+        near_f = [near_u + f32(middle_u[::-1]), near_i + f32(middle_i[::-1])]
+        with jax.named_scope("line pair ffn grad"):
+            pair_f = [along(near[1].astype(BF), 1) for near in near_f]
+        pair_u, pair_i, *got_a = barrier(*pair_f, *got_a)
+        own_a = sum(f32(a[0]) for a in group) + f32(got_a[0]) + f32(got_a[1])
+        done = [line_end(own_a, got_a[2]), line_end(near_f[0][0], pair_u), line_end(near_f[1][0], pair_i)]
+        done = jnp.concatenate(done)
+        with jax.named_scope("plane result"):
+            found = plane(done)
         with jax.named_scope("grad rows 3"):
             go_3, back_3 = rows_round(3, go_2, back_2)
-        with jax.named_scope("line middle ffn grad"):
-            middle_f = line_middle(add(far_f, ends_f[::-1]))
-        group = (own_a, *plane_a)
-        odd_a = add(*[a[1::2] for a in group])
-        with jax.named_scope("line one attention grad"):
-            odd_a = along(odd_a, 1)
-        even_a = sum(f32(a[0::2]) for a in group)
-        odd_a, middle_f = barrier(odd_a, middle_f)
-        near_f = near_f + f32(middle_f[::-1])
-        with jax.named_scope("line pair ffn grad"):
-            pair_f = along(near_f[1].astype(BF), 1)
-        even_a = even_a + f32(odd_a)
-        with jax.named_scope("line two attention grad"):
-            last_a = along(even_a[1].astype(BF), 2)
-        last_a, pair_f = barrier(last_a, pair_f)
-        done = jnp.concatenate([line_end(even_a[0], last_a), line_end(near_f[0], pair_f)])
-        done, go_3, back_3 = barrier(done, go_3, back_3)
-        with jax.named_scope("plane result"):
-            found = plane(done)
-        grad_tokens = place_rows(z, grad_rows, (go_1, go_2, go_3), (back_1, back_2, back_3))
+        go_3, back_3, *found = barrier(go_3, back_3, *found)
         near = jnp.stack([done, *found])
         with jax.named_scope("core result"):
             far = across(near, 1)
+        grad_tokens = place_rows(z, grad_rows, (go_1, go_2, go_3), (back_1, back_2, back_3))
         grads = finish(scalars, near, far, block, QKV)
         grad_wq, grad_wk, grad_wv, grad_wo, grad_wu, grad_wi, *vectors = grads
-        grad_bq, grad_bv, grad_bi, gain_1, shift_1, b_1, gain_2, shift_2, b_2 = [v.reshape(-1) for v in vectors]
+        grad_bq, grad_bv, grad_bi, gain_1, shift_1, b_1, gain_2, shift_2, b_2 = vectors
 
         return (
             layer_out,

time: 334 us -> 299 us (0.90)
  waiting for transfers between devices: 122 us -> 84.1 us
  starting transfers between devices: 75 us -> 98.5 us
  local copies, waits for them, and re-layouts: 23.6 us -> 7.59 us
    ppermute x12 -> x14, waiting for transfers between devices: 47.2 us -> 22.6 us  [along(): return lax.ppermute(array, 'tensor', [(i, i ^ r) for i in range(n_tensor)])]
    ppermute x12 -> x14, starting transfers between devices: 22.5 us -> 44.6 us  [along(): return lax.ppermute(array, 'tensor', [(i, i ^ r) for i in range(n_tensor)])]
    ppermute x6, waiting for transfers between devices: 30.4 us -> 17.7 us  [rows_round(): lax.ppermute(down, 'tensor', [(i + 1, i) for i in range(n_tensor - k)])]
    unnamed x106 -> x88, local copies, waits for them, and re-layouts: 18.2 us -> 5.82 us
    pallas_call x7 -> x0, other arithmetic: 4.23 us -> none  [finish(): pl.pallas_call(kernel, grid_spec=pltpu.PrefetchScalarGridSpec(num_scalar_...]
    pallas_call x1 -> x2, Pallas kernels: 10.8 us -> 10.8 us  [ffn_back(): pl.pallas_call(functools.partial(ffn_back_kernel, final=final), grid=(cou...]
  transfers between devices with their start and end apart: 57 -> 61, of which waited for: 25 -> 27; matrix products, arithmetic and copies ran while one was open for 2% -> 3% of each run, Pallas kernels for 21% -> 23%
where the time goes in v1:
time: 299 us; the launch traced here: 295 us
  starting transfers between devices  98.5 us (33%)
  Pallas kernels  92.7 us (31%)
  waiting for transfers between devices  84.1 us (28%)
  other arithmetic  9.7 us (3%)
  local copies, waits for them, and re-layouts  7.59 us (3%)
    ppermute x14, starting transfers between devices, along(): return lax.ppermute(array, 'tensor', [(i, i ^ r) for i in range(n_tensor)])  44.6 us
    ppermute x31, waiting for transfers between devices, across(): return lax.ppermute(array, 'dp', flip[bit])  41.1 us
    ppermute x31, starting transfers between devices, across(): return lax.ppermute(array, 'dp', flip[bit])  27.3 us
    pallas_call x4, Pallas kernels, attention_backward(): pl.pallas_call(functools.partial(attention_backward_kernel, shard=shard,...  25 us
    ppermute x14, waiting for transfers between devices, along(): return lax.ppermute(array, 'tensor', [(i, i ^ r) for i in range(n_tensor)])  22.6 us
    ppermute x6, waiting for transfers between devices, rows_round(): lax.ppermute(down, 'tensor', [(i + 1, i) for i in range(n_tensor - k)])  17.7 us
    pallas_call x1, Pallas kernels, inner_half(): pl.pallas_call(inner_kernel, grid_spec=pltpu.PrefetchScalarGridSpec(num_s...  11.7 us
    pallas_call x2, Pallas kernels, ffn_back(): pl.pallas_call(functools.partial(ffn_back_kernel, final=final), grid=(cou...  10.8 us
  transfers between devices with their start and end apart: 61, of which 27 were waited for; matrix products, arithmetic and copies ran while one was open for 3% of the time, Pallas kernels for 23%

profile of v1, /device:TPU:0, one launch (start us, length us, event | category | flops | bytes accessed | tf_op | source)
XLA Modules:
  0.0 294.7 jit_solution(7159712306938911731)
XLA Ops:
  1.3 4.0 %shard_map.323 = (bf16[1,768,768]{2,1,0:T(8,128)(2,1)}, bf16[1,208,384]{2,1,0:T(8,128)(2,1)}) custom-call(s32[3]{0:T(128)} %pad_add_fusion.scalars, bf16[192,768]{1,0:T(8,128)(2,1)} %bitcast.79, bf16[192,768]{1,0:T(8,128)(2,1)} %bitcast.80, bf16[192,768]{1,0:T(8,128)(2,1)} %bitcast.81, bf16[192,768]{1,0:T(8,128)(2,1)} %refs_3_.1, bf16[192]{0:T(256)(128)(2,1)} %refs_4_.1, ...), custom_call_target="tpu_custom_call" | custom-call | flops 100000000 | tf_op jit(solution)/shard_map/pallas_call | solution.py:564
  5.3 3.1 %collective-permute-start = (bf16[1,208,384]{2,1,0:T(8,128)(2,1)}, bf16[1,208,384]{2,1,0:T(8,128)(2,1)S(1)}, u32[]{:S(2)}, u32[]{:S(2)}) collective-permute-start(bf16[1,208,384]{2,1,0:T(8,128)(2,1)} %get-tuple-element.167.b_ref.own_ref), channel_id=1, source_target_pairs={{0,1},{1,0},{2,3},{3,2},{4,5},{5,4},{6,7},{7,6},{8,9},{9,8},{10,11... | collective-permute-start | bytes 479240 | tf_op jit(solution)/shard_map/line attention weights/ppermute | solution.py:746
  8.4 2.6 collective-permute-start.1
  11.0 3.4 %shard_map.324 = (bf16[768,768]{1,0:T(8,128)(2,1)}, bf16[192,384]{1,0:T(8,128)(2,1)}, bf16[192,384]{1,0:T(8,128)(2,1)}) custom-call(s32[3]{0:T(128)} %pad_add_fusion.scalars, bf16[768,768]{1,0:T(8,128)(2,1)} %wi_hbm.1, bf16[768,768]{1,0:T(8,128)(2,1)} %own_ref.1), custom_call_target="tpu_custom_call" | custom-call | flops 100000000 | tf_op jit(solution)/shard_map/pallas_call | solution.py:591
  15.8 2.8 shard_map.325
  18.6 4.9 %collective-permute-done.1 = bf16[1,208,384]{2,1,0:T(8,128)(2,1)S(1)} collective-permute-done((bf16[1,208,384]{2,1,0:T(8,128)(2,1)}, bf16[1,208,384]{2,1,0:T(8,128)(2,1)S(1)}, u32[]{:S(2)}, u32[]{:S(2)}) %collective-permute-start.1) | collective-permute-done | bytes 159776 | tf_op jit(solution)/shard_map/line attention weights/ppermute | solution.py:746
  23.5 1.6 collective-permute-start.6
  25.1 1.5 collective-permute-start.7
  27.1 2.5 collective-permute-start.3
  30.6 3.2 %collective-permute-done.3 = bf16[192,384]{1,0:T(8,128)(2,1)S(1)} collective-permute-done((bf16[192,384]{1,0:T(8,128)(2,1)S(1)}, bf16[192,384]{1,0:T(8,128)(2,1)S(1)}, u32[]{:S(2)}, u32[]{:S(2)}) %collective-permute-start.3) | collective-permute-done | bytes 147488 | tf_op jit(solution)/shard_map/line inner weights/ppermute | solution.py:746
  33.8 2.1 collective-permute-start.5
  36.0 5.8 %collective-permute-done.4 = bf16[192,384]{1,0:T(8,128)(2,1)S(1)} collective-permute-done((bf16[192,384]{1,0:T(8,128)(2,1)S(1)}, bf16[192,384]{1,0:T(8,128)(2,1)S(1)}, u32[]{:S(2)}, u32[]{:S(2)}) %collective-permute-start.4) | collective-permute-done | bytes 147488 | tf_op jit(solution)/shard_map/line inner weights/ppermute | solution.py:746
  41.8 3.4 %collective-permute-done.7 = bf16[3,208,384]{2,1,0:T(8,128)(2,1)S(1)} collective-permute-done((bf16[3,208,384]{2,1,0:T(8,128)(2,1)S(1)}, bf16[3,208,384]{2,1,0:T(8,128)(2,1)S(1)}, u32[]{:S(2)}, u32[]{:S(2)}) %collective-permute-start.7) | collective-permute-done | bytes 479264 | tf_op jit(solution)/shard_map/plane attention weights/ppermute | solution.py:743
  45.7 1.3 collective-permute-start.13
  47.8 1.4 collective-permute-start.15
  49.5 3.9 %collective-permute-start.10 = (bf16[192,384]{1,0:T(8,128)(2,1)S(1)}, bf16[192,384]{1,0:T(8,128)(2,1)S(1)}, u32[]{:S(2)}, u32[]{:S(2)}) collective-permute-start(bf16[192,384]{1,0:T(8,128)(2,1)S(1)} %copy-done.41), channel_id=1, source_target_pairs={{0,1},{1,0},{2,3},{3,2},{4,5},{5,4},{6,7},{7,6},{8,9},{9,8},{10,11... | collective-permute-start | bytes 442376 | tf_op jit(solution)/shard_map/line outer weights/ppermute | solution.py:746
  54.6 6.0 %collective-permute-done.10 = bf16[192,384]{1,0:T(8,128)(2,1)S(1)} collective-permute-done((bf16[192,384]{1,0:T(8,128)(2,1)S(1)}, bf16[192,384]{1,0:T(8,128)(2,1)S(1)}, u32[]{:S(2)}, u32[]{:S(2)}) %collective-permute-start.10) | collective-permute-done | bytes 147488 | tf_op jit(solution)/shard_map/line outer weights/ppermute | solution.py:746
  60.6 1.3 collective-permute-start.12
  61.9 1.4 shard_map.326.w_ref.wo_ref.w_hbm
  63.4 7.2 %shard_map.327 = (bf16[4,576,512]{2,1,0:T(8,128)(2,1)S(1)}, bf16[4,192,512]{2,1,0:T(8,128)(2,1)S(1)}, f32[4,8,512]{2,1,0:T(8,128)S(1)}) custom-call(s32[3]{0:T(128)S(1)} %copy-done.19, s32[4]{0:T(128)S(1)} %copy-done.20, bf16[2048,768]{1,0:T(8,128)(2,1)S(1)} %copy-done, ...), custom_call_target="tpu_custom_call", output_to_operand_aliasing={{0}: (7, {}), {1}: (8, {}), {2}: (9, {})} | custom-call | flops 450000000 | bytes 450000 | tf_op jit(solution)/shard_map/pallas_call | solution.py:146
  71.1 1.3 collective-permute-start.17
  73.3 1.4 collective-permute-start.19
  76.1 11.7 %shard_map.329 = (f32[512,768]{1,0:T(8,128)S(1)}, f32[512,1]{1,0:T(8,128)S(1)}, f32[512,768]{1,0:T(8,128)S(1)}, bf16[512,768]{1,0:T(8,128)(2,1)S(1)}, bf16[4,512...) custom-call(s32[3]{0:T(128)S(1)} %copy-done.19, bf16[4,192,512]{2,1,0:T(8,128)(2,1)S(1)} %get-tuple-element.177.o_ref.o_hbm, ...), custom_call_target="tpu_custom_call" | custom-call | flops 600000000 | bytes 1000000 | tf_op jit(solution)/shard_map/pallas_call | solution.py:332
  89.8 2.8 collective-permute-done.18
  92.6 1.6 collective-permute-done.19
  94.7 3.6 %collective-permute-done.20.far_ref = bf16[4,3,192,384]{3,2,1,0:T(8,128)(2,1)S(1)} collective-permute-done((bf16[4,3,192,384]{3,2,1,0:T(8,128)(2,1)S(1)}, bf16[4,3,192,384]{3,2,1,0:T(8,128)(2,1)S(1)}, u32[]{:S(2)}, u32[]{:S(2)}) %collective-permute-start.20) | collective-permute-done | bytes 1769504 | tf_op jit(solution)/shard_map/core outer weights/ppermute | solution.py:743
  99.5 5.1 %shard_map.331 = (bf16[512,768]{1,0:T(8,128)(2,1)S(1)}, f32[512,768]{1,0:T(8,128)S(1)}, f32[8,768]{1,0:T(8,128)S(1)}) custom-call(s32[3]{0:T(128)S(1)} %copy-done.19, bf16[4,512,768]{2,1,0:T(8,128)(2,1)S(1)} %get-tuple-element.184.act_ref.left_ref, bf16[4,768,768]{2,1,0:T(8,128)(2,1)S(1)} %shard_map.330.wu_ref, ...), custom_call_target="tpu_custom_call" | custom-call | flops 250000000 | bytes 700000 | tf_op jit(solution)/shard_map/pallas_call | solution.py:394
  104.7 5.1 %shard_map.332 = (bf16[4,4,192,384]{3,2,1,0:T(8,128)(2,1)S(1)}, bf16[4,4,192,384]{3,2,1,0:T(8,128)(2,1)S(1)}) custom-call(s32[3]{0:T(128)S(1)} %copy-done.19, bf16[4,512,768]{2,1,0:T(8,128)(2,1)S(1)} %get-tuple-element.184.act_ref.left_ref, f32[512,768]{1,0:T(8,128)S(1)} %get-tuple-element.193.right_ref.up_ref.start_ref), custom_call_target="tpu_custom_call" | custom-call | flops 300000000 | bytes 400000 | tf_op jit(solution)/shard_map/pallas_call | solution.py:501
  110.0 4.3 %collective-permute-start.22 = (bf16[512,768]{1,0:T(8,128)(2,1)S(1)}, bf16[512,768]{1,0:T(8,128)(2,1)}, u32[]{:S(2)}, u32[]{:S(2)}) collective-permute-start(bf16[512,768]{1,0:T(8,128)(2,1)S(1)} %get-tuple-element.273), channel_id=1, source_target_pairs={{0,1},{1,2},{2,3},{4,5},{5,6},{6,7},{8,9},{9,10},{10,11},{12,13},{... | collective-permute-start | bytes 2359304 | tf_op jit(solution)/shard_map/rows 1/ppermute | solution.py:760
  114.4 1.3 collective-permute-start.23
  115.7 5.1 %shard_map.333 = (f32[512,768]{1,0:T(8,128)S(1)}, bf16[4,512,768]{2,1,0:T(8,128)(2,1)S(1)}, f32[4,1,768]{2,1,0:T(1,128)S(1)}) custom-call(f32[512,768]{1,0:T(8,128)S(1)} %get-tuple-element.193.right_ref.up_ref.start_ref, f32[512,768]{1,0:T(8,128)S(1)} %get-tuple-element.193.right_ref.up_ref.start_ref, bf16[4,512,768]{2,1,0:T(8,128)(2,1)S(1)} %get-tuple-element.194.slope_ref, ...), custom_call_target="tpu_custom_call" | custom-call | flops 300000000 | bytes 400000 | tf_op jit(solution)/shard_map/pallas_call | solution.py:462
  122.8 1.5 collective-permute-start.24
  124.8 5.7 %shard_map.335 = (f32[512,768]{1,0:T(8,128)S(1)}, bf16[4,512,768]{2,1,0:T(8,128)(2,1)S(1)}, f32[4,1,768]{2,1,0:T(1,128)S(1)}, bf16[512,768]{1,0:T(8,128)(2,1)S(1)}, f32[8,768]{1,0:T(8,128)S(1)}) custom-call(f32[512,768]{1,0:T(8,128)S(1)} %get-tuple-element.193.right_ref.up_ref.start_ref, ...), custom_call_target="tpu_custom_call", output_to_operand_aliasing={{1}: (8, {}), {2}: (9, {})} | custom-call | flops 300000000 | bytes 400000 | tf_op jit(solution)/shard_map/pallas_call | solution.py:462
  130.8 5.1 %collective-permute-done.23 = bf16[512,768]{1,0:T(8,128)(2,1)} collective-permute-done((bf16[512,768]{1,0:T(8,128)(2,1)S(1)}, bf16[512,768]{1,0:T(8,128)(2,1)}, u32[]{:S(2)}, u32[]{:S(2)}) %collective-permute-start.23) | collective-permute-done | bytes 786464 | tf_op jit(solution)/shard_map/rows 1/ppermute | solution.py:761
  136.1 5.1 %shard_map.337 = (bf16[4,4,192,384]{3,2,1,0:T(8,128)(2,1)S(1)}, bf16[4,4,192,384]{3,2,1,0:T(8,128)(2,1)S(1)}) custom-call(s32[3]{0:T(128)S(1)} %copy-done.19, bf16[4,512,768]{2,1,0:T(8,128)(2,1)S(1)} %get-tuple-element.216.left_ref, bf16[512,768]{1,0:T(8,128)(2,1)S(1)} %copy-done.13), custom_call_target="tpu_custom_call" | custom-call | flops 300000000 | bytes 400000 | tf_op jit(solution)/shard_map/pallas_call | solution.py:501
  142.0 1.3 collective-permute-start.28
  143.3 1.3 collective-permute-start.29
  145.4 6.3 %shard_map.338 = (f32[512,768]{1,0:T(8,128)S(1)}, bf16[4,4,208,384]{3,2,1,0:T(8,128)(2,1)S(1)}, bf16[4,4,208,384]{3,2,1,0:T(8,128)(2,1)S(1)}) custom-call(s32[3]{0:T(128)S(1)} %copy-done.19, s32[4]{0:T(128)S(1)} %copy-done.20, bf16[2048,768]{1,0:T(8,128)(2,1)S(1)} %copy-done, bf16[4,768,768]{2,1,0:T(8,128)(2,1)S(1)} %shard_map.326.w_ref.wo_ref.w_hbm, ...), custom_call_target="tpu_custom_call" | custom-call | flops 250000000 | bytes 250000 | tf_op jit(solution)/shard_map/pallas_call | solution.py:240
  152.9 5.9 %shard_map.340 = (f32[512,768]{1,0:T(8,128)S(1)}, bf16[4,4,208,384]{3,2,1,0:T(8,128)(2,1)S(1)}, bf16[4,4,208,384]{3,2,1,0:T(8,128)(2,1)S(1)}) custom-call(s32[3]{0:T(128)S(1)} %copy-done.19, s32[4]{0:T(128)S(1)} %copy-done.20, bf16[2048,768]{1,0:T(8,128)(2,1)S(1)} %copy-done, ...), custom_call_target="tpu_custom_call", output_to_operand_aliasing={{1}: (14, {}), {2}: (15, {})} | custom-call | flops 250000000 | bytes 250000 | tf_op jit(solution)/shard_map/pallas_call | solution.py:240
  160.0 4.5 %collective-permute-done.28 = bf16[512,768]{1,0:T(8,128)(2,1)S(1)} collective-permute-done((bf16[512,768]{1,0:T(8,128)(2,1)}, bf16[512,768]{1,0:T(8,128)(2,1)S(1)}, u32[]{:S(2)}, u32[]{:S(2)}) %collective-permute-start.28) | collective-permute-done | bytes 786464 | tf_op jit(solution)/shard_map/rows 2/ppermute | solution.py:761
  165.2 1.3 collective-permute-start.35
  169.9 4.6 %collective-permute-start.33 = (bf16[2,192,384]{2,1,0:T(8,128)(2,1)S(1)}, bf16[2,192,384]{2,1,0:T(8,128)(2,1)S(1)}, u32[]{:S(2)}, u32[]{:S(2)}) collective-permute-start(bf16[2,192,384]{2,1,0:T(8,128)(2,1)S(1)} %get-tuple-element.323), channel_id=1, source_target_pairs={{0,1},{3,2},{4,5},{7,6},{8,9},{11,10},{12,13},{15,14},{16,17},{19,... | collective-permute-start | bytes 884744 | tf_op jit(solution)/shard_map/line ends outer grad/ppermute | solution.py:785
  174.5 6.1 %shard_map.341 = (f32[512,768]{1,0:T(8,128)S(1)}, bf16[4,4,208,384]{3,2,1,0:T(8,128)(2,1)S(1)}, bf16[4,4,208,384]{3,2,1,0:T(8,128)(2,1)S(1)}) custom-call(s32[3]{0:T(128)S(1)} %copy-done.19, s32[4]{0:T(128)S(1)} %copy-done.20, bf16[2048,768]{1,0:T(8,128)(2,1)S(1)} %copy-done, ...), custom_call_target="tpu_custom_call", output_to_operand_aliasing={{1}: (14, {}), {2}: (15, {})} | custom-call | flops 250000000 | bytes 250000 | tf_op jit(solution)/shard_map/pallas_call | solution.py:240
  180.9 6.7 %shard_map.343 = (bf16[512,768]{1,0:T(8,128)(2,1)}, bf16[4,4,208,384]{3,2,1,0:T(8,128)(2,1)S(1)}, bf16[4,4,208,384]{3,2,1,0:T(8,128)(2,1)S(1)}) custom-call(s32[3]{0:T(128)S(1)} %copy-done.19, s32[4]{0:T(128)S(1)} %copy-done.20, bf16[2048,768]{1,0:T(8,128)(2,1)S(1)} %copy-done, ...), custom_call_target="tpu_custom_call", output_to_operand_aliasing={{1}: (14, {}), {2}: (15, {})} | custom-call | flops 250000000 | bytes 250000 | tf_op jit(solution)/shard_map/pallas_call | solution.py:240
  190.3 3.4 %collective-permute-start.36 = (bf16[512,768]{1,0:T(8,128)(2,1)}, bf16[512,768]{1,0:T(8,128)(2,1)}, u32[]{:S(2)}, u32[]{:S(2)}) collective-permute-start(bf16[512,768]{1,0:T(8,128)(2,1)} %get-tuple-element.260), channel_id=1, source_target_pairs={{0,1},{1,2},{2,3},{4,5},{5,6},{6,7},{8,9},{9,10},{10,11},{12,13},{... | collective-permute-start | bytes 2359304 | tf_op jit(solution)/shard_map/grad rows 1/ppermute | solution.py:760
  193.7 1.3 collective-permute-start.37
  196.2 7.2 %collective-permute-done.40 = bf16[4,192,384]{2,1,0:T(8,128)(2,1)S(1)} collective-permute-done((bf16[4,192,384]{2,1,0:T(8,128)(2,1)S(1)}, bf16[4,192,384]{2,1,0:T(8,128)(2,1)S(1)}, u32[]{:S(2)}, u32[]{:S(2)}) %collective-permute-start.40) | collective-permute-done | bytes 589856 | tf_op jit(solution)/shard_map/plane two inner grad/ppermute | solution.py:743
  207.9 2.0 collective-permute-start.42
  211.0 3.9 %collective-permute-done.37 = bf16[512,768]{1,0:T(8,128)(2,1)} collective-permute-done((bf16[512,768]{1,0:T(8,128)(2,1)}, bf16[512,768]{1,0:T(8,128)(2,1)}, u32[]{:S(2)}, u32[]{:S(2)}) %collective-permute-start.37) | collective-permute-done | bytes 786464 | tf_op jit(solution)/shard_map/grad rows 1/ppermute | solution.py:761
  214.9 1.3 collective-permute-done.42
  220.9 1.3 collective-permute-start.48
  224.7 1.5 select_dynamic-update-slice_fusion.3
  226.2 5.6 %collective-permute-done.45 = bf16[4,208,384]{2,1,0:T(8,128)(2,1)S(1)} collective-permute-done((bf16[4,208,384]{2,1,0:T(8,128)(2,1)S(1)}, bf16[4,208,384]{2,1,0:T(8,128)(2,1)S(1)}, u32[]{:S(2)}, u32[]{:S(2)}) %collective-permute-start.45) | collective-permute-done | bytes 639008 | tf_op jit(solution)/shard_map/plane two attention grad/ppermute | solution.py:743
  232.9 6.0 %collective-permute-start.54 = (bf16[208,384]{1,0:T(8,128)(2,1)S(1)}, bf16[208,384]{1,0:T(8,128)(2,1)S(1)}, u32[]{:S(2)}, u32[]{:S(2)}) collective-permute-start(bf16[208,384]{1,0:T(8,128)(2,1)S(1)} %get-tuple-element.319), channel_id=1, source_target_pairs={{0,1},{1,0},{2,3},{3,2},{4,5},{5,4},{6,7},{7,6},{8,9},{9,8},{10,11... | collective-permute-start | bytes 479240 | tf_op jit(solution)/shard_map/line attention grad/ppermute | solution.py:746
  239.0 7.9 %collective-permute-start.56 = (bf16[208,384]{1,0:T(8,128)(2,1)S(1)}, bf16[208,384]{1,0:T(8,128)(2,1)S(1)}, u32[]{:S(2)}, u32[]{:S(2)}) collective-permute-start(bf16[208,384]{1,0:T(8,128)(2,1)S(1)} %get-tuple-element.317), channel_id=1, source_target_pairs={{0,3},{1,2},{2,1},{3,0},{4,7},{5,6},{6,5},{7,4},{8,11},{9,10},{10,... | collective-permute-start | bytes 479240 | tf_op jit(solution)/shard_map/line attention grad/ppermute | solution.py:746
  246.9 4.2 %collective-permute-done.48 = bf16[512,768]{1,0:T(8,128)(2,1)S(1)} collective-permute-done((bf16[512,768]{1,0:T(8,128)(2,1)}, bf16[512,768]{1,0:T(8,128)(2,1)S(1)}, u32[]{:S(2)}, u32[]{:S(2)}) %collective-permute-start.48) | collective-permute-done | bytes 786464 | tf_op jit(solution)/shard_map/grad rows 2/ppermute | solution.py:761
  251.2 6.7 %collective-permute-start.51 = (bf16[192,384]{1,0:T(8,128)(2,1)S(1)}, bf16[192,384]{1,0:T(8,128)(2,1)S(1)}, u32[]{:S(2)}, u32[]{:S(2)}) collective-permute-start(bf16[192,384]{1,0:T(8,128)(2,1)S(1)} %fusion.10), channel_id=1, source_target_pairs={{0,1},{1,0},{2,3},{3,2},{4,5},{5,4},{6,7},{7,6},{8,9},{9,8},{10,11... | collective-permute-start | bytes 442376 | tf_op jit(solution)/shard_map/line pair ffn grad/ppermute | solution.py:746
  258.0 6.2 %collective-permute-start.53 = (bf16[192,384]{1,0:T(8,128)(2,1)S(1)}, bf16[192,384]{1,0:T(8,128)(2,1)S(1)}, u32[]{:S(2)}, u32[]{:S(2)}) collective-permute-start(bf16[192,384]{1,0:T(8,128)(2,1)S(1)} %fusion.11), channel_id=1, source_target_pairs={{0,1},{1,0},{2,3},{3,2},{4,5},{5,4},{6,7},{7,6},{8,9},{9,8},{10,11... | collective-permute-start | bytes 442376 | tf_op jit(solution)/shard_map/line pair ffn grad/ppermute | solution.py:746
  266.8 2.1 collective-permute-done.53
  271.0 1.8 collective-permute-start.59
  272.7 7.5 %collective-permute-done.57 = bf16[592,384]{1,0:T(8,128)(2,1)S(1)} collective-permute-done((bf16[592,384]{1,0:T(8,128)(2,1)S(1)}, bf16[592,384]{1,0:T(8,128)(2,1)S(1)}, u32[]{:S(2)}, u32[]{:S(2)}) %collective-permute-start.57) | collective-permute-done | bytes 454688 | tf_op jit(solution)/shard_map/plane result/ppermute | solution.py:743
  280.2 5.7 %collective-permute-done.58 = bf16[592,384]{1,0:T(8,128)(2,1)S(1)} collective-permute-done((bf16[592,384]{1,0:T(8,128)(2,1)S(1)}, bf16[592,384]{1,0:T(8,128)(2,1)S(1)}, u32[]{:S(2)}, u32[]{:S(2)}) %collective-permute-start.58) | collective-permute-done | bytes 454688 | tf_op jit(solution)/shard_map/plane result/ppermute | solution.py:743
  288.2 1.4 select_dynamic-update-slice_fusion
  290.1 4.4 %shard_map.346 = (f32[192,768]{1,0:T(8,128)}, f32[192,768]{1,0:T(8,128)}, f32[192,768]{1,0:T(8,128)}, f32[192,768]{1,0:T(8,128)}, f32[768,768]{1,0:T(8,128)}, /*...) custom-call(s32[3]{0:T(128)S(1)} %copy-done.19, ...), custom_call_target="tpu_custom_call" | custom-call | flops 100000000 | tf_op jit(solution)/shard_map/pallas_call | solution.py:667
  (208 shorter events, 49.0 us)
Async XLA Ops:
  5.3 13.2 %collective-permute-start = (bf16[1,208,384]{2,1,0:T(8,128)(2,1)}, bf16[1,208,384]{2,1,0:T(8,128)(2,1)S(1)}, u32[]{:S(2)}, u32[]{:S(2)}) collective-permute-start(bf16[1,208,384]{2,1,0:T(8,128)(2,1)} %get-tuple-element.167.b_ref.own_ref), channel_id=1, source_target_pairs={{0,1},{1,0},{2,3},{3,2},{4,5},{5,4},{6,7},{7,6},{8,9},{9,8},{10,11... | collective-permute-start | bytes 479240 | tf_op jit(solution)/shard_map/line attention weights/ppermute | solution.py:746
  8.4 15.0 %collective-permute-start.1 = (bf16[1,208,384]{2,1,0:T(8,128)(2,1)}, bf16[1,208,384]{2,1,0:T(8,128)(2,1)S(1)}, u32[]{:S(2)}, u32[]{:S(2)}) collective-permute-start(bf16[1,208,384]{2,1,0:T(8,128)(2,1)} %get-tuple-element.167.b_ref.own_ref), channel_id=1, source_target_pairs={{0,2},{1,3},{2,0},{3,1},{4,6},{5,7},{6,4},{7,5},{8,10},{9,11},{10,... | collective-permute-start | bytes 479240 | tf_op jit(solution)/shard_map/line attention weights/ppermute | solution.py:746
  11.0 12.4 %collective-permute-start.2 = (bf16[1,208,384]{2,1,0:T(8,128)(2,1)}, bf16[1,208,384]{2,1,0:T(8,128)(2,1)S(1)}, u32[]{:S(2)}, u32[]{:S(2)}) collective-permute-start(bf16[1,208,384]{2,1,0:T(8,128)(2,1)} %get-tuple-element.167.b_ref.own_ref), channel_id=1, source_target_pairs={{0,3},{1,2},{2,1},{3,0},{4,7},{5,6},{6,5},{7,4},{8,11},{9,10},{10,... | collective-permute-start | bytes 479240 | tf_op jit(solution)/shard_map/line attention weights/ppermute | solution.py:746
  23.5 18.3 %collective-permute-start.6 = (bf16[3,208,384]{2,1,0:T(8,128)(2,1)S(1)}, bf16[3,208,384]{2,1,0:T(8,128)(2,1)S(1)}, u32[]{:S(2)}, u32[]{:S(2)}) collective-permute-start(bf16[3,208,384]{2,1,0:T(8,128)(2,1)S(1)} %constant_dynamic-update-slice_fusion.b_ref.others_ref), channel_id=1, source_target_pairs={{0,8},{4,12},{8,0},{12,4},{16,24},{20,28},{24,16},{28,20},{1,9},{5... | collective-permute-start | bytes 1437704 | tf_op jit(solution)/shard_map/plane attention weights/ppermute | solution.py:743
  25.1 20.2 %collective-permute-start.7 = (bf16[3,208,384]{2,1,0:T(8,128)(2,1)S(1)}, bf16[3,208,384]{2,1,0:T(8,128)(2,1)S(1)}, u32[]{:S(2)}, u32[]{:S(2)}) collective-permute-start(bf16[3,208,384]{2,1,0:T(8,128)(2,1)S(1)} %constant_dynamic-update-slice_fusion.b_ref.others_ref), channel_id=1, source_target_pairs={{0,16},{4,20},{8,24},{12,28},{16,0},{20,4},{24,8},{28,12},{1,17},{... | collective-permute-start | bytes 1437704 | tf_op jit(solution)/shard_map/plane attention weights/ppermute | solution.py:743
  26.6 18.7 %collective-permute-start.8 = (bf16[3,208,384]{2,1,0:T(8,128)(2,1)S(1)}, bf16[3,208,384]{2,1,0:T(8,128)(2,1)S(1)}, u32[]{:S(2)}, u32[]{:S(2)}) collective-permute-start(bf16[3,208,384]{2,1,0:T(8,128)(2,1)S(1)} %constant_dynamic-update-slice_fusion.b_ref.others_ref), channel_id=1, source_target_pairs={{0,24},{4,28},{8,16},{12,20},{16,8},{20,12},{24,0},{28,4},{1,25},{... | collective-permute-start | bytes 1437704 | tf_op jit(solution)/shard_map/plane attention weights/ppermute | solution.py:743
  27.1 6.8 %collective-permute-start.3 = (bf16[192,384]{1,0:T(8,128)(2,1)S(1)}, bf16[192,384]{1,0:T(8,128)(2,1)S(1)}, u32[]{:S(2)}, u32[]{:S(2)}) collective-permute-start(bf16[192,384]{1,0:T(8,128)(2,1)S(1)} %copy-done.42), channel_id=1, source_target_pairs={{0,1},{1,0},{2,3},{3,2},{4,5},{5,4},{6,7},{7,6},{8,9},{9,8},{10,11... | collective-permute-start | bytes 442376 | tf_op jit(solution)/shard_map/line inner weights/ppermute | solution.py:746
  29.6 12.2 %collective-permute-start.4 = (bf16[192,384]{1,0:T(8,128)(2,1)S(1)}, bf16[192,384]{1,0:T(8,128)(2,1)S(1)}, u32[]{:S(2)}, u32[]{:S(2)}) collective-permute-start(bf16[192,384]{1,0:T(8,128)(2,1)S(1)} %copy-done.42), channel_id=1, source_target_pairs={{0,2},{1,3},{2,0},{3,1},{4,6},{5,7},{6,4},{7,5},{8,10},{9,11},{10,... | collective-permute-start | bytes 442376 | tf_op jit(solution)/shard_map/line inner weights/ppermute | solution.py:746
  33.8 8.0 %collective-permute-start.5 = (bf16[192,384]{1,0:T(8,128)(2,1)S(1)}, bf16[192,384]{1,0:T(8,128)(2,1)S(1)}, u32[]{:S(2)}, u32[]{:S(2)}) collective-permute-start(bf16[192,384]{1,0:T(8,128)(2,1)S(1)} %copy-done.42), channel_id=1, source_target_pairs={{0,3},{1,2},{2,1},{3,0},{4,7},{5,6},{6,5},{7,4},{8,11},{9,10},{10,... | collective-permute-start | bytes 442376 | tf_op jit(solution)/shard_map/line inner weights/ppermute | solution.py:746
  45.5 4.0 %collective-permute-start.9 = (bf16[4,3,208,384]{3,2,1,0:T(8,128)(2,1)S(1)}, bf16[4,3,208,384]{3,2,1,0:T(8,128)(2,1)S(1)}, u32[]{:S(2)}, u32[]{:S(2)}) collective-permute-start(bf16[4,3,208,384]{3,2,1,0:T(8,128)(2,1)S(1)} %pad_maximum_fusion.near_ref), channel_id=1, source_target_pairs={{0,4},{4,0},{8,12},{12,8},{16,20},{20,16},{24,28},{28,24},{1,5},{5... | collective-permute-start | bytes 5750792 | tf_op jit(solution)/shard_map/core attention weights/ppermute | solution.py:743
  45.7 25.0 %collective-permute-start.13 = (bf16[3,192,384]{2,1,0:T(8,128)(2,1)S(1)}, bf16[3,192,384]{2,1,0:T(8,128)(2,1)S(1)}, u32[]{:S(2)}, u32[]{:S(2)}) collective-permute-start(bf16[3,192,384]{2,1,0:T(8,128)(2,1)S(1)} %pad_maximum_fusion.5), channel_id=1, source_target_pairs={{0,8},{4,12},{8,0},{12,4},{16,24},{20,28},{24,16},{28,20},{1,9},{5... | collective-permute-start | bytes 1327112 | tf_op jit(solution)/shard_map/plane inner weights/ppermute | solution.py:743
  47.0 23.7 %collective-permute-start.14 = (bf16[3,192,384]{2,1,0:T(8,128)(2,1)S(1)}, bf16[3,192,384]{2,1,0:T(8,128)(2,1)S(1)}, u32[]{:S(2)}, u32[]{:S(2)}) collective-permute-start(bf16[3,192,384]{2,1,0:T(8,128)(2,1)S(1)} %pad_maximum_fusion.5), channel_id=1, source_target_pairs={{0,16},{4,20},{8,24},{12,28},{16,0},{20,4},{24,8},{28,12},{1,17},{... | collective-permute-start | bytes 1327112 | tf_op jit(solution)/shard_map/plane inner weights/ppermute | solution.py:743
  47.8 22.9 %collective-permute-start.15 = (bf16[3,192,384]{2,1,0:T(8,128)(2,1)S(1)}, bf16[3,192,384]{2,1,0:T(8,128)(2,1)S(1)}, u32[]{:S(2)}, u32[]{:S(2)}) collective-permute-start(bf16[3,192,384]{2,1,0:T(8,128)(2,1)S(1)} %pad_maximum_fusion.5), channel_id=1, source_target_pairs={{0,24},{4,28},{8,16},{12,20},{16,8},{20,12},{24,0},{28,4},{1,25},{... | collective-permute-start | bytes 1327112 | tf_op jit(solution)/shard_map/plane inner weights/ppermute | solution.py:743
  49.5 11.1 %collective-permute-start.10 = (bf16[192,384]{1,0:T(8,128)(2,1)S(1)}, bf16[192,384]{1,0:T(8,128)(2,1)S(1)}, u32[]{:S(2)}, u32[]{:S(2)}) collective-permute-start(bf16[192,384]{1,0:T(8,128)(2,1)S(1)} %copy-done.41), channel_id=1, source_target_pairs={{0,1},{1,0},{2,3},{3,2},{4,5},{5,4},{6,7},{7,6},{8,9},{9,8},{10,11... | collective-permute-start | bytes 442376 | tf_op jit(solution)/shard_map/line outer weights/ppermute | solution.py:746
  53.4 17.2 %collective-permute-start.11 = (bf16[192,384]{1,0:T(8,128)(2,1)S(1)}, bf16[192,384]{1,0:T(8,128)(2,1)S(1)}, u32[]{:S(2)}, u32[]{:S(2)}) collective-permute-start(bf16[192,384]{1,0:T(8,128)(2,1)S(1)} %copy-done.41), channel_id=1, source_target_pairs={{0,2},{1,3},{2,0},{3,1},{4,6},{5,7},{6,4},{7,5},{8,10},{9,11},{10,... | collective-permute-start | bytes 442376 | tf_op jit(solution)/shard_map/line outer weights/ppermute | solution.py:746
  60.6 10.0 %collective-permute-start.12 = (bf16[192,384]{1,0:T(8,128)(2,1)S(1)}, bf16[192,384]{1,0:T(8,128)(2,1)S(1)}, u32[]{:S(2)}, u32[]{:S(2)}) collective-permute-start(bf16[192,384]{1,0:T(8,128)(2,1)S(1)} %copy-done.41), channel_id=1, source_target_pairs={{0,3},{1,2},{2,1},{3,0},{4,7},{5,6},{6,5},{7,4},{8,11},{9,10},{10,... | collective-permute-start | bytes 442376 | tf_op jit(solution)/shard_map/line outer weights/ppermute | solution.py:746
  71.0 3.8 %collective-permute-start.16 = (bf16[4,3,192,384]{3,2,1,0:T(8,128)(2,1)S(1)}, bf16[4,3,192,384]{3,2,1,0:T(8,128)(2,1)S(1)}, u32[]{:S(2)}, u32[]{:S(2)}) collective-permute-start(bf16[4,3,192,384]{3,2,1,0:T(8,128)(2,1)S(1)} %pad_maximum_fusion.2.near_ref), channel_id=1, source_target_pairs={{0,4},{4,0},{8,12},{12,8},{16,20},{20,16},{24,28},{28,24},{1,5},{5... | collective-permute-start | bytes 5308424 | tf_op jit(solution)/shard_map/core inner weights/ppermute | solution.py:743
  71.1 18.7 %collective-permute-start.17 = (bf16[3,192,384]{2,1,0:T(8,128)(2,1)S(1)}, bf16[3,192,384]{2,1,0:T(8,128)(2,1)S(1)}, u32[]{:S(2)}, u32[]{:S(2)}) collective-permute-start(bf16[3,192,384]{2,1,0:T(8,128)(2,1)S(1)} %pad_maximum_fusion.6), channel_id=1, source_target_pairs={{0,8},{4,12},{8,0},{12,4},{16,24},{20,28},{24,16},{28,20},{1,9},{5... | collective-permute-start | bytes 1327112 | tf_op jit(solution)/shard_map/plane outer weights/ppermute | solution.py:743
  72.4 20.1 %collective-permute-start.18 = (bf16[3,192,384]{2,1,0:T(8,128)(2,1)S(1)}, bf16[3,192,384]{2,1,0:T(8,128)(2,1)S(1)}, u32[]{:S(2)}, u32[]{:S(2)}) collective-permute-start(bf16[3,192,384]{2,1,0:T(8,128)(2,1)S(1)} %pad_maximum_fusion.6), channel_id=1, source_target_pairs={{0,16},{4,20},{8,24},{12,28},{16,0},{20,4},{24,8},{28,12},{1,17},{... | collective-permute-start | bytes 1327112 | tf_op jit(solution)/shard_map/plane outer weights/ppermute | solution.py:743
  73.3 20.9 %collective-permute-start.19 = (bf16[3,192,384]{2,1,0:T(8,128)(2,1)S(1)}, bf16[3,192,384]{2,1,0:T(8,128)(2,1)S(1)}, u32[]{:S(2)}, u32[]{:S(2)}) collective-permute-start(bf16[3,192,384]{2,1,0:T(8,128)(2,1)S(1)} %pad_maximum_fusion.6), channel_id=1, source_target_pairs={{0,24},{4,28},{8,16},{12,20},{16,8},{20,12},{24,0},{28,4},{1,25},{... | collective-permute-start | bytes 1327112 | tf_op jit(solution)/shard_map/plane outer weights/ppermute | solution.py:743
  94.5 3.8 %collective-permute-start.20 = (bf16[4,3,192,384]{3,2,1,0:T(8,128)(2,1)S(1)}, bf16[4,3,192,384]{3,2,1,0:T(8,128)(2,1)S(1)}, u32[]{:S(2)}, u32[]{:S(2)}) collective-permute-start(bf16[4,3,192,384]{3,2,1,0:T(8,128)(2,1)S(1)} %pad_maximum_fusion.3.near_ref), channel_id=1, source_target_pairs={{0,4},{4,0},{8,12},{12,8},{16,20},{20,16},{24,28},{28,24},{1,5},{5... | collective-permute-start | bytes 5308424 | tf_op jit(solution)/shard_map/core outer weights/ppermute | solution.py:743
  109.8 10.9 %collective-permute-start.21 = (bf16[4,4,192,384]{3,2,1,0:T(8,128)(2,1)S(1)}, bf16[4,4,192,384]{3,2,1,0:T(8,128)(2,1)S(1)}, u32[]{:S(2)}, u32[]{:S(2)}) collective-permute-start(bf16[4,4,192,384]{3,2,1,0:T(8,128)(2,1)S(1)} %get-tuple-element.196), channel_id=1, source_target_pairs={{0,4},{4,0},{8,12},{12,8},{16,20},{20,16},{24,28},{28,24},{1,5},{5... | collective-permute-start | bytes 7077896 | tf_op jit(solution)/shard_map/core outer grad/ppermute | solution.py:743
  110.0 20.7 %collective-permute-start.22 = (bf16[512,768]{1,0:T(8,128)(2,1)S(1)}, bf16[512,768]{1,0:T(8,128)(2,1)}, u32[]{:S(2)}, u32[]{:S(2)}) collective-permute-start(bf16[512,768]{1,0:T(8,128)(2,1)S(1)} %get-tuple-element.273), channel_id=1, source_target_pairs={{0,1},{1,2},{2,3},{4,5},{5,6},{6,7},{8,9},{9,10},{10,11},{12,13},{... | collective-permute-start | bytes 2359304 | tf_op jit(solution)/shard_map/rows 1/ppermute | solution.py:760
  114.4 21.5 %collective-permute-start.23 = (bf16[512,768]{1,0:T(8,128)(2,1)S(1)}, bf16[512,768]{1,0:T(8,128)(2,1)}, u32[]{:S(2)}, u32[]{:S(2)}) collective-permute-start(bf16[512,768]{1,0:T(8,128)(2,1)S(1)} %get-tuple-element.273), channel_id=1, source_target_pairs={{1,0},{2,1},{3,2},{5,4},{6,5},{7,6},{9,8},{10,9},{11,10},{13,12},{... | collective-permute-start | bytes 2359304 | tf_op jit(solution)/shard_map/rows 1/ppermute | solution.py:761
  122.8 13.1 %collective-permute-start.24 = (bf16[2,192,384]{2,1,0:T(8,128)(2,1)S(1)}, bf16[2,192,384]{2,1,0:T(8,128)(2,1)S(1)}, u32[]{:S(2)}, u32[]{:S(2)}) collective-permute-start(bf16[2,192,384]{2,1,0:T(8,128)(2,1)S(1)} %get-tuple-element.207), channel_id=1, source_target_pairs={{0,16},{4,20},{8,24},{12,28},{16,0},{20,4},{24,8},{28,12},{1,17},{... | collective-permute-start | bytes 884744 | tf_op jit(solution)/shard_map/plane one outer grad/ppermute | solution.py:743
  124.3 11.6 %collective-permute-start.25 = (bf16[2,192,384]{2,1,0:T(8,128)(2,1)S(1)}, bf16[2,192,384]{2,1,0:T(8,128)(2,1)S(1)}, u32[]{:S(2)}, u32[]{:S(2)}) collective-permute-start(bf16[2,192,384]{2,1,0:T(8,128)(2,1)S(1)} %get-tuple-element.208), channel_id=1, source_target_pairs={{0,8},{4,12},{8,0},{12,4},{16,24},{20,28},{24,16},{28,20},{1,9},{5... | collective-permute-start | bytes 884744 | tf_op jit(solution)/shard_map/plane one outer grad/ppermute | solution.py:743
  141.2 10.5 %collective-permute-start.26 = (bf16[4,4,192,384]{3,2,1,0:T(8,128)(2,1)S(1)}, bf16[4,4,192,384]{3,2,1,0:T(8,128)(2,1)S(1)}, u32[]{:S(2)}, u32[]{:S(2)}) collective-permute-start(bf16[4,4,192,384]{3,2,1,0:T(8,128)(2,1)S(1)} %get-tuple-element.224), channel_id=1, source_target_pairs={{0,4},{4,0},{8,12},{12,8},{16,20},{20,16},{24,28},{28,24},{1,5},{5... | collective-permute-start | bytes 7077896 | tf_op jit(solution)/shard_map/core inner grad/ppermute | solution.py:743
  141.3 18.8 %collective-permute-start.27 = (bf16[512,768]{1,0:T(8,128)(2,1)}, bf16[512,768]{1,0:T(8,128)(2,1)S(1)}, u32[]{:S(2)}, u32[]{:S(2)}) collective-permute-start(bf16[512,768]{1,0:T(8,128)(2,1)} %collective-permute-done.22), channel_id=1, source_target_pairs={{1,2},{2,3},{5,6},{6,7},{9,10},{10,11},{13,14},{14,15},{17,18},{18... | collective-permute-start | bytes 2359304 | tf_op jit(solution)/shard_map/rows 2/ppermute | solution.py:760
  142.0 22.5 %collective-permute-start.28 = (bf16[512,768]{1,0:T(8,128)(2,1)}, bf16[512,768]{1,0:T(8,128)(2,1)S(1)}, u32[]{:S(2)}, u32[]{:S(2)}) collective-permute-start(bf16[512,768]{1,0:T(8,128)(2,1)} %collective-permute-done.23), channel_id=1, source_target_pairs={{1,0},{2,1},{5,4},{6,5},{9,8},{10,9},{13,12},{14,13},{17,16},{18,1... | collective-permute-start | bytes 2359304 | tf_op jit(solution)/shard_map/rows 2/ppermute | solution.py:761
  143.3 15.8 %collective-permute-start.29 = (bf16[4,192,384]{2,1,0:T(8,128)(2,1)S(1)}, bf16[4,192,384]{2,1,0:T(8,128)(2,1)S(1)}, u32[]{:S(2)}, u32[]{:S(2)}) collective-permute-start(bf16[4,192,384]{2,1,0:T(8,128)(2,1)S(1)} %get-tuple-element.215), channel_id=1, source_target_pairs={{0,8},{4,12},{8,0},{12,4},{16,24},{20,28},{24,16},{28,20},{1,9},{5... | collective-permute-start | bytes 1769480 | tf_op jit(solution)/shard_map/plane two outer grad/ppermute | solution.py:743
  144.6 15.4 %collective-permute-start.30 = (bf16[4,192,384]{2,1,0:T(8,128)(2,1)S(1)}, bf16[4,192,384]{2,1,0:T(8,128)(2,1)S(1)}, u32[]{:S(2)}, u32[]{:S(2)}) collective-permute-start(bf16[4,192,384]{2,1,0:T(8,128)(2,1)S(1)} %get-tuple-element.234), channel_id=1, source_target_pairs={{0,16},{4,20},{8,24},{12,28},{16,0},{20,4},{24,8},{28,12},{1,17},{... | collective-permute-start | bytes 1769480 | tf_op jit(solution)/shard_map/plane two outer grad/ppermute | solution.py:743
  164.5 23.1 %collective-permute-start.34 = (bf16[512,768]{1,0:T(8,128)(2,1)S(1)}, bf16[512,768]{1,0:T(8,128)(2,1)S(1)}, u32[]{:S(2)}, u32[]{:S(2)}) collective-permute-start(bf16[512,768]{1,0:T(8,128)(2,1)S(1)} %collective-permute-done.27), channel_id=1, source_target_pairs={{2,3},{6,7},{10,11},{14,15},{18,19},{22,23},{26,27},{30,31}} | collective-permute-start | bytes 2359304 | tf_op jit(solution)/shard_map/rows 3/ppermute | solution.py:760
  165.2 22.4 %collective-permute-start.35 = (bf16[512,768]{1,0:T(8,128)(2,1)S(1)}, bf16[512,768]{1,0:T(8,128)(2,1)S(1)}, u32[]{:S(2)}, u32[]{:S(2)}) collective-permute-start(bf16[512,768]{1,0:T(8,128)(2,1)S(1)} %collective-permute-done.28), channel_id=1, source_target_pairs={{1,0},{5,4},{9,8},{13,12},{17,16},{21,20},{25,24},{29,28}} | collective-permute-start | bytes 2359304 | tf_op jit(solution)/shard_map/rows 3/ppermute | solution.py:761
  166.5 14.1 %collective-permute-start.32 = (bf16[2,192,384]{2,1,0:T(8,128)(2,1)S(1)}, bf16[2,192,384]{2,1,0:T(8,128)(2,1)S(1)}, u32[]{:S(2)}, u32[]{:S(2)}) collective-permute-start(bf16[2,192,384]{2,1,0:T(8,128)(2,1)S(1)} %get-tuple-element.245), channel_id=1, source_target_pairs={{0,8},{4,12},{8,0},{12,4},{16,24},{20,28},{24,16},{28,20},{1,9},{5... | collective-permute-start | bytes 884744 | tf_op jit(solution)/shard_map/plane one inner grad/ppermute | solution.py:743
  167.7 13.0 %collective-permute-start.31 = (bf16[2,192,384]{2,1,0:T(8,128)(2,1)S(1)}, bf16[2,192,384]{2,1,0:T(8,128)(2,1)S(1)}, u32[]{:S(2)}, u32[]{:S(2)}) collective-permute-start(bf16[2,192,384]{2,1,0:T(8,128)(2,1)S(1)} %get-tuple-element.243), channel_id=1, source_target_pairs={{0,16},{4,20},{8,24},{12,28},{16,0},{20,4},{24,8},{28,12},{1,17},{... | collective-permute-start | bytes 884744 | tf_op jit(solution)/shard_map/plane one inner grad/ppermute | solution.py:743
  169.9 17.6 %collective-permute-start.33 = (bf16[2,192,384]{2,1,0:T(8,128)(2,1)S(1)}, bf16[2,192,384]{2,1,0:T(8,128)(2,1)S(1)}, u32[]{:S(2)}, u32[]{:S(2)}) collective-permute-start(bf16[2,192,384]{2,1,0:T(8,128)(2,1)S(1)} %get-tuple-element.323), channel_id=1, source_target_pairs={{0,1},{3,2},{4,5},{7,6},{8,9},{11,10},{12,13},{15,14},{16,17},{19,... | collective-permute-start | bytes 884744 | tf_op jit(solution)/shard_map/line ends outer grad/ppermute | solution.py:785
  187.6 6.1 %collective-permute-start.38 = (bf16[4,4,208,384]{3,2,1,0:T(8,128)(2,1)S(1)}, bf16[4,4,208,384]{3,2,1,0:T(8,128)(2,1)S(1)}, u32[]{:S(2)}, u32[]{:S(2)}) collective-permute-start(bf16[4,4,208,384]{3,2,1,0:T(8,128)(2,1)S(1)} %get-tuple-element.262), channel_id=1, source_target_pairs={{0,4},{4,0},{8,12},{12,8},{16,20},{20,16},{24,28},{28,24},{1,5},{5... | collective-permute-start | bytes 7667720 | tf_op jit(solution)/shard_map/core attention grad/ppermute | solution.py:743
  187.7 15.7 %collective-permute-start.40 = (bf16[4,192,384]{2,1,0:T(8,128)(2,1)S(1)}, bf16[4,192,384]{2,1,0:T(8,128)(2,1)S(1)}, u32[]{:S(2)}, u32[]{:S(2)}) collective-permute-start(bf16[4,192,384]{2,1,0:T(8,128)(2,1)S(1)} %get-tuple-element.251), channel_id=1, source_target_pairs={{0,8},{4,12},{8,0},{12,4},{16,24},{20,28},{24,16},{28,20},{1,9},{5... | collective-permute-start | bytes 1769480 | tf_op jit(solution)/shard_map/plane two inner grad/ppermute | solution.py:743
  188.9 15.4 %collective-permute-start.41 = (bf16[4,192,384]{2,1,0:T(8,128)(2,1)S(1)}, bf16[4,192,384]{2,1,0:T(8,128)(2,1)S(1)}, u32[]{:S(2)}, u32[]{:S(2)}) collective-permute-start(bf16[4,192,384]{2,1,0:T(8,128)(2,1)S(1)} %get-tuple-element.266), channel_id=1, source_target_pairs={{0,16},{4,20},{8,24},{12,28},{16,0},{20,4},{24,8},{28,12},{1,17},{... | collective-permute-start | bytes 1769480 | tf_op jit(solution)/shard_map/plane two inner grad/ppermute | solution.py:743
  189.6 14.7 %collective-permute-start.39 = (bf16[2,192,384]{2,1,0:T(8,128)(2,1)S(1)}, bf16[2,192,384]{2,1,0:T(8,128)(2,1)S(1)}, u32[]{:S(2)}, u32[]{:S(2)}) collective-permute-start(bf16[2,192,384]{2,1,0:T(8,128)(2,1)S(1)} %add_convert_fusion.2), channel_id=1, source_target_pairs={{1,2},{2,1},{5,6},{6,5},{9,10},{10,9},{13,14},{14,13},{17,18},{18,... | collective-permute-start | bytes 884744 | tf_op jit(solution)/shard_map/line middle outer grad/ppermute | solution.py:788
  190.3 20.8 %collective-permute-start.36 = (bf16[512,768]{1,0:T(8,128)(2,1)}, bf16[512,768]{1,0:T(8,128)(2,1)}, u32[]{:S(2)}, u32[]{:S(2)}) collective-permute-start(bf16[512,768]{1,0:T(8,128)(2,1)} %get-tuple-element.260), channel_id=1, source_target_pairs={{0,1},{1,2},{2,3},{4,5},{5,6},{6,7},{8,9},{9,10},{10,11},{12,13},{... | collective-permute-start | bytes 2359304 | tf_op jit(solution)/shard_map/grad rows 1/ppermute | solution.py:760
  193.7 21.3 %collective-permute-start.37 = (bf16[512,768]{1,0:T(8,128)(2,1)}, bf16[512,768]{1,0:T(8,128)(2,1)}, u32[]{:S(2)}, u32[]{:S(2)}) collective-permute-start(bf16[512,768]{1,0:T(8,128)(2,1)} %get-tuple-element.260), channel_id=1, source_target_pairs={{1,0},{2,1},{3,2},{5,4},{6,5},{7,6},{9,8},{10,9},{11,10},{13,12},{... | collective-permute-start | bytes 2359304 | tf_op jit(solution)/shard_map/grad rows 1/ppermute | solution.py:761
  205.0 11.2 %collective-permute-start.43 = (bf16[2,208,384]{2,1,0:T(8,128)(2,1)S(1)}, bf16[2,208,384]{2,1,0:T(8,128)(2,1)S(1)}, u32[]{:S(2)}, u32[]{:S(2)}) collective-permute-start(bf16[2,208,384]{2,1,0:T(8,128)(2,1)S(1)} %get-tuple-element.269), channel_id=1, source_target_pairs={{0,16},{4,20},{8,24},{12,28},{16,0},{20,4},{24,8},{28,12},{1,17},{... | collective-permute-start | bytes 958472 | tf_op jit(solution)/shard_map/plane one attention grad/ppermute | solution.py:743
  205.6 10.6 %collective-permute-start.44 = (bf16[2,208,384]{2,1,0:T(8,128)(2,1)S(1)}, bf16[2,208,384]{2,1,0:T(8,128)(2,1)S(1)}, u32[]{:S(2)}, u32[]{:S(2)}) collective-permute-start(bf16[2,208,384]{2,1,0:T(8,128)(2,1)S(1)} %get-tuple-element.270), channel_id=1, source_target_pairs={{0,8},{4,12},{8,0},{12,4},{16,24},{20,28},{24,16},{28,20},{1,9},{5... | collective-permute-start | bytes 958472 | tf_op jit(solution)/shard_map/plane one attention grad/ppermute | solution.py:743
  207.9 8.4 %collective-permute-start.42 = (bf16[2,192,384]{2,1,0:T(8,128)(2,1)}, bf16[2,192,384]{2,1,0:T(8,128)(2,1)}, u32[]{:S(2)}, u32[]{:S(2)}) collective-permute-start(bf16[2,192,384]{2,1,0:T(8,128)(2,1)} %get-tuple-element.321), channel_id=1, source_target_pairs={{0,1},{3,2},{4,5},{7,6},{8,9},{11,10},{12,13},{15,14},{16,17},{19,... | collective-permute-start | bytes 884744 | tf_op jit(solution)/shard_map/line ends inner grad/ppermute | solution.py:785
  216.5 15.4 %collective-permute-start.45 = (bf16[4,208,384]{2,1,0:T(8,128)(2,1)S(1)}, bf16[4,208,384]{2,1,0:T(8,128)(2,1)S(1)}, u32[]{:S(2)}, u32[]{:S(2)}) collective-permute-start(bf16[4,208,384]{2,1,0:T(8,128)(2,1)S(1)} %get-tuple-element.279), channel_id=1, source_target_pairs={{0,8},{4,12},{8,0},{12,4},{16,24},{20,28},{24,16},{28,20},{1,9},{5... | collective-permute-start | bytes 1916936 | tf_op jit(solution)/shard_map/plane two attention grad/ppermute | solution.py:743
  217.7 15.0 %collective-permute-start.46 = (bf16[4,208,384]{2,1,0:T(8,128)(2,1)S(1)}, bf16[4,208,384]{2,1,0:T(8,128)(2,1)S(1)}, u32[]{:S(2)}, u32[]{:S(2)}) collective-permute-start(bf16[4,208,384]{2,1,0:T(8,128)(2,1)S(1)} %get-tuple-element.280), channel_id=1, source_target_pairs={{0,16},{4,20},{8,24},{12,28},{16,0},{20,4},{24,8},{28,12},{1,17},{... | collective-permute-start | bytes 1916936 | tf_op jit(solution)/shard_map/plane two attention grad/ppermute | solution.py:743
  220.0 18.9 %collective-permute-start.47 = (bf16[512,768]{1,0:T(8,128)(2,1)}, bf16[512,768]{1,0:T(8,128)(2,1)S(1)}, u32[]{:S(2)}, u32[]{:S(2)}) collective-permute-start(bf16[512,768]{1,0:T(8,128)(2,1)} %collective-permute-done.36), channel_id=1, source_target_pairs={{1,2},{2,3},{5,6},{6,7},{9,10},{10,11},{13,14},{14,15},{17,18},{18... | collective-permute-start | bytes 2359304 | tf_op jit(solution)/shard_map/grad rows 2/ppermute | solution.py:760
  220.9 30.2 %collective-permute-start.48 = (bf16[512,768]{1,0:T(8,128)(2,1)}, bf16[512,768]{1,0:T(8,128)(2,1)S(1)}, u32[]{:S(2)}, u32[]{:S(2)}) collective-permute-start(bf16[512,768]{1,0:T(8,128)(2,1)} %collective-permute-done.37), channel_id=1, source_target_pairs={{1,0},{2,1},{5,4},{6,5},{9,8},{10,9},{13,12},{14,13},{17,16},{18,1... | collective-permute-start | bytes 2359304 | tf_op jit(solution)/shard_map/grad rows 2/ppermute | solution.py:761
  222.2 35.7 %collective-permute-start.52 = (bf16[2,192,384]{2,1,0:T(8,128)(2,1)S(1)}, bf16[2,192,384]{2,1,0:T(8,128)(2,1)S(1)}, u32[]{:S(2)}, u32[]{:S(2)}) collective-permute-start(bf16[2,192,384]{2,1,0:T(8,128)(2,1)S(1)} %add_convert_fusion), channel_id=1, source_target_pairs={{1,2},{2,1},{5,6},{6,5},{9,10},{10,9},{13,14},{14,13},{17,18},{18,... | collective-permute-start | bytes 884744 | tf_op jit(solution)/shard_map/line middle inner grad/ppermute | solution.py:788
  224.7 26.4 %copy-start.23 = (f32[2,192,384]{2,1,0:T(8,128)S(1)}, f32[2,192,384]{2,1,0:T(8,128)}, u32[]{:S(2)}) copy-start(f32[2,192,384]{2,1,0:T(8,128)} %get-tuple-element.289) | copy-start | bytes 1769476
  226.2 31.8 %copy-start.22 = (bf16[2048,768]{1,0:T(8,128)(2,1)}, bf16[2048,768]{1,0:T(8,128)(2,1)S(1)}, u32[]{:S(2)}) copy-start(bf16[2048,768]{1,0:T(8,128)(2,1)S(1)} %select_dynamic-update-slice_fusion.3) | copy-start | bytes 9437188
  226.2 31.7 %copy-start.24 = (f32[2,192,384]{2,1,0:T(8,128)S(1)}, f32[2,192,384]{2,1,0:T(8,128)}, u32[]{:S(2)}) copy-start(f32[2,192,384]{2,1,0:T(8,128)} %get-tuple-element.291) | copy-start | bytes 1769476
  232.9 31.3 %collective-permute-start.54 = (bf16[208,384]{1,0:T(8,128)(2,1)S(1)}, bf16[208,384]{1,0:T(8,128)(2,1)S(1)}, u32[]{:S(2)}, u32[]{:S(2)}) collective-permute-start(bf16[208,384]{1,0:T(8,128)(2,1)S(1)} %get-tuple-element.319), channel_id=1, source_target_pairs={{0,1},{1,0},{2,3},{3,2},{4,5},{5,4},{6,7},{7,6},{8,9},{9,8},{10,11... | collective-permute-start | bytes 479240 | tf_op jit(solution)/shard_map/line attention grad/ppermute | solution.py:746
  239.0 26.5 %collective-permute-start.55 = (bf16[208,384]{1,0:T(8,128)(2,1)S(1)}, bf16[208,384]{1,0:T(8,128)(2,1)S(1)}, u32[]{:S(2)}, u32[]{:S(2)}) collective-permute-start(bf16[208,384]{1,0:T(8,128)(2,1)S(1)} %get-tuple-element.318), channel_id=1, source_target_pairs={{0,2},{1,3},{2,0},{3,1},{4,6},{5,7},{6,4},{7,5},{8,10},{9,11},{10,... | collective-permute-start | bytes 479240 | tf_op jit(solution)/shard_map/line attention grad/ppermute | solution.py:746
  239.0 27.8 %collective-permute-start.56 = (bf16[208,384]{1,0:T(8,128)(2,1)S(1)}, bf16[208,384]{1,0:T(8,128)(2,1)S(1)}, u32[]{:S(2)}, u32[]{:S(2)}) collective-permute-start(bf16[208,384]{1,0:T(8,128)(2,1)S(1)} %get-tuple-element.317), channel_id=1, source_target_pairs={{0,3},{1,2},{2,1},{3,0},{4,7},{5,6},{6,5},{7,4},{8,11},{9,10},{10,... | collective-permute-start | bytes 479240 | tf_op jit(solution)/shard_map/line attention grad/ppermute | solution.py:746
  251.2 15.6 %collective-permute-start.51 = (bf16[192,384]{1,0:T(8,128)(2,1)S(1)}, bf16[192,384]{1,0:T(8,128)(2,1)S(1)}, u32[]{:S(2)}, u32[]{:S(2)}) collective-permute-start(bf16[192,384]{1,0:T(8,128)(2,1)S(1)} %fusion.10), channel_id=1, source_target_pairs={{0,1},{1,0},{2,3},{3,2},{4,5},{5,4},{6,7},{7,6},{8,9},{9,8},{10,11... | collective-permute-start | bytes 442376 | tf_op jit(solution)/shard_map/line pair ffn grad/ppermute | solution.py:746
  258.0 10.9 %collective-permute-start.53 = (bf16[192,384]{1,0:T(8,128)(2,1)S(1)}, bf16[192,384]{1,0:T(8,128)(2,1)S(1)}, u32[]{:S(2)}, u32[]{:S(2)}) collective-permute-start(bf16[192,384]{1,0:T(8,128)(2,1)S(1)} %fusion.11), channel_id=1, source_target_pairs={{0,1},{1,0},{2,3},{3,2},{4,5},{5,4},{6,7},{7,6},{8,9},{9,8},{10,11... | collective-permute-start | bytes 442376 | tf_op jit(solution)/shard_map/line pair ffn grad/ppermute | solution.py:746
  264.2 21.8 %collective-permute-start.49 = (bf16[512,768]{1,0:T(8,128)(2,1)S(1)}, bf16[512,768]{1,0:T(8,128)(2,1)S(1)}, u32[]{:S(2)}, u32[]{:S(2)}) collective-permute-start(bf16[512,768]{1,0:T(8,128)(2,1)S(1)} %collective-permute-done.47), channel_id=1, source_target_pairs={{2,3},{6,7},{10,11},{14,15},{18,19},{22,23},{26,27},{30,31}} | collective-permute-start | bytes 2359304 | tf_op jit(solution)/shard_map/grad rows 3/ppermute | solution.py:760
  265.5 20.5 %collective-permute-start.50 = (bf16[512,768]{1,0:T(8,128)(2,1)S(1)}, bf16[512,768]{1,0:T(8,128)(2,1)S(1)}, u32[]{:S(2)}, u32[]{:S(2)}) collective-permute-start(bf16[512,768]{1,0:T(8,128)(2,1)S(1)} %collective-permute-done.48), channel_id=1, source_target_pairs={{1,0},{5,4},{9,8},{13,12},{17,16},{21,20},{25,24},{29,28}} | collective-permute-start | bytes 2359304 | tf_op jit(solution)/shard_map/grad rows 3/ppermute | solution.py:761
  269.2 11.0 %collective-permute-start.57 = (bf16[592,384]{1,0:T(8,128)(2,1)S(1)}, bf16[592,384]{1,0:T(8,128)(2,1)S(1)}, u32[]{:S(2)}, u32[]{:S(2)}) collective-permute-start(bf16[592,384]{1,0:T(8,128)(2,1)S(1)} %get-tuple-element.325), channel_id=1, source_target_pairs={{0,8},{4,12},{8,0},{12,4},{16,24},{20,28},{24,16},{28,20},{1,9},{5... | collective-permute-start | bytes 1363976 | tf_op jit(solution)/shard_map/plane result/ppermute | solution.py:743
  270.4 15.6 %collective-permute-start.58 = (bf16[592,384]{1,0:T(8,128)(2,1)S(1)}, bf16[592,384]{1,0:T(8,128)(2,1)S(1)}, u32[]{:S(2)}, u32[]{:S(2)}) collective-permute-start(bf16[592,384]{1,0:T(8,128)(2,1)S(1)} %get-tuple-element.325), channel_id=1, source_target_pairs={{0,16},{4,20},{8,24},{12,28},{16,0},{20,4},{24,8},{28,12},{1,17},{... | collective-permute-start | bytes 1363976 | tf_op jit(solution)/shard_map/plane result/ppermute | solution.py:743
  271.0 15.0 %collective-permute-start.59 = (bf16[592,384]{1,0:T(8,128)(2,1)S(1)}, bf16[592,384]{1,0:T(8,128)(2,1)S(1)}, u32[]{:S(2)}, u32[]{:S(2)}) collective-permute-start(bf16[592,384]{1,0:T(8,128)(2,1)S(1)} %get-tuple-element.325), channel_id=1, source_target_pairs={{0,24},{4,28},{8,16},{12,20},{16,8},{20,12},{24,0},{28,4},{1,25},{... | collective-permute-start | bytes 1363976 | tf_op jit(solution)/shard_map/plane result/ppermute | solution.py:743
  286.2 3.8 %collective-permute-start.60 = (bf16[4,592,384]{2,1,0:T(8,128)(2,1)S(1)}, bf16[4,592,384]{2,1,0:T(8,128)(2,1)S(1)}, u32[]{:S(2)}, u32[]{:S(2)}) collective-permute-start(bf16[4,592,384]{2,1,0:T(8,128)(2,1)S(1)} %pad_maximum_fusion.1.near_ref), channel_id=1, source_target_pairs={{0,4},{4,0},{8,12},{12,8},{16,20},{20,16},{24,28},{28,24},{1,5},{5... | collective-permute-start | bytes 5455880 | tf_op jit(solution)/shard_map/core result/ppermute | solution.py:743
  (40 other events, 330.9 us)

commit v2 on v1

--- a/solution.py
+++ b/solution.py
@@ -781,6 +781,9 @@
     def line_sums(group):
         return sum(f32(a[:half]) for a in group), add(*[a[half:] for a in group])
 
+    def line_one(group):
+        return sum(f32(a[0::2]) for a in group), add(*[a[1::2] for a in group])
+
     def line_ends(far):
         return lax.ppermute(far, "tensor", [(0, 1), (3, 2)])
 
@@ -886,59 +889,61 @@
         start, theirs_i = barrier(start, theirs_i)
         own_i, x_i, y_i, *via_i = core_add(mine_i, theirs_i)
         start, *pieces = shard_back(tie(start, own_i), 2)
-        start, up_2, down_2, *plane_u = barrier(start, up_2, down_2, *plane_u)
+        start, *plane_u = barrier(start, *plane_u)
+        with jax.named_scope("plane one inner grad"):
+            via_i = plane_one(*[tie(v, *plane_u) for v in via_i])
+        start, up_2, down_2 = barrier(start, up_2, down_2)
         with jax.named_scope("rows 3"):
             up_3, down_3 = rows_round(3, up_2, down_2)
-        with jax.named_scope("plane one inner grad"):
-            via_i = plane_one(*[tie(v, *plane_u) for v in via_i])
+        start, *pieces = shard_back(start, 1)
+        start, own_u, *via_i = barrier(start, own_u, *via_i)
         near_u, far_u = line_sums((own_u, *plane_u))
         with jax.named_scope("line ends outer grad"):
             ends_u = line_ends(far_u)
-        start, *pieces = shard_back(tie(start, far_u), 1)
-        start, *via_i = barrier(start, *via_i)
         x_i, y_i = plane_add(x_i, y_i, *via_i)
         with jax.named_scope("plane two inner grad"):
             plane_i = plane_two(x_i, y_i)
-        grad_rows, mine_a, other_a = shard_back(tie(start, x_i), 0)
+        grad_rows, mine_a, other_a = shard_back(tie(start, x_i, far_u), 0)
         grad_rows, mine_a, other_a, ends_u, up_3, down_3 = barrier(grad_rows, mine_a, other_a, ends_u, up_3, down_3)
-        far_u = add(far_u, ends_u[::-1])
-        with jax.named_scope("line middle outer grad"):
-            middle_u = line_middle(far_u)
 
         with jax.named_scope("core attention grad"):
             theirs_a = across(other_a, 1)
         with jax.named_scope("grad rows 1"):
             go_1, back_1 = rows_round(1, grad_rows, grad_rows)
         own_a, x_a, y_a, *via_a = core_add(mine_a, theirs_a)
-        *via_a, middle_u, plane_i_x, plane_i_y = barrier(*via_a, middle_u, *plane_i)
+        far_u = add(far_u, tie(ends_u, own_a)[::-1])
+        with jax.named_scope("line middle outer grad"):
+            middle_u = line_middle(far_u)
+        *via_a, plane_i_x, plane_i_y = barrier(*via_a, *plane_i)
         with jax.named_scope("plane one attention grad"):
             via_a = plane_one(*via_a)
-        near_i, far_i = line_sums((own_i, plane_i_x, plane_i_y))
-        with jax.named_scope("line ends inner grad"):
-            ends_i = line_ends(far_i)
-        go_1, back_1, ends_i, *via_a = barrier(go_1, back_1, ends_i, *via_a)
+        even_i, odd_i = line_one((own_i, plane_i_x, plane_i_y))
+        go_1, back_1, odd_i, middle_u, *via_a = barrier(go_1, back_1, odd_i, middle_u, *via_a)
         with jax.named_scope("grad rows 2"):
             go_2, back_2 = rows_round(2, go_1, back_1)
+        with jax.named_scope("line one inner grad"):
+            got_i = along(odd_i, 1)
         x_a, y_a = plane_add(x_a, y_a, *via_a)
         with jax.named_scope("plane two attention grad"):
             plane_a = plane_two(x_a, y_a)
         layer_out = place_rows(z, tie(out_rows, *via_a), (up_1, up_2, up_3), (down_1, down_2, down_3))
-        far_i = add(far_i, ends_i[::-1])
-        with jax.named_scope("line middle inner grad"):
-            middle_i = line_middle(far_i)
-        layer_out, _, *plane_a = barrier(layer_out, far_i, *plane_a)
+        near_u = near_u + f32(middle_u[::-1])
+        layer_out, got_i, *plane_a = barrier(layer_out, got_i, *plane_a)
         group = (own_a, *plane_a)
         low_a = [add(*[a[r] for a in group]) for r in range(1, n_tensor)]
         with jax.named_scope("line attention grad"):
             got_a = [along(a, r) for r, a in enumerate(low_a, 1)]
-        near_u, near_i, go_2, back_2, *_ = barrier(near_u, near_i, go_2, back_2, *plane_a)
-        near_f = [near_u + f32(middle_u[::-1]), near_i + f32(middle_i[::-1])]
-        with jax.named_scope("line pair ffn grad"):
-            pair_f = [along(near[1].astype(BF), 1) for near in near_f]
-        pair_u, pair_i, *got_a = barrier(*pair_f, *got_a)
+        even_i, near_u, go_2, back_2, *_ = barrier(even_i, near_u, go_2, back_2, *plane_a)
+        even_i = even_i + f32(got_i)
+        with jax.named_scope("line two inner grad"):
+            last_i = along(even_i[1].astype(BF), 2)
+        with jax.named_scope("line pair outer grad"):
+            pair_u = along(near_u[1].astype(BF), 1)
+        last_i, pair_u, *got_a = barrier(last_i, pair_u, *got_a)
         own_a = sum(f32(a[0]) for a in group) + f32(got_a[0]) + f32(got_a[1])
-        done = [line_end(own_a, got_a[2]), line_end(near_f[0][0], pair_u), line_end(near_f[1][0], pair_i)]
-        done = jnp.concatenate(done)
+        done = jnp.concatenate(
+            [line_end(own_a, got_a[2]), line_end(near_u[0], pair_u), line_end(even_i[0], last_i)]
+        )
         with jax.named_scope("plane result"):
             found = plane(done)
         with jax.named_scope("grad rows 3"):

time: 299 us -> 294 us (0.983)
  starting transfers between devices: 98.5 us -> 85.6 us
  waiting for transfers between devices: 84.1 us -> 91.3 us
    ppermute x14 -> x15, starting transfers between devices: 44.6 us -> 34.4 us  [along(): return lax.ppermute(array, 'tensor', [(i, i ^ r) for i in range(n_tensor)])]
    ppermute x6, waiting for transfers between devices: 17.7 us -> 25 us  [rows_round(): lax.ppermute(down, 'tensor', [(i + 1, i) for i in range(n_tensor - k)])]
    ppermute x14 -> x15, waiting for transfers between devices: 22.6 us -> 27.1 us  [along(): return lax.ppermute(array, 'tensor', [(i, i ^ r) for i in range(n_tensor)])]
    ppermute x2 -> x1, starting transfers between devices: 6.61 us -> 4.61 us  [line_ends(): return lax.ppermute(far, 'tensor', [(0, 1), (3, 2)])]
  transfers between devices with their start and end apart: 61 -> 60, of which waited for: 27 -> 29; matrix products, arithmetic and copies ran while one was open for 3% -> 3% of each run, Pallas kernels for 23% -> 24%
where the time goes in v2:
time: 294 us; the launch traced here: 289 us
  Pallas kernels  93.8 us (32%)
  waiting for transfers between devices  91.3 us (31%)
  starting transfers between devices  85.6 us (29%)
  other arithmetic  9.63 us (3%)
  local copies, waits for them, and re-layouts  7.13 us (2%)
    ppermute x31, waiting for transfers between devices, across(): return lax.ppermute(array, 'dp', flip[bit])  38.9 us
    ppermute x15, starting transfers between devices, along(): return lax.ppermute(array, 'tensor', [(i, i ^ r) for i in range(n_tensor)])  34.4 us
    ppermute x31, starting transfers between devices, across(): return lax.ppermute(array, 'dp', flip[bit])  27.7 us
    ppermute x15, waiting for transfers between devices, along(): return lax.ppermute(array, 'tensor', [(i, i ^ r) for i in range(n_tensor)])  27.1 us
    ppermute x6, waiting for transfers between devices, rows_round(): lax.ppermute(down, 'tensor', [(i + 1, i) for i in range(n_tensor - k)])  25 us
    pallas_call x4, Pallas kernels, attention_backward(): pl.pallas_call(functools.partial(attention_backward_kernel, shard=shard,...  25 us
    pallas_call x1, Pallas kernels, inner_half(): pl.pallas_call(inner_kernel, grid_spec=pltpu.PrefetchScalarGridSpec(num_s...  11.7 us
    pallas_call x2, Pallas kernels, ffn_back(): pl.pallas_call(functools.partial(ffn_back_kernel, final=final), grid=(cou...  10.8 us
  transfers between devices with their start and end apart: 60, of which 29 were waited for; matrix products, arithmetic and copies ran while one was open for 3% of the time, Pallas kernels for 24%

profile of v2, /device:TPU:0, one launch (start us, length us, event | category | flops | bytes accessed | tf_op | source)
XLA Modules:
  0.0 289.5 jit_solution(3791052699279846883)
XLA Ops:
  1.3 4.0 %shard_map.323 = (bf16[1,768,768]{2,1,0:T(8,128)(2,1)}, bf16[1,208,384]{2,1,0:T(8,128)(2,1)}) custom-call(s32[3]{0:T(128)} %pad_add_fusion.scalars, bf16[192,768]{1,0:T(8,128)(2,1)} %bitcast.77, bf16[192,768]{1,0:T(8,128)(2,1)} %bitcast.78, bf16[192,768]{1,0:T(8,128)(2,1)} %bitcast.79, bf16[192,768]{1,0:T(8,128)(2,1)} %refs_3_.1, bf16[192]{0:T(256)(128)(2,1)} %refs_4_.1, ...), custom_call_target="tpu_custom_call" | custom-call | flops 100000000 | tf_op jit(solution)/shard_map/pallas_call | solution.py:564
  5.3 3.1 %collective-permute-start = (bf16[1,208,384]{2,1,0:T(8,128)(2,1)}, bf16[1,208,384]{2,1,0:T(8,128)(2,1)S(1)}, u32[]{:S(2)}, u32[]{:S(2)}) collective-permute-start(bf16[1,208,384]{2,1,0:T(8,128)(2,1)} %get-tuple-element.170.b_ref.own_ref), channel_id=1, source_target_pairs={{0,1},{1,0},{2,3},{3,2},{4,5},{5,4},{6,7},{7,6},{8,9},{9,8},{10,11... | collective-permute-start | bytes 479240 | tf_op jit(solution)/shard_map/line attention weights/ppermute | solution.py:746
  8.4 2.6 collective-permute-start.1
  11.0 3.4 %shard_map.324 = (bf16[768,768]{1,0:T(8,128)(2,1)}, bf16[192,384]{1,0:T(8,128)(2,1)}, bf16[192,384]{1,0:T(8,128)(2,1)}) custom-call(s32[3]{0:T(128)} %pad_add_fusion.scalars, bf16[768,768]{1,0:T(8,128)(2,1)} %wi_hbm.1, bf16[768,768]{1,0:T(8,128)(2,1)} %own_ref.1), custom_call_target="tpu_custom_call" | custom-call | flops 100000000 | tf_op jit(solution)/shard_map/pallas_call | solution.py:591
  15.8 2.8 shard_map.325
  18.6 4.9 %collective-permute-done.1 = bf16[1,208,384]{2,1,0:T(8,128)(2,1)S(1)} collective-permute-done((bf16[1,208,384]{2,1,0:T(8,128)(2,1)}, bf16[1,208,384]{2,1,0:T(8,128)(2,1)S(1)}, u32[]{:S(2)}, u32[]{:S(2)}) %collective-permute-start.1) | collective-permute-done | bytes 159776 | tf_op jit(solution)/shard_map/line attention weights/ppermute | solution.py:746
  23.5 1.6 collective-permute-start.6
  25.1 1.5 collective-permute-start.7
  27.1 2.5 collective-permute-start.3
  30.6 3.2 %collective-permute-done.3 = bf16[192,384]{1,0:T(8,128)(2,1)S(1)} collective-permute-done((bf16[192,384]{1,0:T(8,128)(2,1)S(1)}, bf16[192,384]{1,0:T(8,128)(2,1)S(1)}, u32[]{:S(2)}, u32[]{:S(2)}) %collective-permute-start.3) | collective-permute-done | bytes 147488 | tf_op jit(solution)/shard_map/line inner weights/ppermute | solution.py:746
  33.8 2.1 collective-permute-start.5
  36.0 5.8 %collective-permute-done.4 = bf16[192,384]{1,0:T(8,128)(2,1)S(1)} collective-permute-done((bf16[192,384]{1,0:T(8,128)(2,1)S(1)}, bf16[192,384]{1,0:T(8,128)(2,1)S(1)}, u32[]{:S(2)}, u32[]{:S(2)}) %collective-permute-start.4) | collective-permute-done | bytes 147488 | tf_op jit(solution)/shard_map/line inner weights/ppermute | solution.py:746
  41.8 3.4 %collective-permute-done.7 = bf16[3,208,384]{2,1,0:T(8,128)(2,1)S(1)} collective-permute-done((bf16[3,208,384]{2,1,0:T(8,128)(2,1)S(1)}, bf16[3,208,384]{2,1,0:T(8,128)(2,1)S(1)}, u32[]{:S(2)}, u32[]{:S(2)}) %collective-permute-start.7) | collective-permute-done | bytes 479264 | tf_op jit(solution)/shard_map/plane attention weights/ppermute | solution.py:743
  45.7 1.3 collective-permute-start.13
  47.8 1.4 collective-permute-start.15
  49.5 3.9 %collective-permute-start.10 = (bf16[192,384]{1,0:T(8,128)(2,1)S(1)}, bf16[192,384]{1,0:T(8,128)(2,1)S(1)}, u32[]{:S(2)}, u32[]{:S(2)}) collective-permute-start(bf16[192,384]{1,0:T(8,128)(2,1)S(1)} %copy-done.44), channel_id=1, source_target_pairs={{0,1},{1,0},{2,3},{3,2},{4,5},{5,4},{6,7},{7,6},{8,9},{9,8},{10,11... | collective-permute-start | bytes 442376 | tf_op jit(solution)/shard_map/line outer weights/ppermute | solution.py:746
  54.6 6.0 %collective-permute-done.10 = bf16[192,384]{1,0:T(8,128)(2,1)S(1)} collective-permute-done((bf16[192,384]{1,0:T(8,128)(2,1)S(1)}, bf16[192,384]{1,0:T(8,128)(2,1)S(1)}, u32[]{:S(2)}, u32[]{:S(2)}) %collective-permute-start.10) | collective-permute-done | bytes 147488 | tf_op jit(solution)/shard_map/line outer weights/ppermute | solution.py:746
  60.6 1.3 collective-permute-start.12
  61.9 1.4 shard_map.326.w_ref.wo_ref.w_hbm
  63.4 7.2 %shard_map.327 = (bf16[4,576,512]{2,1,0:T(8,128)(2,1)S(1)}, bf16[4,192,512]{2,1,0:T(8,128)(2,1)S(1)}, f32[4,8,512]{2,1,0:T(8,128)S(1)}) custom-call(s32[3]{0:T(128)S(1)} %copy-done.22, s32[4]{0:T(128)S(1)} %copy-done.23, bf16[2048,768]{1,0:T(8,128)(2,1)S(1)} %copy-done, ...), custom_call_target="tpu_custom_call", output_to_operand_aliasing={{0}: (7, {}), {1}: (8, {}), {2}: (9, {})} | custom-call | flops 450000000 | bytes 450000 | tf_op jit(solution)/shard_map/pallas_call | solution.py:146
  71.1 1.3 collective-permute-start.17
  73.3 1.4 collective-permute-start.19
  76.1 11.7 %shard_map.329 = (f32[512,768]{1,0:T(8,128)S(1)}, f32[512,1]{1,0:T(8,128)S(1)}, f32[512,768]{1,0:T(8,128)S(1)}, bf16[512,768]{1,0:T(8,128)(2,1)S(1)}, bf16[4,512...) custom-call(s32[3]{0:T(128)S(1)} %copy-done.22, bf16[4,192,512]{2,1,0:T(8,128)(2,1)S(1)} %get-tuple-element.180.o_ref.o_hbm, ...), custom_call_target="tpu_custom_call" | custom-call | flops 600000000 | bytes 1000000 | tf_op jit(solution)/shard_map/pallas_call | solution.py:332
  89.8 2.8 collective-permute-done.18
  92.6 1.6 collective-permute-done.19
  94.7 3.6 %collective-permute-done.20.far_ref = bf16[4,3,192,384]{3,2,1,0:T(8,128)(2,1)S(1)} collective-permute-done((bf16[4,3,192,384]{3,2,1,0:T(8,128)(2,1)S(1)}, bf16[4,3,192,384]{3,2,1,0:T(8,128)(2,1)S(1)}, u32[]{:S(2)}, u32[]{:S(2)}) %collective-permute-start.20) | collective-permute-done | bytes 1769504 | tf_op jit(solution)/shard_map/core outer weights/ppermute | solution.py:743
  99.5 5.1 %shard_map.331 = (bf16[512,768]{1,0:T(8,128)(2,1)S(1)}, f32[512,768]{1,0:T(8,128)S(1)}, f32[8,768]{1,0:T(8,128)S(1)}) custom-call(s32[3]{0:T(128)S(1)} %copy-done.22, bf16[4,512,768]{2,1,0:T(8,128)(2,1)S(1)} %get-tuple-element.187.act_ref.left_ref, bf16[4,768,768]{2,1,0:T(8,128)(2,1)S(1)} %shard_map.330.wu_ref, ...), custom_call_target="tpu_custom_call" | custom-call | flops 250000000 | bytes 700000 | tf_op jit(solution)/shard_map/pallas_call | solution.py:394
  104.7 5.1 %shard_map.332 = (bf16[4,4,192,384]{3,2,1,0:T(8,128)(2,1)S(1)}, bf16[4,4,192,384]{3,2,1,0:T(8,128)(2,1)S(1)}) custom-call(s32[3]{0:T(128)S(1)} %copy-done.22, bf16[4,512,768]{2,1,0:T(8,128)(2,1)S(1)} %get-tuple-element.187.act_ref.left_ref, f32[512,768]{1,0:T(8,128)S(1)} %get-tuple-element.196.right_ref.up_ref.start_ref), custom_call_target="tpu_custom_call" | custom-call | flops 300000000 | bytes 400000 | tf_op jit(solution)/shard_map/pallas_call | solution.py:501
  110.0 4.3 %collective-permute-start.22 = (bf16[512,768]{1,0:T(8,128)(2,1)S(1)}, bf16[512,768]{1,0:T(8,128)(2,1)}, u32[]{:S(2)}, u32[]{:S(2)}) collective-permute-start(bf16[512,768]{1,0:T(8,128)(2,1)S(1)} %get-tuple-element.279), channel_id=1, source_target_pairs={{0,1},{1,2},{2,3},{4,5},{5,6},{6,7},{8,9},{9,10},{10,11},{12,13},{... | collective-permute-start | bytes 2359304 | tf_op jit(solution)/shard_map/rows 1/ppermute | solution.py:760
  115.7 5.1 %shard_map.333 = (f32[512,768]{1,0:T(8,128)S(1)}, bf16[4,512,768]{2,1,0:T(8,128)(2,1)S(1)}, f32[4,1,768]{2,1,0:T(1,128)S(1)}) custom-call(f32[512,768]{1,0:T(8,128)S(1)} %get-tuple-element.196.right_ref.up_ref.start_ref, f32[512,768]{1,0:T(8,128)S(1)} %get-tuple-element.196.right_ref.up_ref.start_ref, bf16[4,512,768]{2,1,0:T(8,128)(2,1)S(1)} %get-tuple-element.197.slope_ref, ...), custom_call_target="tpu_custom_call" | custom-call | flops 300000000 | bytes 400000 | tf_op jit(solution)/shard_map/pallas_call | solution.py:462
  122.8 1.5 collective-permute-start.24
  124.8 5.7 %shard_map.335 = (f32[512,768]{1,0:T(8,128)S(1)}, bf16[4,512,768]{2,1,0:T(8,128)(2,1)S(1)}, f32[4,1,768]{2,1,0:T(1,128)S(1)}, bf16[512,768]{1,0:T(8,128)(2,1)S(1)}, f32[8,768]{1,0:T(8,128)S(1)}) custom-call(f32[512,768]{1,0:T(8,128)S(1)} %get-tuple-element.196.right_ref.up_ref.start_ref, ...), custom_call_target="tpu_custom_call", output_to_operand_aliasing={{1}: (8, {}), {2}: (9, {})} | custom-call | flops 300000000 | bytes 400000 | tf_op jit(solution)/shard_map/pallas_call | solution.py:462
  130.8 5.1 %collective-permute-done.23 = bf16[512,768]{1,0:T(8,128)(2,1)} collective-permute-done((bf16[512,768]{1,0:T(8,128)(2,1)S(1)}, bf16[512,768]{1,0:T(8,128)(2,1)}, u32[]{:S(2)}, u32[]{:S(2)}) %collective-permute-start.23) | collective-permute-done | bytes 786464 | tf_op jit(solution)/shard_map/rows 1/ppermute | solution.py:761
  136.1 5.1 %shard_map.337 = (bf16[4,4,192,384]{3,2,1,0:T(8,128)(2,1)S(1)}, bf16[4,4,192,384]{3,2,1,0:T(8,128)(2,1)S(1)}) custom-call(s32[3]{0:T(128)S(1)} %copy-done.22, bf16[4,512,768]{2,1,0:T(8,128)(2,1)S(1)} %get-tuple-element.219.left_ref, bf16[512,768]{1,0:T(8,128)(2,1)S(1)} %copy-done.13), custom_call_target="tpu_custom_call" | custom-call | flops 300000000 | bytes 400000 | tf_op jit(solution)/shard_map/pallas_call | solution.py:501
  142.0 1.3 collective-permute-start.30
  143.3 1.3 collective-permute-start.27
  145.4 6.3 %shard_map.338 = (f32[512,768]{1,0:T(8,128)S(1)}, bf16[4,4,208,384]{3,2,1,0:T(8,128)(2,1)S(1)}, bf16[4,4,208,384]{3,2,1,0:T(8,128)(2,1)S(1)}) custom-call(s32[3]{0:T(128)S(1)} %copy-done.22, s32[4]{0:T(128)S(1)} %copy-done.23, bf16[2048,768]{1,0:T(8,128)(2,1)S(1)} %copy-done, bf16[4,768,768]{2,1,0:T(8,128)(2,1)S(1)} %shard_map.326.w_ref.wo_ref.w_hbm, ...), custom_call_target="tpu_custom_call" | custom-call | flops 250000000 | bytes 250000 | tf_op jit(solution)/shard_map/pallas_call | solution.py:240
  152.9 5.9 %shard_map.340 = (f32[512,768]{1,0:T(8,128)S(1)}, bf16[4,4,208,384]{3,2,1,0:T(8,128)(2,1)S(1)}, bf16[4,4,208,384]{3,2,1,0:T(8,128)(2,1)S(1)}) custom-call(s32[3]{0:T(128)S(1)} %copy-done.22, s32[4]{0:T(128)S(1)} %copy-done.23, bf16[2048,768]{1,0:T(8,128)(2,1)S(1)} %copy-done, ...), custom_call_target="tpu_custom_call", output_to_operand_aliasing={{1}: (14, {}), {2}: (15, {})} | custom-call | flops 250000000 | bytes 250000 | tf_op jit(solution)/shard_map/pallas_call | solution.py:240
  160.8 1.5 collective-permute-start.31
  162.3 2.2 collective-permute-done.30
  165.2 1.3 collective-permute-start.35
  166.5 6.1 %shard_map.341 = (f32[512,768]{1,0:T(8,128)S(1)}, bf16[4,4,208,384]{3,2,1,0:T(8,128)(2,1)S(1)}, bf16[4,4,208,384]{3,2,1,0:T(8,128)(2,1)S(1)}) custom-call(s32[3]{0:T(128)S(1)} %copy-done.22, s32[4]{0:T(128)S(1)} %copy-done.23, bf16[2048,768]{1,0:T(8,128)(2,1)S(1)} %copy-done, ...), custom_call_target="tpu_custom_call", output_to_operand_aliasing={{1}: (14, {}), {2}: (15, {})} | custom-call | flops 250000000 | bytes 250000 | tf_op jit(solution)/shard_map/pallas_call | solution.py:240
  172.8 4.6 %collective-permute-start.33 = (bf16[2,192,384]{2,1,0:T(8,128)(2,1)S(1)}, bf16[2,192,384]{2,1,0:T(8,128)(2,1)S(1)}, u32[]{:S(2)}, u32[]{:S(2)}) collective-permute-start(bf16[2,192,384]{2,1,0:T(8,128)(2,1)S(1)} %add_convert_fusion.2), channel_id=1, source_target_pairs={{0,1},{3,2},{4,5},{7,6},{8,9},{11,10},{12,13},{15,14},{16,17},{19,... | collective-permute-start | bytes 884744 | tf_op jit(solution)/shard_map/line ends outer grad/ppermute | solution.py:788
  177.6 6.7 %shard_map.343 = (bf16[512,768]{1,0:T(8,128)(2,1)}, bf16[4,4,208,384]{3,2,1,0:T(8,128)(2,1)S(1)}, bf16[4,4,208,384]{3,2,1,0:T(8,128)(2,1)S(1)}) custom-call(s32[3]{0:T(128)S(1)} %copy-done.22, s32[4]{0:T(128)S(1)} %copy-done.23, bf16[2048,768]{1,0:T(8,128)(2,1)S(1)} %copy-done, ...), custom_call_target="tpu_custom_call", output_to_operand_aliasing={{1}: (14, {}), {2}: (15, {})} | custom-call | flops 250000000 | bytes 250000 | tf_op jit(solution)/shard_map/pallas_call | solution.py:240
  184.4 1.9 collective-permute-done.35
  188.6 2.4 collective-permute-start.36
  192.3 2.3 shard_map.344
  194.6 7.5 %collective-permute-done.39 = bf16[4,192,384]{2,1,0:T(8,128)(2,1)} collective-permute-done((bf16[4,192,384]{2,1,0:T(8,128)(2,1)S(1)}, bf16[4,192,384]{2,1,0:T(8,128)(2,1)}, u32[]{:S(2)}, u32[]{:S(2)}) %collective-permute-start.39) | collective-permute-done | bytes 589856 | tf_op jit(solution)/shard_map/plane two inner grad/ppermute | solution.py:743
  206.1 1.4 collective-permute-start.41
  207.5 1.4 convert_add_fusion.2
  208.9 3.5 %collective-permute-done.37 = bf16[512,768]{1,0:T(8,128)(2,1)} collective-permute-done((bf16[512,768]{1,0:T(8,128)(2,1)}, bf16[512,768]{1,0:T(8,128)(2,1)}, u32[]{:S(2)}, u32[]{:S(2)}) %collective-permute-start.37) | collective-permute-done | bytes 786464 | tf_op jit(solution)/shard_map/grad rows 1/ppermute | solution.py:761
  214.7 5.3 %collective-permute-start.44 = (bf16[2,192,384]{2,1,0:T(8,128)(2,1)S(1)}, bf16[2,192,384]{2,1,0:T(8,128)(2,1)S(1)}, u32[]{:S(2)}, u32[]{:S(2)}) collective-permute-start(bf16[2,192,384]{2,1,0:T(8,128)(2,1)S(1)} %get-tuple-element.282), channel_id=1, source_target_pairs={{0,1},{1,0},{2,3},{3,2},{4,5},{5,4},{6,7},{7,6},{8,9},{9,8},{10,11... | collective-permute-start | bytes 884744 | tf_op jit(solution)/shard_map/line one inner grad/ppermute | solution.py:746
  220.7 1.5 collective-permute-start.48
  225.2 1.4 select_dynamic-update-slice_fusion.3
  228.9 5.8 %collective-permute-start.53 = (bf16[208,384]{1,0:T(8,128)(2,1)S(1)}, bf16[208,384]{1,0:T(8,128)(2,1)S(1)}, u32[]{:S(2)}, u32[]{:S(2)}) collective-permute-start(bf16[208,384]{1,0:T(8,128)(2,1)S(1)} %get-tuple-element.325), channel_id=1, source_target_pairs={{0,1},{1,0},{2,3},{3,2},{4,5},{5,4},{6,7},{7,6},{8,9},{9,8},{10,11... | collective-permute-start | bytes 479240 | tf_op jit(solution)/shard_map/line attention grad/ppermute | solution.py:746
  234.7 2.4 collective-permute-start.55
  237.1 12.4 %collective-permute-done.48 = bf16[512,768]{1,0:T(8,128)(2,1)S(1)} collective-permute-done((bf16[512,768]{1,0:T(8,128)(2,1)}, bf16[512,768]{1,0:T(8,128)(2,1)S(1)}, u32[]{:S(2)}, u32[]{:S(2)}) %collective-permute-start.48) | collective-permute-done | bytes 786464 | tf_op jit(solution)/shard_map/grad rows 2/ppermute | solution.py:761
  249.7 2.1 collective-permute-start.51
  254.0 1.5 collective-permute-done.54
  256.8 4.3 %collective-permute-done.51 = bf16[192,384]{1,0:T(8,128)(2,1)S(1)} collective-permute-done((bf16[192,384]{1,0:T(8,128)(2,1)S(1)}, bf16[192,384]{1,0:T(8,128)(2,1)S(1)}, u32[]{:S(2)}, u32[]{:S(2)}) %collective-permute-start.51) | collective-permute-done | bytes 147488 | tf_op jit(solution)/shard_map/line two inner grad/ppermute | solution.py:746
  264.9 9.9 %collective-permute-done.56 = bf16[592,384]{1,0:T(8,128)(2,1)S(1)} collective-permute-done((bf16[592,384]{1,0:T(8,128)(2,1)S(1)}, bf16[592,384]{1,0:T(8,128)(2,1)S(1)}, u32[]{:S(2)}, u32[]{:S(2)}) %collective-permute-start.56) | collective-permute-done | bytes 454688 | tf_op jit(solution)/shard_map/plane result/ppermute | solution.py:743
  274.8 5.9 %collective-permute-done.57 = bf16[592,384]{1,0:T(8,128)(2,1)S(1)} collective-permute-done((bf16[592,384]{1,0:T(8,128)(2,1)S(1)}, bf16[592,384]{1,0:T(8,128)(2,1)S(1)}, u32[]{:S(2)}, u32[]{:S(2)}) %collective-permute-start.57) | collective-permute-done | bytes 454688 | tf_op jit(solution)/shard_map/plane result/ppermute | solution.py:743
  283.0 1.4 select_dynamic-update-slice_fusion
  284.8 4.4 %shard_map.346 = (f32[192,768]{1,0:T(8,128)}, f32[192,768]{1,0:T(8,128)}, f32[192,768]{1,0:T(8,128)}, f32[192,768]{1,0:T(8,128)}, f32[768,768]{1,0:T(8,128)}, /*...) custom-call(s32[3]{0:T(128)S(1)} %copy-done.22, ...), custom_call_target="tpu_custom_call" | custom-call | flops 100000000 | tf_op jit(solution)/shard_map/pallas_call | solution.py:667
  (212 shorter events, 48.6 us)
Async XLA Ops:
  5.3 13.2 %collective-permute-start = (bf16[1,208,384]{2,1,0:T(8,128)(2,1)}, bf16[1,208,384]{2,1,0:T(8,128)(2,1)S(1)}, u32[]{:S(2)}, u32[]{:S(2)}) collective-permute-start(bf16[1,208,384]{2,1,0:T(8,128)(2,1)} %get-tuple-element.170.b_ref.own_ref), channel_id=1, source_target_pairs={{0,1},{1,0},{2,3},{3,2},{4,5},{5,4},{6,7},{7,6},{8,9},{9,8},{10,11... | collective-permute-start | bytes 479240 | tf_op jit(solution)/shard_map/line attention weights/ppermute | solution.py:746
  8.4 15.0 %collective-permute-start.1 = (bf16[1,208,384]{2,1,0:T(8,128)(2,1)}, bf16[1,208,384]{2,1,0:T(8,128)(2,1)S(1)}, u32[]{:S(2)}, u32[]{:S(2)}) collective-permute-start(bf16[1,208,384]{2,1,0:T(8,128)(2,1)} %get-tuple-element.170.b_ref.own_ref), channel_id=1, source_target_pairs={{0,2},{1,3},{2,0},{3,1},{4,6},{5,7},{6,4},{7,5},{8,10},{9,11},{10,... | collective-permute-start | bytes 479240 | tf_op jit(solution)/shard_map/line attention weights/ppermute | solution.py:746
  11.0 12.4 %collective-permute-start.2 = (bf16[1,208,384]{2,1,0:T(8,128)(2,1)}, bf16[1,208,384]{2,1,0:T(8,128)(2,1)S(1)}, u32[]{:S(2)}, u32[]{:S(2)}) collective-permute-start(bf16[1,208,384]{2,1,0:T(8,128)(2,1)} %get-tuple-element.170.b_ref.own_ref), channel_id=1, source_target_pairs={{0,3},{1,2},{2,1},{3,0},{4,7},{5,6},{6,5},{7,4},{8,11},{9,10},{10,... | collective-permute-start | bytes 479240 | tf_op jit(solution)/shard_map/line attention weights/ppermute | solution.py:746
  23.5 18.3 %collective-permute-start.6 = (bf16[3,208,384]{2,1,0:T(8,128)(2,1)S(1)}, bf16[3,208,384]{2,1,0:T(8,128)(2,1)S(1)}, u32[]{:S(2)}, u32[]{:S(2)}) collective-permute-start(bf16[3,208,384]{2,1,0:T(8,128)(2,1)S(1)} %constant_dynamic-update-slice_fusion.b_ref.others_ref), channel_id=1, source_target_pairs={{0,8},{4,12},{8,0},{12,4},{16,24},{20,28},{24,16},{28,20},{1,9},{5... | collective-permute-start | bytes 1437704 | tf_op jit(solution)/shard_map/plane attention weights/ppermute | solution.py:743
  25.1 20.2 %collective-permute-start.7 = (bf16[3,208,384]{2,1,0:T(8,128)(2,1)S(1)}, bf16[3,208,384]{2,1,0:T(8,128)(2,1)S(1)}, u32[]{:S(2)}, u32[]{:S(2)}) collective-permute-start(bf16[3,208,384]{2,1,0:T(8,128)(2,1)S(1)} %constant_dynamic-update-slice_fusion.b_ref.others_ref), channel_id=1, source_target_pairs={{0,16},{4,20},{8,24},{12,28},{16,0},{20,4},{24,8},{28,12},{1,17},{... | collective-permute-start | bytes 1437704 | tf_op jit(solution)/shard_map/plane attention weights/ppermute | solution.py:743
  26.6 18.7 %collective-permute-start.8 = (bf16[3,208,384]{2,1,0:T(8,128)(2,1)S(1)}, bf16[3,208,384]{2,1,0:T(8,128)(2,1)S(1)}, u32[]{:S(2)}, u32[]{:S(2)}) collective-permute-start(bf16[3,208,384]{2,1,0:T(8,128)(2,1)S(1)} %constant_dynamic-update-slice_fusion.b_ref.others_ref), channel_id=1, source_target_pairs={{0,24},{4,28},{8,16},{12,20},{16,8},{20,12},{24,0},{28,4},{1,25},{... | collective-permute-start | bytes 1437704 | tf_op jit(solution)/shard_map/plane attention weights/ppermute | solution.py:743
  27.1 6.8 %collective-permute-start.3 = (bf16[192,384]{1,0:T(8,128)(2,1)S(1)}, bf16[192,384]{1,0:T(8,128)(2,1)S(1)}, u32[]{:S(2)}, u32[]{:S(2)}) collective-permute-start(bf16[192,384]{1,0:T(8,128)(2,1)S(1)} %copy-done.45), channel_id=1, source_target_pairs={{0,1},{1,0},{2,3},{3,2},{4,5},{5,4},{6,7},{7,6},{8,9},{9,8},{10,11... | collective-permute-start | bytes 442376 | tf_op jit(solution)/shard_map/line inner weights/ppermute | solution.py:746
  29.6 12.2 %collective-permute-start.4 = (bf16[192,384]{1,0:T(8,128)(2,1)S(1)}, bf16[192,384]{1,0:T(8,128)(2,1)S(1)}, u32[]{:S(2)}, u32[]{:S(2)}) collective-permute-start(bf16[192,384]{1,0:T(8,128)(2,1)S(1)} %copy-done.45), channel_id=1, source_target_pairs={{0,2},{1,3},{2,0},{3,1},{4,6},{5,7},{6,4},{7,5},{8,10},{9,11},{10,... | collective-permute-start | bytes 442376 | tf_op jit(solution)/shard_map/line inner weights/ppermute | solution.py:746
  33.8 8.0 %collective-permute-start.5 = (bf16[192,384]{1,0:T(8,128)(2,1)S(1)}, bf16[192,384]{1,0:T(8,128)(2,1)S(1)}, u32[]{:S(2)}, u32[]{:S(2)}) collective-permute-start(bf16[192,384]{1,0:T(8,128)(2,1)S(1)} %copy-done.45), channel_id=1, source_target_pairs={{0,3},{1,2},{2,1},{3,0},{4,7},{5,6},{6,5},{7,4},{8,11},{9,10},{10,... | collective-permute-start | bytes 442376 | tf_op jit(solution)/shard_map/line inner weights/ppermute | solution.py:746
  45.2 16.7 %copy-start.5 = (bf16[1,768,768]{2,1,0:T(8,128)(2,1)S(1)}, bf16[1,768,768]{2,1,0:T(8,128)(2,1)}, u32[]{:S(2)}) copy-start(bf16[1,768,768]{2,1,0:T(8,128)(2,1)} %get-tuple-element.171.w_ref) | copy-start | bytes 3538948
  45.5 4.0 %collective-permute-start.9 = (bf16[4,3,208,384]{3,2,1,0:T(8,128)(2,1)S(1)}, bf16[4,3,208,384]{3,2,1,0:T(8,128)(2,1)S(1)}, u32[]{:S(2)}, u32[]{:S(2)}) collective-permute-start(bf16[4,3,208,384]{3,2,1,0:T(8,128)(2,1)S(1)} %pad_maximum_fusion.near_ref), channel_id=1, source_target_pairs={{0,4},{4,0},{8,12},{12,8},{16,20},{20,16},{24,28},{28,24},{1,5},{5... | collective-permute-start | bytes 5750792 | tf_op jit(solution)/shard_map/core attention weights/ppermute | solution.py:743
  45.7 25.0 %collective-permute-start.13 = (bf16[3,192,384]{2,1,0:T(8,128)(2,1)S(1)}, bf16[3,192,384]{2,1,0:T(8,128)(2,1)S(1)}, u32[]{:S(2)}, u32[]{:S(2)}) collective-permute-start(bf16[3,192,384]{2,1,0:T(8,128)(2,1)S(1)} %pad_maximum_fusion.5), channel_id=1, source_target_pairs={{0,8},{4,12},{8,0},{12,4},{16,24},{20,28},{24,16},{28,20},{1,9},{5... | collective-permute-start | bytes 1327112 | tf_op jit(solution)/shard_map/plane inner weights/ppermute | solution.py:743
  47.0 23.7 %collective-permute-start.14 = (bf16[3,192,384]{2,1,0:T(8,128)(2,1)S(1)}, bf16[3,192,384]{2,1,0:T(8,128)(2,1)S(1)}, u32[]{:S(2)}, u32[]{:S(2)}) collective-permute-start(bf16[3,192,384]{2,1,0:T(8,128)(2,1)S(1)} %pad_maximum_fusion.5), channel_id=1, source_target_pairs={{0,16},{4,20},{8,24},{12,28},{16,0},{20,4},{24,8},{28,12},{1,17},{... | collective-permute-start | bytes 1327112 | tf_op jit(solution)/shard_map/plane inner weights/ppermute | solution.py:743
  47.8 22.9 %collective-permute-start.15 = (bf16[3,192,384]{2,1,0:T(8,128)(2,1)S(1)}, bf16[3,192,384]{2,1,0:T(8,128)(2,1)S(1)}, u32[]{:S(2)}, u32[]{:S(2)}) collective-permute-start(bf16[3,192,384]{2,1,0:T(8,128)(2,1)S(1)} %pad_maximum_fusion.5), channel_id=1, source_target_pairs={{0,24},{4,28},{8,16},{12,20},{16,8},{20,12},{24,0},{28,4},{1,25},{... | collective-permute-start | bytes 1327112 | tf_op jit(solution)/shard_map/plane inner weights/ppermute | solution.py:743
  49.5 11.1 %collective-permute-start.10 = (bf16[192,384]{1,0:T(8,128)(2,1)S(1)}, bf16[192,384]{1,0:T(8,128)(2,1)S(1)}, u32[]{:S(2)}, u32[]{:S(2)}) collective-permute-start(bf16[192,384]{1,0:T(8,128)(2,1)S(1)} %copy-done.44), channel_id=1, source_target_pairs={{0,1},{1,0},{2,3},{3,2},{4,5},{5,4},{6,7},{7,6},{8,9},{9,8},{10,11... | collective-permute-start | bytes 442376 | tf_op jit(solution)/shard_map/line outer weights/ppermute | solution.py:746
  53.4 17.2 %collective-permute-start.11 = (bf16[192,384]{1,0:T(8,128)(2,1)S(1)}, bf16[192,384]{1,0:T(8,128)(2,1)S(1)}, u32[]{:S(2)}, u32[]{:S(2)}) collective-permute-start(bf16[192,384]{1,0:T(8,128)(2,1)S(1)} %copy-done.44), channel_id=1, source_target_pairs={{0,2},{1,3},{2,0},{3,1},{4,6},{5,7},{6,4},{7,5},{8,10},{9,11},{10,... | collective-permute-start | bytes 442376 | tf_op jit(solution)/shard_map/line outer weights/ppermute | solution.py:746
  60.6 10.0 %collective-permute-start.12 = (bf16[192,384]{1,0:T(8,128)(2,1)S(1)}, bf16[192,384]{1,0:T(8,128)(2,1)S(1)}, u32[]{:S(2)}, u32[]{:S(2)}) collective-permute-start(bf16[192,384]{1,0:T(8,128)(2,1)S(1)} %copy-done.44), channel_id=1, source_target_pairs={{0,3},{1,2},{2,1},{3,0},{4,7},{5,6},{6,5},{7,4},{8,11},{9,10},{10,... | collective-permute-start | bytes 442376 | tf_op jit(solution)/shard_map/line outer weights/ppermute | solution.py:746
  71.0 3.8 %collective-permute-start.16 = (bf16[4,3,192,384]{3,2,1,0:T(8,128)(2,1)S(1)}, bf16[4,3,192,384]{3,2,1,0:T(8,128)(2,1)S(1)}, u32[]{:S(2)}, u32[]{:S(2)}) collective-permute-start(bf16[4,3,192,384]{3,2,1,0:T(8,128)(2,1)S(1)} %pad_maximum_fusion.2.near_ref), channel_id=1, source_target_pairs={{0,4},{4,0},{8,12},{12,8},{16,20},{20,16},{24,28},{28,24},{1,5},{5... | collective-permute-start | bytes 5308424 | tf_op jit(solution)/shard_map/core inner weights/ppermute | solution.py:743
  71.1 18.7 %collective-permute-start.17 = (bf16[3,192,384]{2,1,0:T(8,128)(2,1)S(1)}, bf16[3,192,384]{2,1,0:T(8,128)(2,1)S(1)}, u32[]{:S(2)}, u32[]{:S(2)}) collective-permute-start(bf16[3,192,384]{2,1,0:T(8,128)(2,1)S(1)} %pad_maximum_fusion.6), channel_id=1, source_target_pairs={{0,8},{4,12},{8,0},{12,4},{16,24},{20,28},{24,16},{28,20},{1,9},{5... | collective-permute-start | bytes 1327112 | tf_op jit(solution)/shard_map/plane outer weights/ppermute | solution.py:743
  72.4 20.1 %collective-permute-start.18 = (bf16[3,192,384]{2,1,0:T(8,128)(2,1)S(1)}, bf16[3,192,384]{2,1,0:T(8,128)(2,1)S(1)}, u32[]{:S(2)}, u32[]{:S(2)}) collective-permute-start(bf16[3,192,384]{2,1,0:T(8,128)(2,1)S(1)} %pad_maximum_fusion.6), channel_id=1, source_target_pairs={{0,16},{4,20},{8,24},{12,28},{16,0},{20,4},{24,8},{28,12},{1,17},{... | collective-permute-start | bytes 1327112 | tf_op jit(solution)/shard_map/plane outer weights/ppermute | solution.py:743
  73.3 20.9 %collective-permute-start.19 = (bf16[3,192,384]{2,1,0:T(8,128)(2,1)S(1)}, bf16[3,192,384]{2,1,0:T(8,128)(2,1)S(1)}, u32[]{:S(2)}, u32[]{:S(2)}) collective-permute-start(bf16[3,192,384]{2,1,0:T(8,128)(2,1)S(1)} %pad_maximum_fusion.6), channel_id=1, source_target_pairs={{0,24},{4,28},{8,16},{12,20},{16,8},{20,12},{24,0},{28,4},{1,25},{... | collective-permute-start | bytes 1327112 | tf_op jit(solution)/shard_map/plane outer weights/ppermute | solution.py:743
  89.8 25.9 %copy-start.1 = (bf16[4,512,768]{2,1,0:T(8,128)(2,1)}, bf16[4,512,768]{2,1,0:T(8,128)(2,1)S(1)}, u32[]{:S(2)}) copy-start(bf16[4,512,768]{2,1,0:T(8,128)(2,1)S(1)} %get-tuple-element.197.slope_ref) | copy-start | bytes 9437188
  94.5 3.8 %collective-permute-start.20 = (bf16[4,3,192,384]{3,2,1,0:T(8,128)(2,1)S(1)}, bf16[4,3,192,384]{3,2,1,0:T(8,128)(2,1)S(1)}, u32[]{:S(2)}, u32[]{:S(2)}) collective-permute-start(bf16[4,3,192,384]{3,2,1,0:T(8,128)(2,1)S(1)} %pad_maximum_fusion.3.near_ref), channel_id=1, source_target_pairs={{0,4},{4,0},{8,12},{12,8},{16,20},{20,16},{24,28},{28,24},{1,5},{5... | collective-permute-start | bytes 5308424 | tf_op jit(solution)/shard_map/core outer weights/ppermute | solution.py:743
  109.8 10.9 %collective-permute-start.21 = (bf16[4,4,192,384]{3,2,1,0:T(8,128)(2,1)S(1)}, bf16[4,4,192,384]{3,2,1,0:T(8,128)(2,1)S(1)}, u32[]{:S(2)}, u32[]{:S(2)}) collective-permute-start(bf16[4,4,192,384]{3,2,1,0:T(8,128)(2,1)S(1)} %get-tuple-element.199), channel_id=1, source_target_pairs={{0,4},{4,0},{8,12},{12,8},{16,20},{20,16},{24,28},{28,24},{1,5},{5... | collective-permute-start | bytes 7077896 | tf_op jit(solution)/shard_map/core outer grad/ppermute | solution.py:743
  110.0 20.7 %collective-permute-start.22 = (bf16[512,768]{1,0:T(8,128)(2,1)S(1)}, bf16[512,768]{1,0:T(8,128)(2,1)}, u32[]{:S(2)}, u32[]{:S(2)}) collective-permute-start(bf16[512,768]{1,0:T(8,128)(2,1)S(1)} %get-tuple-element.279), channel_id=1, source_target_pairs={{0,1},{1,2},{2,3},{4,5},{5,6},{6,7},{8,9},{9,10},{10,11},{12,13},{... | collective-permute-start | bytes 2359304 | tf_op jit(solution)/shard_map/rows 1/ppermute | solution.py:760
  114.4 21.5 %collective-permute-start.23 = (bf16[512,768]{1,0:T(8,128)(2,1)S(1)}, bf16[512,768]{1,0:T(8,128)(2,1)}, u32[]{:S(2)}, u32[]{:S(2)}) collective-permute-start(bf16[512,768]{1,0:T(8,128)(2,1)S(1)} %get-tuple-element.279), channel_id=1, source_target_pairs={{1,0},{2,1},{3,2},{5,4},{6,5},{7,6},{9,8},{10,9},{11,10},{13,12},{... | collective-permute-start | bytes 2359304 | tf_op jit(solution)/shard_map/rows 1/ppermute | solution.py:761
  122.8 13.1 %collective-permute-start.24 = (bf16[2,192,384]{2,1,0:T(8,128)(2,1)S(1)}, bf16[2,192,384]{2,1,0:T(8,128)(2,1)S(1)}, u32[]{:S(2)}, u32[]{:S(2)}) collective-permute-start(bf16[2,192,384]{2,1,0:T(8,128)(2,1)S(1)} %get-tuple-element.210), channel_id=1, source_target_pairs={{0,16},{4,20},{8,24},{12,28},{16,0},{20,4},{24,8},{28,12},{1,17},{... | collective-permute-start | bytes 884744 | tf_op jit(solution)/shard_map/plane one outer grad/ppermute | solution.py:743
  124.3 11.6 %collective-permute-start.25 = (bf16[2,192,384]{2,1,0:T(8,128)(2,1)S(1)}, bf16[2,192,384]{2,1,0:T(8,128)(2,1)S(1)}, u32[]{:S(2)}, u32[]{:S(2)}) collective-permute-start(bf16[2,192,384]{2,1,0:T(8,128)(2,1)S(1)} %get-tuple-element.211), channel_id=1, source_target_pairs={{0,8},{4,12},{8,0},{12,4},{16,24},{20,28},{24,16},{28,20},{1,9},{5... | collective-permute-start | bytes 884744 | tf_op jit(solution)/shard_map/plane one outer grad/ppermute | solution.py:743
  141.2 10.5 %collective-permute-start.26 = (bf16[4,4,192,384]{3,2,1,0:T(8,128)(2,1)S(1)}, bf16[4,4,192,384]{3,2,1,0:T(8,128)(2,1)S(1)}, u32[]{:S(2)}, u32[]{:S(2)}) collective-permute-start(bf16[4,4,192,384]{3,2,1,0:T(8,128)(2,1)S(1)} %get-tuple-element.227), channel_id=1, source_target_pairs={{0,4},{4,0},{8,12},{12,8},{16,20},{20,16},{24,28},{28,24},{1,5},{5... | collective-permute-start | bytes 7077896 | tf_op jit(solution)/shard_map/core inner grad/ppermute | solution.py:743
  141.3 21.1 %collective-permute-start.29 = (bf16[512,768]{1,0:T(8,128)(2,1)}, bf16[512,768]{1,0:T(8,128)(2,1)S(1)}, u32[]{:S(2)}, u32[]{:S(2)}) collective-permute-start(bf16[512,768]{1,0:T(8,128)(2,1)} %collective-permute-done.22), channel_id=1, source_target_pairs={{1,2},{2,3},{5,6},{6,7},{9,10},{10,11},{13,14},{14,15},{17,18},{18... | collective-permute-start | bytes 2359304 | tf_op jit(solution)/shard_map/rows 2/ppermute | solution.py:760
  142.0 22.5 %collective-permute-start.30 = (bf16[512,768]{1,0:T(8,128)(2,1)}, bf16[512,768]{1,0:T(8,128)(2,1)S(1)}, u32[]{:S(2)}, u32[]{:S(2)}) collective-permute-start(bf16[512,768]{1,0:T(8,128)(2,1)} %collective-permute-done.23), channel_id=1, source_target_pairs={{1,0},{2,1},{5,4},{6,5},{9,8},{10,9},{13,12},{14,13},{17,16},{18,1... | collective-permute-start | bytes 2359304 | tf_op jit(solution)/shard_map/rows 2/ppermute | solution.py:761
  143.3 15.8 %collective-permute-start.27 = (bf16[4,192,384]{2,1,0:T(8,128)(2,1)S(1)}, bf16[4,192,384]{2,1,0:T(8,128)(2,1)S(1)}, u32[]{:S(2)}, u32[]{:S(2)}) collective-permute-start(bf16[4,192,384]{2,1,0:T(8,128)(2,1)S(1)} %get-tuple-element.218), channel_id=1, source_target_pairs={{0,8},{4,12},{8,0},{12,4},{16,24},{20,28},{24,16},{28,20},{1,9},{5... | collective-permute-start | bytes 1769480 | tf_op jit(solution)/shard_map/plane two outer grad/ppermute | solution.py:743
  144.6 15.4 %collective-permute-start.28 = (bf16[4,192,384]{2,1,0:T(8,128)(2,1)S(1)}, bf16[4,192,384]{2,1,0:T(8,128)(2,1)S(1)}, u32[]{:S(2)}, u32[]{:S(2)}) collective-permute-start(bf16[4,192,384]{2,1,0:T(8,128)(2,1)S(1)} %get-tuple-element.235), channel_id=1, source_target_pairs={{0,16},{4,20},{8,24},{12,28},{16,0},{20,4},{24,8},{28,12},{1,17},{... | collective-permute-start | bytes 1769480 | tf_op jit(solution)/shard_map/plane two outer grad/ppermute | solution.py:743
  160.0 12.6 %collective-permute-start.32 = (bf16[2,192,384]{2,1,0:T(8,128)(2,1)S(1)}, bf16[2,192,384]{2,1,0:T(8,128)(2,1)S(1)}, u32[]{:S(2)}, u32[]{:S(2)}) collective-permute-start(bf16[2,192,384]{2,1,0:T(8,128)(2,1)S(1)} %get-tuple-element.248), channel_id=1, source_target_pairs={{0,8},{4,12},{8,0},{12,4},{16,24},{20,28},{24,16},{28,20},{1,9},{5... | collective-permute-start | bytes 884744 | tf_op jit(solution)/shard_map/plane one inner grad/ppermute | solution.py:743
  160.8 11.8 %collective-permute-start.31 = (bf16[2,192,384]{2,1,0:T(8,128)(2,1)S(1)}, bf16[2,192,384]{2,1,0:T(8,128)(2,1)S(1)}, u32[]{:S(2)}, u32[]{:S(2)}) collective-permute-start(bf16[2,192,384]{2,1,0:T(8,128)(2,1)S(1)} %get-tuple-element.246), channel_id=1, source_target_pairs={{0,16},{4,20},{8,24},{12,28},{16,0},{20,4},{24,8},{28,12},{1,17},{... | collective-permute-start | bytes 884744 | tf_op jit(solution)/shard_map/plane one inner grad/ppermute | solution.py:743
  164.5 19.9 %collective-permute-start.34 = (bf16[512,768]{1,0:T(8,128)(2,1)S(1)}, bf16[512,768]{1,0:T(8,128)(2,1)S(1)}, u32[]{:S(2)}, u32[]{:S(2)}) collective-permute-start(bf16[512,768]{1,0:T(8,128)(2,1)S(1)} %collective-permute-done.29), channel_id=1, source_target_pairs={{2,3},{6,7},{10,11},{14,15},{18,19},{22,23},{26,27},{30,31}} | collective-permute-start | bytes 2359304 | tf_op jit(solution)/shard_map/rows 3/ppermute | solution.py:760
  165.2 21.0 %collective-permute-start.35 = (bf16[512,768]{1,0:T(8,128)(2,1)S(1)}, bf16[512,768]{1,0:T(8,128)(2,1)S(1)}, u32[]{:S(2)}, u32[]{:S(2)}) collective-permute-start(bf16[512,768]{1,0:T(8,128)(2,1)S(1)} %collective-permute-done.30), channel_id=1, source_target_pairs={{1,0},{5,4},{9,8},{13,12},{17,16},{21,20},{25,24},{29,28}} | collective-permute-start | bytes 2359304 | tf_op jit(solution)/shard_map/rows 3/ppermute | solution.py:761
  172.8 11.5 %collective-permute-start.33 = (bf16[2,192,384]{2,1,0:T(8,128)(2,1)S(1)}, bf16[2,192,384]{2,1,0:T(8,128)(2,1)S(1)}, u32[]{:S(2)}, u32[]{:S(2)}) collective-permute-start(bf16[2,192,384]{2,1,0:T(8,128)(2,1)S(1)} %add_convert_fusion.2), channel_id=1, source_target_pairs={{0,1},{3,2},{4,5},{7,6},{8,9},{11,10},{12,13},{15,14},{16,17},{19,... | collective-permute-start | bytes 884744 | tf_op jit(solution)/shard_map/line ends outer grad/ppermute | solution.py:788
  186.3 6.1 %collective-permute-start.38 = (bf16[4,4,208,384]{3,2,1,0:T(8,128)(2,1)S(1)}, bf16[4,4,208,384]{3,2,1,0:T(8,128)(2,1)S(1)}, u32[]{:S(2)}, u32[]{:S(2)}) collective-permute-start(bf16[4,4,208,384]{3,2,1,0:T(8,128)(2,1)S(1)} %get-tuple-element.266), channel_id=1, source_target_pairs={{0,4},{4,0},{8,12},{12,8},{16,20},{20,16},{24,28},{28,24},{1,5},{5... | collective-permute-start | bytes 7667720 | tf_op jit(solution)/shard_map/core attention grad/ppermute | solution.py:743
  186.3 15.8 %collective-permute-start.39 = (bf16[4,192,384]{2,1,0:T(8,128)(2,1)S(1)}, bf16[4,192,384]{2,1,0:T(8,128)(2,1)}, u32[]{:S(2)}, u32[]{:S(2)}) collective-permute-start(bf16[4,192,384]{2,1,0:T(8,128)(2,1)S(1)} %get-tuple-element.254), channel_id=1, source_target_pairs={{0,8},{4,12},{8,0},{12,4},{16,24},{20,28},{24,16},{28,20},{1,9},{5... | collective-permute-start | bytes 1769480 | tf_op jit(solution)/shard_map/plane two inner grad/ppermute | solution.py:743
  187.4 20.1 %copy-start.19 = (bf16[4,192,384]{2,1,0:T(8,128)(2,1)S(1)}, bf16[4,192,384]{2,1,0:T(8,128)(2,1)}, u32[]{:S(2)}) copy-start(bf16[4,192,384]{2,1,0:T(8,128)(2,1)} %copy-done.18) | copy-start | bytes 1769476
  187.4 15.6 %collective-permute-start.40 = (bf16[4,192,384]{2,1,0:T(8,128)(2,1)S(1)}, bf16[4,192,384]{2,1,0:T(8,128)(2,1)}, u32[]{:S(2)}, u32[]{:S(2)}) collective-permute-start(bf16[4,192,384]{2,1,0:T(8,128)(2,1)S(1)} %get-tuple-element.269), channel_id=1, source_target_pairs={{0,16},{4,20},{8,24},{12,28},{16,0},{20,4},{24,8},{28,12},{1,17},{... | collective-permute-start | bytes 1769480 | tf_op jit(solution)/shard_map/plane two inner grad/ppermute | solution.py:743
  188.6 20.3 %collective-permute-start.36 = (bf16[512,768]{1,0:T(8,128)(2,1)}, bf16[512,768]{1,0:T(8,128)(2,1)}, u32[]{:S(2)}, u32[]{:S(2)}) collective-permute-start(bf16[512,768]{1,0:T(8,128)(2,1)} %get-tuple-element.264), channel_id=1, source_target_pairs={{0,1},{1,2},{2,3},{4,5},{5,6},{6,7},{8,9},{9,10},{10,11},{12,13},{... | collective-permute-start | bytes 2359304 | tf_op jit(solution)/shard_map/grad rows 1/ppermute | solution.py:760
  191.0 21.4 %collective-permute-start.37 = (bf16[512,768]{1,0:T(8,128)(2,1)}, bf16[512,768]{1,0:T(8,128)(2,1)}, u32[]{:S(2)}, u32[]{:S(2)}) collective-permute-start(bf16[512,768]{1,0:T(8,128)(2,1)} %get-tuple-element.264), channel_id=1, source_target_pairs={{1,0},{2,1},{3,2},{5,4},{6,5},{7,6},{9,8},{10,9},{11,10},{13,12},{... | collective-permute-start | bytes 2359304 | tf_op jit(solution)/shard_map/grad rows 1/ppermute | solution.py:761
  203.0 9.4 %collective-permute-start.42 = (bf16[2,208,384]{2,1,0:T(8,128)(2,1)}, bf16[2,208,384]{2,1,0:T(8,128)(2,1)S(1)}, u32[]{:S(2)}, u32[]{:S(2)}) collective-permute-start(bf16[2,208,384]{2,1,0:T(8,128)(2,1)} %get-tuple-element.275), channel_id=1, source_target_pairs={{0,16},{4,20},{8,24},{12,28},{16,0},{20,4},{24,8},{28,12},{1,17},{... | collective-permute-start | bytes 958472 | tf_op jit(solution)/shard_map/plane one attention grad/ppermute | solution.py:743
  204.2 8.6 %collective-permute-start.43 = (bf16[2,208,384]{2,1,0:T(8,128)(2,1)S(1)}, bf16[2,208,384]{2,1,0:T(8,128)(2,1)S(1)}, u32[]{:S(2)}, u32[]{:S(2)}) collective-permute-start(bf16[2,208,384]{2,1,0:T(8,128)(2,1)S(1)} %get-tuple-element.276), channel_id=1, source_target_pairs={{0,8},{4,12},{8,0},{12,4},{16,24},{20,28},{24,16},{28,20},{1,9},{5... | collective-permute-start | bytes 958472 | tf_op jit(solution)/shard_map/plane one attention grad/ppermute | solution.py:743
  206.1 6.3 %collective-permute-start.41 = (bf16[2,192,384]{2,1,0:T(8,128)(2,1)}, bf16[2,192,384]{2,1,0:T(8,128)(2,1)}, u32[]{:S(2)}, u32[]{:S(2)}) collective-permute-start(bf16[2,192,384]{2,1,0:T(8,128)(2,1)} %add_convert_fusion), channel_id=1, source_target_pairs={{1,2},{2,1},{5,6},{6,5},{9,10},{10,9},{13,14},{14,13},{17,18},{18,... | collective-permute-start | bytes 884744 | tf_op jit(solution)/shard_map/line middle outer grad/ppermute | solution.py:791
  212.9 14.9 %collective-permute-start.45 = (bf16[4,208,384]{2,1,0:T(8,128)(2,1)S(1)}, bf16[4,208,384]{2,1,0:T(8,128)(2,1)S(1)}, u32[]{:S(2)}, u32[]{:S(2)}) collective-permute-start(bf16[4,208,384]{2,1,0:T(8,128)(2,1)S(1)} %get-tuple-element.285), channel_id=1, source_target_pairs={{0,8},{4,12},{8,0},{12,4},{16,24},{20,28},{24,16},{28,20},{1,9},{5... | collective-permute-start | bytes 1916936 | tf_op jit(solution)/shard_map/plane two attention grad/ppermute | solution.py:743
  214.1 14.5 %collective-permute-start.46 = (bf16[4,208,384]{2,1,0:T(8,128)(2,1)S(1)}, bf16[4,208,384]{2,1,0:T(8,128)(2,1)S(1)}, u32[]{:S(2)}, u32[]{:S(2)}) collective-permute-start(bf16[4,208,384]{2,1,0:T(8,128)(2,1)S(1)} %get-tuple-element.286), channel_id=1, source_target_pairs={{0,16},{4,20},{8,24},{12,28},{16,0},{20,4},{24,8},{28,12},{1,17},{... | collective-permute-start | bytes 1916936 | tf_op jit(solution)/shard_map/plane two attention grad/ppermute | solution.py:743
  214.7 12.9 %collective-permute-start.44 = (bf16[2,192,384]{2,1,0:T(8,128)(2,1)S(1)}, bf16[2,192,384]{2,1,0:T(8,128)(2,1)S(1)}, u32[]{:S(2)}, u32[]{:S(2)}) collective-permute-start(bf16[2,192,384]{2,1,0:T(8,128)(2,1)S(1)} %get-tuple-element.282), channel_id=1, source_target_pairs={{0,1},{1,0},{2,3},{3,2},{4,5},{5,4},{6,7},{7,6},{8,9},{9,8},{10,11... | collective-permute-start | bytes 884744 | tf_op jit(solution)/shard_map/line one inner grad/ppermute | solution.py:746
  220.0 17.1 %collective-permute-start.47 = (bf16[512,768]{1,0:T(8,128)(2,1)}, bf16[512,768]{1,0:T(8,128)(2,1)S(1)}, u32[]{:S(2)}, u32[]{:S(2)}) collective-permute-start(bf16[512,768]{1,0:T(8,128)(2,1)} %collective-permute-done.36), channel_id=1, source_target_pairs={{1,2},{2,3},{5,6},{6,7},{9,10},{10,11},{13,14},{14,15},{17,18},{18... | collective-permute-start | bytes 2359304 | tf_op jit(solution)/shard_map/grad rows 2/ppermute | solution.py:760
  220.7 28.9 %collective-permute-start.48 = (bf16[512,768]{1,0:T(8,128)(2,1)}, bf16[512,768]{1,0:T(8,128)(2,1)S(1)}, u32[]{:S(2)}, u32[]{:S(2)}) collective-permute-start(bf16[512,768]{1,0:T(8,128)(2,1)} %collective-permute-done.37), channel_id=1, source_target_pairs={{1,0},{2,1},{5,4},{6,5},{9,8},{10,9},{13,12},{14,13},{17,16},{18,1... | collective-permute-start | bytes 2359304 | tf_op jit(solution)/shard_map/grad rows 2/ppermute | solution.py:761
  226.6 34.6 %copy-start.25 = (bf16[2048,768]{1,0:T(8,128)(2,1)}, bf16[2048,768]{1,0:T(8,128)(2,1)S(1)}, u32[]{:S(2)}) copy-start(bf16[2048,768]{1,0:T(8,128)(2,1)S(1)} %select_dynamic-update-slice_fusion.3) | copy-start | bytes 9437188
  228.9 24.4 %collective-permute-start.53 = (bf16[208,384]{1,0:T(8,128)(2,1)S(1)}, bf16[208,384]{1,0:T(8,128)(2,1)S(1)}, u32[]{:S(2)}, u32[]{:S(2)}) collective-permute-start(bf16[208,384]{1,0:T(8,128)(2,1)S(1)} %get-tuple-element.325), channel_id=1, source_target_pairs={{0,1},{1,0},{2,3},{3,2},{4,5},{5,4},{6,7},{7,6},{8,9},{9,8},{10,11... | collective-permute-start | bytes 479240 | tf_op jit(solution)/shard_map/line attention grad/ppermute | solution.py:746
  234.7 20.8 %collective-permute-start.54 = (bf16[208,384]{1,0:T(8,128)(2,1)S(1)}, bf16[208,384]{1,0:T(8,128)(2,1)S(1)}, u32[]{:S(2)}, u32[]{:S(2)}) collective-permute-start(bf16[208,384]{1,0:T(8,128)(2,1)S(1)} %get-tuple-element.324), channel_id=1, source_target_pairs={{0,2},{1,3},{2,0},{3,1},{4,6},{5,7},{6,4},{7,5},{8,10},{9,11},{10,... | collective-permute-start | bytes 479240 | tf_op jit(solution)/shard_map/line attention grad/ppermute | solution.py:746
  234.7 22.0 %collective-permute-start.55 = (bf16[208,384]{1,0:T(8,128)(2,1)S(1)}, bf16[208,384]{1,0:T(8,128)(2,1)S(1)}, u32[]{:S(2)}, u32[]{:S(2)}) collective-permute-start(bf16[208,384]{1,0:T(8,128)(2,1)S(1)} %get-tuple-element.323), channel_id=1, source_target_pairs={{0,3},{1,2},{2,1},{3,0},{4,7},{5,6},{6,5},{7,4},{8,11},{9,10},{10,... | collective-permute-start | bytes 479240 | tf_op jit(solution)/shard_map/line attention grad/ppermute | solution.py:746
  249.7 11.4 %collective-permute-start.51 = (bf16[192,384]{1,0:T(8,128)(2,1)S(1)}, bf16[192,384]{1,0:T(8,128)(2,1)S(1)}, u32[]{:S(2)}, u32[]{:S(2)}) collective-permute-start(bf16[192,384]{1,0:T(8,128)(2,1)S(1)} %fusion.9), channel_id=1, source_target_pairs={{0,2},{1,3},{2,0},{3,1},{4,6},{5,7},{6,4},{7,5},{8,10},{9,11},{10,... | collective-permute-start | bytes 442376 | tf_op jit(solution)/shard_map/line two inner grad/ppermute | solution.py:746
  251.8 9.3 %collective-permute-start.52 = (bf16[192,384]{1,0:T(8,128)(2,1)S(1)}, bf16[192,384]{1,0:T(8,128)(2,1)S(1)}, u32[]{:S(2)}, u32[]{:S(2)}) collective-permute-start(bf16[192,384]{1,0:T(8,128)(2,1)S(1)} %fusion.10), channel_id=1, source_target_pairs={{0,1},{1,0},{2,3},{3,2},{4,5},{5,4},{6,7},{7,6},{8,9},{9,8},{10,11... | collective-permute-start | bytes 442376 | tf_op jit(solution)/shard_map/line pair outer grad/ppermute | solution.py:746
  253.3 27.4 %collective-permute-start.49 = (bf16[512,768]{1,0:T(8,128)(2,1)S(1)}, bf16[512,768]{1,0:T(8,128)(2,1)S(1)}, u32[]{:S(2)}, u32[]{:S(2)}) collective-permute-start(bf16[512,768]{1,0:T(8,128)(2,1)S(1)} %collective-permute-done.47), channel_id=1, source_target_pairs={{2,3},{6,7},{10,11},{14,15},{18,19},{22,23},{26,27},{30,31}} | collective-permute-start | bytes 2359304 | tf_op jit(solution)/shard_map/grad rows 3/ppermute | solution.py:760
  255.5 25.2 %collective-permute-start.50 = (bf16[512,768]{1,0:T(8,128)(2,1)S(1)}, bf16[512,768]{1,0:T(8,128)(2,1)S(1)}, u32[]{:S(2)}, u32[]{:S(2)}) collective-permute-start(bf16[512,768]{1,0:T(8,128)(2,1)S(1)} %collective-permute-done.48), channel_id=1, source_target_pairs={{1,0},{5,4},{9,8},{13,12},{17,16},{21,20},{25,24},{29,28}} | collective-permute-start | bytes 2359304 | tf_op jit(solution)/shard_map/grad rows 3/ppermute | solution.py:761
  261.3 13.4 %collective-permute-start.56 = (bf16[592,384]{1,0:T(8,128)(2,1)S(1)}, bf16[592,384]{1,0:T(8,128)(2,1)S(1)}, u32[]{:S(2)}, u32[]{:S(2)}) collective-permute-start(bf16[592,384]{1,0:T(8,128)(2,1)S(1)} %get-tuple-element.329), channel_id=1, source_target_pairs={{0,8},{4,12},{8,0},{12,4},{16,24},{20,28},{24,16},{28,20},{1,9},{5... | collective-permute-start | bytes 1363976 | tf_op jit(solution)/shard_map/plane result/ppermute | solution.py:743
  262.4 18.2 %collective-permute-start.57 = (bf16[592,384]{1,0:T(8,128)(2,1)S(1)}, bf16[592,384]{1,0:T(8,128)(2,1)S(1)}, u32[]{:S(2)}, u32[]{:S(2)}) collective-permute-start(bf16[592,384]{1,0:T(8,128)(2,1)S(1)} %get-tuple-element.329), channel_id=1, source_target_pairs={{0,16},{4,20},{8,24},{12,28},{16,0},{20,4},{24,8},{28,12},{1,17},{... | collective-permute-start | bytes 1363976 | tf_op jit(solution)/shard_map/plane result/ppermute | solution.py:743
  263.6 17.1 %collective-permute-start.58 = (bf16[592,384]{1,0:T(8,128)(2,1)S(1)}, bf16[592,384]{1,0:T(8,128)(2,1)S(1)}, u32[]{:S(2)}, u32[]{:S(2)}) collective-permute-start(bf16[592,384]{1,0:T(8,128)(2,1)S(1)} %get-tuple-element.329), channel_id=1, source_target_pairs={{0,24},{4,28},{8,16},{12,20},{16,8},{20,12},{24,0},{28,4},{1,25},{... | collective-permute-start | bytes 1363976 | tf_op jit(solution)/shard_map/plane result/ppermute | solution.py:743
  281.0 3.8 %collective-permute-start.59 = (bf16[4,592,384]{2,1,0:T(8,128)(2,1)S(1)}, bf16[4,592,384]{2,1,0:T(8,128)(2,1)S(1)}, u32[]{:S(2)}, u32[]{:S(2)}) collective-permute-start(bf16[4,592,384]{2,1,0:T(8,128)(2,1)S(1)} %pad_maximum_fusion.1.near_ref), channel_id=1, source_target_pairs={{0,4},{4,0},{8,12},{12,8},{16,20},{20,16},{24,28},{28,24},{1,5},{5... | collective-permute-start | bytes 5455880 | tf_op jit(solution)/shard_map/core result/ppermute | solution.py:743
  (42 other events, 281.9 us)

commit v3 on v2

--- a/solution.py
+++ b/solution.py
@@ -867,13 +867,13 @@
         grad_one, grad_inner, db_inner, grad_one_low, sums_one = ffn_back(
             grad_two, tie(partial, own_u), slope, w_up, w_in, half, half, (normed, inv_spread, vectors_one), carried
         )
-        grad_one, grad_inner, up_1, down_1, *via_u = barrier(grad_one, grad_inner, up_1, down_1, *via_u)
+        mine_i, other_i = weight_grad(scalars, grad_inner, low)
+        grad_one, mine_i, other_i, up_1, down_1, *via_u = barrier(grad_one, mine_i, other_i, up_1, down_1, *via_u)
         with jax.named_scope("rows 2"):
             up_2, down_2 = rows_round(2, up_1, down_1)
         x_u, y_u = plane_add(x_u, y_u, *via_u)
         with jax.named_scope("plane two outer grad"):
             plane_u = plane_two(x_u, y_u)
-        mine_i, other_i = weight_grad(scalars, tie(grad_inner, x_u), low)
         with jax.named_scope("core inner grad"):
             theirs_i = across(other_i, 1)
         vectors = (db_inner, sums_one, sums_two)
@@ -885,7 +885,7 @@
                 scalars, lengths, tokens, w_attn, qkv, heads_out, lse, grad_one_low, start, tags, vectors, r, dtype, pieces
             )
 
-        start, *pieces = shard_back(tie(grad_one, mine_i), 3)
+        start, *pieces = shard_back(tie(grad_one, x_u), 3)
         start, theirs_i = barrier(start, theirs_i)
         own_i, x_i, y_i, *via_i = core_add(mine_i, theirs_i)
         start, *pieces = shard_back(tie(start, own_i), 2)

time: 294 us -> 291 us (0.990)
    ppermute x6, waiting for transfers between devices: 25 us -> 21.9 us  [rows_round(): lax.ppermute(down, 'tensor', [(i + 1, i) for i in range(n_tensor - k)])]
  transfers between devices with their start and end apart: 60 -> 60, of which waited for: 29 -> 27; matrix products, arithmetic and copies ran while one was open for 3% -> 3% of each run, Pallas kernels for 24% -> 26%
where the time goes in v3:
time: 291 us; the launch traced here: 286 us
  Pallas kernels  93.8 us (32%)
  waiting for transfers between devices  89 us (31%)
  starting transfers between devices  84.7 us (29%)
  other arithmetic  9.63 us (3%)
  local copies, waits for them, and re-layouts  7.13 us (2%)
    ppermute x31, waiting for transfers between devices, across(): return lax.ppermute(array, 'dp', flip[bit])  40.1 us
    ppermute x15, starting transfers between devices, along(): return lax.ppermute(array, 'tensor', [(i, i ^ r) for i in range(n_tensor)])  34.3 us
    ppermute x15, waiting for transfers between devices, along(): return lax.ppermute(array, 'tensor', [(i, i ^ r) for i in range(n_tensor)])  27 us
    ppermute x31, starting transfers between devices, across(): return lax.ppermute(array, 'dp', flip[bit])  26.9 us
    pallas_call x4, Pallas kernels, attention_backward(): pl.pallas_call(functools.partial(attention_backward_kernel, shard=shard,...  24.5 us
    ppermute x6, waiting for transfers between devices, rows_round(): lax.ppermute(down, 'tensor', [(i + 1, i) for i in range(n_tensor - k)])  21.9 us
    pallas_call x1, Pallas kernels, inner_half(): pl.pallas_call(inner_kernel, grid_spec=pltpu.PrefetchScalarGridSpec(num_s...  11.7 us
    pallas_call x2, Pallas kernels, ffn_back(): pl.pallas_call(functools.partial(ffn_back_kernel, final=final), grid=(cou...  10.8 us
  transfers between devices with their start and end apart: 60, of which 27 were waited for; matrix products, arithmetic and copies ran while one was open for 3% of the time, Pallas kernels for 26%

profile of v3, /device:TPU:0, one launch (start us, length us, event | category | flops | bytes accessed | tf_op | source)
XLA Modules:
  0.0 286.3 jit_solution(14760577604559196618)
XLA Ops:
  1.3 4.0 %shard_map.323 = (bf16[1,768,768]{2,1,0:T(8,128)(2,1)}, bf16[1,208,384]{2,1,0:T(8,128)(2,1)}) custom-call(s32[3]{0:T(128)} %pad_add_fusion.scalars, bf16[192,768]{1,0:T(8,128)(2,1)} %bitcast.77, bf16[192,768]{1,0:T(8,128)(2,1)} %bitcast.78, bf16[192,768]{1,0:T(8,128)(2,1)} %bitcast.79, bf16[192,768]{1,0:T(8,128)(2,1)} %refs_3_.1, bf16[192]{0:T(256)(128)(2,1)} %refs_4_.1, ...), custom_call_target="tpu_custom_call" | custom-call | flops 100000000 | tf_op jit(solution)/shard_map/pallas_call | solution.py:564
  5.3 3.1 %collective-permute-start = (bf16[1,208,384]{2,1,0:T(8,128)(2,1)}, bf16[1,208,384]{2,1,0:T(8,128)(2,1)S(1)}, u32[]{:S(2)}, u32[]{:S(2)}) collective-permute-start(bf16[1,208,384]{2,1,0:T(8,128)(2,1)} %get-tuple-element.170.b_ref.own_ref), channel_id=1, source_target_pairs={{0,1},{1,0},{2,3},{3,2},{4,5},{5,4},{6,7},{7,6},{8,9},{9,8},{10,11... | collective-permute-start | bytes 479240 | tf_op jit(solution)/shard_map/line attention weights/ppermute | solution.py:746
  8.4 2.6 collective-permute-start.1
  11.0 3.4 %shard_map.324 = (bf16[768,768]{1,0:T(8,128)(2,1)}, bf16[192,384]{1,0:T(8,128)(2,1)}, bf16[192,384]{1,0:T(8,128)(2,1)}) custom-call(s32[3]{0:T(128)} %pad_add_fusion.scalars, bf16[768,768]{1,0:T(8,128)(2,1)} %wi_hbm.1, bf16[768,768]{1,0:T(8,128)(2,1)} %own_ref.1), custom_call_target="tpu_custom_call" | custom-call | flops 100000000 | tf_op jit(solution)/shard_map/pallas_call | solution.py:591
  15.8 2.8 shard_map.325
  18.6 4.9 %collective-permute-done.1 = bf16[1,208,384]{2,1,0:T(8,128)(2,1)S(1)} collective-permute-done((bf16[1,208,384]{2,1,0:T(8,128)(2,1)}, bf16[1,208,384]{2,1,0:T(8,128)(2,1)S(1)}, u32[]{:S(2)}, u32[]{:S(2)}) %collective-permute-start.1) | collective-permute-done | bytes 159776 | tf_op jit(solution)/shard_map/line attention weights/ppermute | solution.py:746
  23.5 1.6 collective-permute-start.6
  25.1 1.5 collective-permute-start.7
  27.1 2.5 collective-permute-start.3
  30.6 3.2 %collective-permute-done.3 = bf16[192,384]{1,0:T(8,128)(2,1)S(1)} collective-permute-done((bf16[192,384]{1,0:T(8,128)(2,1)S(1)}, bf16[192,384]{1,0:T(8,128)(2,1)S(1)}, u32[]{:S(2)}, u32[]{:S(2)}) %collective-permute-start.3) | collective-permute-done | bytes 147488 | tf_op jit(solution)/shard_map/line inner weights/ppermute | solution.py:746
  33.8 2.1 collective-permute-start.5
  36.0 5.8 %collective-permute-done.4 = bf16[192,384]{1,0:T(8,128)(2,1)S(1)} collective-permute-done((bf16[192,384]{1,0:T(8,128)(2,1)S(1)}, bf16[192,384]{1,0:T(8,128)(2,1)S(1)}, u32[]{:S(2)}, u32[]{:S(2)}) %collective-permute-start.4) | collective-permute-done | bytes 147488 | tf_op jit(solution)/shard_map/line inner weights/ppermute | solution.py:746
  41.8 3.4 %collective-permute-done.7 = bf16[3,208,384]{2,1,0:T(8,128)(2,1)S(1)} collective-permute-done((bf16[3,208,384]{2,1,0:T(8,128)(2,1)S(1)}, bf16[3,208,384]{2,1,0:T(8,128)(2,1)S(1)}, u32[]{:S(2)}, u32[]{:S(2)}) %collective-permute-start.7) | collective-permute-done | bytes 479264 | tf_op jit(solution)/shard_map/plane attention weights/ppermute | solution.py:743
  45.7 1.3 collective-permute-start.13
  47.8 1.4 collective-permute-start.15
  49.5 3.9 %collective-permute-start.10 = (bf16[192,384]{1,0:T(8,128)(2,1)S(1)}, bf16[192,384]{1,0:T(8,128)(2,1)S(1)}, u32[]{:S(2)}, u32[]{:S(2)}) collective-permute-start(bf16[192,384]{1,0:T(8,128)(2,1)S(1)} %copy-done.44), channel_id=1, source_target_pairs={{0,1},{1,0},{2,3},{3,2},{4,5},{5,4},{6,7},{7,6},{8,9},{9,8},{10,11... | collective-permute-start | bytes 442376 | tf_op jit(solution)/shard_map/line outer weights/ppermute | solution.py:746
  54.6 6.0 %collective-permute-done.10 = bf16[192,384]{1,0:T(8,128)(2,1)S(1)} collective-permute-done((bf16[192,384]{1,0:T(8,128)(2,1)S(1)}, bf16[192,384]{1,0:T(8,128)(2,1)S(1)}, u32[]{:S(2)}, u32[]{:S(2)}) %collective-permute-start.10) | collective-permute-done | bytes 147488 | tf_op jit(solution)/shard_map/line outer weights/ppermute | solution.py:746
  61.9 1.4 shard_map.326.w_ref.wo_ref.w_hbm
  63.4 7.2 %shard_map.327 = (bf16[4,576,512]{2,1,0:T(8,128)(2,1)S(1)}, bf16[4,192,512]{2,1,0:T(8,128)(2,1)S(1)}, f32[4,8,512]{2,1,0:T(8,128)S(1)}) custom-call(s32[3]{0:T(128)S(1)} %copy-done.22, s32[4]{0:T(128)S(1)} %copy-done.23, bf16[2048,768]{1,0:T(8,128)(2,1)S(1)} %copy-done, ...), custom_call_target="tpu_custom_call", output_to_operand_aliasing={{0}: (7, {}), {1}: (8, {}), {2}: (9, {})} | custom-call | flops 450000000 | bytes 450000 | tf_op jit(solution)/shard_map/pallas_call | solution.py:146
  71.1 1.3 collective-permute-start.17
  73.3 1.4 collective-permute-start.19
  76.1 11.7 %shard_map.329 = (f32[512,768]{1,0:T(8,128)S(1)}, f32[512,1]{1,0:T(8,128)S(1)}, f32[512,768]{1,0:T(8,128)S(1)}, bf16[512,768]{1,0:T(8,128)(2,1)S(1)}, bf16[4,512...) custom-call(s32[3]{0:T(128)S(1)} %copy-done.22, bf16[4,192,512]{2,1,0:T(8,128)(2,1)S(1)} %get-tuple-element.180.o_ref.o_hbm, ...), custom_call_target="tpu_custom_call" | custom-call | flops 600000000 | bytes 1000000 | tf_op jit(solution)/shard_map/pallas_call | solution.py:332
  89.8 2.8 collective-permute-done.18
  92.6 1.6 collective-permute-done.19
  94.7 3.6 %collective-permute-done.20.far_ref = bf16[4,3,192,384]{3,2,1,0:T(8,128)(2,1)S(1)} collective-permute-done((bf16[4,3,192,384]{3,2,1,0:T(8,128)(2,1)S(1)}, bf16[4,3,192,384]{3,2,1,0:T(8,128)(2,1)S(1)}, u32[]{:S(2)}, u32[]{:S(2)}) %collective-permute-start.20) | collective-permute-done | bytes 1769504 | tf_op jit(solution)/shard_map/core outer weights/ppermute | solution.py:743
  99.5 5.1 %shard_map.331 = (bf16[512,768]{1,0:T(8,128)(2,1)S(1)}, f32[512,768]{1,0:T(8,128)S(1)}, f32[8,768]{1,0:T(8,128)S(1)}) custom-call(s32[3]{0:T(128)S(1)} %copy-done.22, bf16[4,512,768]{2,1,0:T(8,128)(2,1)S(1)} %get-tuple-element.187.act_ref.left_ref, bf16[4,768,768]{2,1,0:T(8,128)(2,1)S(1)} %shard_map.330.wu_ref, ...), custom_call_target="tpu_custom_call" | custom-call | flops 250000000 | bytes 700000 | tf_op jit(solution)/shard_map/pallas_call | solution.py:394
  104.7 5.1 %shard_map.332 = (bf16[4,4,192,384]{3,2,1,0:T(8,128)(2,1)S(1)}, bf16[4,4,192,384]{3,2,1,0:T(8,128)(2,1)S(1)}) custom-call(s32[3]{0:T(128)S(1)} %copy-done.22, bf16[4,512,768]{2,1,0:T(8,128)(2,1)S(1)} %get-tuple-element.187.act_ref.left_ref, f32[512,768]{1,0:T(8,128)S(1)} %get-tuple-element.196.right_ref.up_ref.start_ref), custom_call_target="tpu_custom_call" | custom-call | flops 300000000 | bytes 400000 | tf_op jit(solution)/shard_map/pallas_call | solution.py:501
  110.0 4.3 %collective-permute-start.22 = (bf16[512,768]{1,0:T(8,128)(2,1)S(1)}, bf16[512,768]{1,0:T(8,128)(2,1)}, u32[]{:S(2)}, u32[]{:S(2)}) collective-permute-start(bf16[512,768]{1,0:T(8,128)(2,1)S(1)} %get-tuple-element.279), channel_id=1, source_target_pairs={{0,1},{1,2},{2,3},{4,5},{5,6},{6,7},{8,9},{9,10},{10,11},{12,13},{... | collective-permute-start | bytes 2359304 | tf_op jit(solution)/shard_map/rows 1/ppermute | solution.py:760
  115.7 5.1 %shard_map.333 = (f32[512,768]{1,0:T(8,128)S(1)}, bf16[4,512,768]{2,1,0:T(8,128)(2,1)S(1)}, f32[4,1,768]{2,1,0:T(1,128)S(1)}) custom-call(f32[512,768]{1,0:T(8,128)S(1)} %get-tuple-element.196.right_ref.up_ref.start_ref, f32[512,768]{1,0:T(8,128)S(1)} %get-tuple-element.196.right_ref.up_ref.start_ref, bf16[4,512,768]{2,1,0:T(8,128)(2,1)S(1)} %get-tuple-element.197.slope_ref, ...), custom_call_target="tpu_custom_call" | custom-call | flops 300000000 | bytes 400000 | tf_op jit(solution)/shard_map/pallas_call | solution.py:462
  122.8 1.5 collective-permute-start.24
  124.8 5.7 %shard_map.335 = (f32[512,768]{1,0:T(8,128)S(1)}, bf16[4,512,768]{2,1,0:T(8,128)(2,1)S(1)}, f32[4,1,768]{2,1,0:T(1,128)S(1)}, bf16[512,768]{1,0:T(8,128)(2,1)S(1)}, f32[8,768]{1,0:T(8,128)S(1)}) custom-call(f32[512,768]{1,0:T(8,128)S(1)} %get-tuple-element.196.right_ref.up_ref.start_ref, ...), custom_call_target="tpu_custom_call", output_to_operand_aliasing={{1}: (8, {}), {2}: (9, {})} | custom-call | flops 300000000 | bytes 400000 | tf_op jit(solution)/shard_map/pallas_call | solution.py:462
  130.6 5.1 %shard_map.336 = (bf16[4,4,192,384]{3,2,1,0:T(8,128)(2,1)S(1)}, bf16[4,4,192,384]{3,2,1,0:T(8,128)(2,1)S(1)}) custom-call(s32[3]{0:T(128)S(1)} %copy-done.22, bf16[4,512,768]{2,1,0:T(8,128)(2,1)S(1)} %get-tuple-element.209.left_ref, bf16[512,768]{1,0:T(8,128)(2,1)S(1)} %copy-done.13), custom_call_target="tpu_custom_call" | custom-call | flops 300000000 | bytes 400000 | tf_op jit(solution)/shard_map/pallas_call | solution.py:501
  138.5 1.5 collective-permute-start.27
  140.6 5.9 %shard_map.338 = (f32[512,768]{1,0:T(8,128)S(1)}, bf16[4,4,208,384]{3,2,1,0:T(8,128)(2,1)S(1)}, bf16[4,4,208,384]{3,2,1,0:T(8,128)(2,1)S(1)}) custom-call(s32[3]{0:T(128)S(1)} %copy-done.22, s32[4]{0:T(128)S(1)} %copy-done.23, bf16[2048,768]{1,0:T(8,128)(2,1)S(1)} %copy-done, bf16[4,768,768]{2,1,0:T(8,128)(2,1)S(1)} %shard_map.326.w_ref.wo_ref.w_hbm, ...), custom_call_target="tpu_custom_call" | custom-call | flops 250000000 | bytes 250000 | tf_op jit(solution)/shard_map/pallas_call | solution.py:240
  147.7 5.9 %shard_map.340 = (f32[512,768]{1,0:T(8,128)S(1)}, bf16[4,4,208,384]{3,2,1,0:T(8,128)(2,1)S(1)}, bf16[4,4,208,384]{3,2,1,0:T(8,128)(2,1)S(1)}) custom-call(s32[3]{0:T(128)S(1)} %copy-done.22, s32[4]{0:T(128)S(1)} %copy-done.23, bf16[2048,768]{1,0:T(8,128)(2,1)S(1)} %copy-done, ...), custom_call_target="tpu_custom_call", output_to_operand_aliasing={{1}: (14, {}), {2}: (15, {})} | custom-call | flops 250000000 | bytes 250000 | tf_op jit(solution)/shard_map/pallas_call | solution.py:240
  156.0 1.5 collective-permute-start.31
  157.6 3.7 %collective-permute-done.30 = bf16[512,768]{1,0:T(8,128)(2,1)S(1)} collective-permute-done((bf16[512,768]{1,0:T(8,128)(2,1)}, bf16[512,768]{1,0:T(8,128)(2,1)S(1)}, u32[]{:S(2)}, u32[]{:S(2)}) %collective-permute-start.30) | collective-permute-done | bytes 786464 | tf_op jit(solution)/shard_map/rows 2/ppermute | solution.py:761
  162.0 1.3 collective-permute-start.35
  163.3 6.1 %shard_map.341 = (f32[512,768]{1,0:T(8,128)S(1)}, bf16[4,4,208,384]{3,2,1,0:T(8,128)(2,1)S(1)}, bf16[4,4,208,384]{3,2,1,0:T(8,128)(2,1)S(1)}) custom-call(s32[3]{0:T(128)S(1)} %copy-done.22, s32[4]{0:T(128)S(1)} %copy-done.23, bf16[2048,768]{1,0:T(8,128)(2,1)S(1)} %copy-done, ...), custom_call_target="tpu_custom_call", output_to_operand_aliasing={{1}: (14, {}), {2}: (15, {})} | custom-call | flops 250000000 | bytes 250000 | tf_op jit(solution)/shard_map/pallas_call | solution.py:240
  169.6 4.6 %collective-permute-start.33 = (bf16[2,192,384]{2,1,0:T(8,128)(2,1)S(1)}, bf16[2,192,384]{2,1,0:T(8,128)(2,1)S(1)}, u32[]{:S(2)}, u32[]{:S(2)}) collective-permute-start(bf16[2,192,384]{2,1,0:T(8,128)(2,1)S(1)} %add_convert_fusion.2), channel_id=1, source_target_pairs={{0,1},{3,2},{4,5},{7,6},{8,9},{11,10},{12,13},{15,14},{16,17},{19,... | collective-permute-start | bytes 884744 | tf_op jit(solution)/shard_map/line ends outer grad/ppermute | solution.py:788
  174.4 6.7 %shard_map.343 = (bf16[512,768]{1,0:T(8,128)(2,1)}, bf16[4,4,208,384]{3,2,1,0:T(8,128)(2,1)S(1)}, bf16[4,4,208,384]{3,2,1,0:T(8,128)(2,1)S(1)}) custom-call(s32[3]{0:T(128)S(1)} %copy-done.22, s32[4]{0:T(128)S(1)} %copy-done.23, bf16[2048,768]{1,0:T(8,128)(2,1)S(1)} %copy-done, ...), custom_call_target="tpu_custom_call", output_to_operand_aliasing={{1}: (14, {}), {2}: (15, {})} | custom-call | flops 250000000 | bytes 250000 | tf_op jit(solution)/shard_map/pallas_call | solution.py:240
  181.2 1.9 collective-permute-done.35
  183.1 1.5 collective-permute-start.39
  185.1 2.4 collective-permute-start.36
  188.8 2.3 shard_map.344
  191.1 7.8 %collective-permute-done.39 = bf16[4,192,384]{2,1,0:T(8,128)(2,1)} collective-permute-done((bf16[4,192,384]{2,1,0:T(8,128)(2,1)S(1)}, bf16[4,192,384]{2,1,0:T(8,128)(2,1)}, u32[]{:S(2)}, u32[]{:S(2)}) %collective-permute-start.39) | collective-permute-done | bytes 589856 | tf_op jit(solution)/shard_map/plane two inner grad/ppermute | solution.py:743
  202.7 1.4 collective-permute-start.41
  204.1 1.4 convert_add_fusion.2
  205.5 3.4 %collective-permute-done.37 = bf16[512,768]{1,0:T(8,128)(2,1)} collective-permute-done((bf16[512,768]{1,0:T(8,128)(2,1)}, bf16[512,768]{1,0:T(8,128)(2,1)}, u32[]{:S(2)}, u32[]{:S(2)}) %collective-permute-start.37) | collective-permute-done | bytes 786464 | tf_op jit(solution)/shard_map/grad rows 1/ppermute | solution.py:761
  211.6 5.2 %collective-permute-start.44 = (bf16[2,192,384]{2,1,0:T(8,128)(2,1)S(1)}, bf16[2,192,384]{2,1,0:T(8,128)(2,1)S(1)}, u32[]{:S(2)}, u32[]{:S(2)}) collective-permute-start(bf16[2,192,384]{2,1,0:T(8,128)(2,1)S(1)} %get-tuple-element.282), channel_id=1, source_target_pairs={{0,1},{1,0},{2,3},{3,2},{4,5},{5,4},{6,7},{7,6},{8,9},{9,8},{10,11... | collective-permute-start | bytes 884744 | tf_op jit(solution)/shard_map/line one inner grad/ppermute | solution.py:746
  217.5 1.5 collective-permute-start.48
  222.1 1.4 select_dynamic-update-slice_fusion.3
  225.4 5.8 %collective-permute-start.53 = (bf16[208,384]{1,0:T(8,128)(2,1)S(1)}, bf16[208,384]{1,0:T(8,128)(2,1)S(1)}, u32[]{:S(2)}, u32[]{:S(2)}) collective-permute-start(bf16[208,384]{1,0:T(8,128)(2,1)S(1)} %get-tuple-element.325), channel_id=1, source_target_pairs={{0,1},{1,0},{2,3},{3,2},{4,5},{5,4},{6,7},{7,6},{8,9},{9,8},{10,11... | collective-permute-start | bytes 479240 | tf_op jit(solution)/shard_map/line attention grad/ppermute | solution.py:746
  231.3 2.4 collective-permute-start.55
  233.7 12.7 %collective-permute-done.48 = bf16[512,768]{1,0:T(8,128)(2,1)S(1)} collective-permute-done((bf16[512,768]{1,0:T(8,128)(2,1)}, bf16[512,768]{1,0:T(8,128)(2,1)S(1)}, u32[]{:S(2)}, u32[]{:S(2)}) %collective-permute-start.48) | collective-permute-done | bytes 786464 | tf_op jit(solution)/shard_map/grad rows 2/ppermute | solution.py:761
  246.5 2.1 collective-permute-start.51
  250.8 1.5 collective-permute-done.54
  253.6 4.1 %collective-permute-done.51 = bf16[192,384]{1,0:T(8,128)(2,1)S(1)} collective-permute-done((bf16[192,384]{1,0:T(8,128)(2,1)S(1)}, bf16[192,384]{1,0:T(8,128)(2,1)S(1)}, u32[]{:S(2)}, u32[]{:S(2)}) %collective-permute-start.51) | collective-permute-done | bytes 147488 | tf_op jit(solution)/shard_map/line two inner grad/ppermute | solution.py:746
  258.0 1.6 collective-permute-start.56
  260.2 1.3 collective-permute-start.58
  261.6 9.1 %collective-permute-done.56 = bf16[592,384]{1,0:T(8,128)(2,1)S(1)} collective-permute-done((bf16[592,384]{1,0:T(8,128)(2,1)S(1)}, bf16[592,384]{1,0:T(8,128)(2,1)S(1)}, u32[]{:S(2)}, u32[]{:S(2)}) %collective-permute-start.56) | collective-permute-done | bytes 454688 | tf_op jit(solution)/shard_map/plane result/ppermute | solution.py:743
  270.7 6.8 %collective-permute-done.57 = bf16[592,384]{1,0:T(8,128)(2,1)S(1)} collective-permute-done((bf16[592,384]{1,0:T(8,128)(2,1)S(1)}, bf16[592,384]{1,0:T(8,128)(2,1)S(1)}, u32[]{:S(2)}, u32[]{:S(2)}) %collective-permute-start.57) | collective-permute-done | bytes 454688 | tf_op jit(solution)/shard_map/plane result/ppermute | solution.py:743
  279.8 1.4 select_dynamic-update-slice_fusion
  281.6 4.4 %shard_map.346 = (f32[192,768]{1,0:T(8,128)}, f32[192,768]{1,0:T(8,128)}, f32[192,768]{1,0:T(8,128)}, f32[192,768]{1,0:T(8,128)}, f32[768,768]{1,0:T(8,128)}, /*...) custom-call(s32[3]{0:T(128)S(1)} %copy-done.22, ...), custom_call_target="tpu_custom_call" | custom-call | flops 100000000 | tf_op jit(solution)/shard_map/pallas_call | solution.py:667
  (212 shorter events, 46.9 us)
Async XLA Ops:
  5.3 13.2 %collective-permute-start = (bf16[1,208,384]{2,1,0:T(8,128)(2,1)}, bf16[1,208,384]{2,1,0:T(8,128)(2,1)S(1)}, u32[]{:S(2)}, u32[]{:S(2)}) collective-permute-start(bf16[1,208,384]{2,1,0:T(8,128)(2,1)} %get-tuple-element.170.b_ref.own_ref), channel_id=1, source_target_pairs={{0,1},{1,0},{2,3},{3,2},{4,5},{5,4},{6,7},{7,6},{8,9},{9,8},{10,11... | collective-permute-start | bytes 479240 | tf_op jit(solution)/shard_map/line attention weights/ppermute | solution.py:746
  8.4 15.0 %collective-permute-start.1 = (bf16[1,208,384]{2,1,0:T(8,128)(2,1)}, bf16[1,208,384]{2,1,0:T(8,128)(2,1)S(1)}, u32[]{:S(2)}, u32[]{:S(2)}) collective-permute-start(bf16[1,208,384]{2,1,0:T(8,128)(2,1)} %get-tuple-element.170.b_ref.own_ref), channel_id=1, source_target_pairs={{0,2},{1,3},{2,0},{3,1},{4,6},{5,7},{6,4},{7,5},{8,10},{9,11},{10,... | collective-permute-start | bytes 479240 | tf_op jit(solution)/shard_map/line attention weights/ppermute | solution.py:746
  11.0 12.4 %collective-permute-start.2 = (bf16[1,208,384]{2,1,0:T(8,128)(2,1)}, bf16[1,208,384]{2,1,0:T(8,128)(2,1)S(1)}, u32[]{:S(2)}, u32[]{:S(2)}) collective-permute-start(bf16[1,208,384]{2,1,0:T(8,128)(2,1)} %get-tuple-element.170.b_ref.own_ref), channel_id=1, source_target_pairs={{0,3},{1,2},{2,1},{3,0},{4,7},{5,6},{6,5},{7,4},{8,11},{9,10},{10,... | collective-permute-start | bytes 479240 | tf_op jit(solution)/shard_map/line attention weights/ppermute | solution.py:746
  23.5 18.3 %collective-permute-start.6 = (bf16[3,208,384]{2,1,0:T(8,128)(2,1)S(1)}, bf16[3,208,384]{2,1,0:T(8,128)(2,1)S(1)}, u32[]{:S(2)}, u32[]{:S(2)}) collective-permute-start(bf16[3,208,384]{2,1,0:T(8,128)(2,1)S(1)} %constant_dynamic-update-slice_fusion.b_ref.others_ref), channel_id=1, source_target_pairs={{0,8},{4,12},{8,0},{12,4},{16,24},{20,28},{24,16},{28,20},{1,9},{5... | collective-permute-start | bytes 1437704 | tf_op jit(solution)/shard_map/plane attention weights/ppermute | solution.py:743
  25.1 20.2 %collective-permute-start.7 = (bf16[3,208,384]{2,1,0:T(8,128)(2,1)S(1)}, bf16[3,208,384]{2,1,0:T(8,128)(2,1)S(1)}, u32[]{:S(2)}, u32[]{:S(2)}) collective-permute-start(bf16[3,208,384]{2,1,0:T(8,128)(2,1)S(1)} %constant_dynamic-update-slice_fusion.b_ref.others_ref), channel_id=1, source_target_pairs={{0,16},{4,20},{8,24},{12,28},{16,0},{20,4},{24,8},{28,12},{1,17},{... | collective-permute-start | bytes 1437704 | tf_op jit(solution)/shard_map/plane attention weights/ppermute | solution.py:743
  26.6 18.7 %collective-permute-start.8 = (bf16[3,208,384]{2,1,0:T(8,128)(2,1)S(1)}, bf16[3,208,384]{2,1,0:T(8,128)(2,1)S(1)}, u32[]{:S(2)}, u32[]{:S(2)}) collective-permute-start(bf16[3,208,384]{2,1,0:T(8,128)(2,1)S(1)} %constant_dynamic-update-slice_fusion.b_ref.others_ref), channel_id=1, source_target_pairs={{0,24},{4,28},{8,16},{12,20},{16,8},{20,12},{24,0},{28,4},{1,25},{... | collective-permute-start | bytes 1437704 | tf_op jit(solution)/shard_map/plane attention weights/ppermute | solution.py:743
  27.1 6.8 %collective-permute-start.3 = (bf16[192,384]{1,0:T(8,128)(2,1)S(1)}, bf16[192,384]{1,0:T(8,128)(2,1)S(1)}, u32[]{:S(2)}, u32[]{:S(2)}) collective-permute-start(bf16[192,384]{1,0:T(8,128)(2,1)S(1)} %copy-done.45), channel_id=1, source_target_pairs={{0,1},{1,0},{2,3},{3,2},{4,5},{5,4},{6,7},{7,6},{8,9},{9,8},{10,11... | collective-permute-start | bytes 442376 | tf_op jit(solution)/shard_map/line inner weights/ppermute | solution.py:746
  29.6 12.2 %collective-permute-start.4 = (bf16[192,384]{1,0:T(8,128)(2,1)S(1)}, bf16[192,384]{1,0:T(8,128)(2,1)S(1)}, u32[]{:S(2)}, u32[]{:S(2)}) collective-permute-start(bf16[192,384]{1,0:T(8,128)(2,1)S(1)} %copy-done.45), channel_id=1, source_target_pairs={{0,2},{1,3},{2,0},{3,1},{4,6},{5,7},{6,4},{7,5},{8,10},{9,11},{10,... | collective-permute-start | bytes 442376 | tf_op jit(solution)/shard_map/line inner weights/ppermute | solution.py:746
  33.8 8.0 %collective-permute-start.5 = (bf16[192,384]{1,0:T(8,128)(2,1)S(1)}, bf16[192,384]{1,0:T(8,128)(2,1)S(1)}, u32[]{:S(2)}, u32[]{:S(2)}) collective-permute-start(bf16[192,384]{1,0:T(8,128)(2,1)S(1)} %copy-done.45), channel_id=1, source_target_pairs={{0,3},{1,2},{2,1},{3,0},{4,7},{5,6},{6,5},{7,4},{8,11},{9,10},{10,... | collective-permute-start | bytes 442376 | tf_op jit(solution)/shard_map/line inner weights/ppermute | solution.py:746
  45.2 16.7 %copy-start.5 = (bf16[1,768,768]{2,1,0:T(8,128)(2,1)S(1)}, bf16[1,768,768]{2,1,0:T(8,128)(2,1)}, u32[]{:S(2)}) copy-start(bf16[1,768,768]{2,1,0:T(8,128)(2,1)} %get-tuple-element.171.w_ref) | copy-start | bytes 3538948
  45.5 4.0 %collective-permute-start.9 = (bf16[4,3,208,384]{3,2,1,0:T(8,128)(2,1)S(1)}, bf16[4,3,208,384]{3,2,1,0:T(8,128)(2,1)S(1)}, u32[]{:S(2)}, u32[]{:S(2)}) collective-permute-start(bf16[4,3,208,384]{3,2,1,0:T(8,128)(2,1)S(1)} %pad_maximum_fusion.near_ref), channel_id=1, source_target_pairs={{0,4},{4,0},{8,12},{12,8},{16,20},{20,16},{24,28},{28,24},{1,5},{5... | collective-permute-start | bytes 5750792 | tf_op jit(solution)/shard_map/core attention weights/ppermute | solution.py:743
  45.7 25.0 %collective-permute-start.13 = (bf16[3,192,384]{2,1,0:T(8,128)(2,1)S(1)}, bf16[3,192,384]{2,1,0:T(8,128)(2,1)S(1)}, u32[]{:S(2)}, u32[]{:S(2)}) collective-permute-start(bf16[3,192,384]{2,1,0:T(8,128)(2,1)S(1)} %pad_maximum_fusion.5), channel_id=1, source_target_pairs={{0,8},{4,12},{8,0},{12,4},{16,24},{20,28},{24,16},{28,20},{1,9},{5... | collective-permute-start | bytes 1327112 | tf_op jit(solution)/shard_map/plane inner weights/ppermute | solution.py:743
  47.0 23.7 %collective-permute-start.14 = (bf16[3,192,384]{2,1,0:T(8,128)(2,1)S(1)}, bf16[3,192,384]{2,1,0:T(8,128)(2,1)S(1)}, u32[]{:S(2)}, u32[]{:S(2)}) collective-permute-start(bf16[3,192,384]{2,1,0:T(8,128)(2,1)S(1)} %pad_maximum_fusion.5), channel_id=1, source_target_pairs={{0,16},{4,20},{8,24},{12,28},{16,0},{20,4},{24,8},{28,12},{1,17},{... | collective-permute-start | bytes 1327112 | tf_op jit(solution)/shard_map/plane inner weights/ppermute | solution.py:743
  47.8 22.9 %collective-permute-start.15 = (bf16[3,192,384]{2,1,0:T(8,128)(2,1)S(1)}, bf16[3,192,384]{2,1,0:T(8,128)(2,1)S(1)}, u32[]{:S(2)}, u32[]{:S(2)}) collective-permute-start(bf16[3,192,384]{2,1,0:T(8,128)(2,1)S(1)} %pad_maximum_fusion.5), channel_id=1, source_target_pairs={{0,24},{4,28},{8,16},{12,20},{16,8},{20,12},{24,0},{28,4},{1,25},{... | collective-permute-start | bytes 1327112 | tf_op jit(solution)/shard_map/plane inner weights/ppermute | solution.py:743
  49.5 11.1 %collective-permute-start.10 = (bf16[192,384]{1,0:T(8,128)(2,1)S(1)}, bf16[192,384]{1,0:T(8,128)(2,1)S(1)}, u32[]{:S(2)}, u32[]{:S(2)}) collective-permute-start(bf16[192,384]{1,0:T(8,128)(2,1)S(1)} %copy-done.44), channel_id=1, source_target_pairs={{0,1},{1,0},{2,3},{3,2},{4,5},{5,4},{6,7},{7,6},{8,9},{9,8},{10,11... | collective-permute-start | bytes 442376 | tf_op jit(solution)/shard_map/line outer weights/ppermute | solution.py:746
  53.4 17.2 %collective-permute-start.11 = (bf16[192,384]{1,0:T(8,128)(2,1)S(1)}, bf16[192,384]{1,0:T(8,128)(2,1)S(1)}, u32[]{:S(2)}, u32[]{:S(2)}) collective-permute-start(bf16[192,384]{1,0:T(8,128)(2,1)S(1)} %copy-done.44), channel_id=1, source_target_pairs={{0,2},{1,3},{2,0},{3,1},{4,6},{5,7},{6,4},{7,5},{8,10},{9,11},{10,... | collective-permute-start | bytes 442376 | tf_op jit(solution)/shard_map/line outer weights/ppermute | solution.py:746
  60.6 10.0 %collective-permute-start.12 = (bf16[192,384]{1,0:T(8,128)(2,1)S(1)}, bf16[192,384]{1,0:T(8,128)(2,1)S(1)}, u32[]{:S(2)}, u32[]{:S(2)}) collective-permute-start(bf16[192,384]{1,0:T(8,128)(2,1)S(1)} %copy-done.44), channel_id=1, source_target_pairs={{0,3},{1,2},{2,1},{3,0},{4,7},{5,6},{6,5},{7,4},{8,11},{9,10},{10,... | collective-permute-start | bytes 442376 | tf_op jit(solution)/shard_map/line outer weights/ppermute | solution.py:746
  71.0 3.8 %collective-permute-start.16 = (bf16[4,3,192,384]{3,2,1,0:T(8,128)(2,1)S(1)}, bf16[4,3,192,384]{3,2,1,0:T(8,128)(2,1)S(1)}, u32[]{:S(2)}, u32[]{:S(2)}) collective-permute-start(bf16[4,3,192,384]{3,2,1,0:T(8,128)(2,1)S(1)} %pad_maximum_fusion.2.near_ref), channel_id=1, source_target_pairs={{0,4},{4,0},{8,12},{12,8},{16,20},{20,16},{24,28},{28,24},{1,5},{5... | collective-permute-start | bytes 5308424 | tf_op jit(solution)/shard_map/core inner weights/ppermute | solution.py:743
  71.1 18.7 %collective-permute-start.17 = (bf16[3,192,384]{2,1,0:T(8,128)(2,1)S(1)}, bf16[3,192,384]{2,1,0:T(8,128)(2,1)S(1)}, u32[]{:S(2)}, u32[]{:S(2)}) collective-permute-start(bf16[3,192,384]{2,1,0:T(8,128)(2,1)S(1)} %pad_maximum_fusion.6), channel_id=1, source_target_pairs={{0,8},{4,12},{8,0},{12,4},{16,24},{20,28},{24,16},{28,20},{1,9},{5... | collective-permute-start | bytes 1327112 | tf_op jit(solution)/shard_map/plane outer weights/ppermute | solution.py:743
  72.4 20.1 %collective-permute-start.18 = (bf16[3,192,384]{2,1,0:T(8,128)(2,1)S(1)}, bf16[3,192,384]{2,1,0:T(8,128)(2,1)S(1)}, u32[]{:S(2)}, u32[]{:S(2)}) collective-permute-start(bf16[3,192,384]{2,1,0:T(8,128)(2,1)S(1)} %pad_maximum_fusion.6), channel_id=1, source_target_pairs={{0,16},{4,20},{8,24},{12,28},{16,0},{20,4},{24,8},{28,12},{1,17},{... | collective-permute-start | bytes 1327112 | tf_op jit(solution)/shard_map/plane outer weights/ppermute | solution.py:743
  73.3 20.9 %collective-permute-start.19 = (bf16[3,192,384]{2,1,0:T(8,128)(2,1)S(1)}, bf16[3,192,384]{2,1,0:T(8,128)(2,1)S(1)}, u32[]{:S(2)}, u32[]{:S(2)}) collective-permute-start(bf16[3,192,384]{2,1,0:T(8,128)(2,1)S(1)} %pad_maximum_fusion.6), channel_id=1, source_target_pairs={{0,24},{4,28},{8,16},{12,20},{16,8},{20,12},{24,0},{28,4},{1,25},{... | collective-permute-start | bytes 1327112 | tf_op jit(solution)/shard_map/plane outer weights/ppermute | solution.py:743
  89.8 25.9 %copy-start.1 = (bf16[4,512,768]{2,1,0:T(8,128)(2,1)}, bf16[4,512,768]{2,1,0:T(8,128)(2,1)S(1)}, u32[]{:S(2)}) copy-start(bf16[4,512,768]{2,1,0:T(8,128)(2,1)S(1)} %get-tuple-element.197.slope_ref) | copy-start | bytes 9437188
  94.5 3.8 %collective-permute-start.20 = (bf16[4,3,192,384]{3,2,1,0:T(8,128)(2,1)S(1)}, bf16[4,3,192,384]{3,2,1,0:T(8,128)(2,1)S(1)}, u32[]{:S(2)}, u32[]{:S(2)}) collective-permute-start(bf16[4,3,192,384]{3,2,1,0:T(8,128)(2,1)S(1)} %pad_maximum_fusion.3.near_ref), channel_id=1, source_target_pairs={{0,4},{4,0},{8,12},{12,8},{16,20},{20,16},{24,28},{28,24},{1,5},{5... | collective-permute-start | bytes 5308424 | tf_op jit(solution)/shard_map/core outer weights/ppermute | solution.py:743
  109.8 10.9 %collective-permute-start.21 = (bf16[4,4,192,384]{3,2,1,0:T(8,128)(2,1)S(1)}, bf16[4,4,192,384]{3,2,1,0:T(8,128)(2,1)S(1)}, u32[]{:S(2)}, u32[]{:S(2)}) collective-permute-start(bf16[4,4,192,384]{3,2,1,0:T(8,128)(2,1)S(1)} %get-tuple-element.199), channel_id=1, source_target_pairs={{0,4},{4,0},{8,12},{12,8},{16,20},{20,16},{24,28},{28,24},{1,5},{5... | collective-permute-start | bytes 7077896 | tf_op jit(solution)/shard_map/core outer grad/ppermute | solution.py:743
  110.0 25.7 %collective-permute-start.22 = (bf16[512,768]{1,0:T(8,128)(2,1)S(1)}, bf16[512,768]{1,0:T(8,128)(2,1)}, u32[]{:S(2)}, u32[]{:S(2)}) collective-permute-start(bf16[512,768]{1,0:T(8,128)(2,1)S(1)} %get-tuple-element.279), channel_id=1, source_target_pairs={{0,1},{1,2},{2,3},{4,5},{5,6},{6,7},{8,9},{9,10},{10,11},{12,13},{... | collective-permute-start | bytes 2359304 | tf_op jit(solution)/shard_map/rows 1/ppermute | solution.py:760
  114.4 21.5 %collective-permute-start.23 = (bf16[512,768]{1,0:T(8,128)(2,1)S(1)}, bf16[512,768]{1,0:T(8,128)(2,1)}, u32[]{:S(2)}, u32[]{:S(2)}) collective-permute-start(bf16[512,768]{1,0:T(8,128)(2,1)S(1)} %get-tuple-element.279), channel_id=1, source_target_pairs={{1,0},{2,1},{3,2},{5,4},{6,5},{7,6},{9,8},{10,9},{11,10},{13,12},{... | collective-permute-start | bytes 2359304 | tf_op jit(solution)/shard_map/rows 1/ppermute | solution.py:761
  122.8 13.1 %collective-permute-start.24 = (bf16[2,192,384]{2,1,0:T(8,128)(2,1)S(1)}, bf16[2,192,384]{2,1,0:T(8,128)(2,1)S(1)}, u32[]{:S(2)}, u32[]{:S(2)}) collective-permute-start(bf16[2,192,384]{2,1,0:T(8,128)(2,1)S(1)} %get-tuple-element.213), channel_id=1, source_target_pairs={{0,16},{4,20},{8,24},{12,28},{16,0},{20,4},{24,8},{28,12},{1,17},{... | collective-permute-start | bytes 884744 | tf_op jit(solution)/shard_map/plane one outer grad/ppermute | solution.py:743
  124.3 11.6 %collective-permute-start.25 = (bf16[2,192,384]{2,1,0:T(8,128)(2,1)S(1)}, bf16[2,192,384]{2,1,0:T(8,128)(2,1)S(1)}, u32[]{:S(2)}, u32[]{:S(2)}) collective-permute-start(bf16[2,192,384]{2,1,0:T(8,128)(2,1)S(1)} %get-tuple-element.214), channel_id=1, source_target_pairs={{0,8},{4,12},{8,0},{12,4},{16,24},{20,28},{24,16},{28,20},{1,9},{5... | collective-permute-start | bytes 884744 | tf_op jit(solution)/shard_map/plane one outer grad/ppermute | solution.py:743
  135.9 10.6 %collective-permute-start.26 = (bf16[4,4,192,384]{3,2,1,0:T(8,128)(2,1)S(1)}, bf16[4,4,192,384]{3,2,1,0:T(8,128)(2,1)S(1)}, u32[]{:S(2)}, u32[]{:S(2)}) collective-permute-start(bf16[4,4,192,384]{3,2,1,0:T(8,128)(2,1)S(1)} %get-tuple-element.226), channel_id=1, source_target_pairs={{0,4},{4,0},{8,12},{12,8},{16,20},{20,16},{24,28},{28,24},{1,5},{5... | collective-permute-start | bytes 7077896 | tf_op jit(solution)/shard_map/core inner grad/ppermute | solution.py:743
  135.9 21.7 %collective-permute-start.29 = (bf16[512,768]{1,0:T(8,128)(2,1)}, bf16[512,768]{1,0:T(8,128)(2,1)S(1)}, u32[]{:S(2)}, u32[]{:S(2)}) collective-permute-start(bf16[512,768]{1,0:T(8,128)(2,1)} %collective-permute-done.22), channel_id=1, source_target_pairs={{1,2},{2,3},{5,6},{6,7},{9,10},{10,11},{13,14},{14,15},{17,18},{18... | collective-permute-start | bytes 2359304 | tf_op jit(solution)/shard_map/rows 2/ppermute | solution.py:760
  136.6 24.7 %collective-permute-start.30 = (bf16[512,768]{1,0:T(8,128)(2,1)}, bf16[512,768]{1,0:T(8,128)(2,1)S(1)}, u32[]{:S(2)}, u32[]{:S(2)}) collective-permute-start(bf16[512,768]{1,0:T(8,128)(2,1)} %collective-permute-done.23), channel_id=1, source_target_pairs={{1,0},{2,1},{5,4},{6,5},{9,8},{10,9},{13,12},{14,13},{17,16},{18,1... | collective-permute-start | bytes 2359304 | tf_op jit(solution)/shard_map/rows 2/ppermute | solution.py:761
  138.5 15.8 %collective-permute-start.27 = (bf16[4,192,384]{2,1,0:T(8,128)(2,1)S(1)}, bf16[4,192,384]{2,1,0:T(8,128)(2,1)S(1)}, u32[]{:S(2)}, u32[]{:S(2)}) collective-permute-start(bf16[4,192,384]{2,1,0:T(8,128)(2,1)S(1)} %get-tuple-element.220), channel_id=1, source_target_pairs={{0,8},{4,12},{8,0},{12,4},{16,24},{20,28},{24,16},{28,20},{1,9},{5... | collective-permute-start | bytes 1769480 | tf_op jit(solution)/shard_map/plane two outer grad/ppermute | solution.py:743
  140.0 15.4 %collective-permute-start.28 = (bf16[4,192,384]{2,1,0:T(8,128)(2,1)S(1)}, bf16[4,192,384]{2,1,0:T(8,128)(2,1)S(1)}, u32[]{:S(2)}, u32[]{:S(2)}) collective-permute-start(bf16[4,192,384]{2,1,0:T(8,128)(2,1)S(1)} %get-tuple-element.235), channel_id=1, source_target_pairs={{0,16},{4,20},{8,24},{12,28},{16,0},{20,4},{24,8},{28,12},{1,17},{... | collective-permute-start | bytes 1769480 | tf_op jit(solution)/shard_map/plane two outer grad/ppermute | solution.py:743
  155.5 14.0 %collective-permute-start.32 = (bf16[2,192,384]{2,1,0:T(8,128)(2,1)S(1)}, bf16[2,192,384]{2,1,0:T(8,128)(2,1)S(1)}, u32[]{:S(2)}, u32[]{:S(2)}) collective-permute-start(bf16[2,192,384]{2,1,0:T(8,128)(2,1)S(1)} %get-tuple-element.248), channel_id=1, source_target_pairs={{0,8},{4,12},{8,0},{12,4},{16,24},{20,28},{24,16},{28,20},{1,9},{5... | collective-permute-start | bytes 884744 | tf_op jit(solution)/shard_map/plane one inner grad/ppermute | solution.py:743
  156.0 13.4 %collective-permute-start.31 = (bf16[2,192,384]{2,1,0:T(8,128)(2,1)S(1)}, bf16[2,192,384]{2,1,0:T(8,128)(2,1)S(1)}, u32[]{:S(2)}, u32[]{:S(2)}) collective-permute-start(bf16[2,192,384]{2,1,0:T(8,128)(2,1)S(1)} %get-tuple-element.246), channel_id=1, source_target_pairs={{0,16},{4,20},{8,24},{12,28},{16,0},{20,4},{24,8},{28,12},{1,17},{... | collective-permute-start | bytes 884744 | tf_op jit(solution)/shard_map/plane one inner grad/ppermute | solution.py:743
  161.3 19.8 %collective-permute-start.34 = (bf16[512,768]{1,0:T(8,128)(2,1)S(1)}, bf16[512,768]{1,0:T(8,128)(2,1)S(1)}, u32[]{:S(2)}, u32[]{:S(2)}) collective-permute-start(bf16[512,768]{1,0:T(8,128)(2,1)S(1)} %collective-permute-done.29), channel_id=1, source_target_pairs={{2,3},{6,7},{10,11},{14,15},{18,19},{22,23},{26,27},{30,31}} | collective-permute-start | bytes 2359304 | tf_op jit(solution)/shard_map/rows 3/ppermute | solution.py:760
  162.0 21.0 %collective-permute-start.35 = (bf16[512,768]{1,0:T(8,128)(2,1)S(1)}, bf16[512,768]{1,0:T(8,128)(2,1)S(1)}, u32[]{:S(2)}, u32[]{:S(2)}) collective-permute-start(bf16[512,768]{1,0:T(8,128)(2,1)S(1)} %collective-permute-done.30), channel_id=1, source_target_pairs={{1,0},{5,4},{9,8},{13,12},{17,16},{21,20},{25,24},{29,28}} | collective-permute-start | bytes 2359304 | tf_op jit(solution)/shard_map/rows 3/ppermute | solution.py:761
  169.6 11.5 %collective-permute-start.33 = (bf16[2,192,384]{2,1,0:T(8,128)(2,1)S(1)}, bf16[2,192,384]{2,1,0:T(8,128)(2,1)S(1)}, u32[]{:S(2)}, u32[]{:S(2)}) collective-permute-start(bf16[2,192,384]{2,1,0:T(8,128)(2,1)S(1)} %add_convert_fusion.2), channel_id=1, source_target_pairs={{0,1},{3,2},{4,5},{7,6},{8,9},{11,10},{12,13},{15,14},{16,17},{19,... | collective-permute-start | bytes 884744 | tf_op jit(solution)/shard_map/line ends outer grad/ppermute | solution.py:788
  183.1 5.7 %collective-permute-start.38 = (bf16[4,4,208,384]{3,2,1,0:T(8,128)(2,1)S(1)}, bf16[4,4,208,384]{3,2,1,0:T(8,128)(2,1)S(1)}, u32[]{:S(2)}, u32[]{:S(2)}) collective-permute-start(bf16[4,4,208,384]{3,2,1,0:T(8,128)(2,1)S(1)} %get-tuple-element.266), channel_id=1, source_target_pairs={{0,4},{4,0},{8,12},{12,8},{16,20},{20,16},{24,28},{28,24},{1,5},{5... | collective-permute-start | bytes 7667720 | tf_op jit(solution)/shard_map/core attention grad/ppermute | solution.py:743
  183.1 15.8 %collective-permute-start.39 = (bf16[4,192,384]{2,1,0:T(8,128)(2,1)S(1)}, bf16[4,192,384]{2,1,0:T(8,128)(2,1)}, u32[]{:S(2)}, u32[]{:S(2)}) collective-permute-start(bf16[4,192,384]{2,1,0:T(8,128)(2,1)S(1)} %get-tuple-element.254), channel_id=1, source_target_pairs={{0,8},{4,12},{8,0},{12,4},{16,24},{20,28},{24,16},{28,20},{1,9},{5... | collective-permute-start | bytes 1769480 | tf_op jit(solution)/shard_map/plane two inner grad/ppermute | solution.py:743
  184.6 19.5 %copy-start.19 = (bf16[4,192,384]{2,1,0:T(8,128)(2,1)S(1)}, bf16[4,192,384]{2,1,0:T(8,128)(2,1)}, u32[]{:S(2)}) copy-start(bf16[4,192,384]{2,1,0:T(8,128)(2,1)} %copy-done.18) | copy-start | bytes 1769476
  184.6 15.6 %collective-permute-start.40 = (bf16[4,192,384]{2,1,0:T(8,128)(2,1)S(1)}, bf16[4,192,384]{2,1,0:T(8,128)(2,1)}, u32[]{:S(2)}, u32[]{:S(2)}) collective-permute-start(bf16[4,192,384]{2,1,0:T(8,128)(2,1)S(1)} %get-tuple-element.269), channel_id=1, source_target_pairs={{0,16},{4,20},{8,24},{12,28},{16,0},{20,4},{24,8},{28,12},{1,17},{... | collective-permute-start | bytes 1769480 | tf_op jit(solution)/shard_map/plane two inner grad/ppermute | solution.py:743
  185.1 20.4 %collective-permute-start.36 = (bf16[512,768]{1,0:T(8,128)(2,1)}, bf16[512,768]{1,0:T(8,128)(2,1)}, u32[]{:S(2)}, u32[]{:S(2)}) collective-permute-start(bf16[512,768]{1,0:T(8,128)(2,1)} %get-tuple-element.264), channel_id=1, source_target_pairs={{0,1},{1,2},{2,3},{4,5},{5,6},{6,7},{8,9},{9,10},{10,11},{12,13},{... | collective-permute-start | bytes 2359304 | tf_op jit(solution)/shard_map/grad rows 1/ppermute | solution.py:760
  187.5 21.4 %collective-permute-start.37 = (bf16[512,768]{1,0:T(8,128)(2,1)}, bf16[512,768]{1,0:T(8,128)(2,1)}, u32[]{:S(2)}, u32[]{:S(2)}) collective-permute-start(bf16[512,768]{1,0:T(8,128)(2,1)} %get-tuple-element.264), channel_id=1, source_target_pairs={{1,0},{2,1},{3,2},{5,4},{6,5},{7,6},{9,8},{10,9},{11,10},{13,12},{... | collective-permute-start | bytes 2359304 | tf_op jit(solution)/shard_map/grad rows 1/ppermute | solution.py:761
  200.1 9.1 %collective-permute-start.42 = (bf16[2,208,384]{2,1,0:T(8,128)(2,1)}, bf16[2,208,384]{2,1,0:T(8,128)(2,1)S(1)}, u32[]{:S(2)}, u32[]{:S(2)}) collective-permute-start(bf16[2,208,384]{2,1,0:T(8,128)(2,1)} %get-tuple-element.275), channel_id=1, source_target_pairs={{0,16},{4,20},{8,24},{12,28},{16,0},{20,4},{24,8},{28,12},{1,17},{... | collective-permute-start | bytes 958472 | tf_op jit(solution)/shard_map/plane one attention grad/ppermute | solution.py:743
  200.6 8.6 %collective-permute-start.43 = (bf16[2,208,384]{2,1,0:T(8,128)(2,1)S(1)}, bf16[2,208,384]{2,1,0:T(8,128)(2,1)S(1)}, u32[]{:S(2)}, u32[]{:S(2)}) collective-permute-start(bf16[2,208,384]{2,1,0:T(8,128)(2,1)S(1)} %get-tuple-element.276), channel_id=1, source_target_pairs={{0,8},{4,12},{8,0},{12,4},{16,24},{20,28},{24,16},{28,20},{1,9},{5... | collective-permute-start | bytes 958472 | tf_op jit(solution)/shard_map/plane one attention grad/ppermute | solution.py:743
  202.7 6.2 %collective-permute-start.41 = (bf16[2,192,384]{2,1,0:T(8,128)(2,1)}, bf16[2,192,384]{2,1,0:T(8,128)(2,1)}, u32[]{:S(2)}, u32[]{:S(2)}) collective-permute-start(bf16[2,192,384]{2,1,0:T(8,128)(2,1)} %add_convert_fusion), channel_id=1, source_target_pairs={{1,2},{2,1},{5,6},{6,5},{9,10},{10,9},{13,14},{14,13},{17,18},{18,... | collective-permute-start | bytes 884744 | tf_op jit(solution)/shard_map/line middle outer grad/ppermute | solution.py:791
  209.4 15.0 %collective-permute-start.45 = (bf16[4,208,384]{2,1,0:T(8,128)(2,1)S(1)}, bf16[4,208,384]{2,1,0:T(8,128)(2,1)S(1)}, u32[]{:S(2)}, u32[]{:S(2)}) collective-permute-start(bf16[4,208,384]{2,1,0:T(8,128)(2,1)S(1)} %get-tuple-element.285), channel_id=1, source_target_pairs={{0,8},{4,12},{8,0},{12,4},{16,24},{20,28},{24,16},{28,20},{1,9},{5... | collective-permute-start | bytes 1916936 | tf_op jit(solution)/shard_map/plane two attention grad/ppermute | solution.py:743
  210.7 14.6 %collective-permute-start.46 = (bf16[4,208,384]{2,1,0:T(8,128)(2,1)S(1)}, bf16[4,208,384]{2,1,0:T(8,128)(2,1)S(1)}, u32[]{:S(2)}, u32[]{:S(2)}) collective-permute-start(bf16[4,208,384]{2,1,0:T(8,128)(2,1)S(1)} %get-tuple-element.286), channel_id=1, source_target_pairs={{0,16},{4,20},{8,24},{12,28},{16,0},{20,4},{24,8},{28,12},{1,17},{... | collective-permute-start | bytes 1916936 | tf_op jit(solution)/shard_map/plane two attention grad/ppermute | solution.py:743
  211.6 12.8 %collective-permute-start.44 = (bf16[2,192,384]{2,1,0:T(8,128)(2,1)S(1)}, bf16[2,192,384]{2,1,0:T(8,128)(2,1)S(1)}, u32[]{:S(2)}, u32[]{:S(2)}) collective-permute-start(bf16[2,192,384]{2,1,0:T(8,128)(2,1)S(1)} %get-tuple-element.282), channel_id=1, source_target_pairs={{0,1},{1,0},{2,3},{3,2},{4,5},{5,4},{6,7},{7,6},{8,9},{9,8},{10,11... | collective-permute-start | bytes 884744 | tf_op jit(solution)/shard_map/line one inner grad/ppermute | solution.py:746
  216.8 16.9 %collective-permute-start.47 = (bf16[512,768]{1,0:T(8,128)(2,1)}, bf16[512,768]{1,0:T(8,128)(2,1)S(1)}, u32[]{:S(2)}, u32[]{:S(2)}) collective-permute-start(bf16[512,768]{1,0:T(8,128)(2,1)} %collective-permute-done.36), channel_id=1, source_target_pairs={{1,2},{2,3},{5,6},{6,7},{9,10},{10,11},{13,14},{14,15},{17,18},{18... | collective-permute-start | bytes 2359304 | tf_op jit(solution)/shard_map/grad rows 2/ppermute | solution.py:760
  217.5 28.9 %collective-permute-start.48 = (bf16[512,768]{1,0:T(8,128)(2,1)}, bf16[512,768]{1,0:T(8,128)(2,1)S(1)}, u32[]{:S(2)}, u32[]{:S(2)}) collective-permute-start(bf16[512,768]{1,0:T(8,128)(2,1)} %collective-permute-done.37), channel_id=1, source_target_pairs={{1,0},{2,1},{5,4},{6,5},{9,8},{10,9},{13,12},{14,13},{17,16},{18,1... | collective-permute-start | bytes 2359304 | tf_op jit(solution)/shard_map/grad rows 2/ppermute | solution.py:761
  223.5 34.4 %copy-start.25 = (bf16[2048,768]{1,0:T(8,128)(2,1)}, bf16[2048,768]{1,0:T(8,128)(2,1)S(1)}, u32[]{:S(2)}) copy-start(bf16[2048,768]{1,0:T(8,128)(2,1)S(1)} %select_dynamic-update-slice_fusion.3) | copy-start | bytes 9437188
  225.4 24.6 %collective-permute-start.53 = (bf16[208,384]{1,0:T(8,128)(2,1)S(1)}, bf16[208,384]{1,0:T(8,128)(2,1)S(1)}, u32[]{:S(2)}, u32[]{:S(2)}) collective-permute-start(bf16[208,384]{1,0:T(8,128)(2,1)S(1)} %get-tuple-element.325), channel_id=1, source_target_pairs={{0,1},{1,0},{2,3},{3,2},{4,5},{5,4},{6,7},{7,6},{8,9},{9,8},{10,11... | collective-permute-start | bytes 479240 | tf_op jit(solution)/shard_map/line attention grad/ppermute | solution.py:746
  231.3 21.0 %collective-permute-start.54 = (bf16[208,384]{1,0:T(8,128)(2,1)S(1)}, bf16[208,384]{1,0:T(8,128)(2,1)S(1)}, u32[]{:S(2)}, u32[]{:S(2)}) collective-permute-start(bf16[208,384]{1,0:T(8,128)(2,1)S(1)} %get-tuple-element.324), channel_id=1, source_target_pairs={{0,2},{1,3},{2,0},{3,1},{4,6},{5,7},{6,4},{7,5},{8,10},{9,11},{10,... | collective-permute-start | bytes 479240 | tf_op jit(solution)/shard_map/line attention grad/ppermute | solution.py:746
  231.3 22.3 %collective-permute-start.55 = (bf16[208,384]{1,0:T(8,128)(2,1)S(1)}, bf16[208,384]{1,0:T(8,128)(2,1)S(1)}, u32[]{:S(2)}, u32[]{:S(2)}) collective-permute-start(bf16[208,384]{1,0:T(8,128)(2,1)S(1)} %get-tuple-element.323), channel_id=1, source_target_pairs={{0,3},{1,2},{2,1},{3,0},{4,7},{5,6},{6,5},{7,4},{8,11},{9,10},{10,... | collective-permute-start | bytes 479240 | tf_op jit(solution)/shard_map/line attention grad/ppermute | solution.py:746
  246.5 11.2 %collective-permute-start.51 = (bf16[192,384]{1,0:T(8,128)(2,1)S(1)}, bf16[192,384]{1,0:T(8,128)(2,1)S(1)}, u32[]{:S(2)}, u32[]{:S(2)}) collective-permute-start(bf16[192,384]{1,0:T(8,128)(2,1)S(1)} %fusion.9), channel_id=1, source_target_pairs={{0,2},{1,3},{2,0},{3,1},{4,6},{5,7},{6,4},{7,5},{8,10},{9,11},{10,... | collective-permute-start | bytes 442376 | tf_op jit(solution)/shard_map/line two inner grad/ppermute | solution.py:746
  248.6 9.1 %collective-permute-start.52 = (bf16[192,384]{1,0:T(8,128)(2,1)S(1)}, bf16[192,384]{1,0:T(8,128)(2,1)S(1)}, u32[]{:S(2)}, u32[]{:S(2)}) collective-permute-start(bf16[192,384]{1,0:T(8,128)(2,1)S(1)} %fusion.10), channel_id=1, source_target_pairs={{0,1},{1,0},{2,3},{3,2},{4,5},{5,4},{6,7},{7,6},{8,9},{9,8},{10,11... | collective-permute-start | bytes 442376 | tf_op jit(solution)/shard_map/line pair outer grad/ppermute | solution.py:746
  250.1 27.4 %collective-permute-start.49 = (bf16[512,768]{1,0:T(8,128)(2,1)S(1)}, bf16[512,768]{1,0:T(8,128)(2,1)S(1)}, u32[]{:S(2)}, u32[]{:S(2)}) collective-permute-start(bf16[512,768]{1,0:T(8,128)(2,1)S(1)} %collective-permute-done.47), channel_id=1, source_target_pairs={{2,3},{6,7},{10,11},{14,15},{18,19},{22,23},{26,27},{30,31}} | collective-permute-start | bytes 2359304 | tf_op jit(solution)/shard_map/grad rows 3/ppermute | solution.py:760
  252.3 25.2 %collective-permute-start.50 = (bf16[512,768]{1,0:T(8,128)(2,1)S(1)}, bf16[512,768]{1,0:T(8,128)(2,1)S(1)}, u32[]{:S(2)}, u32[]{:S(2)}) collective-permute-start(bf16[512,768]{1,0:T(8,128)(2,1)S(1)} %collective-permute-done.48), channel_id=1, source_target_pairs={{1,0},{5,4},{9,8},{13,12},{17,16},{21,20},{25,24},{29,28}} | collective-permute-start | bytes 2359304 | tf_op jit(solution)/shard_map/grad rows 3/ppermute | solution.py:761
  258.0 12.7 %collective-permute-start.56 = (bf16[592,384]{1,0:T(8,128)(2,1)S(1)}, bf16[592,384]{1,0:T(8,128)(2,1)S(1)}, u32[]{:S(2)}, u32[]{:S(2)}) collective-permute-start(bf16[592,384]{1,0:T(8,128)(2,1)S(1)} %get-tuple-element.329), channel_id=1, source_target_pairs={{0,8},{4,12},{8,0},{12,4},{16,24},{20,28},{24,16},{28,20},{1,9},{5... | collective-permute-start | bytes 1363976 | tf_op jit(solution)/shard_map/plane result/ppermute | solution.py:743
  259.6 17.9 %collective-permute-start.57 = (bf16[592,384]{1,0:T(8,128)(2,1)S(1)}, bf16[592,384]{1,0:T(8,128)(2,1)S(1)}, u32[]{:S(2)}, u32[]{:S(2)}) collective-permute-start(bf16[592,384]{1,0:T(8,128)(2,1)S(1)} %get-tuple-element.329), channel_id=1, source_target_pairs={{0,16},{4,20},{8,24},{12,28},{16,0},{20,4},{24,8},{28,12},{1,17},{... | collective-permute-start | bytes 1363976 | tf_op jit(solution)/shard_map/plane result/ppermute | solution.py:743
  260.2 17.3 %collective-permute-start.58 = (bf16[592,384]{1,0:T(8,128)(2,1)S(1)}, bf16[592,384]{1,0:T(8,128)(2,1)S(1)}, u32[]{:S(2)}, u32[]{:S(2)}) collective-permute-start(bf16[592,384]{1,0:T(8,128)(2,1)S(1)} %get-tuple-element.329), channel_id=1, source_target_pairs={{0,24},{4,28},{8,16},{12,20},{16,8},{20,12},{24,0},{28,4},{1,25},{... | collective-permute-start | bytes 1363976 | tf_op jit(solution)/shard_map/plane result/ppermute | solution.py:743
  277.8 3.8 %collective-permute-start.59 = (bf16[4,592,384]{2,1,0:T(8,128)(2,1)S(1)}, bf16[4,592,384]{2,1,0:T(8,128)(2,1)S(1)}, u32[]{:S(2)}, u32[]{:S(2)}) collective-permute-start(bf16[4,592,384]{2,1,0:T(8,128)(2,1)S(1)} %pad_maximum_fusion.1.near_ref), channel_id=1, source_target_pairs={{0,4},{4,0},{8,12},{12,8},{16,20},{20,16},{24,28},{28,24},{1,5},{5... | collective-permute-start | bytes 5455880 | tf_op jit(solution)/shard_map/core result/ppermute | solution.py:743
  (42 other events, 281.0 us)

commit v4 on v3

--- a/solution.py
+++ b/solution.py
@@ -16,7 +16,7 @@
 QKV = 48
 epsilon = 1e-12
 masked_value = -1e30
-CHUNK = 128
+CHUNK = 512
 SCALE = 0.05
 VECTORS = 16
 

time: 291 us -> 289 us (level)
  Pallas kernels: 93.8 us -> 88.6 us
    pallas_call x2, Pallas kernels: 10.8 us -> 7.89 us  [ffn_back(): pl.pallas_call(functools.partial(ffn_back_kernel, final=final), grid=(cou...]
  transfers between devices with their start and end apart: 60 -> 60, of which waited for: 27 -> 27; matrix products, arithmetic and copies ran while one was open for 3% -> 3% of each run, Pallas kernels for 26% -> 24%
where the time goes in v4:
time: 289 us; the launch traced here: 284 us
  waiting for transfers between devices  90.7 us (31%)
  Pallas kernels  88.6 us (31%)
  starting transfers between devices  86.2 us (30%)
  other arithmetic  9.63 us (3%)
  local copies, waits for them, and re-layouts  7.13 us (2%)
    ppermute x31, waiting for transfers between devices, across(): return lax.ppermute(array, 'dp', flip[bit])  40.7 us
    ppermute x15, starting transfers between devices, along(): return lax.ppermute(array, 'tensor', [(i, i ^ r) for i in range(n_tensor)])  34.8 us
    ppermute x31, starting transfers between devices, across(): return lax.ppermute(array, 'dp', flip[bit])  27.7 us
    ppermute x15, waiting for transfers between devices, along(): return lax.ppermute(array, 'tensor', [(i, i ^ r) for i in range(n_tensor)])  27.2 us
    pallas_call x4, Pallas kernels, attention_backward(): pl.pallas_call(functools.partial(attention_backward_kernel, shard=shard,...  24.8 us
    ppermute x6, waiting for transfers between devices, rows_round(): lax.ppermute(down, 'tensor', [(i + 1, i) for i in range(n_tensor - k)])  22.8 us
    pallas_call x2, Pallas kernels, weight_grad(): pl.pallas_call(weight_grad_kernel, grid_spec=pltpu.PrefetchScalarGridSpec...  10.2 us
    pallas_call x2, Pallas kernels, attention_forward(): pl.pallas_call(attention_forward_kernel, grid_spec=pltpu.PrefetchScalarGr...  9.99 us
  transfers between devices with their start and end apart: 60, of which 27 were waited for; matrix products, arithmetic and copies ran while one was open for 3% of the time, Pallas kernels for 24%

profile of v4, /device:TPU:0, one launch (start us, length us, event | category | flops | bytes accessed | tf_op | source)
XLA Modules:
  0.0 284.3 jit_solution(8206291480985780047)
XLA Ops:
  1.3 4.0 %shard_map.323 = (bf16[1,768,768]{2,1,0:T(8,128)(2,1)}, bf16[1,208,384]{2,1,0:T(8,128)(2,1)}) custom-call(s32[3]{0:T(128)} %pad_add_fusion.scalars, bf16[192,768]{1,0:T(8,128)(2,1)} %bitcast.77, bf16[192,768]{1,0:T(8,128)(2,1)} %bitcast.78, bf16[192,768]{1,0:T(8,128)(2,1)} %bitcast.79, bf16[192,768]{1,0:T(8,128)(2,1)} %refs_3_.1, bf16[192]{0:T(256)(128)(2,1)} %refs_4_.1, ...), custom_call_target="tpu_custom_call" | custom-call | flops 100000000 | tf_op jit(solution)/shard_map/pallas_call | solution.py:564
  5.3 3.1 %collective-permute-start = (bf16[1,208,384]{2,1,0:T(8,128)(2,1)}, bf16[1,208,384]{2,1,0:T(8,128)(2,1)S(1)}, u32[]{:S(2)}, u32[]{:S(2)}) collective-permute-start(bf16[1,208,384]{2,1,0:T(8,128)(2,1)} %get-tuple-element.170.b_ref.own_ref), channel_id=1, source_target_pairs={{0,1},{1,0},{2,3},{3,2},{4,5},{5,4},{6,7},{7,6},{8,9},{9,8},{10,11... | collective-permute-start | bytes 479240 | tf_op jit(solution)/shard_map/line attention weights/ppermute | solution.py:746
  8.4 2.6 collective-permute-start.1
  11.0 3.4 %shard_map.324 = (bf16[768,768]{1,0:T(8,128)(2,1)}, bf16[192,384]{1,0:T(8,128)(2,1)}, bf16[192,384]{1,0:T(8,128)(2,1)}) custom-call(s32[3]{0:T(128)} %pad_add_fusion.scalars, bf16[768,768]{1,0:T(8,128)(2,1)} %wi_hbm.1, bf16[768,768]{1,0:T(8,128)(2,1)} %own_ref.1), custom_call_target="tpu_custom_call" | custom-call | flops 100000000 | tf_op jit(solution)/shard_map/pallas_call | solution.py:591
  15.8 2.8 shard_map.325
  18.6 4.9 %collective-permute-done.1 = bf16[1,208,384]{2,1,0:T(8,128)(2,1)S(1)} collective-permute-done((bf16[1,208,384]{2,1,0:T(8,128)(2,1)}, bf16[1,208,384]{2,1,0:T(8,128)(2,1)S(1)}, u32[]{:S(2)}, u32[]{:S(2)}) %collective-permute-start.1) | collective-permute-done | bytes 159776 | tf_op jit(solution)/shard_map/line attention weights/ppermute | solution.py:746
  23.5 1.6 collective-permute-start.6
  25.1 1.5 collective-permute-start.7
  27.1 2.5 collective-permute-start.3
  30.6 3.2 %collective-permute-done.3 = bf16[192,384]{1,0:T(8,128)(2,1)S(1)} collective-permute-done((bf16[192,384]{1,0:T(8,128)(2,1)S(1)}, bf16[192,384]{1,0:T(8,128)(2,1)S(1)}, u32[]{:S(2)}, u32[]{:S(2)}) %collective-permute-start.3) | collective-permute-done | bytes 147488 | tf_op jit(solution)/shard_map/line inner weights/ppermute | solution.py:746
  33.8 2.1 collective-permute-start.5
  36.0 5.8 %collective-permute-done.4 = bf16[192,384]{1,0:T(8,128)(2,1)S(1)} collective-permute-done((bf16[192,384]{1,0:T(8,128)(2,1)S(1)}, bf16[192,384]{1,0:T(8,128)(2,1)S(1)}, u32[]{:S(2)}, u32[]{:S(2)}) %collective-permute-start.4) | collective-permute-done | bytes 147488 | tf_op jit(solution)/shard_map/line inner weights/ppermute | solution.py:746
  41.8 3.4 %collective-permute-done.7 = bf16[3,208,384]{2,1,0:T(8,128)(2,1)S(1)} collective-permute-done((bf16[3,208,384]{2,1,0:T(8,128)(2,1)S(1)}, bf16[3,208,384]{2,1,0:T(8,128)(2,1)S(1)}, u32[]{:S(2)}, u32[]{:S(2)}) %collective-permute-start.7) | collective-permute-done | bytes 479264 | tf_op jit(solution)/shard_map/plane attention weights/ppermute | solution.py:743
  45.7 1.3 collective-permute-start.13
  47.8 1.4 collective-permute-start.15
  49.5 3.9 %collective-permute-start.10 = (bf16[192,384]{1,0:T(8,128)(2,1)S(1)}, bf16[192,384]{1,0:T(8,128)(2,1)S(1)}, u32[]{:S(2)}, u32[]{:S(2)}) collective-permute-start(bf16[192,384]{1,0:T(8,128)(2,1)S(1)} %copy-done.44), channel_id=1, source_target_pairs={{0,1},{1,0},{2,3},{3,2},{4,5},{5,4},{6,7},{7,6},{8,9},{9,8},{10,11... | collective-permute-start | bytes 442376 | tf_op jit(solution)/shard_map/line outer weights/ppermute | solution.py:746
  54.6 6.0 %collective-permute-done.10 = bf16[192,384]{1,0:T(8,128)(2,1)S(1)} collective-permute-done((bf16[192,384]{1,0:T(8,128)(2,1)S(1)}, bf16[192,384]{1,0:T(8,128)(2,1)S(1)}, u32[]{:S(2)}, u32[]{:S(2)}) %collective-permute-start.10) | collective-permute-done | bytes 147488 | tf_op jit(solution)/shard_map/line outer weights/ppermute | solution.py:746
  61.9 1.4 shard_map.326.w_ref.wo_ref.w_hbm
  63.4 7.2 %shard_map.327 = (bf16[4,576,512]{2,1,0:T(8,128)(2,1)S(1)}, bf16[4,192,512]{2,1,0:T(8,128)(2,1)S(1)}, f32[4,8,512]{2,1,0:T(8,128)S(1)}) custom-call(s32[3]{0:T(128)S(1)} %copy-done.22, s32[4]{0:T(128)S(1)} %copy-done.23, bf16[2048,768]{1,0:T(8,128)(2,1)S(1)} %copy-done, ...), custom_call_target="tpu_custom_call", output_to_operand_aliasing={{0}: (7, {}), {1}: (8, {}), {2}: (9, {})} | custom-call | flops 450000000 | bytes 450000 | tf_op jit(solution)/shard_map/pallas_call | solution.py:146
  71.1 1.3 collective-permute-start.17
  73.3 1.4 collective-permute-start.19
  76.1 9.7 %shard_map.329 = (f32[512,768]{1,0:T(8,128)S(1)}, f32[512,1]{1,0:T(8,128)S(1)}, f32[512,768]{1,0:T(8,128)S(1)}, bf16[512,768]{1,0:T(8,128)(2,1)S(1)}, bf16[4,512...) custom-call(s32[3]{0:T(128)S(1)} %copy-done.22, bf16[4,192,512]{2,1,0:T(8,128)(2,1)S(1)} %get-tuple-element.180.o_ref.o_hbm, ...), custom_call_target="tpu_custom_call" | custom-call | flops 600000000 | bytes 1000000 | tf_op jit(solution)/shard_map/pallas_call | solution.py:332
  87.8 4.8 %collective-permute-done.18 = bf16[3,192,384]{2,1,0:T(8,128)(2,1)S(1)} collective-permute-done((bf16[3,192,384]{2,1,0:T(8,128)(2,1)S(1)}, bf16[3,192,384]{2,1,0:T(8,128)(2,1)S(1)}, u32[]{:S(2)}, u32[]{:S(2)}) %collective-permute-start.18) | collective-permute-done | bytes 442400 | tf_op jit(solution)/shard_map/plane outer weights/ppermute | solution.py:743
  92.6 1.6 collective-permute-done.19
  94.7 3.6 %collective-permute-done.20.far_ref = bf16[4,3,192,384]{3,2,1,0:T(8,128)(2,1)S(1)} collective-permute-done((bf16[4,3,192,384]{3,2,1,0:T(8,128)(2,1)S(1)}, bf16[4,3,192,384]{3,2,1,0:T(8,128)(2,1)S(1)}, u32[]{:S(2)}, u32[]{:S(2)}) %collective-permute-start.20) | collective-permute-done | bytes 1769504 | tf_op jit(solution)/shard_map/core outer weights/ppermute | solution.py:743
  99.5 5.1 %shard_map.331 = (bf16[512,768]{1,0:T(8,128)(2,1)S(1)}, f32[512,768]{1,0:T(8,128)S(1)}, f32[8,768]{1,0:T(8,128)S(1)}) custom-call(s32[3]{0:T(128)S(1)} %copy-done.22, bf16[4,512,768]{2,1,0:T(8,128)(2,1)S(1)} %get-tuple-element.187.act_ref.left_ref, bf16[4,768,768]{2,1,0:T(8,128)(2,1)S(1)} %shard_map.330.wu_ref, ...), custom_call_target="tpu_custom_call" | custom-call | flops 250000000 | bytes 700000 | tf_op jit(solution)/shard_map/pallas_call | solution.py:394
  104.6 5.1 %shard_map.332 = (bf16[4,4,192,384]{3,2,1,0:T(8,128)(2,1)S(1)}, bf16[4,4,192,384]{3,2,1,0:T(8,128)(2,1)S(1)}) custom-call(s32[3]{0:T(128)S(1)} %copy-done.22, bf16[4,512,768]{2,1,0:T(8,128)(2,1)S(1)} %get-tuple-element.187.act_ref.left_ref, f32[512,768]{1,0:T(8,128)S(1)} %get-tuple-element.196.right_ref.up_ref.start_ref), custom_call_target="tpu_custom_call" | custom-call | flops 300000000 | bytes 400000 | tf_op jit(solution)/shard_map/pallas_call | solution.py:501
  110.0 4.3 %collective-permute-start.22 = (bf16[512,768]{1,0:T(8,128)(2,1)S(1)}, bf16[512,768]{1,0:T(8,128)(2,1)}, u32[]{:S(2)}, u32[]{:S(2)}) collective-permute-start(bf16[512,768]{1,0:T(8,128)(2,1)S(1)} %get-tuple-element.279), channel_id=1, source_target_pairs={{0,1},{1,2},{2,3},{4,5},{5,6},{6,7},{8,9},{9,10},{10,11},{12,13},{... | collective-permute-start | bytes 2359304 | tf_op jit(solution)/shard_map/rows 1/ppermute | solution.py:760
  115.6 3.6 %shard_map.333 = (f32[512,768]{1,0:T(8,128)S(1)}, bf16[4,512,768]{2,1,0:T(8,128)(2,1)S(1)}, f32[4,1,768]{2,1,0:T(1,128)S(1)}) custom-call(f32[512,768]{1,0:T(8,128)S(1)} %get-tuple-element.196.right_ref.up_ref.start_ref, f32[512,768]{1,0:T(8,128)S(1)} %get-tuple-element.196.right_ref.up_ref.start_ref, bf16[4,512,768]{2,1,0:T(8,128)(2,1)S(1)} %get-tuple-element.197.slope_ref, ...), custom_call_target="tpu_custom_call" | custom-call | flops 300000000 | bytes 400000 | tf_op jit(solution)/shard_map/pallas_call | solution.py:462
  121.2 1.5 collective-permute-start.24
  123.3 4.3 %shard_map.335 = (f32[512,768]{1,0:T(8,128)S(1)}, bf16[4,512,768]{2,1,0:T(8,128)(2,1)S(1)}, f32[4,1,768]{2,1,0:T(1,128)S(1)}, bf16[512,768]{1,0:T(8,128)(2,1)S(1)}, f32[8,768]{1,0:T(8,128)S(1)}) custom-call(f32[512,768]{1,0:T(8,128)S(1)} %get-tuple-element.196.right_ref.up_ref.start_ref, ...), custom_call_target="tpu_custom_call", output_to_operand_aliasing={{1}: (8, {}), {2}: (9, {})} | custom-call | flops 300000000 | bytes 400000 | tf_op jit(solution)/shard_map/pallas_call | solution.py:462
  127.6 5.1 %shard_map.336 = (bf16[4,4,192,384]{3,2,1,0:T(8,128)(2,1)S(1)}, bf16[4,4,192,384]{3,2,1,0:T(8,128)(2,1)S(1)}) custom-call(s32[3]{0:T(128)S(1)} %copy-done.22, bf16[4,512,768]{2,1,0:T(8,128)(2,1)S(1)} %get-tuple-element.209.left_ref, bf16[512,768]{1,0:T(8,128)(2,1)S(1)} %copy-done.13), custom_call_target="tpu_custom_call" | custom-call | flops 300000000 | bytes 400000 | tf_op jit(solution)/shard_map/pallas_call | solution.py:501
  132.7 3.1 %collective-permute-done.23 = bf16[512,768]{1,0:T(8,128)(2,1)} collective-permute-done((bf16[512,768]{1,0:T(8,128)(2,1)S(1)}, bf16[512,768]{1,0:T(8,128)(2,1)}, u32[]{:S(2)}, u32[]{:S(2)}) %collective-permute-start.23) | collective-permute-done | bytes 786464 | tf_op jit(solution)/shard_map/rows 1/ppermute | solution.py:761
  136.5 1.3 collective-permute-start.30
  138.1 1.3 collective-permute-start.27
  140.2 5.9 %shard_map.338 = (f32[512,768]{1,0:T(8,128)S(1)}, bf16[4,4,208,384]{3,2,1,0:T(8,128)(2,1)S(1)}, bf16[4,4,208,384]{3,2,1,0:T(8,128)(2,1)S(1)}) custom-call(s32[3]{0:T(128)S(1)} %copy-done.22, s32[4]{0:T(128)S(1)} %copy-done.23, bf16[2048,768]{1,0:T(8,128)(2,1)S(1)} %copy-done, bf16[4,768,768]{2,1,0:T(8,128)(2,1)S(1)} %shard_map.326.w_ref.wo_ref.w_hbm, ...), custom_call_target="tpu_custom_call" | custom-call | flops 250000000 | bytes 250000 | tf_op jit(solution)/shard_map/pallas_call | solution.py:240
  147.2 5.9 %shard_map.340 = (f32[512,768]{1,0:T(8,128)S(1)}, bf16[4,4,208,384]{3,2,1,0:T(8,128)(2,1)S(1)}, bf16[4,4,208,384]{3,2,1,0:T(8,128)(2,1)S(1)}) custom-call(s32[3]{0:T(128)S(1)} %copy-done.22, s32[4]{0:T(128)S(1)} %copy-done.23, bf16[2048,768]{1,0:T(8,128)(2,1)S(1)} %copy-done, ...), custom_call_target="tpu_custom_call", output_to_operand_aliasing={{1}: (14, {}), {2}: (15, {})} | custom-call | flops 250000000 | bytes 250000 | tf_op jit(solution)/shard_map/pallas_call | solution.py:240
  155.6 1.5 collective-permute-start.31
  157.1 2.0 collective-permute-done.30
  159.8 1.3 collective-permute-start.35
  161.1 6.3 %shard_map.341 = (f32[512,768]{1,0:T(8,128)S(1)}, bf16[4,4,208,384]{3,2,1,0:T(8,128)(2,1)S(1)}, bf16[4,4,208,384]{3,2,1,0:T(8,128)(2,1)S(1)}) custom-call(s32[3]{0:T(128)S(1)} %copy-done.22, s32[4]{0:T(128)S(1)} %copy-done.23, bf16[2048,768]{1,0:T(8,128)(2,1)S(1)} %copy-done, ...), custom_call_target="tpu_custom_call", output_to_operand_aliasing={{1}: (14, {}), {2}: (15, {})} | custom-call | flops 250000000 | bytes 250000 | tf_op jit(solution)/shard_map/pallas_call | solution.py:240
  167.6 4.6 %collective-permute-start.33 = (bf16[2,192,384]{2,1,0:T(8,128)(2,1)S(1)}, bf16[2,192,384]{2,1,0:T(8,128)(2,1)S(1)}, u32[]{:S(2)}, u32[]{:S(2)}) collective-permute-start(bf16[2,192,384]{2,1,0:T(8,128)(2,1)S(1)} %add_convert_fusion.2), channel_id=1, source_target_pairs={{0,1},{3,2},{4,5},{7,6},{8,9},{11,10},{12,13},{15,14},{16,17},{19,... | collective-permute-start | bytes 884744 | tf_op jit(solution)/shard_map/line ends outer grad/ppermute | solution.py:788
  172.5 6.7 %shard_map.343 = (bf16[512,768]{1,0:T(8,128)(2,1)}, bf16[4,4,208,384]{3,2,1,0:T(8,128)(2,1)S(1)}, bf16[4,4,208,384]{3,2,1,0:T(8,128)(2,1)S(1)}) custom-call(s32[3]{0:T(128)S(1)} %copy-done.22, s32[4]{0:T(128)S(1)} %copy-done.23, bf16[2048,768]{1,0:T(8,128)(2,1)S(1)} %copy-done, ...), custom_call_target="tpu_custom_call", output_to_operand_aliasing={{1}: (14, {}), {2}: (15, {})} | custom-call | flops 250000000 | bytes 250000 | tf_op jit(solution)/shard_map/pallas_call | solution.py:240
  179.2 1.7 collective-permute-done.35
  183.2 2.7 collective-permute-start.36
  187.1 2.3 shard_map.344
  189.4 7.3 %collective-permute-done.39 = bf16[4,192,384]{2,1,0:T(8,128)(2,1)} collective-permute-done((bf16[4,192,384]{2,1,0:T(8,128)(2,1)S(1)}, bf16[4,192,384]{2,1,0:T(8,128)(2,1)}, u32[]{:S(2)}, u32[]{:S(2)}) %collective-permute-start.39) | collective-permute-done | bytes 589856 | tf_op jit(solution)/shard_map/plane two inner grad/ppermute | solution.py:743
  200.7 1.4 collective-permute-start.41
  202.0 1.4 convert_add_fusion.2
  203.5 3.6 %collective-permute-done.37 = bf16[512,768]{1,0:T(8,128)(2,1)} collective-permute-done((bf16[512,768]{1,0:T(8,128)(2,1)}, bf16[512,768]{1,0:T(8,128)(2,1)}, u32[]{:S(2)}, u32[]{:S(2)}) %collective-permute-start.37) | collective-permute-done | bytes 786464 | tf_op jit(solution)/shard_map/grad rows 1/ppermute | solution.py:761
  209.3 5.5 %collective-permute-start.44 = (bf16[2,192,384]{2,1,0:T(8,128)(2,1)S(1)}, bf16[2,192,384]{2,1,0:T(8,128)(2,1)S(1)}, u32[]{:S(2)}, u32[]{:S(2)}) collective-permute-start(bf16[2,192,384]{2,1,0:T(8,128)(2,1)S(1)} %get-tuple-element.282), channel_id=1, source_target_pairs={{0,1},{1,0},{2,3},{3,2},{4,5},{5,4},{6,7},{7,6},{8,9},{9,8},{10,11... | collective-permute-start | bytes 884744 | tf_op jit(solution)/shard_map/line one inner grad/ppermute | solution.py:746
  215.5 1.5 collective-permute-start.48
  220.0 1.4 select_dynamic-update-slice_fusion.3
  223.4 6.1 %collective-permute-start.53 = (bf16[208,384]{1,0:T(8,128)(2,1)S(1)}, bf16[208,384]{1,0:T(8,128)(2,1)S(1)}, u32[]{:S(2)}, u32[]{:S(2)}) collective-permute-start(bf16[208,384]{1,0:T(8,128)(2,1)S(1)} %get-tuple-element.325), channel_id=1, source_target_pairs={{0,1},{1,0},{2,3},{3,2},{4,5},{5,4},{6,7},{7,6},{8,9},{9,8},{10,11... | collective-permute-start | bytes 479240 | tf_op jit(solution)/shard_map/line attention grad/ppermute | solution.py:746
  229.5 2.4 collective-permute-start.55
  232.0 12.5 %collective-permute-done.48 = bf16[512,768]{1,0:T(8,128)(2,1)S(1)} collective-permute-done((bf16[512,768]{1,0:T(8,128)(2,1)}, bf16[512,768]{1,0:T(8,128)(2,1)S(1)}, u32[]{:S(2)}, u32[]{:S(2)}) %collective-permute-start.48) | collective-permute-done | bytes 786464 | tf_op jit(solution)/shard_map/grad rows 2/ppermute | solution.py:761
  244.5 2.1 collective-permute-start.51
  248.8 1.5 collective-permute-done.54
  251.6 4.3 %collective-permute-done.51 = bf16[192,384]{1,0:T(8,128)(2,1)S(1)} collective-permute-done((bf16[192,384]{1,0:T(8,128)(2,1)S(1)}, bf16[192,384]{1,0:T(8,128)(2,1)S(1)}, u32[]{:S(2)}, u32[]{:S(2)}) %collective-permute-start.51) | collective-permute-done | bytes 147488 | tf_op jit(solution)/shard_map/line two inner grad/ppermute | solution.py:746
  258.4 1.3 collective-permute-start.58
  259.8 9.9 %collective-permute-done.56 = bf16[592,384]{1,0:T(8,128)(2,1)S(1)} collective-permute-done((bf16[592,384]{1,0:T(8,128)(2,1)S(1)}, bf16[592,384]{1,0:T(8,128)(2,1)S(1)}, u32[]{:S(2)}, u32[]{:S(2)}) %collective-permute-start.56) | collective-permute-done | bytes 454688 | tf_op jit(solution)/shard_map/plane result/ppermute | solution.py:743
  269.6 5.9 %collective-permute-done.57 = bf16[592,384]{1,0:T(8,128)(2,1)S(1)} collective-permute-done((bf16[592,384]{1,0:T(8,128)(2,1)S(1)}, bf16[592,384]{1,0:T(8,128)(2,1)S(1)}, u32[]{:S(2)}, u32[]{:S(2)}) %collective-permute-start.57) | collective-permute-done | bytes 454688 | tf_op jit(solution)/shard_map/plane result/ppermute | solution.py:743
  277.8 1.4 select_dynamic-update-slice_fusion
  279.7 4.4 %shard_map.346 = (f32[192,768]{1,0:T(8,128)}, f32[192,768]{1,0:T(8,128)}, f32[192,768]{1,0:T(8,128)}, f32[192,768]{1,0:T(8,128)}, f32[768,768]{1,0:T(8,128)}, /*...) custom-call(s32[3]{0:T(128)S(1)} %copy-done.22, ...), custom_call_target="tpu_custom_call" | custom-call | flops 100000000 | tf_op jit(solution)/shard_map/pallas_call | solution.py:667
  (212 shorter events, 48.4 us)
Async XLA Ops:
  5.3 13.2 %collective-permute-start = (bf16[1,208,384]{2,1,0:T(8,128)(2,1)}, bf16[1,208,384]{2,1,0:T(8,128)(2,1)S(1)}, u32[]{:S(2)}, u32[]{:S(2)}) collective-permute-start(bf16[1,208,384]{2,1,0:T(8,128)(2,1)} %get-tuple-element.170.b_ref.own_ref), channel_id=1, source_target_pairs={{0,1},{1,0},{2,3},{3,2},{4,5},{5,4},{6,7},{7,6},{8,9},{9,8},{10,11... | collective-permute-start | bytes 479240 | tf_op jit(solution)/shard_map/line attention weights/ppermute | solution.py:746
  8.4 15.0 %collective-permute-start.1 = (bf16[1,208,384]{2,1,0:T(8,128)(2,1)}, bf16[1,208,384]{2,1,0:T(8,128)(2,1)S(1)}, u32[]{:S(2)}, u32[]{:S(2)}) collective-permute-start(bf16[1,208,384]{2,1,0:T(8,128)(2,1)} %get-tuple-element.170.b_ref.own_ref), channel_id=1, source_target_pairs={{0,2},{1,3},{2,0},{3,1},{4,6},{5,7},{6,4},{7,5},{8,10},{9,11},{10,... | collective-permute-start | bytes 479240 | tf_op jit(solution)/shard_map/line attention weights/ppermute | solution.py:746
  11.0 12.4 %collective-permute-start.2 = (bf16[1,208,384]{2,1,0:T(8,128)(2,1)}, bf16[1,208,384]{2,1,0:T(8,128)(2,1)S(1)}, u32[]{:S(2)}, u32[]{:S(2)}) collective-permute-start(bf16[1,208,384]{2,1,0:T(8,128)(2,1)} %get-tuple-element.170.b_ref.own_ref), channel_id=1, source_target_pairs={{0,3},{1,2},{2,1},{3,0},{4,7},{5,6},{6,5},{7,4},{8,11},{9,10},{10,... | collective-permute-start | bytes 479240 | tf_op jit(solution)/shard_map/line attention weights/ppermute | solution.py:746
  23.5 18.3 %collective-permute-start.6 = (bf16[3,208,384]{2,1,0:T(8,128)(2,1)S(1)}, bf16[3,208,384]{2,1,0:T(8,128)(2,1)S(1)}, u32[]{:S(2)}, u32[]{:S(2)}) collective-permute-start(bf16[3,208,384]{2,1,0:T(8,128)(2,1)S(1)} %constant_dynamic-update-slice_fusion.b_ref.others_ref), channel_id=1, source_target_pairs={{0,8},{4,12},{8,0},{12,4},{16,24},{20,28},{24,16},{28,20},{1,9},{5... | collective-permute-start | bytes 1437704 | tf_op jit(solution)/shard_map/plane attention weights/ppermute | solution.py:743
  25.1 20.2 %collective-permute-start.7 = (bf16[3,208,384]{2,1,0:T(8,128)(2,1)S(1)}, bf16[3,208,384]{2,1,0:T(8,128)(2,1)S(1)}, u32[]{:S(2)}, u32[]{:S(2)}) collective-permute-start(bf16[3,208,384]{2,1,0:T(8,128)(2,1)S(1)} %constant_dynamic-update-slice_fusion.b_ref.others_ref), channel_id=1, source_target_pairs={{0,16},{4,20},{8,24},{12,28},{16,0},{20,4},{24,8},{28,12},{1,17},{... | collective-permute-start | bytes 1437704 | tf_op jit(solution)/shard_map/plane attention weights/ppermute | solution.py:743
  26.6 18.7 %collective-permute-start.8 = (bf16[3,208,384]{2,1,0:T(8,128)(2,1)S(1)}, bf16[3,208,384]{2,1,0:T(8,128)(2,1)S(1)}, u32[]{:S(2)}, u32[]{:S(2)}) collective-permute-start(bf16[3,208,384]{2,1,0:T(8,128)(2,1)S(1)} %constant_dynamic-update-slice_fusion.b_ref.others_ref), channel_id=1, source_target_pairs={{0,24},{4,28},{8,16},{12,20},{16,8},{20,12},{24,0},{28,4},{1,25},{... | collective-permute-start | bytes 1437704 | tf_op jit(solution)/shard_map/plane attention weights/ppermute | solution.py:743
  27.1 6.8 %collective-permute-start.3 = (bf16[192,384]{1,0:T(8,128)(2,1)S(1)}, bf16[192,384]{1,0:T(8,128)(2,1)S(1)}, u32[]{:S(2)}, u32[]{:S(2)}) collective-permute-start(bf16[192,384]{1,0:T(8,128)(2,1)S(1)} %copy-done.45), channel_id=1, source_target_pairs={{0,1},{1,0},{2,3},{3,2},{4,5},{5,4},{6,7},{7,6},{8,9},{9,8},{10,11... | collective-permute-start | bytes 442376 | tf_op jit(solution)/shard_map/line inner weights/ppermute | solution.py:746
  29.6 12.2 %collective-permute-start.4 = (bf16[192,384]{1,0:T(8,128)(2,1)S(1)}, bf16[192,384]{1,0:T(8,128)(2,1)S(1)}, u32[]{:S(2)}, u32[]{:S(2)}) collective-permute-start(bf16[192,384]{1,0:T(8,128)(2,1)S(1)} %copy-done.45), channel_id=1, source_target_pairs={{0,2},{1,3},{2,0},{3,1},{4,6},{5,7},{6,4},{7,5},{8,10},{9,11},{10,... | collective-permute-start | bytes 442376 | tf_op jit(solution)/shard_map/line inner weights/ppermute | solution.py:746
  33.8 8.0 %collective-permute-start.5 = (bf16[192,384]{1,0:T(8,128)(2,1)S(1)}, bf16[192,384]{1,0:T(8,128)(2,1)S(1)}, u32[]{:S(2)}, u32[]{:S(2)}) collective-permute-start(bf16[192,384]{1,0:T(8,128)(2,1)S(1)} %copy-done.45), channel_id=1, source_target_pairs={{0,3},{1,2},{2,1},{3,0},{4,7},{5,6},{6,5},{7,4},{8,11},{9,10},{10,... | collective-permute-start | bytes 442376 | tf_op jit(solution)/shard_map/line inner weights/ppermute | solution.py:746
  45.2 16.7 %copy-start.5 = (bf16[1,768,768]{2,1,0:T(8,128)(2,1)S(1)}, bf16[1,768,768]{2,1,0:T(8,128)(2,1)}, u32[]{:S(2)}) copy-start(bf16[1,768,768]{2,1,0:T(8,128)(2,1)} %get-tuple-element.171.w_ref) | copy-start | bytes 3538948
  45.5 4.0 %collective-permute-start.9 = (bf16[4,3,208,384]{3,2,1,0:T(8,128)(2,1)S(1)}, bf16[4,3,208,384]{3,2,1,0:T(8,128)(2,1)S(1)}, u32[]{:S(2)}, u32[]{:S(2)}) collective-permute-start(bf16[4,3,208,384]{3,2,1,0:T(8,128)(2,1)S(1)} %pad_maximum_fusion.near_ref), channel_id=1, source_target_pairs={{0,4},{4,0},{8,12},{12,8},{16,20},{20,16},{24,28},{28,24},{1,5},{5... | collective-permute-start | bytes 5750792 | tf_op jit(solution)/shard_map/core attention weights/ppermute | solution.py:743
  45.7 25.0 %collective-permute-start.13 = (bf16[3,192,384]{2,1,0:T(8,128)(2,1)S(1)}, bf16[3,192,384]{2,1,0:T(8,128)(2,1)S(1)}, u32[]{:S(2)}, u32[]{:S(2)}) collective-permute-start(bf16[3,192,384]{2,1,0:T(8,128)(2,1)S(1)} %pad_maximum_fusion.5), channel_id=1, source_target_pairs={{0,8},{4,12},{8,0},{12,4},{16,24},{20,28},{24,16},{28,20},{1,9},{5... | collective-permute-start | bytes 1327112 | tf_op jit(solution)/shard_map/plane inner weights/ppermute | solution.py:743
  47.0 23.7 %collective-permute-start.14 = (bf16[3,192,384]{2,1,0:T(8,128)(2,1)S(1)}, bf16[3,192,384]{2,1,0:T(8,128)(2,1)S(1)}, u32[]{:S(2)}, u32[]{:S(2)}) collective-permute-start(bf16[3,192,384]{2,1,0:T(8,128)(2,1)S(1)} %pad_maximum_fusion.5), channel_id=1, source_target_pairs={{0,16},{4,20},{8,24},{12,28},{16,0},{20,4},{24,8},{28,12},{1,17},{... | collective-permute-start | bytes 1327112 | tf_op jit(solution)/shard_map/plane inner weights/ppermute | solution.py:743
  47.8 22.9 %collective-permute-start.15 = (bf16[3,192,384]{2,1,0:T(8,128)(2,1)S(1)}, bf16[3,192,384]{2,1,0:T(8,128)(2,1)S(1)}, u32[]{:S(2)}, u32[]{:S(2)}) collective-permute-start(bf16[3,192,384]{2,1,0:T(8,128)(2,1)S(1)} %pad_maximum_fusion.5), channel_id=1, source_target_pairs={{0,24},{4,28},{8,16},{12,20},{16,8},{20,12},{24,0},{28,4},{1,25},{... | collective-permute-start | bytes 1327112 | tf_op jit(solution)/shard_map/plane inner weights/ppermute | solution.py:743
  49.5 11.1 %collective-permute-start.10 = (bf16[192,384]{1,0:T(8,128)(2,1)S(1)}, bf16[192,384]{1,0:T(8,128)(2,1)S(1)}, u32[]{:S(2)}, u32[]{:S(2)}) collective-permute-start(bf16[192,384]{1,0:T(8,128)(2,1)S(1)} %copy-done.44), channel_id=1, source_target_pairs={{0,1},{1,0},{2,3},{3,2},{4,5},{5,4},{6,7},{7,6},{8,9},{9,8},{10,11... | collective-permute-start | bytes 442376 | tf_op jit(solution)/shard_map/line outer weights/ppermute | solution.py:746
  53.4 17.2 %collective-permute-start.11 = (bf16[192,384]{1,0:T(8,128)(2,1)S(1)}, bf16[192,384]{1,0:T(8,128)(2,1)S(1)}, u32[]{:S(2)}, u32[]{:S(2)}) collective-permute-start(bf16[192,384]{1,0:T(8,128)(2,1)S(1)} %copy-done.44), channel_id=1, source_target_pairs={{0,2},{1,3},{2,0},{3,1},{4,6},{5,7},{6,4},{7,5},{8,10},{9,11},{10,... | collective-permute-start | bytes 442376 | tf_op jit(solution)/shard_map/line outer weights/ppermute | solution.py:746
  60.6 10.0 %collective-permute-start.12 = (bf16[192,384]{1,0:T(8,128)(2,1)S(1)}, bf16[192,384]{1,0:T(8,128)(2,1)S(1)}, u32[]{:S(2)}, u32[]{:S(2)}) collective-permute-start(bf16[192,384]{1,0:T(8,128)(2,1)S(1)} %copy-done.44), channel_id=1, source_target_pairs={{0,3},{1,2},{2,1},{3,0},{4,7},{5,6},{6,5},{7,4},{8,11},{9,10},{10,... | collective-permute-start | bytes 442376 | tf_op jit(solution)/shard_map/line outer weights/ppermute | solution.py:746
  71.0 3.8 %collective-permute-start.16 = (bf16[4,3,192,384]{3,2,1,0:T(8,128)(2,1)S(1)}, bf16[4,3,192,384]{3,2,1,0:T(8,128)(2,1)S(1)}, u32[]{:S(2)}, u32[]{:S(2)}) collective-permute-start(bf16[4,3,192,384]{3,2,1,0:T(8,128)(2,1)S(1)} %pad_maximum_fusion.2.near_ref), channel_id=1, source_target_pairs={{0,4},{4,0},{8,12},{12,8},{16,20},{20,16},{24,28},{28,24},{1,5},{5... | collective-permute-start | bytes 5308424 | tf_op jit(solution)/shard_map/core inner weights/ppermute | solution.py:743
  71.1 16.7 %collective-permute-start.17 = (bf16[3,192,384]{2,1,0:T(8,128)(2,1)S(1)}, bf16[3,192,384]{2,1,0:T(8,128)(2,1)S(1)}, u32[]{:S(2)}, u32[]{:S(2)}) collective-permute-start(bf16[3,192,384]{2,1,0:T(8,128)(2,1)S(1)} %pad_maximum_fusion.6), channel_id=1, source_target_pairs={{0,8},{4,12},{8,0},{12,4},{16,24},{20,28},{24,16},{28,20},{1,9},{5... | collective-permute-start | bytes 1327112 | tf_op jit(solution)/shard_map/plane outer weights/ppermute | solution.py:743
  72.4 20.1 %collective-permute-start.18 = (bf16[3,192,384]{2,1,0:T(8,128)(2,1)S(1)}, bf16[3,192,384]{2,1,0:T(8,128)(2,1)S(1)}, u32[]{:S(2)}, u32[]{:S(2)}) collective-permute-start(bf16[3,192,384]{2,1,0:T(8,128)(2,1)S(1)} %pad_maximum_fusion.6), channel_id=1, source_target_pairs={{0,16},{4,20},{8,24},{12,28},{16,0},{20,4},{24,8},{28,12},{1,17},{... | collective-permute-start | bytes 1327112 | tf_op jit(solution)/shard_map/plane outer weights/ppermute | solution.py:743
  73.3 20.9 %collective-permute-start.19 = (bf16[3,192,384]{2,1,0:T(8,128)(2,1)S(1)}, bf16[3,192,384]{2,1,0:T(8,128)(2,1)S(1)}, u32[]{:S(2)}, u32[]{:S(2)}) collective-permute-start(bf16[3,192,384]{2,1,0:T(8,128)(2,1)S(1)} %pad_maximum_fusion.6), channel_id=1, source_target_pairs={{0,24},{4,28},{8,16},{12,20},{16,8},{20,12},{24,0},{28,4},{1,25},{... | collective-permute-start | bytes 1327112 | tf_op jit(solution)/shard_map/plane outer weights/ppermute | solution.py:743
  87.8 27.8 %copy-start.1 = (bf16[4,512,768]{2,1,0:T(8,128)(2,1)}, bf16[4,512,768]{2,1,0:T(8,128)(2,1)S(1)}, u32[]{:S(2)}) copy-start(bf16[4,512,768]{2,1,0:T(8,128)(2,1)S(1)} %get-tuple-element.197.slope_ref) | copy-start | bytes 9437188
  94.5 3.8 %collective-permute-start.20 = (bf16[4,3,192,384]{3,2,1,0:T(8,128)(2,1)S(1)}, bf16[4,3,192,384]{3,2,1,0:T(8,128)(2,1)S(1)}, u32[]{:S(2)}, u32[]{:S(2)}) collective-permute-start(bf16[4,3,192,384]{3,2,1,0:T(8,128)(2,1)S(1)} %pad_maximum_fusion.3.near_ref), channel_id=1, source_target_pairs={{0,4},{4,0},{8,12},{12,8},{16,20},{20,16},{24,28},{28,24},{1,5},{5... | collective-permute-start | bytes 5308424 | tf_op jit(solution)/shard_map/core outer weights/ppermute | solution.py:743
  109.8 9.5 %collective-permute-start.21 = (bf16[4,4,192,384]{3,2,1,0:T(8,128)(2,1)S(1)}, bf16[4,4,192,384]{3,2,1,0:T(8,128)(2,1)S(1)}, u32[]{:S(2)}, u32[]{:S(2)}) collective-permute-start(bf16[4,4,192,384]{3,2,1,0:T(8,128)(2,1)S(1)} %get-tuple-element.199), channel_id=1, source_target_pairs={{0,4},{4,0},{8,12},{12,8},{16,20},{20,16},{24,28},{28,24},{1,5},{5... | collective-permute-start | bytes 7077896 | tf_op jit(solution)/shard_map/core outer grad/ppermute | solution.py:743
  110.0 22.7 %collective-permute-start.22 = (bf16[512,768]{1,0:T(8,128)(2,1)S(1)}, bf16[512,768]{1,0:T(8,128)(2,1)}, u32[]{:S(2)}, u32[]{:S(2)}) collective-permute-start(bf16[512,768]{1,0:T(8,128)(2,1)S(1)} %get-tuple-element.279), channel_id=1, source_target_pairs={{0,1},{1,2},{2,3},{4,5},{5,6},{6,7},{8,9},{9,10},{10,11},{12,13},{... | collective-permute-start | bytes 2359304 | tf_op jit(solution)/shard_map/rows 1/ppermute | solution.py:760
  114.3 21.5 %collective-permute-start.23 = (bf16[512,768]{1,0:T(8,128)(2,1)S(1)}, bf16[512,768]{1,0:T(8,128)(2,1)}, u32[]{:S(2)}, u32[]{:S(2)}) collective-permute-start(bf16[512,768]{1,0:T(8,128)(2,1)S(1)} %get-tuple-element.279), channel_id=1, source_target_pairs={{1,0},{2,1},{3,2},{5,4},{6,5},{7,6},{9,8},{10,9},{11,10},{13,12},{... | collective-permute-start | bytes 2359304 | tf_op jit(solution)/shard_map/rows 1/ppermute | solution.py:761
  121.2 14.6 %collective-permute-start.24 = (bf16[2,192,384]{2,1,0:T(8,128)(2,1)S(1)}, bf16[2,192,384]{2,1,0:T(8,128)(2,1)S(1)}, u32[]{:S(2)}, u32[]{:S(2)}) collective-permute-start(bf16[2,192,384]{2,1,0:T(8,128)(2,1)S(1)} %get-tuple-element.213), channel_id=1, source_target_pairs={{0,16},{4,20},{8,24},{12,28},{16,0},{20,4},{24,8},{28,12},{1,17},{... | collective-permute-start | bytes 884744 | tf_op jit(solution)/shard_map/plane one outer grad/ppermute | solution.py:743
  122.8 13.1 %collective-permute-start.25 = (bf16[2,192,384]{2,1,0:T(8,128)(2,1)S(1)}, bf16[2,192,384]{2,1,0:T(8,128)(2,1)S(1)}, u32[]{:S(2)}, u32[]{:S(2)}) collective-permute-start(bf16[2,192,384]{2,1,0:T(8,128)(2,1)S(1)} %get-tuple-element.214), channel_id=1, source_target_pairs={{0,8},{4,12},{8,0},{12,4},{16,24},{20,28},{24,16},{28,20},{1,9},{5... | collective-permute-start | bytes 884744 | tf_op jit(solution)/shard_map/plane one outer grad/ppermute | solution.py:743
  135.8 10.2 %collective-permute-start.26 = (bf16[4,4,192,384]{3,2,1,0:T(8,128)(2,1)S(1)}, bf16[4,4,192,384]{3,2,1,0:T(8,128)(2,1)S(1)}, u32[]{:S(2)}, u32[]{:S(2)}) collective-permute-start(bf16[4,4,192,384]{3,2,1,0:T(8,128)(2,1)S(1)} %get-tuple-element.226), channel_id=1, source_target_pairs={{0,4},{4,0},{8,12},{12,8},{16,20},{20,16},{24,28},{28,24},{1,5},{5... | collective-permute-start | bytes 7077896 | tf_op jit(solution)/shard_map/core inner grad/ppermute | solution.py:743
  135.8 21.3 %collective-permute-start.29 = (bf16[512,768]{1,0:T(8,128)(2,1)}, bf16[512,768]{1,0:T(8,128)(2,1)S(1)}, u32[]{:S(2)}, u32[]{:S(2)}) collective-permute-start(bf16[512,768]{1,0:T(8,128)(2,1)} %collective-permute-done.22), channel_id=1, source_target_pairs={{1,2},{2,3},{5,6},{6,7},{9,10},{10,11},{13,14},{14,15},{17,18},{18... | collective-permute-start | bytes 2359304 | tf_op jit(solution)/shard_map/rows 2/ppermute | solution.py:760
  136.5 22.5 %collective-permute-start.30 = (bf16[512,768]{1,0:T(8,128)(2,1)}, bf16[512,768]{1,0:T(8,128)(2,1)S(1)}, u32[]{:S(2)}, u32[]{:S(2)}) collective-permute-start(bf16[512,768]{1,0:T(8,128)(2,1)} %collective-permute-done.23), channel_id=1, source_target_pairs={{1,0},{2,1},{5,4},{6,5},{9,8},{10,9},{13,12},{14,13},{17,16},{18,1... | collective-permute-start | bytes 2359304 | tf_op jit(solution)/shard_map/rows 2/ppermute | solution.py:761
  138.1 15.8 %collective-permute-start.27 = (bf16[4,192,384]{2,1,0:T(8,128)(2,1)S(1)}, bf16[4,192,384]{2,1,0:T(8,128)(2,1)S(1)}, u32[]{:S(2)}, u32[]{:S(2)}) collective-permute-start(bf16[4,192,384]{2,1,0:T(8,128)(2,1)S(1)} %get-tuple-element.220), channel_id=1, source_target_pairs={{0,8},{4,12},{8,0},{12,4},{16,24},{20,28},{24,16},{28,20},{1,9},{5... | collective-permute-start | bytes 1769480 | tf_op jit(solution)/shard_map/plane two outer grad/ppermute | solution.py:743
  139.3 15.4 %collective-permute-start.28 = (bf16[4,192,384]{2,1,0:T(8,128)(2,1)S(1)}, bf16[4,192,384]{2,1,0:T(8,128)(2,1)S(1)}, u32[]{:S(2)}, u32[]{:S(2)}) collective-permute-start(bf16[4,192,384]{2,1,0:T(8,128)(2,1)S(1)} %get-tuple-element.235), channel_id=1, source_target_pairs={{0,16},{4,20},{8,24},{12,28},{16,0},{20,4},{24,8},{28,12},{1,17},{... | collective-permute-start | bytes 1769480 | tf_op jit(solution)/shard_map/plane two outer grad/ppermute | solution.py:743
  154.8 12.7 %collective-permute-start.32 = (bf16[2,192,384]{2,1,0:T(8,128)(2,1)S(1)}, bf16[2,192,384]{2,1,0:T(8,128)(2,1)S(1)}, u32[]{:S(2)}, u32[]{:S(2)}) collective-permute-start(bf16[2,192,384]{2,1,0:T(8,128)(2,1)S(1)} %get-tuple-element.248), channel_id=1, source_target_pairs={{0,8},{4,12},{8,0},{12,4},{16,24},{20,28},{24,16},{28,20},{1,9},{5... | collective-permute-start | bytes 884744 | tf_op jit(solution)/shard_map/plane one inner grad/ppermute | solution.py:743
  155.6 11.9 %collective-permute-start.31 = (bf16[2,192,384]{2,1,0:T(8,128)(2,1)S(1)}, bf16[2,192,384]{2,1,0:T(8,128)(2,1)S(1)}, u32[]{:S(2)}, u32[]{:S(2)}) collective-permute-start(bf16[2,192,384]{2,1,0:T(8,128)(2,1)S(1)} %get-tuple-element.246), channel_id=1, source_target_pairs={{0,16},{4,20},{8,24},{12,28},{16,0},{20,4},{24,8},{28,12},{1,17},{... | collective-permute-start | bytes 884744 | tf_op jit(solution)/shard_map/plane one inner grad/ppermute | solution.py:743
  159.1 20.1 %collective-permute-start.34 = (bf16[512,768]{1,0:T(8,128)(2,1)S(1)}, bf16[512,768]{1,0:T(8,128)(2,1)S(1)}, u32[]{:S(2)}, u32[]{:S(2)}) collective-permute-start(bf16[512,768]{1,0:T(8,128)(2,1)S(1)} %collective-permute-done.29), channel_id=1, source_target_pairs={{2,3},{6,7},{10,11},{14,15},{18,19},{22,23},{26,27},{30,31}} | collective-permute-start | bytes 2359304 | tf_op jit(solution)/shard_map/rows 3/ppermute | solution.py:760
  159.8 21.0 %collective-permute-start.35 = (bf16[512,768]{1,0:T(8,128)(2,1)S(1)}, bf16[512,768]{1,0:T(8,128)(2,1)S(1)}, u32[]{:S(2)}, u32[]{:S(2)}) collective-permute-start(bf16[512,768]{1,0:T(8,128)(2,1)S(1)} %collective-permute-done.30), channel_id=1, source_target_pairs={{1,0},{5,4},{9,8},{13,12},{17,16},{21,20},{25,24},{29,28}} | collective-permute-start | bytes 2359304 | tf_op jit(solution)/shard_map/rows 3/ppermute | solution.py:761
  167.6 11.5 %collective-permute-start.33 = (bf16[2,192,384]{2,1,0:T(8,128)(2,1)S(1)}, bf16[2,192,384]{2,1,0:T(8,128)(2,1)S(1)}, u32[]{:S(2)}, u32[]{:S(2)}) collective-permute-start(bf16[2,192,384]{2,1,0:T(8,128)(2,1)S(1)} %add_convert_fusion.2), channel_id=1, source_target_pairs={{0,1},{3,2},{4,5},{7,6},{8,9},{11,10},{12,13},{15,14},{16,17},{19,... | collective-permute-start | bytes 884744 | tf_op jit(solution)/shard_map/line ends outer grad/ppermute | solution.py:788
  180.9 6.3 %collective-permute-start.38 = (bf16[4,4,208,384]{3,2,1,0:T(8,128)(2,1)S(1)}, bf16[4,4,208,384]{3,2,1,0:T(8,128)(2,1)S(1)}, u32[]{:S(2)}, u32[]{:S(2)}) collective-permute-start(bf16[4,4,208,384]{3,2,1,0:T(8,128)(2,1)S(1)} %get-tuple-element.266), channel_id=1, source_target_pairs={{0,4},{4,0},{8,12},{12,8},{16,20},{20,16},{24,28},{28,24},{1,5},{5... | collective-permute-start | bytes 7667720 | tf_op jit(solution)/shard_map/core attention grad/ppermute | solution.py:743
  180.9 15.8 %collective-permute-start.39 = (bf16[4,192,384]{2,1,0:T(8,128)(2,1)S(1)}, bf16[4,192,384]{2,1,0:T(8,128)(2,1)}, u32[]{:S(2)}, u32[]{:S(2)}) collective-permute-start(bf16[4,192,384]{2,1,0:T(8,128)(2,1)S(1)} %get-tuple-element.254), channel_id=1, source_target_pairs={{0,8},{4,12},{8,0},{12,4},{16,24},{20,28},{24,16},{28,20},{1,9},{5... | collective-permute-start | bytes 1769480 | tf_op jit(solution)/shard_map/plane two inner grad/ppermute | solution.py:743
  182.0 20.1 %copy-start.19 = (bf16[4,192,384]{2,1,0:T(8,128)(2,1)S(1)}, bf16[4,192,384]{2,1,0:T(8,128)(2,1)}, u32[]{:S(2)}) copy-start(bf16[4,192,384]{2,1,0:T(8,128)(2,1)} %copy-done.18) | copy-start | bytes 1769476
  182.0 15.6 %collective-permute-start.40 = (bf16[4,192,384]{2,1,0:T(8,128)(2,1)S(1)}, bf16[4,192,384]{2,1,0:T(8,128)(2,1)}, u32[]{:S(2)}, u32[]{:S(2)}) collective-permute-start(bf16[4,192,384]{2,1,0:T(8,128)(2,1)S(1)} %get-tuple-element.269), channel_id=1, source_target_pairs={{0,16},{4,20},{8,24},{12,28},{16,0},{20,4},{24,8},{28,12},{1,17},{... | collective-permute-start | bytes 1769480 | tf_op jit(solution)/shard_map/plane two inner grad/ppermute | solution.py:743
  183.2 20.3 %collective-permute-start.36 = (bf16[512,768]{1,0:T(8,128)(2,1)}, bf16[512,768]{1,0:T(8,128)(2,1)}, u32[]{:S(2)}, u32[]{:S(2)}) collective-permute-start(bf16[512,768]{1,0:T(8,128)(2,1)} %get-tuple-element.264), channel_id=1, source_target_pairs={{0,1},{1,2},{2,3},{4,5},{5,6},{6,7},{8,9},{9,10},{10,11},{12,13},{... | collective-permute-start | bytes 2359304 | tf_op jit(solution)/shard_map/grad rows 1/ppermute | solution.py:760
  185.8 21.3 %collective-permute-start.37 = (bf16[512,768]{1,0:T(8,128)(2,1)}, bf16[512,768]{1,0:T(8,128)(2,1)}, u32[]{:S(2)}, u32[]{:S(2)}) collective-permute-start(bf16[512,768]{1,0:T(8,128)(2,1)} %get-tuple-element.264), channel_id=1, source_target_pairs={{1,0},{2,1},{3,2},{5,4},{6,5},{7,6},{9,8},{10,9},{11,10},{13,12},{... | collective-permute-start | bytes 2359304 | tf_op jit(solution)/shard_map/grad rows 1/ppermute | solution.py:761
  197.5 9.6 %collective-permute-start.42 = (bf16[2,208,384]{2,1,0:T(8,128)(2,1)}, bf16[2,208,384]{2,1,0:T(8,128)(2,1)S(1)}, u32[]{:S(2)}, u32[]{:S(2)}) collective-permute-start(bf16[2,208,384]{2,1,0:T(8,128)(2,1)} %get-tuple-element.275), channel_id=1, source_target_pairs={{0,16},{4,20},{8,24},{12,28},{16,0},{20,4},{24,8},{28,12},{1,17},{... | collective-permute-start | bytes 958472 | tf_op jit(solution)/shard_map/plane one attention grad/ppermute | solution.py:743
  198.7 8.6 %collective-permute-start.43 = (bf16[2,208,384]{2,1,0:T(8,128)(2,1)S(1)}, bf16[2,208,384]{2,1,0:T(8,128)(2,1)S(1)}, u32[]{:S(2)}, u32[]{:S(2)}) collective-permute-start(bf16[2,208,384]{2,1,0:T(8,128)(2,1)S(1)} %get-tuple-element.276), channel_id=1, source_target_pairs={{0,8},{4,12},{8,0},{12,4},{16,24},{20,28},{24,16},{28,20},{1,9},{5... | collective-permute-start | bytes 958472 | tf_op jit(solution)/shard_map/plane one attention grad/ppermute | solution.py:743
  200.7 6.4 %collective-permute-start.41 = (bf16[2,192,384]{2,1,0:T(8,128)(2,1)}, bf16[2,192,384]{2,1,0:T(8,128)(2,1)}, u32[]{:S(2)}, u32[]{:S(2)}) collective-permute-start(bf16[2,192,384]{2,1,0:T(8,128)(2,1)} %add_convert_fusion), channel_id=1, source_target_pairs={{1,2},{2,1},{5,6},{6,5},{9,10},{10,9},{13,14},{14,13},{17,18},{18,... | collective-permute-start | bytes 884744 | tf_op jit(solution)/shard_map/line middle outer grad/ppermute | solution.py:791
  207.5 14.9 %collective-permute-start.45 = (bf16[4,208,384]{2,1,0:T(8,128)(2,1)S(1)}, bf16[4,208,384]{2,1,0:T(8,128)(2,1)S(1)}, u32[]{:S(2)}, u32[]{:S(2)}) collective-permute-start(bf16[4,208,384]{2,1,0:T(8,128)(2,1)S(1)} %get-tuple-element.285), channel_id=1, source_target_pairs={{0,8},{4,12},{8,0},{12,4},{16,24},{20,28},{24,16},{28,20},{1,9},{5... | collective-permute-start | bytes 1916936 | tf_op jit(solution)/shard_map/plane two attention grad/ppermute | solution.py:743
  208.7 14.5 %collective-permute-start.46 = (bf16[4,208,384]{2,1,0:T(8,128)(2,1)S(1)}, bf16[4,208,384]{2,1,0:T(8,128)(2,1)S(1)}, u32[]{:S(2)}, u32[]{:S(2)}) collective-permute-start(bf16[4,208,384]{2,1,0:T(8,128)(2,1)S(1)} %get-tuple-element.286), channel_id=1, source_target_pairs={{0,16},{4,20},{8,24},{12,28},{16,0},{20,4},{24,8},{28,12},{1,17},{... | collective-permute-start | bytes 1916936 | tf_op jit(solution)/shard_map/plane two attention grad/ppermute | solution.py:743
  209.3 13.1 %collective-permute-start.44 = (bf16[2,192,384]{2,1,0:T(8,128)(2,1)S(1)}, bf16[2,192,384]{2,1,0:T(8,128)(2,1)S(1)}, u32[]{:S(2)}, u32[]{:S(2)}) collective-permute-start(bf16[2,192,384]{2,1,0:T(8,128)(2,1)S(1)} %get-tuple-element.282), channel_id=1, source_target_pairs={{0,1},{1,0},{2,3},{3,2},{4,5},{5,4},{6,7},{7,6},{8,9},{9,8},{10,11... | collective-permute-start | bytes 884744 | tf_op jit(solution)/shard_map/line one inner grad/ppermute | solution.py:746
  214.8 17.1 %collective-permute-start.47 = (bf16[512,768]{1,0:T(8,128)(2,1)}, bf16[512,768]{1,0:T(8,128)(2,1)S(1)}, u32[]{:S(2)}, u32[]{:S(2)}) collective-permute-start(bf16[512,768]{1,0:T(8,128)(2,1)} %collective-permute-done.36), channel_id=1, source_target_pairs={{1,2},{2,3},{5,6},{6,7},{9,10},{10,11},{13,14},{14,15},{17,18},{18... | collective-permute-start | bytes 2359304 | tf_op jit(solution)/shard_map/grad rows 2/ppermute | solution.py:760
  215.5 28.9 %collective-permute-start.48 = (bf16[512,768]{1,0:T(8,128)(2,1)}, bf16[512,768]{1,0:T(8,128)(2,1)S(1)}, u32[]{:S(2)}, u32[]{:S(2)}) collective-permute-start(bf16[512,768]{1,0:T(8,128)(2,1)} %collective-permute-done.37), channel_id=1, source_target_pairs={{1,0},{2,1},{5,4},{6,5},{9,8},{10,9},{13,12},{14,13},{17,16},{18,1... | collective-permute-start | bytes 2359304 | tf_op jit(solution)/shard_map/grad rows 2/ppermute | solution.py:761
  221.4 34.6 %copy-start.25 = (bf16[2048,768]{1,0:T(8,128)(2,1)}, bf16[2048,768]{1,0:T(8,128)(2,1)S(1)}, u32[]{:S(2)}) copy-start(bf16[2048,768]{1,0:T(8,128)(2,1)S(1)} %select_dynamic-update-slice_fusion.3) | copy-start | bytes 9437188
  223.4 24.7 %collective-permute-start.53 = (bf16[208,384]{1,0:T(8,128)(2,1)S(1)}, bf16[208,384]{1,0:T(8,128)(2,1)S(1)}, u32[]{:S(2)}, u32[]{:S(2)}) collective-permute-start(bf16[208,384]{1,0:T(8,128)(2,1)S(1)} %get-tuple-element.325), channel_id=1, source_target_pairs={{0,1},{1,0},{2,3},{3,2},{4,5},{5,4},{6,7},{7,6},{8,9},{9,8},{10,11... | collective-permute-start | bytes 479240 | tf_op jit(solution)/shard_map/line attention grad/ppermute | solution.py:746
  229.5 20.8 %collective-permute-start.54 = (bf16[208,384]{1,0:T(8,128)(2,1)S(1)}, bf16[208,384]{1,0:T(8,128)(2,1)S(1)}, u32[]{:S(2)}, u32[]{:S(2)}) collective-permute-start(bf16[208,384]{1,0:T(8,128)(2,1)S(1)} %get-tuple-element.324), channel_id=1, source_target_pairs={{0,2},{1,3},{2,0},{3,1},{4,6},{5,7},{6,4},{7,5},{8,10},{9,11},{10,... | collective-permute-start | bytes 479240 | tf_op jit(solution)/shard_map/line attention grad/ppermute | solution.py:746
  229.5 22.1 %collective-permute-start.55 = (bf16[208,384]{1,0:T(8,128)(2,1)S(1)}, bf16[208,384]{1,0:T(8,128)(2,1)S(1)}, u32[]{:S(2)}, u32[]{:S(2)}) collective-permute-start(bf16[208,384]{1,0:T(8,128)(2,1)S(1)} %get-tuple-element.323), channel_id=1, source_target_pairs={{0,3},{1,2},{2,1},{3,0},{4,7},{5,6},{6,5},{7,4},{8,11},{9,10},{10,... | collective-permute-start | bytes 479240 | tf_op jit(solution)/shard_map/line attention grad/ppermute | solution.py:746
  244.5 11.4 %collective-permute-start.51 = (bf16[192,384]{1,0:T(8,128)(2,1)S(1)}, bf16[192,384]{1,0:T(8,128)(2,1)S(1)}, u32[]{:S(2)}, u32[]{:S(2)}) collective-permute-start(bf16[192,384]{1,0:T(8,128)(2,1)S(1)} %fusion.9), channel_id=1, source_target_pairs={{0,2},{1,3},{2,0},{3,1},{4,6},{5,7},{6,4},{7,5},{8,10},{9,11},{10,... | collective-permute-start | bytes 442376 | tf_op jit(solution)/shard_map/line two inner grad/ppermute | solution.py:746
  246.6 9.3 %collective-permute-start.52 = (bf16[192,384]{1,0:T(8,128)(2,1)S(1)}, bf16[192,384]{1,0:T(8,128)(2,1)S(1)}, u32[]{:S(2)}, u32[]{:S(2)}) collective-permute-start(bf16[192,384]{1,0:T(8,128)(2,1)S(1)} %fusion.10), channel_id=1, source_target_pairs={{0,1},{1,0},{2,3},{3,2},{4,5},{5,4},{6,7},{7,6},{8,9},{9,8},{10,11... | collective-permute-start | bytes 442376 | tf_op jit(solution)/shard_map/line pair outer grad/ppermute | solution.py:746
  248.1 27.4 %collective-permute-start.49 = (bf16[512,768]{1,0:T(8,128)(2,1)S(1)}, bf16[512,768]{1,0:T(8,128)(2,1)S(1)}, u32[]{:S(2)}, u32[]{:S(2)}) collective-permute-start(bf16[512,768]{1,0:T(8,128)(2,1)S(1)} %collective-permute-done.47), channel_id=1, source_target_pairs={{2,3},{6,7},{10,11},{14,15},{18,19},{22,23},{26,27},{30,31}} | collective-permute-start | bytes 2359304 | tf_op jit(solution)/shard_map/grad rows 3/ppermute | solution.py:760
  250.3 25.2 %collective-permute-start.50 = (bf16[512,768]{1,0:T(8,128)(2,1)S(1)}, bf16[512,768]{1,0:T(8,128)(2,1)S(1)}, u32[]{:S(2)}, u32[]{:S(2)}) collective-permute-start(bf16[512,768]{1,0:T(8,128)(2,1)S(1)} %collective-permute-done.48), channel_id=1, source_target_pairs={{1,0},{5,4},{9,8},{13,12},{17,16},{21,20},{25,24},{29,28}} | collective-permute-start | bytes 2359304 | tf_op jit(solution)/shard_map/grad rows 3/ppermute | solution.py:761
  256.2 13.4 %collective-permute-start.56 = (bf16[592,384]{1,0:T(8,128)(2,1)S(1)}, bf16[592,384]{1,0:T(8,128)(2,1)S(1)}, u32[]{:S(2)}, u32[]{:S(2)}) collective-permute-start(bf16[592,384]{1,0:T(8,128)(2,1)S(1)} %get-tuple-element.329), channel_id=1, source_target_pairs={{0,8},{4,12},{8,0},{12,4},{16,24},{20,28},{24,16},{28,20},{1,9},{5... | collective-permute-start | bytes 1363976 | tf_op jit(solution)/shard_map/plane result/ppermute | solution.py:743
  257.2 18.3 %collective-permute-start.57 = (bf16[592,384]{1,0:T(8,128)(2,1)S(1)}, bf16[592,384]{1,0:T(8,128)(2,1)S(1)}, u32[]{:S(2)}, u32[]{:S(2)}) collective-permute-start(bf16[592,384]{1,0:T(8,128)(2,1)S(1)} %get-tuple-element.329), channel_id=1, source_target_pairs={{0,16},{4,20},{8,24},{12,28},{16,0},{20,4},{24,8},{28,12},{1,17},{... | collective-permute-start | bytes 1363976 | tf_op jit(solution)/shard_map/plane result/ppermute | solution.py:743
  258.4 17.1 %collective-permute-start.58 = (bf16[592,384]{1,0:T(8,128)(2,1)S(1)}, bf16[592,384]{1,0:T(8,128)(2,1)S(1)}, u32[]{:S(2)}, u32[]{:S(2)}) collective-permute-start(bf16[592,384]{1,0:T(8,128)(2,1)S(1)} %get-tuple-element.329), channel_id=1, source_target_pairs={{0,24},{4,28},{8,16},{12,20},{16,8},{20,12},{24,0},{28,4},{1,25},{... | collective-permute-start | bytes 1363976 | tf_op jit(solution)/shard_map/plane result/ppermute | solution.py:743
  275.8 3.8 %collective-permute-start.59 = (bf16[4,592,384]{2,1,0:T(8,128)(2,1)S(1)}, bf16[4,592,384]{2,1,0:T(8,128)(2,1)S(1)}, u32[]{:S(2)}, u32[]{:S(2)}) collective-permute-start(bf16[4,592,384]{2,1,0:T(8,128)(2,1)S(1)} %pad_maximum_fusion.1.near_ref), channel_id=1, source_target_pairs={{0,4},{4,0},{8,12},{12,8},{16,20},{20,16},{24,28},{28,24},{1,5},{5... | collective-permute-start | bytes 5455880 | tf_op jit(solution)/shard_map/core result/ppermute | solution.py:743
  (42 other events, 284.5 us)
